TPU v7x, 32 devices: a whole 2x2x4 slice. The times are simulated.
32 devices in a mesh: section: 4 (over x, core), seq: 4 (over z), shard: 2 (over y).
Axes of the slice: x: 2, y: 2, z: 4, core: 2. Of those that a mesh axis runs over, the one named last changes fastest.
Arguments:
- frames: bfloat16 [2, 1536, 768], P(None, ('seq', 'shard')), may hold values from -6 to 6
- out_grad: bfloat16 [2, 1536, 768], P(None, ('seq', 'shard')), may hold values from -6 to 6
- norm_gain: bfloat16 [4, 2, 768], P('section', None, 'shard'), may hold values from 0.5 to 1.5
- norm_bias: bfloat16 [4, 2, 768], P('section', None, 'shard'), may hold values from -3 to 3
- w_qkv: bfloat16 [4, 768, 2304], P('section', 'shard'), may hold values from -0.20412415 to 0.20412415, as said below
- w_out: bfloat16 [4, 768, 768], P('section', 'shard'), may hold values from -0.4375 to 0.4375
- w_up: bfloat16 [4, 768, 3072], P('section', 'shard'), may hold values from -0.21875 to 0.21875
- w_down: bfloat16 [4, 3072, 768], P('section', 'shard'), may hold values from -0.109375 to 0.109375
- proj_bias: bfloat16 [4, 4, 768], P('section', None, 'shard'), may hold values from -1.5 to 1.5, as said below
- up_bias: bfloat16 [4, 3072], P('section', 'shard'), may hold values from -3 to 3
Outputs:
- hidden_states: bfloat16 [4, 2, 1536, 768], P('section', None, ('seq', 'shard'))
- input_grads: bfloat16 [4, 2, 1536, 768], P('section', None, ('seq', 'shard'))
- grad_norm_gain: float32 [4, 2, 768], P('section', None, 'shard')
- grad_norm_bias: float32 [4, 2, 768], P('section', None, 'shard')
- grad_qkv: float32 [4, 768, 2304], P('section', 'shard')
- grad_out: float32 [4, 768, 768], P('section', 'shard')
- grad_up: float32 [4, 768, 3072], P('section', 'shard')
- grad_down: float32 [4, 3072, 768], P('section', 'shard')
- grad_proj_bias: float32 [4, 4, 768], P('section', None, 'shard')
- grad_up_bias: float32 [4, 3072], P('section', 'shard')
Inputs may be any that keep to these rules, and one draw needn't show every extreme that they name: `w_qkv`: independent entries of mean 0. `proj_bias`: independent entries of mean 0.
All inputs are finite; a program needn't handle non-finite values.
Results may differ from a plain program's by a relative error of at most 0.02.
Values may be sent and summed in bfloat16 or wider, within the bound.
No kernel may reach another device: no remote copies, remote signals or barrier semaphores. Data moves between devices by JAX's collectives and lax.ppermute only.
A program may use at most 192 MiB of HBM per device.

v0:
```python
import math

import jax
import jax.numpy as jnp
from jax import lax
from jax.sharding import PartitionSpec as P

HEADS = 12


norm_eps = 1e-05


def from_behind(block, axis, distance):
    devices = range(lax.axis_size(axis))
    route = [(i - distance, i) for i in devices if i - distance in devices]
    return lax.ppermute(block, axis, route)


def layer_norm(values, gain_row, bias_row):
    center = values - jnp.mean(values, axis=-1, keepdims=True)
    inverse = lax.rsqrt(jnp.mean(center * center, axis=-1, keepdims=True) + norm_eps)
    scaled = center * inverse
    return (scaled, inverse, scaled * gain_row + bias_row)


def norm_back(upstream, scaled, inverse, gain_row):
    weighted = upstream * gain_row
    return inverse * (
        weighted
        - jnp.mean(weighted, axis=-1, keepdims=True)
        - scaled * jnp.mean(weighted * scaled, axis=-1, keepdims=True)
    )


def exact_gelu(values):
    return jax.nn.gelu(values, approximate=False)


def contract_rows(left_side, right_side):
    return lax.dot_general(
        left_side, right_side, (((0,), (0,)), ((), ())), preferred_element_type=jnp.float32
    )


def times_transpose(left_side, matrix):
    return lax.dot_general(
        left_side, matrix, (((1,), (1,)), ((), ())), preferred_element_type=jnp.float32
    )


def forward_layer(inputs, weights):
    norm_gains, shifts, mix_qkv, mix_out, mix_up, mix_down, proj_bias, up_bias = weights
    norm_gains = norm_gains.astype(jnp.float32)
    shifts = shifts.astype(jnp.float32)
    proj_bias = proj_bias.astype(jnp.float32)
    up_bias = up_bias.astype(jnp.float32)
    rows_local, model_width = inputs.shape
    groups = lax.axis_size("seq")
    head_span = model_width // groups
    heads_local = HEADS // groups
    head_size = model_width // HEADS
    score_scale = 1.0 / math.sqrt(head_size)
    residual = inputs.astype(jnp.float32)
    scaled_one, inverse_one, normed = layer_norm(residual, norm_gains[0], shifts[0])
    normed_one = normed.astype(jnp.bfloat16)
    qkv_bias = jnp.concatenate([proj_bias[0], jnp.zeros_like(proj_bias[0]), proj_bias[1]])
    projected = (
        jnp.dot(normed_one, mix_qkv, preferred_element_type=jnp.float32) + qkv_bias
    ).astype(jnp.bfloat16)
    by_heads = lax.all_to_all(
        projected.reshape(rows_local, 3, groups, head_span),
        "seq",
        split_axis=2,
        concat_axis=0,
        tiled=True,
    )
    query_rows = by_heads.shape[0]
    queries = by_heads[:, 0, 0]
    key_value = lax.all_gather(
        by_heads[:, 1:, 0].reshape(query_rows, 2 * head_span), "shard", axis=0, tiled=True
    )
    key_rows = key_value.shape[0]
    query_view = queries.reshape(query_rows, heads_local, head_size)
    key_view = key_value[:, :head_span].reshape(key_rows, heads_local, head_size)
    value_view = key_value[:, head_span:].reshape(key_rows, heads_local, head_size)
    scores = (
        jnp.einsum("qhe,khe->hqk", query_view, key_view, preferred_element_type=jnp.float32)
        * score_scale
    )
    top_score = jnp.max(scores, axis=-1, keepdims=True)
    exponent = jnp.exp(scores - top_score)
    row_total = jnp.sum(exponent, axis=-1, keepdims=True)
    log_total = top_score + jnp.log(row_total)
    attn_probs = (exponent / row_total).astype(jnp.bfloat16)
    attended = jnp.einsum(
        "hqk,khe->qhe", attn_probs, value_view, preferred_element_type=jnp.float32
    )
    attended = attended.astype(jnp.bfloat16).reshape(query_rows, 1, head_span)
    attended_tok = lax.all_to_all(attended, "seq", split_axis=0, concat_axis=1, tiled=True).reshape(
        rows_local, model_width
    )
    middle = (
        residual + jnp.dot(attended_tok, mix_out, preferred_element_type=jnp.float32) + proj_bias[2]
    )
    scaled_two, inverse_two, normed = layer_norm(middle, norm_gains[1], shifts[1])
    normed_two = normed.astype(jnp.bfloat16)
    upper_pre = jnp.dot(normed_two, mix_up, preferred_element_type=jnp.float32) + up_bias
    lifted = exact_gelu(upper_pre).astype(jnp.bfloat16)
    output = middle + jnp.dot(lifted, mix_down, preferred_element_type=jnp.float32) + proj_bias[3]
    kept_values = (
        scaled_one,
        inverse_one,
        normed_one,
        queries,
        key_value,
        log_total,
        attended_tok,
        scaled_two,
        inverse_two,
        normed_two,
        upper_pre,
        lifted,
    )
    return (output.astype(jnp.bfloat16), kept_values)


def backward_layer(kept_values, upstream, weights):
    (
        scaled_one,
        inverse_one,
        normed_one,
        queries,
        key_value,
        log_total,
        attended_tok,
        scaled_two,
        inverse_two,
        normed_two,
        upper_pre,
        lifted,
    ) = kept_values
    norm_gains, shifts, mix_qkv, mix_out, mix_up, mix_down, proj_bias, up_bias = weights
    norm_gains = norm_gains.astype(jnp.float32)
    rows_local, model_width = attended_tok.shape
    groups = lax.axis_size("seq")
    head_span = model_width // groups
    heads_local = HEADS // groups
    head_size = model_width // HEADS
    score_scale = 1.0 / math.sqrt(head_size)
    flow_grad = upstream.astype(jnp.float32)
    grad_down = contract_rows(lifted, upstream)
    grad_lifted = times_transpose(upstream, mix_down)
    unused_value, gelu_pull = jax.vjp(exact_gelu, upper_pre)
    grad_upper = gelu_pull(grad_lifted)[0].astype(jnp.bfloat16)
    grad_up = contract_rows(normed_two, grad_upper)
    grad_normed_two = times_transpose(grad_upper, mix_up)
    grad_middle = flow_grad + norm_back(grad_normed_two, scaled_two, inverse_two, norm_gains[1])
    grad_branch = grad_middle.astype(jnp.bfloat16)
    grad_out = contract_rows(attended_tok, grad_branch)
    grad_attended = times_transpose(grad_branch, mix_out).astype(jnp.bfloat16)
    grad_heads = lax.all_to_all(
        grad_attended.reshape(rows_local, groups, head_span),
        "seq",
        split_axis=1,
        concat_axis=0,
        tiled=True,
    )
    query_rows = grad_heads.shape[0]
    key_rows = key_value.shape[0]
    grad_view = grad_heads.reshape(query_rows, heads_local, head_size)
    query_view = queries.reshape(query_rows, heads_local, head_size)
    key_view = key_value[:, :head_span].reshape(key_rows, heads_local, head_size)
    value_view = key_value[:, head_span:].reshape(key_rows, heads_local, head_size)
    scores = (
        jnp.einsum("qhe,khe->hqk", query_view, key_view, preferred_element_type=jnp.float32)
        * score_scale
    )
    attn_probs = jnp.exp(scores - log_total)
    grad_probs = jnp.einsum(
        "qhe,khe->hqk", grad_view, value_view, preferred_element_type=jnp.float32
    )
    row_term = jnp.sum(attn_probs * grad_probs, axis=-1, keepdims=True)
    grad_scores = (attn_probs * (grad_probs - row_term)).astype(jnp.bfloat16)
    grad_query = (
        jnp.einsum("hqk,khe->qhe", grad_scores, key_view, preferred_element_type=jnp.float32)
        * score_scale
    )
    grad_value = jnp.einsum(
        "hqk,qhe->khe",
        attn_probs.astype(jnp.bfloat16),
        grad_view,
        preferred_element_type=jnp.float32,
    )
    grad_key = (
        jnp.einsum("hqk,qhe->khe", grad_scores, query_view, preferred_element_type=jnp.float32)
        * score_scale
    )
    pair_grads = jnp.concatenate(
        [grad_key.reshape(key_rows, head_span), grad_value.reshape(key_rows, head_span)], axis=1
    )
    own_grads = lax.psum_scatter(
        pair_grads.astype(jnp.bfloat16), "shard", scatter_dimension=0, tiled=True
    ).astype(jnp.float32)
    grad_projected = jnp.concatenate([grad_query.reshape(query_rows, head_span), own_grads], axis=1)
    grad_projected = grad_projected.astype(jnp.bfloat16).reshape(query_rows, 3, 1, head_span)
    grad_tokens = lax.all_to_all(
        grad_projected, "seq", split_axis=0, concat_axis=2, tiled=True
    ).reshape(rows_local, 3 * model_width)
    grad_qkv = contract_rows(normed_one, grad_tokens)
    grad_normed_one = times_transpose(grad_tokens, mix_qkv)
    grad_inputs = grad_middle + norm_back(grad_normed_one, scaled_one, inverse_one, norm_gains[0])
    token_sums = jnp.sum(grad_tokens.astype(jnp.float32), axis=0)
    grad_gain = jnp.stack(
        [
            jnp.sum(grad_normed_one * scaled_one, axis=0),
            jnp.sum(grad_normed_two * scaled_two, axis=0),
        ]
    )
    grad_shift = jnp.stack([jnp.sum(grad_normed_one, axis=0), jnp.sum(grad_normed_two, axis=0)])
    grad_bias = jnp.stack(
        [
            token_sums[:model_width],
            token_sums[2 * model_width :],
            jnp.sum(grad_branch.astype(jnp.float32), axis=0),
            jnp.sum(flow_grad, axis=0),
        ]
    )
    grad_up_bias = jnp.sum(grad_upper.astype(jnp.float32), axis=0)
    grads_now = (
        grad_gain,
        grad_shift,
        grad_qkv,
        grad_out,
        grad_up,
        grad_down,
        grad_bias,
        grad_up_bias,
    )
    return (grad_inputs.astype(jnp.bfloat16), grads_now)


def take_row(buffer, index_now):
    return lax.dynamic_index_in_dim(buffer, index_now, 0, keepdims=False)


def put_row(buffer, update, index_now, active):
    previous = take_row(buffer, index_now)
    return lax.dynamic_update_index_in_dim(
        buffer, jnp.where(active, update, previous), index_now, 0
    )


def per_device(
    frames, out_grad, norm_gain, norm_bias, w_qkv, w_out, w_up, w_down, proj_bias, up_bias
):
    gathered = (
        lax.all_gather(norm_gain, "shard", axis=2, tiled=True),
        lax.all_gather(norm_bias, "shard", axis=2, tiled=True),
        lax.all_gather(w_qkv, "shard", axis=1, tiled=True),
        lax.all_gather(w_out, "shard", axis=1, tiled=True),
        lax.all_gather(w_up, "shard", axis=1, tiled=True),
        lax.all_gather(w_down, "shard", axis=1, tiled=True),
        lax.all_gather(proj_bias, "shard", axis=2, tiled=True),
        lax.all_gather(up_bias, "shard", axis=1, tiled=True),
    )
    weights = tuple((member[0] for member in gathered))
    sections = lax.axis_size("section")
    position = lax.axis_index("section")
    groups = lax.axis_size("seq")
    sharded = lax.axis_size("shard")
    micro_count, rows_local, model_width = frames.shape
    query_rows = rows_local * groups
    key_rows = query_rows * sharded
    heads_local = HEADS // groups
    head_span = model_width // groups
    hidden_width = w_up.shape[2]
    steps_total = micro_count + sections - 1
    stored = (
        jnp.zeros((micro_count, rows_local, model_width), jnp.float32),
        jnp.zeros((micro_count, rows_local, 1), jnp.float32),
        jnp.zeros((micro_count, rows_local, model_width), jnp.bfloat16),
        jnp.zeros((micro_count, query_rows, head_span), jnp.bfloat16),
        jnp.zeros((micro_count, key_rows, 2 * head_span), jnp.bfloat16),
        jnp.zeros((micro_count, heads_local, query_rows, 1), jnp.float32),
        jnp.zeros((micro_count, rows_local, model_width), jnp.bfloat16),
        jnp.zeros((micro_count, rows_local, model_width), jnp.float32),
        jnp.zeros((micro_count, rows_local, 1), jnp.float32),
        jnp.zeros((micro_count, rows_local, model_width), jnp.bfloat16),
        jnp.zeros((micro_count, rows_local, hidden_width), jnp.float32),
        jnp.zeros((micro_count, rows_local, hidden_width), jnp.bfloat16),
    )

    def forward_step(step_now, loop_state):
        incoming, hidden, stored = loop_state
        index_now = step_now - position
        active = (index_now >= 0) & (index_now < micro_count)
        clipped = jnp.clip(index_now, 0, micro_count - 1)
        inputs = jnp.where(position == 0, take_row(frames, clipped), incoming)
        output, kept_values = forward_layer(inputs, weights)
        hidden = put_row(hidden, output, clipped, active)
        stored = tuple(
            (
                put_row(buffer, member, clipped, active)
                for buffer, member in zip(stored, kept_values)
            )
        )
        incoming = from_behind(output, "section", 1)
        return (incoming, hidden, stored)

    unused_last, hidden, stored = lax.fori_loop(
        0, steps_total, forward_step, (jnp.zeros_like(frames[0]), jnp.zeros_like(frames), stored)
    )

    def backward_step(step_now, loop_state):
        incoming, totals, input_grads = loop_state
        index_now = step_now - (sections - 1 - position)
        active = (index_now >= 0) & (index_now < micro_count)
        clipped = jnp.clip(index_now, 0, micro_count - 1)
        upstream = jnp.where(position == sections - 1, take_row(out_grad, clipped), incoming)
        upstream = jnp.where(active, upstream, jnp.zeros_like(upstream))
        kept_values = tuple((take_row(buffer, clipped) for buffer in stored))
        grad_inputs, grads_now = backward_layer(kept_values, upstream, weights)
        totals = tuple((total_one + grad_one for total_one, grad_one in zip(totals, grads_now)))
        input_grads = put_row(input_grads, grad_inputs, clipped, active)
        incoming = from_behind(grad_inputs, "section", -1)
        return (incoming, totals, input_grads)

    zero_grads = tuple((jnp.zeros(member.shape, jnp.float32) for member in weights))
    unused_first, totals, input_grads = lax.fori_loop(
        0,
        steps_total,
        backward_step,
        (jnp.zeros_like(frames[0]), zero_grads, jnp.zeros_like(frames)),
    )
    expanded = tuple((member[None] for member in totals))
    scattered = (
        lax.psum_scatter(
            expanded[0].astype(jnp.bfloat16), "shard", scatter_dimension=2, tiled=True
        ).astype(jnp.float32),
        lax.psum_scatter(
            expanded[1].astype(jnp.bfloat16), "shard", scatter_dimension=2, tiled=True
        ).astype(jnp.float32),
        lax.psum_scatter(
            expanded[2].astype(jnp.bfloat16), "shard", scatter_dimension=1, tiled=True
        ).astype(jnp.float32),
        lax.psum_scatter(
            expanded[3].astype(jnp.bfloat16), "shard", scatter_dimension=1, tiled=True
        ).astype(jnp.float32),
        lax.psum_scatter(
            expanded[4].astype(jnp.bfloat16), "shard", scatter_dimension=1, tiled=True
        ).astype(jnp.float32),
        lax.psum_scatter(
            expanded[5].astype(jnp.bfloat16), "shard", scatter_dimension=1, tiled=True
        ).astype(jnp.float32),
        lax.psum_scatter(
            expanded[6].astype(jnp.bfloat16), "shard", scatter_dimension=2, tiled=True
        ).astype(jnp.float32),
        lax.psum_scatter(
            expanded[7].astype(jnp.bfloat16), "shard", scatter_dimension=1, tiled=True
        ).astype(jnp.float32),
    )
    reduced = (
        lax.psum(scattered[0].astype(jnp.bfloat16), "seq").astype(jnp.float32),
        lax.psum(scattered[1].astype(jnp.bfloat16), "seq").astype(jnp.float32),
        lax.psum(scattered[2].astype(jnp.bfloat16), "seq").astype(jnp.float32),
        lax.psum(scattered[3].astype(jnp.bfloat16), "seq").astype(jnp.float32),
        lax.psum(scattered[4].astype(jnp.bfloat16), "seq").astype(jnp.float32),
        lax.psum(scattered[5].astype(jnp.bfloat16), "seq").astype(jnp.float32),
        lax.psum(scattered[6].astype(jnp.bfloat16), "seq").astype(jnp.float32),
        lax.psum(scattered[7].astype(jnp.bfloat16), "seq").astype(jnp.float32),
    )
    return (
        hidden[None],
        input_grads[None],
        reduced[0],
        reduced[1],
        reduced[2],
        reduced[3],
        reduced[4],
        reduced[5],
        reduced[6],
        reduced[7],
    )


def solution(mesh):
    placed = (
        P(None, ("seq", "shard"), None),
        P(None, ("seq", "shard"), None),
        P("section", None, "shard"),
        P("section", None, "shard"),
        P("section", "shard", None),
        P("section", "shard", None),
        P("section", "shard", None),
        P("section", "shard", None),
        P("section", None, "shard"),
        P("section", "shard"),
    )
    return jax.shard_map(
        per_device,
        mesh=mesh,
        in_specs=placed,
        out_specs=(
            P("section", None, ("seq", "shard"), None),
            P("section", None, ("seq", "shard"), None),
            P("section", None, "shard"),
            P("section", None, "shard"),
            P("section", "shard", None),
            P("section", "shard", None),
            P("section", "shard", None),
            P("section", "shard", None),
            P("section", None, "shard"),
            P("section", "shard"),
        ),
        check_vma=False,
    )
```

profile of v0, /device:TPU:0, one launch (start us, length us, event | category | flops | bytes accessed | tf_op | source)
XLA Modules:
  0.0 2209.5 jit_solution(1147208831487019051)
XLA Ops:
  35.2 50.9 %all-gather.6.cloned.1.call-done = bf16[1,768,2304]{2,1,0:T(8,128)(2,1)} async-done(((bf16[1,384,2304]{2,1,0:T(8,128)(2,1)}), bf16[1,768,2304]{2,1,0:T(8,128)(2,1)}) %all-gather.6.cloned.1.call-update) | async-done | bytes 3538960 | tf_op jit(solution)/shard_map/all_gather | solution.py:260
  86.1 64.2 %all-gather.10.cloned.1.call-done = bf16[1,768,3072]{2,1,0:T(8,128)(2,1)} async-done(((bf16[1,384,3072]{2,1,0:T(8,128)(2,1)}), bf16[1,768,3072]{2,1,0:T(8,128)(2,1)}) %all-gather.10.cloned.1.call-update) | async-done | bytes 4718608 | tf_op jit(solution)/shard_map/all_gather | solution.py:262
  150.3 64.1 %all-gather.12.cloned.1.call-done = bf16[1,3072,768]{2,1,0:T(8,128)(2,1)} async-done(((bf16[1,1536,768]{2,1,0:T(8,128)(2,1)}), bf16[1,3072,768]{2,1,0:T(8,128)(2,1)}) %all-gather.12.cloned.1.call-update) | async-done | bytes 4718608 | tf_op jit(solution)/shard_map/all_gather | solution.py:263
  227.6 699.4 %while.74 = (s32[]{:T(128)}, bf16[192,768]{1,0:T(8,128)(2,1)}, bf16[2,192,768]{2,1,0:T(8,128)(2,1)S(1)}, f32[2,192,768]{2,1,0:T(8,128)}, f32[2,192,1]{1,2,0:T(1,...) while((s32[]{:T(128)}, bf16[192,768]{1,0:T(8,128)(2,1)}, ...), condition=%wide.region_7.8_spmd, body=%wide.region_0.7_spmd.sunk | while | flops 3704994304 | bytes 237147088 | solution.py:311
  254.8 19.3 all-to-all-done
  283.3 14.9 all-gather.14.cloned.1.call-done
  394.6 20.0 all-to-all-done
  423.9 13.9 all-gather.14.cloned.1.call-done
  534.3 20.0 all-to-all-done
  563.6 13.9 all-gather.14.cloned.1.call-done
  674.0 20.0 all-to-all-done
  703.3 13.9 all-gather.14.cloned.1.call-done
  813.6 20.0 all-to-all-done
  842.9 13.9 all-gather.14.cloned.1.call-done
  928.7 751.0 %while.75 = (s32[]{:T(128)}, bf16[192,768]{1,0:T(8,128)(2,1)}, f32[2,768]{1,0:T(2,128)}, f32[2,768]{1,0:T(2,128)}, f32[768,2304]{1,0:T(8,128)}, /*index=5*/f32[7...) while((s32[]{:T(128)}, bf16[192,768]{1,0:T(8,128)(2,1)}, ...), condition=%wide.region_23.24_spmd.clone, body=%wide.region_8.23_spmd.clone.sunk | while | flops 7812975616 | bytes 371793600 | solution.py:330
  1015.0 9.6 reduce-scatter.34.cloned.1.call-done
  1045.0 24.6 %all-to-all-done.3 = bf16[768,3,1,192]{3,1,2,0:T(4,128)(2,1)S(1)} async-done(((bf16[768,3,1,192]{3,1,2,0:T(4,128)(2,1)}), bf16[768,3,1,192]{3,1,2,0:T(4,128)(2,1)S(1)}, u32[]{:S(2)}, u32[]{:S(2)}) %all-to-all-start.3) | async-done | bytes 884768 | tf_op jit(solution)/shard_map/while/body/eval_jaxpr/all_to_all | solution.py:207
  1177.3 9.1 select_add_fusion.13
  1195.2 19.0 all-to-all-done.3
  1343.0 19.0 all-to-all-done.3
  1490.9 19.0 all-to-all-done.3
  1620.7 9.1 select_add_fusion.13
  1638.7 19.0 all-to-all-done.3
  1707.1 47.9 %reduce-scatter.18.cloned.1.call-done = bf16[1,384,2304]{2,1,0:T(8,128)(2,1)} async-done(((bf16[1,768,2304]{2,1,0:T(8,128)(2,1)}), bf16[1,384,2304]{2,1,0:T(8,128)(2,1)}) %reduce-scatter.18.cloned.1.call-update) | async-done | bytes 1769488 | tf_op jit(solution)/shard_map/reduce_scatter | solution.py:344
  1754.9 62.8 %reduce-scatter.22.cloned.1.call-done = bf16[1,384,3072]{2,1,0:T(8,128)(2,1)} async-done(((bf16[1,768,3072]{2,1,0:T(8,128)(2,1)}), bf16[1,384,3072]{2,1,0:T(8,128)(2,1)}) %reduce-scatter.22.cloned.1.call-update) | async-done | bytes 2359312 | tf_op jit(solution)/shard_map/reduce_scatter | solution.py:350
  1817.7 62.9 %reduce-scatter.24.cloned.1.call-done = bf16[1,1536,768]{2,1,0:T(8,128)(2,1)} async-done(((bf16[1,3072,768]{2,1,0:T(8,128)(2,1)}), bf16[1,1536,768]{2,1,0:T(8,128)(2,1)}) %reduce-scatter.24.cloned.1.call-update) | async-done | bytes 2359312 | tf_op jit(solution)/shard_map/reduce_scatter | solution.py:353
  1880.6 13.2 reduce-scatter.28.cloned.1.call-done
  1894.9 12.0 reduce-scatter.26.cloned.1.call-done
  1908.0 12.1 reduce-scatter.30.cloned.1.call-done
  1921.2 18.6 reduce-scatter.32.cloned.1.call-done
  1941.0 23.1 %all-reduce = (bf16[1,2,384]{2,1,0:T(2,128)(2,1)S(1)}, bf16[1,2,384]{2,1,0:T(2,128)(2,1)S(1)}, bf16[1,4,384]{2,1,0:T(4,128)(2,1)S(1)}, bf16[1,1536]{1,0:T(2,128)(2,1)S(1)}) all-reduce(bf16[1,2,384]{2,1,0:T(2,128)(2,1)S(1)} %copy.94, bf16[1,2,384]{2,1,0:T(2,128)(2,1)S(1)} %copy.96, ...), channel_id=1, replica_groups=mesh['section'=4,'seq'=4,'shard'=2] {'seq'}, use_global_device_ids=true, to_apply=%region_25.26 | all-reduce | flops 4608 | bytes 18432 | tf_op jit(solution)/shard_map/psum | solution.py:364
  1966.4 225.7 %all-reduce.4.cloned.1.call-done = (bf16[1,384,2304]{2,1,0:T(8,128)(2,1)}, bf16[1,384,768]{2,1,0:T(8,128)(2,1)}, bf16[1,384,3072]{2,1,0:T(8,128)(2,1)}, bf16[1,1536,768]{2,1,0:T(8,128)(2,1)}) async-done(((bf16[1,384,2304]{2,1,0:T(8,128)(2,1)}, bf16[1,384,768]{2,1,0:T(8,128)(2,1)}, bf16[1,384,3072]{2,1,0:T(8,128)(2,1)}, bf16[1,1536,768]{2,1,0:T(8,128)(2,1)}), (bf16[1,384,2304]{2,1,0:T(8,128)(2,1)}, ...) | async-done | bytes 7077904 | tf_op jit(solution)/shard_map/psum | solution.py:366
  (1467 shorter events, 1217.6 us)
Async XLA Ops:
  7.2 28.0 %all-gather.8.cloned.1.call-start = ((), (), s32[]{:S(2)}) async-start(), calls=%async_computation.14 | async-start | bytes 1769472 | tf_op jit(solution)/shard_map/all_gather | solution.py:261
  7.9 78.2 %all-gather.6.cloned.1.call-start = ((), (), s32[]{:S(2)}) async-start(), calls=%async_computation.13 | async-start | bytes 5308416 | tf_op jit(solution)/shard_map/all_gather | solution.py:260
  8.7 141.6 %all-gather.10.cloned.1.call-start = ((), (), s32[]{:S(2)}) async-start(), calls=%async_computation.15 | async-start | bytes 7077888 | tf_op jit(solution)/shard_map/all_gather | solution.py:262
  9.4 205.0 %all-gather.12.cloned.1.call-start = ((), (), s32[]{:S(2)}) async-start(), calls=%async_computation.16 | async-start | bytes 7077888 | tf_op jit(solution)/shard_map/all_gather | solution.py:263
  240.9 33.2 %all-to-all-start = ((bf16[192,3,4,192]{3,0,1,2:T(8,128)(2,1)}), bf16[192,3,4,192]{3,0,1,2:T(8,128)(2,1)S(1)}, u32[]{:S(2)}, u32[]{:S(2)}) async-start(bf16[192,3,4,192]{3,0,1,2:T(8,128)(2,1)} %copy.124), calls=%async_computation | async-start | bytes 2359296 | tf_op jit(solution)/shard_map/while/body/eval_jaxpr/all_to_all | solution.py:71
  245.5 52.7 %all-gather.14.cloned.1.call-start = ((), (), s32[]{:S(2)}) async-start(), calls=%async_computation.26 | async-start | bytes 1769472 | tf_op jit(solution)/shard_map/while/body/eval_jaxpr/all_gather | solution.py:80
  381.7 32.9 %all-to-all-start = ((bf16[192,3,4,192]{3,0,1,2:T(8,128)(2,1)}), bf16[192,3,4,192]{3,0,1,2:T(8,128)(2,1)S(1)}, u32[]{:S(2)}, u32[]{:S(2)}) async-start(bf16[192,3,4,192]{3,0,1,2:T(8,128)(2,1)} %copy.124), calls=%async_computation | async-start | bytes 2359296 | tf_op jit(solution)/shard_map/while/body/eval_jaxpr/all_to_all | solution.py:71
  385.3 52.6 %all-gather.14.cloned.1.call-start = ((), (), s32[]{:S(2)}) async-start(), calls=%async_computation.26 | async-start | bytes 1769472 | tf_op jit(solution)/shard_map/while/body/eval_jaxpr/all_gather | solution.py:80
  521.4 32.9 %all-to-all-start = ((bf16[192,3,4,192]{3,0,1,2:T(8,128)(2,1)}), bf16[192,3,4,192]{3,0,1,2:T(8,128)(2,1)S(1)}, u32[]{:S(2)}, u32[]{:S(2)}) async-start(bf16[192,3,4,192]{3,0,1,2:T(8,128)(2,1)} %copy.124), calls=%async_computation | async-start | bytes 2359296 | tf_op jit(solution)/shard_map/while/body/eval_jaxpr/all_to_all | solution.py:71
  524.9 52.6 %all-gather.14.cloned.1.call-start = ((), (), s32[]{:S(2)}) async-start(), calls=%async_computation.26 | async-start | bytes 1769472 | tf_op jit(solution)/shard_map/while/body/eval_jaxpr/all_gather | solution.py:80
  661.1 32.9 %all-to-all-start = ((bf16[192,3,4,192]{3,0,1,2:T(8,128)(2,1)}), bf16[192,3,4,192]{3,0,1,2:T(8,128)(2,1)S(1)}, u32[]{:S(2)}, u32[]{:S(2)}) async-start(bf16[192,3,4,192]{3,0,1,2:T(8,128)(2,1)} %copy.124), calls=%async_computation | async-start | bytes 2359296 | tf_op jit(solution)/shard_map/while/body/eval_jaxpr/all_to_all | solution.py:71
  664.6 52.6 %all-gather.14.cloned.1.call-start = ((), (), s32[]{:S(2)}) async-start(), calls=%async_computation.26 | async-start | bytes 1769472 | tf_op jit(solution)/shard_map/while/body/eval_jaxpr/all_gather | solution.py:80
  800.7 32.9 %all-to-all-start = ((bf16[192,3,4,192]{3,0,1,2:T(8,128)(2,1)}), bf16[192,3,4,192]{3,0,1,2:T(8,128)(2,1)S(1)}, u32[]{:S(2)}, u32[]{:S(2)}) async-start(bf16[192,3,4,192]{3,0,1,2:T(8,128)(2,1)} %copy.124), calls=%async_computation | async-start | bytes 2359296 | tf_op jit(solution)/shard_map/while/body/eval_jaxpr/all_to_all | solution.py:71
  804.3 52.6 %all-gather.14.cloned.1.call-start = ((), (), s32[]{:S(2)}) async-start(), calls=%async_computation.26 | async-start | bytes 1769472 | tf_op jit(solution)/shard_map/while/body/eval_jaxpr/all_gather | solution.py:80
  964.1 60.5 %reduce-scatter.34.cloned.1.call-start = ((), (), s32[]{:S(2)}) async-start(), calls=%async_computation.27 | async-start | bytes 1769472 | tf_op jit(solution)/shard_map/while/body/eval_jaxpr/reduce_scatter | solution.py:202
  1028.0 41.6 %all-to-all-start.3 = ((bf16[768,3,1,192]{3,1,2,0:T(4,128)(2,1)}), bf16[768,3,1,192]{3,1,2,0:T(4,128)(2,1)S(1)}, u32[]{:S(2)}, u32[]{:S(2)}) async-start(bf16[768,3,1,192]{3,1,2,0:T(4,128)(2,1)} %copy.131), calls=%async_computation.4 | async-start | bytes 3145728 | tf_op jit(solution)/shard_map/while/body/eval_jaxpr/all_to_all | solution.py:207
  1108.2 61.1 %reduce-scatter.34.cloned.1.call-start = ((), (), s32[]{:S(2)}) async-start(), calls=%async_computation.27 | async-start | bytes 1769472 | tf_op jit(solution)/shard_map/while/body/eval_jaxpr/reduce_scatter | solution.py:202
  1172.7 41.6 %all-to-all-start.3 = ((bf16[768,3,1,192]{3,1,2,0:T(4,128)(2,1)}), bf16[768,3,1,192]{3,1,2,0:T(4,128)(2,1)S(1)}, u32[]{:S(2)}, u32[]{:S(2)}) async-start(bf16[768,3,1,192]{3,1,2,0:T(4,128)(2,1)} %copy.131), calls=%async_computation.4 | async-start | bytes 3145728 | tf_op jit(solution)/shard_map/while/body/eval_jaxpr/all_to_all | solution.py:207
  1255.9 61.2 %reduce-scatter.34.cloned.1.call-start = ((), (), s32[]{:S(2)}) async-start(), calls=%async_computation.27 | async-start | bytes 1769472 | tf_op jit(solution)/shard_map/while/body/eval_jaxpr/reduce_scatter | solution.py:202
  1320.5 41.5 %all-to-all-start.3 = ((bf16[768,3,1,192]{3,1,2,0:T(4,128)(2,1)}), bf16[768,3,1,192]{3,1,2,0:T(4,128)(2,1)S(1)}, u32[]{:S(2)}, u32[]{:S(2)}) async-start(bf16[768,3,1,192]{3,1,2,0:T(4,128)(2,1)} %copy.131), calls=%async_computation.4 | async-start | bytes 3145728 | tf_op jit(solution)/shard_map/while/body/eval_jaxpr/all_to_all | solution.py:207
  1403.8 61.2 %reduce-scatter.34.cloned.1.call-start = ((), (), s32[]{:S(2)}) async-start(), calls=%async_computation.27 | async-start | bytes 1769472 | tf_op jit(solution)/shard_map/while/body/eval_jaxpr/reduce_scatter | solution.py:202
  1468.3 41.6 %all-to-all-start.3 = ((bf16[768,3,1,192]{3,1,2,0:T(4,128)(2,1)}), bf16[768,3,1,192]{3,1,2,0:T(4,128)(2,1)S(1)}, u32[]{:S(2)}, u32[]{:S(2)}) async-start(bf16[768,3,1,192]{3,1,2,0:T(4,128)(2,1)} %copy.131), calls=%async_computation.4 | async-start | bytes 3145728 | tf_op jit(solution)/shard_map/while/body/eval_jaxpr/all_to_all | solution.py:207
  1551.6 61.2 %reduce-scatter.34.cloned.1.call-start = ((), (), s32[]{:S(2)}) async-start(), calls=%async_computation.27 | async-start | bytes 1769472 | tf_op jit(solution)/shard_map/while/body/eval_jaxpr/reduce_scatter | solution.py:202
  1616.1 41.5 %all-to-all-start.3 = ((bf16[768,3,1,192]{3,1,2,0:T(4,128)(2,1)}), bf16[768,3,1,192]{3,1,2,0:T(4,128)(2,1)S(1)}, u32[]{:S(2)}, u32[]{:S(2)}) async-start(bf16[768,3,1,192]{3,1,2,0:T(4,128)(2,1)} %copy.131), calls=%async_computation.4 | async-start | bytes 3145728 | tf_op jit(solution)/shard_map/while/body/eval_jaxpr/all_to_all | solution.py:207
  1682.6 72.3 %reduce-scatter.18.cloned.1.call-start = ((), (), s32[]{:S(2)}) async-start(), calls=%async_computation.17 | async-start | bytes 5308416 | tf_op jit(solution)/shard_map/reduce_scatter | solution.py:344
  1687.8 129.9 %reduce-scatter.22.cloned.1.call-start = ((), (), s32[]{:S(2)}) async-start(), calls=%async_computation.19 | async-start | bytes 7077888 | tf_op jit(solution)/shard_map/reduce_scatter | solution.py:350
  1694.8 185.8 %reduce-scatter.24.cloned.1.call-start = ((), (), s32[]{:S(2)}) async-start(), calls=%async_computation.20 | async-start | bytes 7077888 | tf_op jit(solution)/shard_map/reduce_scatter | solution.py:353
  1701.2 192.5 %reduce-scatter.28.cloned.1.call-start = ((), (), s32[]{:S(2)}) async-start(), calls=%async_computation.22 | async-start | bytes 294912
  1703.1 203.8 %reduce-scatter.26.cloned.1.call-start = ((), (), s32[]{:S(2)}) async-start(), calls=%async_computation.21 | async-start | bytes 294912
  1704.3 215.8 %reduce-scatter.30.cloned.1.call-start = ((), (), s32[]{:S(2)}) async-start(), calls=%async_computation.23 | async-start | bytes 294912
  1705.6 234.2 %reduce-scatter.32.cloned.1.call-start = ((), (), s32[]{:S(2)}) async-start(), calls=%async_computation.24 | async-start | bytes 1179648
  1707.0 485.1 %all-reduce.4.cloned.1.call-start = ((), (), s32[]{:S(2)}) async-start(), calls=%async_computation.25 | async-start | bytes 14155776 | tf_op jit(solution)/shard_map/psum | solution.py:366
  (393 other events, 3110.6 us)
Sparse Core Ops, SparseCore 0:
  9.6 25.5 all-gather.7
  36.7 49.3 all-gather.5
  87.6 62.6 all-gather.9
  151.7 62.6 all-gather.11
  277.2 20.9 all-gather.13
  417.7 20.0 all-gather.13
  557.4 20.0 all-gather.13
  697.1 20.0 all-gather.13
  836.7 20.0 all-gather.13
  1004.4 20.2 reduce-scatter.33
  1148.1 21.2 reduce-scatter.33
  1296.5 20.5 reduce-scatter.33
  1444.3 20.5 reduce-scatter.33
  1592.2 20.5 reduce-scatter.33
  1683.1 21.3 reduce-scatter.19
  1707.2 47.6 reduce-scatter.17
  1757.7 59.9 reduce-scatter.21
  1820.5 59.9 reduce-scatter.23
  1882.8 10.9 reduce-scatter.27
  1895.9 10.9 reduce-scatter.25
  1909.1 10.9 reduce-scatter.29
  1922.3 17.4 reduce-scatter.31
  1942.6 249.4 all-reduce.3
where the time goes:
time: 2230 us; the launch traced here: 2210 us
  waiting for transfers between devices  1010 us (45%)
  matrix products  495 us (22%)
  local copies, waits for them, and re-layouts  304 us (14%)
  other arithmetic  227 us (10%)
  starting transfers between devices  99.4 us (4%)
  blocking collectives  41.7 us (2%)
    psum x1, waiting for transfers between devices, per_device(): lax.psum(scattered[2].astype(jnp.bfloat16), 'seq').astype(jnp.float32)  226 us
    dot_general x20, matrix products, contract_rows(): lax.dot_general(left_side, right_side, (((0,), (0,)), ((), ())), preferre...  134 us
    all_to_all x5, waiting for transfers between devices, backward_layer(): lax.all_to_all(grad_projected, 'seq', split_axis=0, concat_axis=2, tiled=...  101 us
    all_to_all x5, waiting for transfers between devices, forward_layer(): lax.all_to_all(projected.reshape(rows_local, 3, groups, head_span), 'seq'...  99.3 us
    dot_general x20, matrix products, times_transpose(): lax.dot_general(left_side, matrix, (((1,), (1,)), ((), ())), preferred_el...  74 us
    all_gather x5, waiting for transfers between devices, forward_layer(): lax.all_gather(by_heads[:, 1:, 0].reshape(query_rows, 2 * head_span), 'sh...  70.5 us
    all_gather x1, waiting for transfers between devices, per_device(): lax.all_gather(w_up, 'shard', axis=1, tiled=True)  64.2 us
    all_gather x1, waiting for transfers between devices, per_device(): lax.all_gather(w_down, 'shard', axis=1, tiled=True)  64.1 us
  transfers between devices with their start and end apart: 53, of which 42 were waited for; matrix products, arithmetic and copies ran while one was open for 16% of the time, Pallas kernels for 0%

commit v1 on v0

v1 whole, which is shorter than its diff:
```python
import math

import jax
import jax.numpy as jnp
from jax import lax
from jax.experimental import pallas as pl
from jax.experimental.pallas import tpu as pltpu
from jax.sharding import Mesh
from jax.sharding import PartitionSpec as P

HEADS = 12
norm_eps = 1e-05
F32 = jnp.float32
BF16 = jnp.bfloat16
VMEM_LIMIT = 56 * 1024 * 1024
AXES = ("pair", "core", "half", "quad", "side", "rest")
HEAD_GROUPS = 4


def call(body, out_shapes, grid=None, in_specs=None, out_specs=None, scratch=(), flops=0, moved=0):
    extra = {} if grid is None else dict(grid=grid, in_specs=in_specs, out_specs=out_specs)
    return pl.pallas_call(
        body,
        out_shape=out_shapes,
        scratch_shapes=scratch,
        compiler_params=pltpu.CompilerParams(vmem_limit_bytes=VMEM_LIMIT),
        cost_estimate=pl.CostEstimate(flops=flops, bytes_accessed=moved, transcendentals=0),
        **extra,
    )


def dot(left, right):
    return jnp.dot(left, right, preferred_element_type=F32)


def dot_t(left, right):
    return lax.dot_general(left, right, (((1,), (1,)), ((), ())), preferred_element_type=F32)


def t_dot(left, right):
    return lax.dot_general(left, right, (((0,), (0,)), ((), ())), preferred_element_type=F32)


def norm_parts(values):
    center = values - jnp.mean(values, axis=-1, keepdims=True)
    inverse = lax.rsqrt(jnp.mean(center * center, axis=-1, keepdims=True) + norm_eps)
    return center * inverse, inverse


def norm_back(upstream, scaled, inverse, gain_row):
    weighted = upstream * gain_row
    return inverse * (
        weighted
        - jnp.mean(weighted, axis=-1, keepdims=True)
        - scaled * jnp.mean(weighted * scaled, axis=-1, keepdims=True)
    )


def qkv_body(x_ref, gain_ref, shift_ref, w_ref, bias_ref, out_ref, normed_ref):
    scaled, _ = norm_parts(x_ref[...].astype(F32))
    normed = (scaled * gain_ref[...] + shift_ref[...]).astype(BF16)
    normed_ref[...] = normed
    span = out_ref.shape[2] // 3
    width = x_ref.shape[1]
    for part in range(3):
        cols = slice(part * width, (part + 1) * width)
        piece = (dot(normed, w_ref[:, cols]) + bias_ref[:, cols]).astype(BF16)
        for g in range(HEAD_GROUPS):
            out_ref[g, :, part * span : (part + 1) * span] = piece[:, g * span : (g + 1) * span]


def qkv_forward(x, gain, shift, w_qkv, bias):
    rows, width = x.shape
    span = width // HEAD_GROUPS
    return call(
        qkv_body,
        (
            jax.ShapeDtypeStruct((HEAD_GROUPS, rows, 3 * span), BF16),
            jax.ShapeDtypeStruct((rows, width), BF16),
        ),
        flops=2 * rows * width * 3 * width,
        moved=2 * w_qkv.size + 10 * x.size,
    )(x, gain, shift, w_qkv, bias)


def key_chunks(own_ref, other_ref):
    place = 0
    for ref in (own_ref, other_ref):
        total = ref.shape[1]
        step = 256 if total % 256 == 0 else total
        for start in range(0, total, step):
            yield ref, start, place, step
            place += step


def attend_body(q_ref, own_ref, other_ref, out_ref, log_ref, score_ref, *, head):
    span = q_ref.shape[2] // 3
    queries = q_ref.shape[1]
    scale = 1.0 / math.sqrt(head)
    for h in range(span // head):
        q = q_ref[0, :, h * head : (h + 1) * head] * scale
        top = jnp.full((1, queries), -jnp.inf, F32)
        for ref, start, place, step in key_chunks(own_ref, other_ref):
            k = ref[0, start : start + step, span + h * head : span + (h + 1) * head]
            scores = dot_t(k, q)
            score_ref[place : place + step, :] = scores
            top = jnp.maximum(top, jnp.max(scores, axis=0, keepdims=True))
        total = jnp.zeros((1, queries), F32)
        acc = jnp.zeros((head, queries), F32)
        for ref, start, place, step in key_chunks(own_ref, other_ref):
            v = ref[0, start : start + step, 2 * span + h * head : 2 * span + (h + 1) * head]
            e = jnp.exp(score_ref[place : place + step, :] - top)
            total = total + jnp.sum(e, axis=0, keepdims=True)
            acc = acc + t_dot(v, e.astype(BF16))
        out_ref[0, :, h * head : (h + 1) * head] = jnp.transpose(acc / total).astype(BF16)
        log_ref[0, h : h + 1, :] = top + jnp.log(total)


def query_block(queries):
    return 256 if queries % 256 == 0 else queries


def attend_forward(own, other, head):
    clips, queries, wide = own.shape
    span = wide // 3
    keys = queries + other.shape[1]
    block = query_block(queries)

    def body(*refs):
        attend_body(*refs, head=head)

    return call(
        body,
        (
            jax.ShapeDtypeStruct((clips, queries, span), BF16),
            jax.ShapeDtypeStruct((clips, span // head, queries), F32),
        ),
        grid=(clips, queries // block),
        in_specs=[
            pl.BlockSpec((1, block, wide), lambda m, i: (m, i, 0)),
            pl.BlockSpec((1, queries, wide), lambda m, i: (m, 0, 0)),
            pl.BlockSpec((1, other.shape[1], wide), lambda m, i: (m, 0, 0)),
        ],
        out_specs=(
            pl.BlockSpec((1, block, span), lambda m, i: (m, i, 0)),
            pl.BlockSpec((1, span // head, block), lambda m, i: (m, 0, i)),
        ),
        scratch=[pltpu.VMEM((keys, block), F32)],
        flops=16 * clips * queries * keys * span,
        moved=4 * (own.size + other.size),
    )(own, own, other)


def attend_back_body(
    q_ref,
    own_ref,
    other_ref,
    grad_ref,
    log_ref,
    dq_ref,
    dkv_own_ref,
    dkv_other_ref,
    p_ref,
    dp_ref,
    dk_acc,
    dv_acc,
    *,
    head,
):
    span = q_ref.shape[2] // 3
    queries = q_ref.shape[1]
    heads = span // head
    scale = 1.0 / math.sqrt(head)

    @pl.when(pl.program_id(1) == 0)
    def _():
        dk_acc[...] = jnp.zeros_like(dk_acc)
        dv_acc[...] = jnp.zeros_like(dv_acc)

    for h in range(heads):
        q = q_ref[0, :, h * head : (h + 1) * head] * scale
        d_out = grad_ref[0, :, h * head : (h + 1) * head]
        log_total = log_ref[0, h : h + 1, :]
        row_term = jnp.zeros((1, queries), F32)
        for ref, start, place, step in key_chunks(own_ref, other_ref):
            k = ref[0, start : start + step, span + h * head : span + (h + 1) * head]
            v = ref[0, start : start + step, 2 * span + h * head : 2 * span + (h + 1) * head]
            probs = jnp.exp(dot_t(k, q) - log_total)
            d_probs = dot_t(v, d_out)
            p_ref[place : place + step, :] = probs
            dp_ref[place : place + step, :] = d_probs
            row_term = row_term + jnp.sum(probs * d_probs, axis=0, keepdims=True)
            dv_acc[h, place : place + step, :] += dot(probs.astype(BF16), d_out)
        dq = jnp.zeros((head, queries), F32)
        for ref, start, place, step in key_chunks(own_ref, other_ref):
            k = ref[0, start : start + step, span + h * head : span + (h + 1) * head]
            d_scores = (
                p_ref[place : place + step, :] * (dp_ref[place : place + step, :] - row_term)
            ).astype(BF16)
            dk_acc[h, place : place + step, :] += dot(d_scores, q)
            dq = dq + t_dot(k, d_scores)
        dq_ref[0, :, h * head : (h + 1) * head] = jnp.transpose(dq * scale).astype(BF16)

    @pl.when(pl.program_id(1) == pl.num_programs(1) - 1)
    def _():
        place = 0
        for ref in (dkv_own_ref, dkv_other_ref):
            rows = ref.shape[1]
            for h in range(heads):
                ref[0, :, h * head : (h + 1) * head] = dk_acc[h, place : place + rows, :].astype(
                    ref.dtype
                )
                ref[0, :, span + h * head : span + (h + 1) * head] = dv_acc[
                    h, place : place + rows, :
                ].astype(ref.dtype)
            place += rows


def attend_backward(own, other, grad, log_total, head):
    clips, queries, wide = own.shape
    span = wide // 3
    others = other.shape[1]
    keys = queries + others
    block = query_block(queries)
    heads = span // head

    def body(*refs):
        attend_back_body(*refs, head=head)

    return call(
        body,
        (
            jax.ShapeDtypeStruct((clips, queries, span), BF16),
            jax.ShapeDtypeStruct((clips, queries, 2 * span), F32),
            jax.ShapeDtypeStruct((clips, others, 2 * span), BF16),
        ),
        grid=(clips, queries // block),
        in_specs=[
            pl.BlockSpec((1, block, wide), lambda m, i: (m, i, 0)),
            pl.BlockSpec((1, queries, wide), lambda m, i: (m, 0, 0)),
            pl.BlockSpec((1, others, wide), lambda m, i: (m, 0, 0)),
            pl.BlockSpec((1, block, span), lambda m, i: (m, i, 0)),
            pl.BlockSpec((1, heads, block), lambda m, i: (m, 0, i)),
        ],
        out_specs=(
            pl.BlockSpec((1, block, span), lambda m, i: (m, i, 0)),
            pl.BlockSpec((1, queries, 2 * span), lambda m, i: (m, 0, 0)),
            pl.BlockSpec((1, others, 2 * span), lambda m, i: (m, 0, 0)),
        ),
        scratch=[
            pltpu.VMEM((keys, block), F32),
            pltpu.VMEM((keys, block), F32),
            pltpu.VMEM((heads, keys, head), F32),
            pltpu.VMEM((heads, keys, head), F32),
        ],
        flops=40 * clips * queries * keys * span,
        moved=8 * (own.size + other.size),
    )(own, own, other, grad, log_total)


def feed_body(
    x_ref,
    att_ref,
    w_out_ref,
    b_out_ref,
    gain_ref,
    shift_ref,
    w_up_ref,
    b_up_ref,
    w_down_ref,
    b_down_ref,
    y_ref,
    x1_ref,
    normed_ref,
    slope_ref,
    lifted_ref,
    acc,
):
    @pl.when(pl.program_id(0) == 0)
    def _():
        middle = x_ref[...].astype(F32) + b_out_ref[...]
        for g in range(HEAD_GROUPS):
            middle = middle + dot(att_ref[g], w_out_ref[g])
        x1_ref[...] = middle
        scaled, _ = norm_parts(middle)
        normed_ref[...] = (scaled * gain_ref[...] + shift_ref[...]).astype(BF16)
        acc[...] = middle + b_down_ref[...]

    upper = dot(normed_ref[...], w_up_ref[...]) + b_up_ref[...]
    phi = 0.5 * (1.0 + lax.erf(upper * math.sqrt(0.5)))
    density = jnp.exp(-0.5 * upper * upper) * (1.0 / math.sqrt(2.0 * math.pi))
    slope_ref[...] = phi + upper * density
    lifted = (upper * phi).astype(BF16)
    lifted_ref[...] = lifted
    acc[...] += dot(lifted, w_down_ref[...])

    @pl.when(pl.program_id(0) == pl.num_programs(0) - 1)
    def _():
        y_ref[...] = acc[...].astype(BF16)


def whole(shape):
    return pl.BlockSpec(shape, lambda i: (0,) * len(shape))


def feed_forward(x, att, w_out, b_out, gain, shift, w_up, b_up, w_down, b_down):
    rows, width = x.shape
    hidden = w_up.shape[1]
    chunk = hidden // 4
    row = whole((1, width))
    full = whole((rows, width))
    return call(
        feed_body,
        (
            jax.ShapeDtypeStruct((rows, width), BF16),
            jax.ShapeDtypeStruct((rows, width), F32),
            jax.ShapeDtypeStruct((rows, width), BF16),
            jax.ShapeDtypeStruct((rows, hidden), F32),
            jax.ShapeDtypeStruct((rows, hidden), BF16),
        ),
        grid=(hidden // chunk,),
        in_specs=[
            full,
            whole(att.shape),
            whole(w_out.shape),
            row,
            row,
            row,
            pl.BlockSpec((width, chunk), lambda i: (0, i)),
            pl.BlockSpec((1, chunk), lambda i: (0, i)),
            pl.BlockSpec((chunk, width), lambda i: (i, 0)),
            row,
        ],
        out_specs=(
            full,
            full,
            full,
            pl.BlockSpec((rows, chunk), lambda i: (0, i)),
            pl.BlockSpec((rows, chunk), lambda i: (0, i)),
        ),
        scratch=[pltpu.VMEM((rows, width), F32)],
        flops=2 * rows * width * (2 * hidden + width),
        moved=4 * w_up.size + 2 * w_out.size + 10 * rows * hidden,
    )(x, att, w_out, b_out, gain, shift, w_up, b_up, w_down, b_down)


def feed_back_body(
    g_ref,
    slope_ref,
    w_down_ref,
    w_up_ref,
    w_out_ref,
    x1_ref,
    gain_ref,
    d_upper_ref,
    dx1_ref,
    branch_ref,
    datt_ref,
    sums_ref,
    up_sum_ref,
    acc,
):
    @pl.when(pl.program_id(0) == 0)
    def _():
        acc[...] = jnp.zeros_like(acc)

    d_upper = (dot_t(g_ref[...], w_down_ref[...]) * slope_ref[...]).astype(BF16)
    d_upper_ref[...] = d_upper
    up_sum_ref[...] = jnp.sum(d_upper.astype(F32), axis=0, keepdims=True)
    acc[...] += dot_t(d_upper, w_up_ref[...])

    @pl.when(pl.program_id(0) == pl.num_programs(0) - 1)
    def _():
        d_normed = acc[...]
        upstream = g_ref[...].astype(F32)
        scaled, inverse = norm_parts(x1_ref[...])
        d_middle = upstream + norm_back(d_normed, scaled, inverse, gain_ref[...])
        dx1_ref[...] = d_middle
        branch = d_middle.astype(BF16)
        branch_ref[...] = branch
        for g in range(HEAD_GROUPS):
            datt_ref[g] = dot_t(branch, w_out_ref[g]).astype(BF16)
        sums_ref[0:1, :] = jnp.sum(d_normed * scaled, axis=0, keepdims=True)
        sums_ref[1:2, :] = jnp.sum(d_normed, axis=0, keepdims=True)
        sums_ref[2:3, :] = jnp.sum(branch.astype(F32), axis=0, keepdims=True)
        sums_ref[3:4, :] = jnp.sum(upstream, axis=0, keepdims=True)


def feed_backward(g, slope, w_down, w_up, w_out, x1, gain):
    rows, width = g.shape
    hidden = w_up.shape[1]
    chunk = hidden // 4
    full = whole((rows, width))
    return call(
        feed_back_body,
        (
            jax.ShapeDtypeStruct((rows, hidden), BF16),
            jax.ShapeDtypeStruct((rows, width), F32),
            jax.ShapeDtypeStruct((rows, width), BF16),
            jax.ShapeDtypeStruct((HEAD_GROUPS, rows, width // HEAD_GROUPS), BF16),
            jax.ShapeDtypeStruct((4, width), F32),
            jax.ShapeDtypeStruct((1, hidden), F32),
        ),
        grid=(hidden // chunk,),
        in_specs=[
            full,
            pl.BlockSpec((rows, chunk), lambda i: (0, i)),
            pl.BlockSpec((chunk, width), lambda i: (i, 0)),
            pl.BlockSpec((width, chunk), lambda i: (0, i)),
            whole(w_out.shape),
            full,
            whole((1, width)),
        ],
        out_specs=(
            pl.BlockSpec((rows, chunk), lambda i: (0, i)),
            full,
            full,
            whole((HEAD_GROUPS, rows, width // HEAD_GROUPS)),
            whole((4, width)),
            pl.BlockSpec((1, chunk), lambda i: (0, i)),
        ),
        scratch=[pltpu.VMEM((rows, width), F32)],
        flops=2 * rows * width * (2 * hidden + width),
        moved=4 * w_up.size + 2 * w_out.size + 6 * rows * hidden,
    )(g, slope, w_down, w_up, w_out, x1, gain)


def qkv_back_body(
    grads_ref, w_ref, x_ref, dx1_ref, gain_ref, dx_ref, flat_ref, sums_ref
):
    width = x_ref.shape[1]
    span = grads_ref.shape[2] // 3
    for g in range(HEAD_GROUPS):
        for part in range(3):
            flat_ref[:, part * width + g * span : part * width + (g + 1) * span] = grads_ref[
                g, :, part * span : (part + 1) * span
            ]
    d_normed = dot_t(flat_ref[...], w_ref[...])
    scaled, inverse = norm_parts(x_ref[...].astype(F32))
    dx = dx1_ref[...] + norm_back(d_normed, scaled, inverse, gain_ref[...])
    dx_ref[...] = dx.astype(BF16)
    sums_ref[0:1, :] = jnp.sum(d_normed * scaled, axis=0, keepdims=True)
    sums_ref[1:2, :] = jnp.sum(d_normed, axis=0, keepdims=True)
    sums_ref[2:3, :] = jnp.sum(flat_ref[:, :width].astype(F32), axis=0, keepdims=True)
    sums_ref[3:4, :] = jnp.sum(flat_ref[:, 2 * width :].astype(F32), axis=0, keepdims=True)


def qkv_backward(grads, w_qkv, x, dx1, gain):
    rows, width = x.shape
    return call(
        qkv_back_body,
        (
            jax.ShapeDtypeStruct((rows, width), BF16),
            jax.ShapeDtypeStruct((rows, 3 * width), BF16),
            jax.ShapeDtypeStruct((4, width), F32),
        ),
        flops=2 * rows * width * 3 * width,
        moved=2 * w_qkv.size + 20 * x.size,
    )(grads, w_qkv, x, dx1, gain)


def swap(block, axis):
    return lax.ppermute(block, axis, [(0, 1), (1, 0)])


def shift(block, distance):
    count = lax.axis_size("rest")
    return lax.ppermute(block, "rest", [(i, (i + distance) % count) for i in range(count)])


def spread(block):
    return lax.all_to_all(block, ("quad", "side"), 0, 0, tiled=True)


def to_clips(block, clips):
    groups, rows, wide = block.shape
    block = block.reshape(groups, clips, rows // clips, wide)
    return jnp.swapaxes(block, 0, 1).reshape(clips, groups * (rows // clips), wide)


def to_tokens(block):
    clips, rows, wide = block.shape
    block = block.reshape(clips, HEAD_GROUPS, rows // HEAD_GROUPS, wide)
    return jnp.swapaxes(block, 0, 1).reshape(HEAD_GROUPS, -1, wide)


def other_keys(own):
    near = [shift(own, k) for k in range(1, lax.axis_size("rest"))]
    far = swap(jnp.concatenate([own] + near, axis=1) if near else own, "core")
    return jnp.concatenate(near + [far], axis=1) if near else far


def return_keys(kept, sent):
    queries = kept.shape[1]
    count = lax.axis_size("rest")
    near = (count - 1) * queries
    back = swap(sent[:, near:], "core").astype(F32)
    total = kept + back[:, :queries]
    for k in range(1, count):
        part = sent[:, (k - 1) * queries : k * queries].astype(F32)
        part = part + back[:, k * queries : (k + 1) * queries]
        total = total + shift(part.astype(BF16), -k).astype(F32)
    return total


def pick(flag, one, two):
    return jnp.where(flag, one, two)


def gather_weight(block):
    core = lax.axis_index("core")
    quads = lax.axis_size("quad")
    part = block.shape[0] // (2 * quads)
    quad = lax.axis_index("quad")

    def cut(which):
        return lax.dynamic_slice_in_dim(block, (which * quads + quad) * part, part, 0)

    own = cut(core)
    came = swap(cut(1 - core), "core")
    first = pick(core == 0, own, came)
    second = pick(core == 0, came, own)
    return [
        lax.all_gather(item, ("side", "rest", "core", "quad"), axis=0, tiled=True)
        for item in (first, second)
    ]


def add(one, two):
    return (one.astype(F32) + two.astype(F32)).astype(one.dtype)


def reduce_rows(grad, layer):
    side = lax.axis_index("side")
    paired = lax.ppermute(grad, "core", [(1 - layer, layer)])
    half = grad.shape[0] // 2

    def cut(which):
        start = which * half
        return add(
            lax.dynamic_slice_in_dim(grad, start, half, 0),
            lax.dynamic_slice_in_dim(paired, start, half, 0),
        )

    two = 2 * layer
    came = lax.ppermute(cut(1 - side), ("core", "side"), [(two, two + 1), (two + 1, two)])
    total = add(cut(side), came)
    if lax.axis_size("rest") > 1:
        total = lax.psum_scatter(total, "rest", scatter_dimension=0, tiled=True)
    quads = lax.axis_size("quad")
    if quads != 2:
        return lax.psum(total, ("half", "quad"))
    base = 4 * layer
    line = ("core", "half", "quad")

    def hop(block, pairs):
        return lax.ppermute(block, line, [(base + a, base + b) for a, b in pairs])

    total = add(total, hop(total, [(0, 1), (3, 2)]))
    total = add(total, hop(total, [(1, 2), (2, 1)]))
    came = hop(total, [(1, 0), (2, 3)])
    inner = lax.axis_index("half") != lax.axis_index("quad")
    return pick(inner, total, came)


def swap_in(block):
    core, half = lax.axis_index("core"), lax.axis_index("half")
    micro, rows, wide = block.shape
    block = block.reshape(2, (micro // 2) * rows, wide)
    own = lax.dynamic_index_in_dim(block, half, 0, keepdims=False)
    other = lax.dynamic_index_in_dim(block, 1 - half, 0, keepdims=False)
    came = lax.ppermute(other, ("core", "half"), [(1, 2), (2, 1)])
    return pick(core == half, own, came)


def swap_out(first, second, micro):
    rows, wide = first.shape
    both = jnp.stack([first, second])
    both = lax.all_to_all(both, "core", 0, 0, tiled=True)
    both = lax.all_to_all(both, "half", 0, 0, tiled=True)
    return both.reshape(micro, 2 * rows // micro, wide)


def forward_layer(x, weights, clips, head):
    w_qkv, w_out, w_up, w_down, gains, shifts, b_qkv, b_out, b_down, b_up = weights
    width = x.shape[1]
    grouped, normed_one = qkv_forward(x, gains[0:1], shifts[0:1], w_qkv, b_qkv)
    own = to_clips(spread(grouped), clips)
    other = other_keys(own)
    att, log_total = attend_forward(own, other, head)
    att = spread(to_tokens(att))
    y, x1, normed_two, slope, lifted = feed_forward(
        x,
        att,
        w_out.reshape(HEAD_GROUPS, width // HEAD_GROUPS, width),
        b_out,
        gains[1:2],
        shifts[1:2],
        w_up,
        b_up,
        w_down,
        b_down,
    )
    return y, (x, normed_one, own, other, log_total, att, x1, normed_two, slope, lifted)


def backward_layer(kept, g, weights, clips, head, with_weights):
    x, normed_one, own, other, log_total, att, x1, normed_two, slope, lifted = kept
    w_qkv, w_out, w_up, w_down, gains, shifts, b_qkv, b_out, b_down, b_up = weights
    width = x.shape[1]
    d_upper, dx1, branch, d_att, sums_two, up_sum = feed_backward(
        g,
        slope,
        w_down,
        w_up,
        w_out.reshape(HEAD_GROUPS, width // HEAD_GROUPS, width),
        x1,
        gains[1:2],
    )
    d_heads = to_clips(spread(d_att), clips)
    dq, kept_kv, sent_kv = attend_backward(own, other, d_heads, log_total, head)
    dkv = return_keys(kept_kv, sent_kv).astype(BF16)
    d_own = jnp.concatenate([dq, dkv], axis=2)
    d_tokens = spread(to_tokens(d_own))
    dx, flat, sums_one = qkv_backward(d_tokens, w_qkv, x, dx1, gains[0:1])
    if not with_weights:
        return dx, None
    grad_down = t_dot(lifted, g).astype(BF16)
    grad_up = t_dot(normed_two, d_upper).astype(BF16)
    grad_out = jnp.einsum("gtf,td->gfd", att, branch, preferred_element_type=F32)
    grad_out = grad_out.astype(BF16).reshape(width, width)
    grad_qkv = t_dot(normed_one, flat).astype(BF16)
    return dx, (grad_qkv, grad_out, grad_up, grad_down, sums_one, sums_two, up_sum)


def pack_small(sums_one, sums_two, up_sum, shards):
    rows = jnp.concatenate(
        [
            sums_one[0:1],
            sums_two[0:1],
            sums_one[1:2],
            sums_two[1:2],
            sums_one[2:4],
            sums_two[2:4],
        ]
    )
    rows = jnp.swapaxes(rows.reshape(8, shards, -1), 0, 1).reshape(shards, -1)
    packed = jnp.concatenate([rows, up_sum.reshape(shards, -1)], axis=1)
    return packed.reshape(-1, 128)


def per_device(
    frames, out_grad, norm_gain, norm_bias, w_qkv, w_out, w_up, w_down, proj_bias, up_bias
):
    pairs = lax.axis_size("pair")
    pair = lax.axis_index("pair")
    core = lax.axis_index("core")
    shards = lax.axis_size("side") * lax.axis_size("rest")
    micro, _, width = frames.shape
    clips = micro // 2
    head = width // HEADS
    part = width // shards

    small = jnp.concatenate(
        [norm_gain.reshape(-1), norm_bias.reshape(-1), proj_bias.reshape(-1), up_bias.reshape(-1)]
    )
    small = lax.all_gather(small, ("core", "side", "rest"), axis=0, tiled=False)
    small = small.reshape(2, shards, -1).astype(F32)
    rows = jnp.swapaxes(small[:, :, : 8 * part].reshape(2, shards, 8, part), 1, 2)
    rows = rows.reshape(2, 8, width)
    ups = small[:, :, 8 * part :].reshape(2, 1, -1)
    x_start = swap_in(frames)
    matrices = [gather_weight(item[0]) for item in (w_qkv, w_out, w_up, w_down)]
    layers = []
    for layer in range(2):
        r = rows[layer]
        b_qkv = jnp.concatenate([r[4:5], jnp.zeros_like(r[4:5]), r[5:6]], axis=1)
        layers.append(
            tuple(m[layer] for m in matrices)
            + (r[0:2], r[2:4], b_qkv, r[6:7], r[7:8], ups[layer])
        )

    x = x_start
    for phase in range(pairs):
        if phase > 0:
            came = lax.ppermute(second, "pair", [(i, i + 1) for i in range(pairs - 1)])
            x = pick(pair == 0, x_start, came)
        first, kept_first = forward_layer(x, layers[0], clips, head)
        second, kept_second = forward_layer(first, layers[1], clips, head)
    hidden = swap_out(first, second, micro)

    g_start = swap_in(out_grad)
    g = g_start
    for phase in range(pairs):
        if phase > 0:
            came = lax.ppermute(d_first, "pair", [(i + 1, i) for i in range(pairs - 1)])
            g = pick(pair == pairs - 1, g_start, came)
        last = phase == pairs - 1
        d_second, grads_second = backward_layer(kept_second, g, layers[1], clips, head, last)
        d_first, grads_first = backward_layer(kept_first, d_second, layers[0], clips, head, last)
    input_grads = swap_out(d_first, d_second, micro)

    reduced = []
    for layer, grads in ((1, grads_second), (0, grads_first)):
        items = [reduce_rows(item, layer) for item in (grads[3], grads[2], grads[1], grads[0])]
        items.append(reduce_rows(pack_small(*grads[4:], shards), layer))
        reduced.append(items)
    down, up, out, qkv, packed = [
        pick(core == 0, zero, one).astype(F32) for one, zero in zip(*reduced)
    ]
    packed = packed.reshape(-1)
    heads = packed[: 8 * part].reshape(8, part)
    return (
        hidden[None],
        input_grads[None],
        heads[0:2][None],
        heads[2:4][None],
        qkv[None],
        out[None],
        up[None],
        down[None],
        heads[4:8][None],
        packed[8 * part :][None],
    )


def solution(mesh):
    sections, groups, shards = (mesh.shape[name] for name in ("section", "seq", "shard"))
    cut = Mesh(
        mesh.devices.reshape(sections // 2, 2, 2, groups // 2, 2, shards // 2),
        AXES,
    )
    section, seq, shard = ("pair", "core"), ("half", "quad"), ("side", "rest")
    rows = seq + shard
    return jax.shard_map(
        per_device,
        mesh=cut,
        in_specs=(
            P(None, rows, None),
            P(None, rows, None),
            P(section, None, shard),
            P(section, None, shard),
            P(section, shard, None),
            P(section, shard, None),
            P(section, shard, None),
            P(section, shard, None),
            P(section, None, shard),
            P(section, shard),
        ),
        out_specs=(
            P(section, None, rows, None),
            P(section, None, rows, None),
            P(section, None, shard),
            P(section, None, shard),
            P(section, shard, None),
            P(section, shard, None),
            P(section, shard, None),
            P(section, shard, None),
            P(section, None, shard),
            P(section, shard),
        ),
        check_vma=False,
    )
```

time: 2230 us -> 1220 us (0.55)
  waiting for transfers between devices: 1010 us -> 472 us
  matrix products: 495 us -> 21.8 us
  local copies, waits for them, and re-layouts: 304 us -> 47.6 us
  Pallas kernels: 0 us -> 222 us
  blocking collectives: 41.7 us -> 180 us
  other arithmetic: 227 us -> 112 us
  starting transfers between devices: 99.4 us -> 142 us
    dot_general x95 -> x8, matrix products: 495 us -> 21.8 us  [the longest x6 19.8 us: t_dot(): lax.dot_general(left, right, (((0,), (0,)), ((), ())), preferred_element_...]
    ppermute x10 -> x66, waiting for transfers between devices: 0.03 us -> 315 us  [the longest x30 211 us: hop(): return lax.ppermute(block, line, [(base + a, base + b) for a, b in pairs])]
    all_to_all x20 -> x9, waiting for transfers between devices: 250 us -> 19.7 us  [the longest x6 14.9 us: spread(): return lax.all_to_all(block, ('quad', 'side'), 0, 0, tiled=True)]
    psum x1 -> x0, waiting for transfers between devices: 226 us -> none  [per_device(): lax.psum(scattered[2].astype(jnp.bfloat16), 'seq').astype(jnp.float32)]
    pallas_call x0 -> x24, Pallas kernels: none -> 222 us  [the longest x4 70.9 us: attend_backward(): call(body, (jax.ShapeDtypeStruct((clips, queries, span), BF16), jax.Shape...]
    reduce_scatter x9 -> x0, waiting for transfers between devices: 216 us -> none  [the longest x1 62.9 us: per_device(): lax.psum_scatter(expanded[5].astype(jnp.bfloat16), 'shard', scatter_dimen...]
    all_to_all x0 -> x11, blocking collectives: none -> 165 us  [the longest x10 156 us: spread(): return lax.all_to_all(block, ('quad', 'side'), 0, 0, tiled=True)]
    all_gather x9 -> x8, waiting for transfers between devices: 256 us -> 135 us  [gather_weight(): lax.all_gather(item, ('side', 'rest', 'core', 'quad'), axis=0, tiled=True)]
  transfers between devices with their start and end apart: 53 -> 83, of which waited for: 42 -> 30; matrix products, arithmetic and copies ran while one was open for 16% -> 12% of each run, Pallas kernels for 0% -> 7%
where the time goes in v1:
time: 1220 us; the launch traced here: 1210 us
  waiting for transfers between devices  472 us (39%)
  Pallas kernels  222 us (18%)
  blocking collectives  180 us (15%)
  starting transfers between devices  142 us (12%)
  other arithmetic  112 us (9%)
  local copies, waits for them, and re-layouts  47.6 us (4%)
  matrix products  21.8 us (2%)
  between operations  16.3 us (1%)
    ppermute x30, waiting for transfers between devices, hop(): return lax.ppermute(block, line, [(base + a, base + b) for a, b in pairs])  211 us
    all_to_all x10, blocking collectives, spread(): return lax.all_to_all(block, ('quad', 'side'), 0, 0, tiled=True)  156 us
    all_gather x8, waiting for transfers between devices, gather_weight(): lax.all_gather(item, ('side', 'rest', 'core', 'quad'), axis=0, tiled=True)  135 us
    pallas_call x4, Pallas kernels, attend_backward(): call(body, (jax.ShapeDtypeStruct((clips, queries, span), BF16), jax.Shape...  70.9 us
    convert_element_type x32, other arithmetic, add(): return (one.astype(F32) + two.astype(F32)).astype(one.dtype)  68 us
    ppermute x10, waiting for transfers between devices, reduce_rows(): lax.ppermute(cut(1 - side), ('core', 'side'), [(two, two + 1), (two + 1,...  64 us
    ppermute x30, starting transfers between devices, hop(): return lax.ppermute(block, line, [(base + a, base + b) for a, b in pairs])  52.4 us
    pallas_call x4, Pallas kernels, feed_backward(): call(feed_back_body, (jax.ShapeDtypeStruct((rows, hidden), BF16), jax.Sha...  39.9 us
  transfers between devices with their start and end apart: 83, of which 30 were waited for; matrix products, arithmetic and copies ran while one was open for 12% of the time, Pallas kernels for 7%

profile of v1, /device:TPU:0, one launch (start us, length us, event | category | flops | bytes accessed | tf_op | source)
XLA Modules:
  0.0 1212.7 jit_solution(3701909320130698666)
XLA Ops:
  29.2 14.6 %all-gather.1 = bf16[4,1,4608]{2,1,0:T(2,128)(2,1)S(1)} all-gather(bf16[1,1,4608]{2,1,0:T(2,128)(2,1)S(1)} %reshape.155), channel_id=2, replica_groups=mesh['pair'=2,'core'=2,'half'=2,'quad'=2,'side'=2,'rest'=1] {'core','sid..., dimensions={0}, use_global_device_ids=true | all-gather | bytes 46080 | tf_op jit(solution)/shard_map/all_gather | solution.py:667
  50.8 21.0 %all_to_all.100 = bf16[4,192,576]{2,1,0:T(8,128)(2,1)S(1)} all-to-all(bf16[4,192,576]{2,1,0:T(8,128)(2,1)} %get-tuple-element.70), channel_id=1, replica_groups=mesh['pair'=2,'core'=2,'half'=2,'quad'=2,'side'=2,'rest'=1] {'quad','side'}, dimensions={0} | all-to-all | bytes 1769472 | tf_op jit(solution)/shard_map/all_to_all | solution.py:472
  91.3 24.0 %all-gather.15.cloned.1.call-done.w_up_ref = bf16[768,3072]{1,0:T(8,128)(2,1)} async-done(((bf16[96,3072]{1,0:T(8,128)(2,1)}), bf16[768,3072]{1,0:T(8,128)(2,1)}) %all-gather.15.cloned.1.call-update) | async-done | bytes 4718608 | tf_op jit(solution)/shard_map/all_gather | solution.py:524
  115.3 33.6 %all-gather.17.cloned.1.call-done.w_down_ref = bf16[3072,768]{1,0:T(8,128)(2,1)} async-done(((bf16[384,768]{1,0:T(8,128)(2,1)}), bf16[3072,768]{1,0:T(8,128)(2,1)}) %all-gather.17.cloned.1.call-update) | async-done | bytes 4718608 | tf_op jit(solution)/shard_map/all_gather | solution.py:524
  158.7 20.8 %all-gather.19.cloned.1.call-done.w_ref = bf16[768,2304]{1,0:T(8,128)(2,1)} async-done(((bf16[96,2304]{1,0:T(8,128)(2,1)}), bf16[768,2304]{1,0:T(8,128)(2,1)}) %all-gather.19.cloned.1.call-update) | async-done | bytes 3538960 | tf_op jit(solution)/shard_map/all_gather | solution.py:524
  183.6 21.1 %all_to_all.101 = bf16[4,192,576]{2,1,0:T(8,128)(2,1)S(1)} all-to-all(bf16[4,192,576]{2,1,0:T(8,128)(2,1)} %get-tuple-element.73), channel_id=1, replica_groups=mesh['pair'=2,'core'=2,'half'=2,'quad'=2,'side'=2,'rest'=1] {'quad','side'}, dimensions={0} | all-to-all | bytes 1769472 | tf_op jit(solution)/shard_map/all_to_all | solution.py:472
  225.4 23.1 %all-gather.23.cloned.1.call-done.w_up_ref = bf16[768,3072]{1,0:T(8,128)(2,1)} async-done(((bf16[96,3072]{1,0:T(8,128)(2,1)}), bf16[768,3072]{1,0:T(8,128)(2,1)}) %all-gather.23.cloned.1.call-update) | async-done | bytes 4718608 | tf_op jit(solution)/shard_map/all_gather | solution.py:524
  248.5 33.7 %all-gather.25.cloned.1.call-done.w_down_ref = bf16[3072,768]{1,0:T(8,128)(2,1)} async-done(((bf16[384,768]{1,0:T(8,128)(2,1)}), bf16[3072,768]{1,0:T(8,128)(2,1)}) %all-gather.25.cloned.1.call-update) | async-done | bytes 4718608 | tf_op jit(solution)/shard_map/all_gather | solution.py:524
  307.3 17.0 %all_to_all.102 = bf16[4,192,576]{2,1,0:T(8,128)(2,1)S(1)} all-to-all(bf16[4,192,576]{2,1,0:T(8,128)(2,1)} %get-tuple-element.76), channel_id=1, replica_groups=mesh['pair'=2,'core'=2,'half'=2,'quad'=2,'side'=2,'rest'=1] {'quad','side'}, dimensions={0} | all-to-all | bytes 1769472 | tf_op jit(solution)/shard_map/all_to_all | solution.py:472
  338.5 11.9 all_to_all.103.att_ref
  363.6 16.6 %all_to_all.104 = bf16[4,192,576]{2,1,0:T(8,128)(2,1)S(1)} all-to-all(bf16[4,192,576]{2,1,0:T(8,128)(2,1)} %get-tuple-element.79), channel_id=1, replica_groups=mesh['pair'=2,'core'=2,'half'=2,'quad'=2,'side'=2,'rest'=1] {'quad','side'}, dimensions={0} | all-to-all | bytes 1769472 | tf_op jit(solution)/shard_map/all_to_all | solution.py:472
  413.7 10.0 shard_map.189
  423.6 11.5 all_to_all.105
  435.1 17.7 %shard_map.190 = (bf16[1,768,192]{2,1,0:T(8,128)(2,1)}, f32[1,768,384]{2,1,0:T(8,128)}, bf16[1,768,384]{2,1,0:T(8,128)(2,1)}) custom-call(bf16[1,768,576]{2,1,0:T(8,128)(2,1)} %bitcast.197, bf16[1,768,576]{2,1,0:T(8,128)(2,1)} %bitcast.198, bf16[1,768,576]{2,1,0:T(8,128)(2,1)} %copy.29.refs_2_, bf16[1,768,192]{2,1,0:T(8,128)(2,1)} %bitcast.215, ...), custom_call_target="tpu_custom_call" | custom-call | flops 9059696640 | bytes 7077888 | tf_op jit(solution)/shard_map/pallas_call | solution.py:230
  457.6 17.7 %all_to_all.106.grads_ref = bf16[4,192,576]{2,1,0:T(8,128)(2,1)} all-to-all(bf16[4,192,576]{2,1,0:T(8,128)(2,1)S(1)} %bitcast.207), channel_id=1, replica_groups=mesh['pair'=2,'core'=2,'half'=2,'quad'=2,'side'=2,'rest'=1] {'quad','side'}, dimensions={0} | all-to-all | bytes 1769472 | tf_op jit(solution)/shard_map/all_to_all | solution.py:472
  480.1 10.0 shard_map.192
  490.1 11.1 all_to_all.107
  501.2 17.7 %shard_map.193 = (bf16[1,768,192]{2,1,0:T(8,128)(2,1)}, f32[1,768,384]{2,1,0:T(8,128)}, bf16[1,768,384]{2,1,0:T(8,128)(2,1)}) custom-call(bf16[1,768,576]{2,1,0:T(8,128)(2,1)} %bitcast.190, bf16[1,768,576]{2,1,0:T(8,128)(2,1)} %bitcast.191, bf16[1,768,576]{2,1,0:T(8,128)(2,1)} %copy.27.refs_2_, bf16[1,768,192]{2,1,0:T(8,128)(2,1)} %bitcast.216, ...), custom_call_target="tpu_custom_call" | custom-call | flops 9059696640 | bytes 7077888 | tf_op jit(solution)/shard_map/pallas_call | solution.py:230
  523.1 17.3 %all_to_all.108.grads_ref = bf16[4,192,576]{2,1,0:T(8,128)(2,1)} all-to-all(bf16[4,192,576]{2,1,0:T(8,128)(2,1)S(1)} %bitcast.208), channel_id=1, replica_groups=mesh['pair'=2,'core'=2,'half'=2,'quad'=2,'side'=2,'rest'=1] {'quad','side'}, dimensions={0} | all-to-all | bytes 1769472 | tf_op jit(solution)/shard_map/all_to_all | solution.py:472
  556.1 9.9 shard_map.195
  566.0 10.8 all_to_all.109
  576.9 17.7 %shard_map.196 = (bf16[1,768,192]{2,1,0:T(8,128)(2,1)}, f32[1,768,384]{2,1,0:T(8,128)}, bf16[1,768,384]{2,1,0:T(8,128)(2,1)}) custom-call(bf16[1,768,576]{2,1,0:T(8,128)(2,1)} %bitcast.199, bf16[1,768,576]{2,1,0:T(8,128)(2,1)} %bitcast.200, bf16[1,768,576]{2,1,0:T(8,128)(2,1)} %copy.29.refs_2_, bf16[1,768,192]{2,1,0:T(8,128)(2,1)} %bitcast.214, ...), custom_call_target="tpu_custom_call" | custom-call | flops 9059696640 | bytes 7077888 | tf_op jit(solution)/shard_map/pallas_call | solution.py:230
  606.8 9.8 all-to-all-done.15.grads_ref
  622.3 10.0 shard_map.198
  647.9 17.8 %shard_map.199 = (bf16[1,768,192]{2,1,0:T(8,128)(2,1)}, f32[1,768,384]{2,1,0:T(8,128)}, bf16[1,768,384]{2,1,0:T(8,128)(2,1)}) custom-call(bf16[1,768,576]{2,1,0:T(8,128)(2,1)} %bitcast.192, bf16[1,768,576]{2,1,0:T(8,128)(2,1)} %bitcast.193, bf16[1,768,576]{2,1,0:T(8,128)(2,1)} %copy.27.refs_2_, bf16[1,768,192]{2,1,0:T(8,128)(2,1)} %bitcast.210, ...), custom_call_target="tpu_custom_call" | custom-call | flops 9059696640 | bytes 7077888 | tf_op jit(solution)/shard_map/pallas_call | solution.py:230
  850.0 31.6 %collective-permute-done.57 = bf16[1536,768]{1,0:T(8,128)(2,1)S(1)} collective-permute-done((bf16[1536,768]{1,0:T(8,128)(2,1)S(1)}, bf16[1536,768]{1,0:T(8,128)(2,1)S(1)}, u32[]{:S(2)}, u32[]{:S(2)}) %collective-permute-start.57) | collective-permute-done | bytes 2359328 | tf_op jit(solution)/shard_map/ppermute | solution.py:546
  894.2 31.6 %collective-permute-done.27 = bf16[384,2304]{1,0:T(8,128)(2,1)S(1)} collective-permute-done((bf16[384,2304]{1,0:T(8,128)(2,1)S(1)}, bf16[384,2304]{1,0:T(8,128)(2,1)S(1)}, u32[]{:S(2)}, u32[]{:S(2)}) %collective-permute-start.27) | collective-permute-done | bytes 1769504 | tf_op jit(solution)/shard_map/ppermute | solution.py:546
  944.0 35.1 %collective-permute-done.28 = bf16[384,2304]{1,0:T(8,128)(2,1)} collective-permute-done((bf16[384,2304]{1,0:T(8,128)(2,1)S(1)}, bf16[384,2304]{1,0:T(8,128)(2,1)}, u32[]{:S(2)}, u32[]{:S(2)}) %collective-permute-start.28) | collective-permute-done | bytes 1769504 | tf_op jit(solution)/shard_map/ppermute | solution.py:557
  981.8 22.5 %collective-permute-done.48 = bf16[384,3072]{1,0:T(8,128)(2,1)S(1)} collective-permute-done((bf16[384,3072]{1,0:T(8,128)(2,1)S(1)}, bf16[384,3072]{1,0:T(8,128)(2,1)S(1)}, u32[]{:S(2)}, u32[]{:S(2)}) %collective-permute-start.48) | collective-permute-done | bytes 2359328 | tf_op jit(solution)/shard_map/ppermute | solution.py:557
  1036.9 82.6 %collective-permute-done.30 = bf16[384,2304]{1,0:T(8,128)(2,1)} collective-permute-done((bf16[384,2304]{1,0:T(8,128)(2,1)}, bf16[384,2304]{1,0:T(8,128)(2,1)}, u32[]{:S(2)}, u32[]{:S(2)}) %collective-permute-start.30) | collective-permute-done | bytes 1769504 | tf_op jit(solution)/shard_map/ppermute | solution.py:557
  1123.2 46.9 %collective-permute-done.60 = bf16[1536,768]{1,0:T(8,128)(2,1)} collective-permute-done((bf16[1536,768]{1,0:T(8,128)(2,1)}, bf16[1536,768]{1,0:T(8,128)(2,1)}, u32[]{:S(2)}, u32[]{:S(2)}) %collective-permute-start.60) | collective-permute-done | bytes 2359328 | tf_op jit(solution)/shard_map/ppermute | solution.py:557
  1175.2 21.3 %collective-permute-done.50 = bf16[384,3072]{1,0:T(8,128)(2,1)} collective-permute-done((bf16[384,3072]{1,0:T(8,128)(2,1)}, bf16[384,3072]{1,0:T(8,128)(2,1)}, u32[]{:S(2)}, u32[]{:S(2)}) %collective-permute-start.50) | collective-permute-done | bytes 2359328 | tf_op jit(solution)/shard_map/ppermute | solution.py:557
  (470 shorter events, 498.1 us)
Async XLA Ops:
  12.5 78.8 %all-gather.13.cloned.1.call-start = ((), (), s32[]{:S(2)}) async-start(), calls=%async_computation.21 | async-start | bytes 1327104 | tf_op jit(solution)/shard_map/all_gather | solution.py:524
  16.6 98.7 %all-gather.15.cloned.1.call-start = ((), (), s32[]{:S(2)}) async-start(), calls=%async_computation.22 | async-start | bytes 5308416 | tf_op jit(solution)/shard_map/all_gather | solution.py:524
  20.1 128.8 %all-gather.17.cloned.1.call-start = ((), (), s32[]{:S(2)}) async-start(), calls=%async_computation.23 | async-start | bytes 5308416 | tf_op jit(solution)/shard_map/all_gather | solution.py:524
  25.6 153.9 %all-gather.19.cloned.1.call-start = ((), (), s32[]{:S(2)}) async-start(), calls=%async_computation.24 | async-start | bytes 3981312 | tf_op jit(solution)/shard_map/all_gather | solution.py:524
  26.2 199.2 %all-gather.21.cloned.1.call-start = ((), (), s32[]{:S(2)}) async-start(), calls=%async_computation.25 | async-start | bytes 1327104 | tf_op jit(solution)/shard_map/all_gather | solution.py:524
  26.8 221.7 %all-gather.23.cloned.1.call-start = ((), (), s32[]{:S(2)}) async-start(), calls=%async_computation.26 | async-start | bytes 5308416 | tf_op jit(solution)/shard_map/all_gather | solution.py:524
  27.5 254.7 %all-gather.25.cloned.1.call-start = ((), (), s32[]{:S(2)}) async-start(), calls=%async_computation.27 | async-start | bytes 5308416 | tf_op jit(solution)/shard_map/all_gather | solution.py:524
  86.0 62.9 %all-to-all-start.1 = ((bf16[4,192,192]{2,1,0:T(8,128)(2,1)}), bf16[4,192,192]{2,1,0:T(8,128)(2,1)S(1)}, u32[]{:S(2)}, u32[]{:S(2)}) async-start(bf16[4,192,192]{2,1,0:T(8,128)(2,1)} %bitcast.212), calls=%async_computation.1 | async-start | bytes 786432 | tf_op jit(solution)/shard_map/all_to_all | solution.py:472
  218.9 63.3 %all-to-all-start.3 = ((bf16[4,192,192]{2,1,0:T(8,128)(2,1)}), bf16[4,192,192]{2,1,0:T(8,128)(2,1)S(1)}, u32[]{:S(2)}, u32[]{:S(2)}) async-start(bf16[4,192,192]{2,1,0:T(8,128)(2,1)} %bitcast.211), calls=%async_computation.3 | async-start | bytes 786432 | tf_op jit(solution)/shard_map/all_to_all | solution.py:472
  603.7 40.3 %collective-permute-start.41 = (bf16[768,768]{1,0:T(8,128)(2,1)S(1)}, bf16[768,768]{1,0:T(8,128)(2,1)}, u32[]{:S(2)}, u32[]{:S(2)}) collective-permute-start(bf16[768,768]{1,0:T(8,128)(2,1)S(1)} %bitcast.184), channel_id=1, source_target_pairs={{0,8},{1,9},{2,10},{3,11},{4,12},{5,13},{6,14},{7,15},{16,24},{17,... | collective-permute-start | bytes 3538952 | tf_op jit(solution)/shard_map/ppermute | solution.py:535
  639.4 142.5 %collective-permute-start.61 = (bf16[3072,768]{1,0:T(8,128)(2,1)}, bf16[3072,768]{1,0:T(8,128)(2,1)}, u32[]{:S(2)}, u32[]{:S(2)}) collective-permute-start(bf16[3072,768]{1,0:T(8,128)(2,1)} %convolution_convert_fusion.2), channel_id=1, source_target_pairs={{0,8},{1,9},{2,10},{3,11},{4,12},{5,13},{6,14},{7,15},{16,24},{17,... | collective-permute-start | bytes 14155784 | tf_op jit(solution)/shard_map/ppermute | solution.py:535
  669.3 96.9 %collective-permute-start.51 = (bf16[768,3072]{1,0:T(8,128)(2,1)}, bf16[768,3072]{1,0:T(8,128)(2,1)}, u32[]{:S(2)}, u32[]{:S(2)}) collective-permute-start(bf16[768,3072]{1,0:T(8,128)(2,1)} %convolution_convert_fusion.4), channel_id=1, source_target_pairs={{0,8},{1,9},{2,10},{3,11},{4,12},{5,13},{6,14},{7,15},{16,24},{17,... | collective-permute-start | bytes 14155784 | tf_op jit(solution)/shard_map/ppermute | solution.py:535
  678.4 49.1 %collective-permute-start.43 = (bf16[384,768]{1,0:T(8,128)(2,1)}, bf16[384,768]{1,0:T(8,128)(2,1)}, u32[]{:S(2)}, u32[]{:S(2)}) collective-permute-start(bf16[384,768]{1,0:T(8,128)(2,1)} %add_convert_fusion.32), channel_id=1, source_target_pairs={{8,10},{14,12},{9,11},{15,13},{24,26},{30,28},{25,27},{31,29}} | collective-permute-start | bytes 1769480 | tf_op jit(solution)/shard_map/ppermute | solution.py:557
  737.1 76.6 %collective-permute-start.31 = (bf16[768,2304]{1,0:T(8,128)(2,1)S(1)}, bf16[768,2304]{1,0:T(8,128)(2,1)}, u32[]{:S(2)}, u32[]{:S(2)}) collective-permute-start(bf16[768,2304]{1,0:T(8,128)(2,1)S(1)} %convolution_convert_fusion), channel_id=1, source_target_pairs={{0,8},{1,9},{2,10},{3,11},{4,12},{5,13},{6,14},{7,15},{16,24},{17,... | collective-permute-start | bytes 10616840 | tf_op jit(solution)/shard_map/ppermute | solution.py:535
  746.0 78.2 %collective-permute-start.56 = (bf16[3072,768]{1,0:T(8,128)(2,1)}, bf16[3072,768]{1,0:T(8,128)(2,1)}, u32[]{:S(2)}, u32[]{:S(2)}) collective-permute-start(bf16[3072,768]{1,0:T(8,128)(2,1)} %convolution_convert_fusion.3), channel_id=1, source_target_pairs={{8,0},{9,1},{10,2},{11,3},{12,4},{13,5},{14,6},{15,7},{24,16},{25,... | collective-permute-start | bytes 14155784 | tf_op jit(solution)/shard_map/ppermute | solution.py:535
  771.1 62.7 %collective-permute-start.46 = (bf16[768,3072]{1,0:T(8,128)(2,1)}, bf16[768,3072]{1,0:T(8,128)(2,1)}, u32[]{:S(2)}, u32[]{:S(2)}) collective-permute-start(bf16[768,3072]{1,0:T(8,128)(2,1)} %convolution_convert_fusion.5), channel_id=1, source_target_pairs={{8,0},{9,1},{10,2},{11,3},{12,4},{13,5},{14,6},{15,7},{24,16},{25,... | collective-permute-start | bytes 14155784 | tf_op jit(solution)/shard_map/ppermute | solution.py:535
  808.7 225.6 %all-to-all-start.19 = ((bf16[2,192,768]{2,1,0:T(8,128)(2,1)}), bf16[2,192,768]{2,1,0:T(8,128)(2,1)}, u32[]{:S(2)}, u32[]{:S(2)}) async-start(bf16[2,192,768]{2,1,0:T(8,128)(2,1)} %all-to-all-done.18), calls=%async_computation.19 | async-start | bytes 1179648 | tf_op jit(solution)/shard_map/all_to_all | solution.py:580
  828.2 190.7 %collective-permute-start.45 = (bf16[384,768]{1,0:T(8,128)(2,1)S(1)}, bf16[384,768]{1,0:T(8,128)(2,1)}, u32[]{:S(2)}, u32[]{:S(2)}) collective-permute-start(bf16[384,768]{1,0:T(8,128)(2,1)S(1)} %copy-done.19), channel_id=1, source_target_pairs={{10,8},{12,14},{11,9},{13,15},{26,24},{28,30},{27,25},{29,31}} | collective-permute-start | bytes 1769480 | tf_op jit(solution)/shard_map/ppermute | solution.py:557
  833.8 47.8 %collective-permute-start.57 = (bf16[1536,768]{1,0:T(8,128)(2,1)S(1)}, bf16[1536,768]{1,0:T(8,128)(2,1)S(1)}, u32[]{:S(2)}, u32[]{:S(2)}) collective-permute-start(bf16[1536,768]{1,0:T(8,128)(2,1)S(1)} %add_convert_fusion.8), channel_id=1, source_target_pairs={{0,1},{1,0},{2,3},{3,2},{4,5},{5,4},{6,7},{7,6},{16,17},{17,16},{1... | collective-permute-start | bytes 7077896 | tf_op jit(solution)/shard_map/ppermute | solution.py:546
  839.5 87.8 %collective-permute-start.47 = (bf16[384,3072]{1,0:T(8,128)(2,1)S(1)}, bf16[384,3072]{1,0:T(8,128)(2,1)}, u32[]{:S(2)}, u32[]{:S(2)}) collective-permute-start(bf16[384,3072]{1,0:T(8,128)(2,1)S(1)} %add_convert_fusion.18), channel_id=1, source_target_pairs={{0,1},{1,0},{2,3},{3,2},{4,5},{5,4},{6,7},{7,6},{16,17},{17,16},{1... | collective-permute-start | bytes 7077896 | tf_op jit(solution)/shard_map/ppermute | solution.py:546
  845.4 40.4 %collective-permute-start.33 = (bf16[384,2304]{1,0:T(8,128)(2,1)S(1)}, bf16[384,2304]{1,0:T(8,128)(2,1)S(1)}, u32[]{:S(2)}, u32[]{:S(2)}) collective-permute-start(bf16[384,2304]{1,0:T(8,128)(2,1)S(1)} %add_convert_fusion.22), channel_id=1, source_target_pairs={{8,10},{14,12},{9,11},{15,13},{24,26},{30,28},{25,27},{31,29}} | collective-permute-start | bytes 5308424 | tf_op jit(solution)/shard_map/ppermute | solution.py:557
  846.7 79.1 %collective-permute-start.27 = (bf16[384,2304]{1,0:T(8,128)(2,1)S(1)}, bf16[384,2304]{1,0:T(8,128)(2,1)S(1)}, u32[]{:S(2)}, u32[]{:S(2)}) collective-permute-start(bf16[384,2304]{1,0:T(8,128)(2,1)S(1)} %add_convert_fusion.28), channel_id=1, source_target_pairs={{0,1},{1,0},{2,3},{3,2},{4,5},{5,4},{6,7},{7,6},{16,17},{17,16},{1... | collective-permute-start | bytes 5308424 | tf_op jit(solution)/shard_map/ppermute | solution.py:546
  881.6 59.0 %collective-permute-start.63 = (bf16[1536,768]{1,0:T(8,128)(2,1)S(1)}, bf16[1536,768]{1,0:T(8,128)(2,1)S(1)}, u32[]{:S(2)}, u32[]{:S(2)}) collective-permute-start(bf16[1536,768]{1,0:T(8,128)(2,1)S(1)} %add_convert_fusion.2), channel_id=1, source_target_pairs={{8,10},{14,12},{9,11},{15,13},{24,26},{30,28},{25,27},{31,29}} | collective-permute-start | bytes 7077896 | tf_op jit(solution)/shard_map/ppermute | solution.py:557
  885.8 121.0 %collective-permute-start.58 = (bf16[1536,768]{1,0:T(8,128)(2,1)S(1)}, bf16[1536,768]{1,0:T(8,128)(2,1)S(1)}, u32[]{:S(2)}, u32[]{:S(2)}) collective-permute-start(bf16[1536,768]{1,0:T(8,128)(2,1)S(1)} %add_convert_fusion.7), channel_id=1, source_target_pairs={{0,2},{6,4},{1,3},{7,5},{16,18},{22,20},{17,19},{23,21}} | collective-permute-start | bytes 7077896 | tf_op jit(solution)/shard_map/ppermute | solution.py:557
  927.2 51.8 %collective-permute-start.28 = (bf16[384,2304]{1,0:T(8,128)(2,1)S(1)}, bf16[384,2304]{1,0:T(8,128)(2,1)}, u32[]{:S(2)}, u32[]{:S(2)}) collective-permute-start(bf16[384,2304]{1,0:T(8,128)(2,1)S(1)} %add_convert_fusion.27), channel_id=1, source_target_pairs={{0,2},{6,4},{1,3},{7,5},{16,18},{22,20},{17,19},{23,21}} | collective-permute-start | bytes 5308424 | tf_op jit(solution)/shard_map/ppermute | solution.py:557
  940.6 63.8 %collective-permute-start.48 = (bf16[384,3072]{1,0:T(8,128)(2,1)S(1)}, bf16[384,3072]{1,0:T(8,128)(2,1)S(1)}, u32[]{:S(2)}, u32[]{:S(2)}) collective-permute-start(bf16[384,3072]{1,0:T(8,128)(2,1)S(1)} %add_convert_fusion.17), channel_id=1, source_target_pairs={{0,2},{6,4},{1,3},{7,5},{16,18},{22,20},{17,19},{23,21}} | collective-permute-start | bytes 7077896 | tf_op jit(solution)/shard_map/ppermute | solution.py:557
  942.7 65.6 %collective-permute-start.64 = (bf16[1536,768]{1,0:T(8,128)(2,1)S(1)}, bf16[1536,768]{1,0:T(8,128)(2,1)S(1)}, u32[]{:S(2)}, u32[]{:S(2)}) collective-permute-start(bf16[1536,768]{1,0:T(8,128)(2,1)S(1)} %add_convert_fusion.1), channel_id=1, source_target_pairs={{10,12},{12,10},{11,13},{13,11},{26,28},{28,26},{27,29},{29,27}} | collective-permute-start | bytes 7077896 | tf_op jit(solution)/shard_map/ppermute | solution.py:557
  1015.4 104.2 %collective-permute-start.30 = (bf16[384,2304]{1,0:T(8,128)(2,1)}, bf16[384,2304]{1,0:T(8,128)(2,1)}, u32[]{:S(2)}, u32[]{:S(2)}) collective-permute-start(bf16[384,2304]{1,0:T(8,128)(2,1)} %add_convert_fusion.25), channel_id=1, source_target_pairs={{2,0},{4,6},{3,1},{5,7},{18,16},{20,22},{19,17},{21,23}} | collective-permute-start | bytes 5308424 | tf_op jit(solution)/shard_map/ppermute | solution.py:557
  1018.9 104.3 %collective-permute-start.65 = (bf16[1536,768]{1,0:T(8,128)(2,1)}, bf16[1536,768]{1,0:T(8,128)(2,1)}, u32[]{:S(2)}, u32[]{:S(2)}) collective-permute-start(bf16[1536,768]{1,0:T(8,128)(2,1)} %add_convert_fusion), channel_id=1, source_target_pairs={{10,8},{12,14},{11,9},{13,15},{26,24},{28,30},{27,25},{29,31}} | collective-permute-start | bytes 7077896 | tf_op jit(solution)/shard_map/ppermute | solution.py:557
  1021.1 149.0 %collective-permute-start.60 = (bf16[1536,768]{1,0:T(8,128)(2,1)}, bf16[1536,768]{1,0:T(8,128)(2,1)}, u32[]{:S(2)}, u32[]{:S(2)}) collective-permute-start(bf16[1536,768]{1,0:T(8,128)(2,1)} %add_convert_fusion.5), channel_id=1, source_target_pairs={{2,0},{4,6},{3,1},{5,7},{18,16},{20,22},{19,17},{21,23}} | collective-permute-start | bytes 7077896 | tf_op jit(solution)/shard_map/ppermute | solution.py:557
  1024.7 150.5 %collective-permute-start.55 = (bf16[384,3072]{1,0:T(8,128)(2,1)S(1)}, bf16[384,3072]{1,0:T(8,128)(2,1)}, u32[]{:S(2)}, u32[]{:S(2)}) collective-permute-start(bf16[384,3072]{1,0:T(8,128)(2,1)S(1)} %add_convert_fusion.10), channel_id=1, source_target_pairs={{10,8},{12,14},{11,9},{13,15},{26,24},{28,30},{27,25},{29,31}} | collective-permute-start | bytes 7077896 | tf_op jit(solution)/shard_map/ppermute | solution.py:557
  1028.0 168.5 %collective-permute-start.50 = (bf16[384,3072]{1,0:T(8,128)(2,1)}, bf16[384,3072]{1,0:T(8,128)(2,1)}, u32[]{:S(2)}, u32[]{:S(2)}) collective-permute-start(bf16[384,3072]{1,0:T(8,128)(2,1)} %add_convert_fusion.15), channel_id=1, source_target_pairs={{2,0},{4,6},{3,1},{5,7},{18,16},{20,22},{19,17},{21,23}} | collective-permute-start | bytes 7077896 | tf_op jit(solution)/shard_map/ppermute | solution.py:557
  (124 other events, 1621.8 us)
Sparse Core Ops, SparseCore 0:
  12.6 33.5 all-gather.10
  47.7 29.7 all-gather.12
  79.7 35.5 all-gather.14
  117.2 31.5 all-gather.16
  150.3 29.1 all-gather.18
  180.9 29.3 all-gather.20
  212.4 36.0 all-gather.22
  250.6 31.5 all-gather.24

commit v2 on v1

--- a/solution.py
+++ b/solution.py
@@ -57,19 +57,22 @@
 
 
 def qkv_body(x_ref, gain_ref, shift_ref, w_ref, bias_ref, out_ref, normed_ref):
-    scaled, _ = norm_parts(x_ref[...].astype(F32))
-    normed = (scaled * gain_ref[...] + shift_ref[...]).astype(BF16)
-    normed_ref[...] = normed
+    @pl.when(pl.program_id(0) == 0)
+    def _():
+        scaled, _ = norm_parts(x_ref[...].astype(F32))
+        normed_ref[...] = (scaled * gain_ref[...] + shift_ref[...]).astype(BF16)
+
     span = out_ref.shape[2] // 3
-    width = x_ref.shape[1]
+    piece = (dot(normed_ref[...], w_ref[...]) + bias_ref[...]).astype(BF16)
     for part in range(3):
-        cols = slice(part * width, (part + 1) * width)
-        piece = (dot(normed, w_ref[:, cols]) + bias_ref[:, cols]).astype(BF16)
-        for g in range(HEAD_GROUPS):
-            out_ref[g, :, part * span : (part + 1) * span] = piece[:, g * span : (g + 1) * span]
-
-
-def qkv_forward(x, gain, shift, w_qkv, bias):
+
+        @pl.when(pl.program_id(0) == part)
+        def _(part=part):
+            for g in range(HEAD_GROUPS):
+                out_ref[g, :, part * span : (part + 1) * span] = piece[:, g * span : (g + 1) * span]
+
+
+def qkv_forward(x, gain, shift, joined, bias):
     rows, width = x.shape
     span = width // HEAD_GROUPS
     return call(
@@ -78,9 +81,18 @@
             jax.ShapeDtypeStruct((HEAD_GROUPS, rows, 3 * span), BF16),
             jax.ShapeDtypeStruct((rows, width), BF16),
         ),
+        grid=(3,),
+        in_specs=[
+            whole((rows, width)),
+            whole((1, width)),
+            whole((1, width)),
+            pl.BlockSpec((width, width), lambda i: (0, i)),
+            pl.BlockSpec((1, width), lambda i: (0, i)),
+        ],
+        out_specs=(whole((HEAD_GROUPS, rows, 3 * span)), whole((rows, width))),
         flops=2 * rows * width * 3 * width,
-        moved=2 * w_qkv.size + 10 * x.size,
-    )(x, gain, shift, w_qkv, bias)
+        moved=6 * width * width + 10 * x.size,
+    )(x, gain, shift, joined, bias)
 
 
 def key_chunks(own_ref, other_ref):
@@ -216,7 +228,7 @@
             place += rows
 
 
-def attend_backward(own, other, grad, log_total, head):
+def attend_backward(own, other, grad, log_total, head, after=()):
     clips, queries, wide = own.shape
     span = wide // 3
     others = other.shape[1]
@@ -225,7 +237,7 @@
     heads = span // head
 
     def body(*refs):
-        attend_back_body(*refs, head=head)
+        attend_back_body(*refs[:5], *refs[5 + len(after) :], head=head)
 
     return call(
         body,
@@ -241,7 +253,8 @@
             pl.BlockSpec((1, others, wide), lambda m, i: (m, 0, 0)),
             pl.BlockSpec((1, block, span), lambda m, i: (m, i, 0)),
             pl.BlockSpec((1, heads, block), lambda m, i: (m, 0, i)),
-        ],
+        ]
+        + [pl.BlockSpec(memory_space=pl.ANY)] * len(after),
         out_specs=(
             pl.BlockSpec((1, block, span), lambda m, i: (m, i, 0)),
             pl.BlockSpec((1, queries, 2 * span), lambda m, i: (m, 0, 0)),
@@ -255,7 +268,7 @@
         ],
         flops=40 * clips * queries * keys * span,
         moved=8 * (own.size + other.size),
-    )(own, own, other, grad, log_total)
+    )(own, own, other, grad, log_total, *after)
 
 
 def feed_body(
@@ -270,28 +283,34 @@
     w_down_ref,
     b_down_ref,
     y_ref,
-    x1_ref,
-    normed_ref,
-    slope_ref,
-    lifted_ref,
-    acc,
+    *rest,
 ):
+    if len(rest) > 2:
+        x1_ref, normed_ref, slope_ref, lifted_ref, flat_ref, acc = rest
+    else:
+        normed_ref, acc = rest
+    span = att_ref.shape[2]
+
     @pl.when(pl.program_id(0) == 0)
     def _():
         middle = x_ref[...].astype(F32) + b_out_ref[...]
         for g in range(HEAD_GROUPS):
-            middle = middle + dot(att_ref[g], w_out_ref[g])
-        x1_ref[...] = middle
+            middle = middle + dot(att_ref[g], w_out_ref[g * span : (g + 1) * span, :])
+            if len(rest) > 2:
+                flat_ref[:, g * span : (g + 1) * span] = att_ref[g]
+        if len(rest) > 2:
+            x1_ref[...] = middle
         scaled, _ = norm_parts(middle)
         normed_ref[...] = (scaled * gain_ref[...] + shift_ref[...]).astype(BF16)
         acc[...] = middle + b_down_ref[...]
 
     upper = dot(normed_ref[...], w_up_ref[...]) + b_up_ref[...]
     phi = 0.5 * (1.0 + lax.erf(upper * math.sqrt(0.5)))
-    density = jnp.exp(-0.5 * upper * upper) * (1.0 / math.sqrt(2.0 * math.pi))
-    slope_ref[...] = phi + upper * density
     lifted = (upper * phi).astype(BF16)
-    lifted_ref[...] = lifted
+    if len(rest) > 2:
+        density = jnp.exp(-0.5 * upper * upper) * (1.0 / math.sqrt(2.0 * math.pi))
+        slope_ref[...] = phi + upper * density
+        lifted_ref[...] = lifted
     acc[...] += dot(lifted, w_down_ref[...])
 
     @pl.when(pl.program_id(0) == pl.num_programs(0) - 1)
@@ -303,45 +322,47 @@
     return pl.BlockSpec(shape, lambda i: (0,) * len(shape))
 
 
-def feed_forward(x, att, w_out, b_out, gain, shift, w_up, b_up, w_down, b_down):
+def feed_forward(x, att, joined, b_out, gain, shift, b_up, w_down, b_down, keep):
     rows, width = x.shape
-    hidden = w_up.shape[1]
-    chunk = hidden // 4
+    hidden = w_down.shape[0]
     row = whole((1, width))
     full = whole((rows, width))
-    return call(
-        feed_body,
-        (
-            jax.ShapeDtypeStruct((rows, width), BF16),
+    part = pl.BlockSpec((rows, width), lambda i: (0, i))
+    shapes = [jax.ShapeDtypeStruct((rows, width), BF16)]
+    specs = [full]
+    scratch = [pltpu.VMEM((rows, width), F32)]
+    if keep:
+        shapes += [
             jax.ShapeDtypeStruct((rows, width), F32),
             jax.ShapeDtypeStruct((rows, width), BF16),
             jax.ShapeDtypeStruct((rows, hidden), F32),
             jax.ShapeDtypeStruct((rows, hidden), BF16),
-        ),
-        grid=(hidden // chunk,),
+            jax.ShapeDtypeStruct((rows, width), BF16),
+        ]
+        specs += [full, full, part, part, full]
+    else:
+        scratch = [pltpu.VMEM((rows, width), BF16)] + scratch
+    return call(
+        feed_body,
+        tuple(shapes),
+        grid=(hidden // width,),
         in_specs=[
             full,
             whole(att.shape),
-            whole(w_out.shape),
+            pl.BlockSpec((width, width), lambda i: (0, 3)),
             row,
             row,
             row,
-            pl.BlockSpec((width, chunk), lambda i: (0, i)),
-            pl.BlockSpec((1, chunk), lambda i: (0, i)),
-            pl.BlockSpec((chunk, width), lambda i: (i, 0)),
+            pl.BlockSpec((width, width), lambda i: (0, 4 + i)),
+            pl.BlockSpec((1, width), lambda i: (0, i)),
+            pl.BlockSpec((width, width), lambda i: (i, 0)),
             row,
         ],
-        out_specs=(
-            full,
-            full,
-            full,
-            pl.BlockSpec((rows, chunk), lambda i: (0, i)),
-            pl.BlockSpec((rows, chunk), lambda i: (0, i)),
-        ),
-        scratch=[pltpu.VMEM((rows, width), F32)],
+        out_specs=tuple(specs),
+        scratch=scratch,
         flops=2 * rows * width * (2 * hidden + width),
-        moved=4 * w_up.size + 2 * w_out.size + 10 * rows * hidden,
-    )(x, att, w_out, b_out, gain, shift, w_up, b_up, w_down, b_down)
+        moved=4 * w_down.size + 2 * width * width + 10 * rows * hidden,
+    )(x, att, joined, b_out, gain, shift, joined, b_up, w_down, b_down)
 
 
 def feed_back_body(
@@ -378,18 +399,19 @@
         dx1_ref[...] = d_middle
         branch = d_middle.astype(BF16)
         branch_ref[...] = branch
+        span = datt_ref.shape[2]
         for g in range(HEAD_GROUPS):
-            datt_ref[g] = dot_t(branch, w_out_ref[g]).astype(BF16)
+            datt_ref[g] = dot_t(branch, w_out_ref[g * span : (g + 1) * span, :]).astype(BF16)
         sums_ref[0:1, :] = jnp.sum(d_normed * scaled, axis=0, keepdims=True)
         sums_ref[1:2, :] = jnp.sum(d_normed, axis=0, keepdims=True)
         sums_ref[2:3, :] = jnp.sum(branch.astype(F32), axis=0, keepdims=True)
         sums_ref[3:4, :] = jnp.sum(upstream, axis=0, keepdims=True)
 
 
-def feed_backward(g, slope, w_down, w_up, w_out, x1, gain):
+def feed_backward(g, slope, w_down, joined, x1, gain):
     rows, width = g.shape
-    hidden = w_up.shape[1]
-    chunk = hidden // 4
+    hidden = w_down.shape[0]
+    chunk = width
     full = whole((rows, width))
     return call(
         feed_back_body,
@@ -406,8 +428,8 @@
             full,
             pl.BlockSpec((rows, chunk), lambda i: (0, i)),
             pl.BlockSpec((chunk, width), lambda i: (i, 0)),
-            pl.BlockSpec((width, chunk), lambda i: (0, i)),
-            whole(w_out.shape),
+            pl.BlockSpec((width, chunk), lambda i: (0, 4 + i)),
+            pl.BlockSpec((width, width), lambda i: (0, 3)),
             full,
             whole((1, width)),
         ],
@@ -421,42 +443,67 @@
         ),
         scratch=[pltpu.VMEM((rows, width), F32)],
         flops=2 * rows * width * (2 * hidden + width),
-        moved=4 * w_up.size + 2 * w_out.size + 6 * rows * hidden,
-    )(g, slope, w_down, w_up, w_out, x1, gain)
+        moved=4 * w_down.size + 2 * width * width + 6 * rows * hidden,
+    )(g, slope, w_down, joined, joined, x1, gain)
 
 
 def qkv_back_body(
-    grads_ref, w_ref, x_ref, dx1_ref, gain_ref, dx_ref, flat_ref, sums_ref
+    grads_ref, w_ref, x_ref, dx1_ref, gain_ref, dx_ref, flat_ref, sums_ref, acc
 ):
     width = x_ref.shape[1]
     span = grads_ref.shape[2] // 3
-    for g in range(HEAD_GROUPS):
-        for part in range(3):
-            flat_ref[:, part * width + g * span : part * width + (g + 1) * span] = grads_ref[
-                g, :, part * span : (part + 1) * span
-            ]
-    d_normed = dot_t(flat_ref[...], w_ref[...])
-    scaled, inverse = norm_parts(x_ref[...].astype(F32))
-    dx = dx1_ref[...] + norm_back(d_normed, scaled, inverse, gain_ref[...])
-    dx_ref[...] = dx.astype(BF16)
-    sums_ref[0:1, :] = jnp.sum(d_normed * scaled, axis=0, keepdims=True)
-    sums_ref[1:2, :] = jnp.sum(d_normed, axis=0, keepdims=True)
-    sums_ref[2:3, :] = jnp.sum(flat_ref[:, :width].astype(F32), axis=0, keepdims=True)
-    sums_ref[3:4, :] = jnp.sum(flat_ref[:, 2 * width :].astype(F32), axis=0, keepdims=True)
-
-
-def qkv_backward(grads, w_qkv, x, dx1, gain):
+    step = pl.program_id(0)
+    for part in range(3):
+
+        @pl.when(step == part)
+        def _(part=part):
+            cols = slice(part * width, (part + 1) * width)
+            for g in range(HEAD_GROUPS):
+                flat_ref[:, part * width + g * span : part * width + (g + 1) * span] = grads_ref[
+                    g, :, part * span : (part + 1) * span
+                ]
+            came = dot_t(flat_ref[:, cols], w_ref[...])
+            acc[...] = came if part == 0 else acc[...] + came
+
+    @pl.when(step == 2)
+    def _():
+        d_normed = acc[...]
+        scaled, inverse = norm_parts(x_ref[...].astype(F32))
+        dx = dx1_ref[...] + norm_back(d_normed, scaled, inverse, gain_ref[...])
+        dx_ref[...] = dx.astype(BF16)
+        sums_ref[0:1, :] = jnp.sum(d_normed * scaled, axis=0, keepdims=True)
+        sums_ref[1:2, :] = jnp.sum(d_normed, axis=0, keepdims=True)
+        sums_ref[2:3, :] = jnp.sum(flat_ref[:, :width].astype(F32), axis=0, keepdims=True)
+        sums_ref[3:4, :] = jnp.sum(flat_ref[:, 2 * width :].astype(F32), axis=0, keepdims=True)
+
+
+def qkv_backward(grads, joined, x, dx1, gain, after=()):
     rows, width = x.shape
+
+    def body(*refs):
+        qkv_back_body(*refs[:5], *refs[5 + len(after) :])
+
     return call(
-        qkv_back_body,
+        body,
         (
             jax.ShapeDtypeStruct((rows, width), BF16),
             jax.ShapeDtypeStruct((rows, 3 * width), BF16),
             jax.ShapeDtypeStruct((4, width), F32),
         ),
+        grid=(3,),
+        in_specs=[
+            whole(grads.shape),
+            pl.BlockSpec((width, width), lambda i: (0, i)),
+            whole((rows, width)),
+            whole((rows, width)),
+            whole((1, width)),
+        ]
+        + [pl.BlockSpec(memory_space=pl.ANY)] * len(after),
+        out_specs=(whole((rows, width)), whole((rows, 3 * width)), whole((4, width))),
+        scratch=[pltpu.VMEM((rows, width), F32)],
         flops=2 * rows * width * 3 * width,
-        moved=2 * w_qkv.size + 20 * x.size,
-    )(grads, w_qkv, x, dx1, gain)
+        moved=6 * width * width + 20 * x.size,
+    )(grads, joined, x, dx1, gain, *after)
 
 
 def swap(block, axis):
@@ -474,12 +521,16 @@
 
 def to_clips(block, clips):
     groups, rows, wide = block.shape
+    if clips == 1:
+        return block.reshape(1, groups * rows, wide)
     block = block.reshape(groups, clips, rows // clips, wide)
     return jnp.swapaxes(block, 0, 1).reshape(clips, groups * (rows // clips), wide)
 
 
 def to_tokens(block):
     clips, rows, wide = block.shape
+    if clips == 1:
+        return block.reshape(HEAD_GROUPS, rows // HEAD_GROUPS, wide)
     block = block.reshape(clips, HEAD_GROUPS, rows // HEAD_GROUPS, wide)
     return jnp.swapaxes(block, 0, 1).reshape(HEAD_GROUPS, -1, wide)
 
@@ -530,37 +581,55 @@
     return (one.astype(F32) + two.astype(F32)).astype(one.dtype)
 
 
-def reduce_rows(grad, layer):
+def cut_columns(left, which):
+    shards = lax.axis_size("side") * lax.axis_size("rest")
+    part = left.shape[1] // (2 * shards)
+    return jnp.concatenate(
+        [
+            lax.dynamic_slice_in_dim(left, (2 * s + which) * part, part, 1)
+            for s in range(shards)
+        ],
+        axis=1,
+    )
+
+
+def weight_halves(left, right):
+    core = lax.axis_index("core")
+    return [
+        t_dot(cut_columns(left, which), right).astype(BF16) for which in (1 - core, core)
+    ]
+
+
+def side_parts(sent, kept):
     side = lax.axis_index("side")
-    paired = lax.ppermute(grad, "core", [(1 - layer, layer)])
-    half = grad.shape[0] // 2
+    came = swap(sent, "core")
+    half = kept.shape[0] // 2
 
     def cut(which):
-        start = which * half
         return add(
-            lax.dynamic_slice_in_dim(grad, start, half, 0),
-            lax.dynamic_slice_in_dim(paired, start, half, 0),
+            lax.dynamic_slice_in_dim(kept, which * half, half, 0),
+            lax.dynamic_slice_in_dim(came, which * half, half, 0),
         )
 
-    two = 2 * layer
-    came = lax.ppermute(cut(1 - side), ("core", "side"), [(two, two + 1), (two + 1, two)])
-    total = add(cut(side), came)
+    return cut(1 - side), cut(side)
+
+
+def side_sum(sent, kept):
+    total = add(kept, swap(sent, "side"))
     if lax.axis_size("rest") > 1:
         total = lax.psum_scatter(total, "rest", scatter_dimension=0, tiled=True)
-    quads = lax.axis_size("quad")
-    if quads != 2:
-        return lax.psum(total, ("half", "quad"))
-    base = 4 * layer
-    line = ("core", "half", "quad")
-
-    def hop(block, pairs):
-        return lax.ppermute(block, line, [(base + a, base + b) for a, b in pairs])
-
-    total = add(total, hop(total, [(0, 1), (3, 2)]))
-    total = add(total, hop(total, [(1, 2), (2, 1)]))
-    came = hop(total, [(1, 0), (2, 3)])
-    inner = lax.axis_index("half") != lax.axis_index("quad")
-    return pick(inner, total, came)
+    return total
+
+
+def line_sum(*items):
+    return lax.psum(items, ("half", "quad"))
+
+
+def join_cores(first, second):
+    core = lax.axis_index("core")
+    came = swap(pick(core == 0, second, first), "core")
+    mine = pick(core == 0, first, second)
+    return jnp.concatenate([pick(core == 0, mine, came), pick(core == 0, came, mine)], axis=0)
 
 
 def swap_in(block):
@@ -581,59 +650,36 @@
     return both.reshape(micro, 2 * rows // micro, wide)
 
 
-def forward_layer(x, weights, clips, head):
-    w_qkv, w_out, w_up, w_down, gains, shifts, b_qkv, b_out, b_down, b_up = weights
-    width = x.shape[1]
-    grouped, normed_one = qkv_forward(x, gains[0:1], shifts[0:1], w_qkv, b_qkv)
+def forward_layer(x, weights, clips, head, keep):
+    joined, w_down, gains, shifts, b_qkv, b_out, b_down, b_up = weights
+    grouped, normed_one = qkv_forward(x, gains[0:1], shifts[0:1], joined, b_qkv)
     own = to_clips(spread(grouped), clips)
     other = other_keys(own)
     att, log_total = attend_forward(own, other, head)
     att = spread(to_tokens(att))
-    y, x1, normed_two, slope, lifted = feed_forward(
-        x,
-        att,
-        w_out.reshape(HEAD_GROUPS, width // HEAD_GROUPS, width),
-        b_out,
-        gains[1:2],
-        shifts[1:2],
-        w_up,
-        b_up,
-        w_down,
-        b_down,
-    )
-    return y, (x, normed_one, own, other, log_total, att, x1, normed_two, slope, lifted)
-
-
-def backward_layer(kept, g, weights, clips, head, with_weights):
-    x, normed_one, own, other, log_total, att, x1, normed_two, slope, lifted = kept
-    w_qkv, w_out, w_up, w_down, gains, shifts, b_qkv, b_out, b_down, b_up = weights
-    width = x.shape[1]
-    d_upper, dx1, branch, d_att, sums_two, up_sum = feed_backward(
-        g,
-        slope,
-        w_down,
-        w_up,
-        w_out.reshape(HEAD_GROUPS, width // HEAD_GROUPS, width),
-        x1,
-        gains[1:2],
-    )
+    y, *kept = feed_forward(
+        x, att, joined, b_out, gains[1:2], shifts[1:2], b_up, w_down, b_down, keep
+    )
+    return y, (x, normed_one, own, other, log_total, *kept)
+
+
+def attention_grads(kept, d_att, clips, head, after):
+    own, other, log_total = kept[2:5]
     d_heads = to_clips(spread(d_att), clips)
-    dq, kept_kv, sent_kv = attend_backward(own, other, d_heads, log_total, head)
+    dq, kept_kv, sent_kv = attend_backward(own, other, d_heads, log_total, head, after)
     dkv = return_keys(kept_kv, sent_kv).astype(BF16)
-    d_own = jnp.concatenate([dq, dkv], axis=2)
-    d_tokens = spread(to_tokens(d_own))
-    dx, flat, sums_one = qkv_backward(d_tokens, w_qkv, x, dx1, gains[0:1])
-    if not with_weights:
-        return dx, None
-    grad_down = t_dot(lifted, g).astype(BF16)
-    grad_up = t_dot(normed_two, d_upper).astype(BF16)
-    grad_out = jnp.einsum("gtf,td->gfd", att, branch, preferred_element_type=F32)
-    grad_out = grad_out.astype(BF16).reshape(width, width)
-    grad_qkv = t_dot(normed_one, flat).astype(BF16)
-    return dx, (grad_qkv, grad_out, grad_up, grad_down, sums_one, sums_two, up_sum)
-
-
-def pack_small(sums_one, sums_two, up_sum, shards):
+    return spread(to_tokens(jnp.concatenate([dq, dkv], axis=2)))
+
+
+def backward_lean(kept, g, weights, clips, head):
+    x, _, _, _, _, x1, _, slope, _, _ = kept
+    joined, w_down, gains = weights[:3]
+    _, dx1, _, d_att, _, _ = feed_backward(g, slope, w_down, joined, x1, gains[1:2])
+    d_tokens = attention_grads(kept, d_att, clips, head, ())
+    return qkv_backward(d_tokens, joined, x, dx1, gains[0:1])[0]
+
+
+def small_rows(sums_one, sums_two, up_sum, shards, wide):
     rows = jnp.concatenate(
         [
             sums_one[0:1],
@@ -645,8 +691,89 @@
         ]
     )
     rows = jnp.swapaxes(rows.reshape(8, shards, -1), 0, 1).reshape(shards, -1)
-    packed = jnp.concatenate([rows, up_sum.reshape(shards, -1)], axis=1)
-    return packed.reshape(-1, 128)
+    packed = jnp.concatenate([rows, up_sum.reshape(shards, -1)], axis=1).astype(BF16)
+    packed = packed.reshape(shards, 2, -1)
+    lines = -(-packed.shape[2] // wide)
+    room = 16 * (-(-lines // 16)) * wide
+    packed = jnp.pad(packed, ((0, 0), (0, 0), (0, room - packed.shape[2])))
+    return packed.reshape(shards, 2, -1, wide)
+
+
+def beside(weight, rows):
+    shards, _, wide = rows.shape
+    return jnp.concatenate([weight.reshape(shards, -1, wide), rows], axis=1).reshape(-1, wide)
+
+
+def qkv_halves(normed_one, flat, sums_one, sums_two, up_sum, shards):
+    core = lax.axis_index("core")
+    rows = small_rows(sums_one, sums_two, up_sum, shards, flat.shape[1])
+    return [
+        beside(item, lax.dynamic_index_in_dim(rows, which, 1, keepdims=False))
+        for item, which in zip(weight_halves(normed_one, flat), (1 - core, core))
+    ]
+
+
+def backward_all(kept_first, kept_second, g, layers, clips, head, shards):
+    x, normed_one, _, _, _, x1, normed_two, slope, lifted, att = kept_second
+    joined, w_down, gains = layers[1][:3]
+    d_upper, dx1, branch, d_att, sums_two, up_sum = feed_backward(
+        g, slope, w_down, joined, x1, gains[1:2]
+    )
+    down = weight_halves(lifted, g)
+    up = weight_halves(normed_two, d_upper)
+    d_tokens = attention_grads(kept_second, d_att, clips, head, (*down, *up))
+    down, up = side_parts(*down), side_parts(*up)
+    out = weight_halves(att, branch)
+    d_second, flat, sums_one = qkv_backward(
+        d_tokens, joined, x, dx1, gains[0:1], (*down, *up, *out)
+    )
+    qkv = qkv_halves(normed_one, flat, sums_one, sums_two, up_sum, shards)
+
+    x, normed_one, _, _, _, x1, normed_two, slope, lifted, att = kept_first
+    joined, w_down, gains = layers[0][:3]
+    d_upper, dx1, branch, d_att, sums_two, up_sum = feed_backward(
+        d_second, slope, w_down, joined, x1, gains[1:2]
+    )
+    down_two = side_sum(*down)
+    down_one = weight_halves(lifted, d_second)
+    up_one = weight_halves(normed_two, d_upper)
+    d_tokens = attention_grads(
+        kept_first, d_att, clips, head, (*qkv, *down_one, *up_one, down_two)
+    )
+    (down_two,) = line_sum(down_two)
+    up_two = side_sum(*up)
+    out, qkv = side_parts(*out), side_parts(*qkv)
+    down_one, up_one = side_parts(*down_one), side_parts(*up_one)
+    out_one = weight_halves(att, branch)
+    d_first, flat, sums_one = qkv_backward(
+        d_tokens, joined, x, dx1, gains[0:1], (up_two, *out, *qkv, *down_one, *up_one, *out_one)
+    )
+    up_two, held = lax.optimization_barrier((up_two, down_two))
+    (up_two,) = line_sum(up_two)
+    qkv_one = qkv_halves(normed_one, flat, sums_one, sums_two, up_sum, shards)
+    out_two, qkv_two, _ = lax.optimization_barrier((side_sum(*out), side_sum(*qkv), up_two))
+    out_two, qkv_two = line_sum(out_two, qkv_two)
+    out_one, qkv_one = side_parts(*out_one), side_parts(*qkv_one)
+    down_one, up_one, _ = lax.optimization_barrier(
+        (side_sum(*down_one), side_sum(*up_one), qkv_two)
+    )
+    down_one, up_one = line_sum(down_one, up_one)
+    out_one, qkv_one, _ = lax.optimization_barrier((side_sum(*out_one), side_sum(*qkv_one), up_one))
+    out_one, qkv_one = line_sum(out_one, qkv_one)
+    firsts = (qkv_one, out_one, up_one, down_one)
+    seconds = (qkv_two, out_two, up_two, down_two)
+    return d_first, d_second, [join_cores(a, b) for a, b in zip(firsts, seconds)]
+
+
+def gather_small(block):
+    core, side = lax.axis_index("core"), lax.axis_index("side")
+    if lax.axis_size("rest") > 1:
+        whole_block = lax.all_gather(block, ("core", "side", "rest"), axis=0, tiled=False)
+        return whole_block.reshape(2, -1, block.shape[0])
+    came = swap(block, "side")
+    layer = jnp.stack([pick(side == 0, block, came), pick(side == 0, came, block)])
+    came = swap(layer, "core")
+    return jnp.stack([pick(core == 0, layer, came), pick(core == 0, came, layer)])
 
 
 def per_device(
@@ -654,30 +781,28 @@
 ):
     pairs = lax.axis_size("pair")
     pair = lax.axis_index("pair")
-    core = lax.axis_index("core")
     shards = lax.axis_size("side") * lax.axis_size("rest")
     micro, _, width = frames.shape
     clips = micro // 2
     head = width // HEADS
     part = width // shards
 
+    joined = gather_weight(jnp.concatenate([w_qkv[0], w_out[0], w_up[0]], axis=1))
+    downs = gather_weight(w_down[0])
     small = jnp.concatenate(
         [norm_gain.reshape(-1), norm_bias.reshape(-1), proj_bias.reshape(-1), up_bias.reshape(-1)]
     )
-    small = lax.all_gather(small, ("core", "side", "rest"), axis=0, tiled=False)
-    small = small.reshape(2, shards, -1).astype(F32)
+    small = gather_small(small).astype(F32)
     rows = jnp.swapaxes(small[:, :, : 8 * part].reshape(2, shards, 8, part), 1, 2)
     rows = rows.reshape(2, 8, width)
     ups = small[:, :, 8 * part :].reshape(2, 1, -1)
     x_start = swap_in(frames)
-    matrices = [gather_weight(item[0]) for item in (w_qkv, w_out, w_up, w_down)]
     layers = []
     for layer in range(2):
         r = rows[layer]
         b_qkv = jnp.concatenate([r[4:5], jnp.zeros_like(r[4:5]), r[5:6]], axis=1)
         layers.append(
-            tuple(m[layer] for m in matrices)
-            + (r[0:2], r[2:4], b_qkv, r[6:7], r[7:8], ups[layer])
+            (joined[layer], downs[layer], r[0:2], r[2:4], b_qkv, r[6:7], r[7:8], ups[layer])
         )
 
     x = x_start
@@ -685,40 +810,37 @@
         if phase > 0:
             came = lax.ppermute(second, "pair", [(i, i + 1) for i in range(pairs - 1)])
             x = pick(pair == 0, x_start, came)
-        first, kept_first = forward_layer(x, layers[0], clips, head)
-        second, kept_second = forward_layer(first, layers[1], clips, head)
+        keep = phase == pairs - 1
+        first, kept_first = forward_layer(x, layers[0], clips, head, keep)
+        second, kept_second = forward_layer(first, layers[1], clips, head, keep)
     hidden = swap_out(first, second, micro)
 
     g_start = swap_in(out_grad)
     g = g_start
-    for phase in range(pairs):
-        if phase > 0:
-            came = lax.ppermute(d_first, "pair", [(i + 1, i) for i in range(pairs - 1)])
-            g = pick(pair == pairs - 1, g_start, came)
-        last = phase == pairs - 1
-        d_second, grads_second = backward_layer(kept_second, g, layers[1], clips, head, last)
-        d_first, grads_first = backward_layer(kept_first, d_second, layers[0], clips, head, last)
+    for phase in range(pairs - 1):
+        d_second = backward_lean(kept_second, g, layers[1], clips, head)
+        d_first = backward_lean(kept_first, d_second, layers[0], clips, head)
+        came = lax.ppermute(d_first, "pair", [(i + 1, i) for i in range(pairs - 1)])
+        g = pick(pair == pairs - 1, g_start, came)
+    d_first, d_second, (qkv, out, up, down) = backward_all(
+        kept_first, kept_second, g, layers, clips, head, shards
+    )
     input_grads = swap_out(d_first, d_second, micro)
 
-    reduced = []
-    for layer, grads in ((1, grads_second), (0, grads_first)):
-        items = [reduce_rows(item, layer) for item in (grads[3], grads[2], grads[1], grads[0])]
-        items.append(reduce_rows(pack_small(*grads[4:], shards), layer))
-        reduced.append(items)
-    down, up, out, qkv, packed = [
-        pick(core == 0, zero, one).astype(F32) for one, zero in zip(*reduced)
-    ]
-    packed = packed.reshape(-1)
+    own_rows = part // 2
+    qkv = qkv.reshape(2, -1, 3 * width).astype(F32)
+    packed = qkv[:, own_rows:].reshape(2, -1)[:, : (8 * part + up_bias.shape[1]) // 2].reshape(-1)
     heads = packed[: 8 * part].reshape(8, part)
+    qkv = qkv[:, :own_rows].reshape(-1, 3 * width)
     return (
         hidden[None],
         input_grads[None],
         heads[0:2][None],
         heads[2:4][None],
         qkv[None],
-        out[None],
-        up[None],
-        down[None],
+        out.astype(F32)[None],
+        up.astype(F32)[None],
+        down.astype(F32)[None],
         heads[4:8][None],
         packed[8 * part :][None],
     )

time: 1220 us -> 1120 us (0.918)
  starting transfers between devices: 142 us -> 64.9 us
  blocking collectives: 180 us -> 142 us
  waiting for transfers between devices: 472 us -> 508 us
  other arithmetic: 112 us -> 85.7 us
    ppermute x50 -> x0, waiting for transfers between devices: 282 us -> none  [the longest x30 211 us: hop(): return lax.ppermute(block, line, [(base + a, base + b) for a, b in pairs])]
    psum x0 -> x5, waiting for transfers between devices: none -> 223 us  [line_sum(): return lax.psum(items, ('half', 'quad'))]
    ppermute x12 -> x32, waiting for transfers between devices: 16.8 us -> 127 us  [swap(): return lax.ppermute(block, axis, [(0, 1), (1, 0)])]
    ppermute x50 -> x0, starting transfers between devices: 96.6 us -> none  [the longest x30 52.4 us: hop(): return lax.ppermute(block, line, [(base + a, base + b) for a, b in pairs])]
    all_gather x8 -> x4, waiting for transfers between devices: 135 us -> 83.6 us  [gather_weight(): lax.all_gather(item, ('side', 'rest', 'core', 'quad'), axis=0, tiled=True)]
    all_to_all x2, waiting for transfers between devices: 4.77 us -> 34.7 us  [swap_out(): both = lax.all_to_all(both, 'half', 0, 0, tiled=True)]
    all_to_all x10 -> x8, blocking collectives: 156 us -> 131 us  [spread(): return lax.all_to_all(block, ('quad', 'side'), 0, 0, tiled=True)]
    convert_element_type x32 -> x16, other arithmetic: 68 us -> 43.2 us  [add(): return (one.astype(F32) + two.astype(F32)).astype(one.dtype)]
  transfers between devices with their start and end apart: 83 -> 55, of which waited for: 30 -> 29; matrix products, arithmetic and copies ran while one was open for 12% -> 11% of each run, Pallas kernels for 7% -> 9%
where the time goes in v2:
time: 1120 us; the launch traced here: 1110 us
  waiting for transfers between devices  508 us (45%)
  Pallas kernels  227 us (20%)
  blocking collectives  142 us (13%)
  other arithmetic  85.7 us (8%)
  starting transfers between devices  64.9 us (6%)
  local copies, waits for them, and re-layouts  40.3 us (4%)
  matrix products  29.1 us (3%)
  between operations  15.8 us (1%)
    psum x5, waiting for transfers between devices, line_sum(): return lax.psum(items, ('half', 'quad'))  223 us
    all_to_all x8, blocking collectives, spread(): return lax.all_to_all(block, ('quad', 'side'), 0, 0, tiled=True)  131 us
    ppermute x32, waiting for transfers between devices, swap(): return lax.ppermute(block, axis, [(0, 1), (1, 0)])  127 us
    all_gather x4, waiting for transfers between devices, gather_weight(): lax.all_gather(item, ('side', 'rest', 'core', 'quad'), axis=0, tiled=True)  83.6 us
    pallas_call x4, Pallas kernels, attend_backward(): call(body, (jax.ShapeDtypeStruct((clips, queries, span), BF16), jax.Shape...  71 us
    convert_element_type x16, other arithmetic, add(): return (one.astype(F32) + two.astype(F32)).astype(one.dtype)  43.2 us
    pallas_call x4, Pallas kernels, feed_backward(): call(feed_back_body, (jax.ShapeDtypeStruct((rows, hidden), BF16), jax.Sha...  39.8 us
    pallas_call x4, Pallas kernels, attend_forward(): call(body, (jax.ShapeDtypeStruct((clips, queries, span), BF16), jax.Shape...  39.2 us
  transfers between devices with their start and end apart: 55, of which 29 were waited for; matrix products, arithmetic and copies ran while one was open for 11% of the time, Pallas kernels for 9%

profile of v2, /device:TPU:0, one launch (start us, length us, event | category | flops | bytes accessed | tf_op | source)
XLA Modules:
  0.0 1112.5 jit_solution(10229105529358260818)
XLA Ops:
  32.7 45.0 %all-gather.5.cloned.1.call-done.w_ref.w_out_ref.w_up_ref.refs_1_ = bf16[768,6144]{1,0:T(8,128)(2,1)} async-done(((bf16[96,6144]{1,0:T(8,128)(2,1)}), bf16[768,6144]{1,0:T(8,128)(2,1)}) %all-gather.5.cloned.1.call-update) | async-done | bytes 9437200 | tf_op jit(solution)/shard_map/all_gather | solution.py:575
  82.7 22.4 %all_to_all.100 = bf16[4,192,576]{2,1,0:T(8,128)(2,1)S(1)} all-to-all(bf16[4,192,576]{2,1,0:T(8,128)(2,1)} %get-tuple-element.77), channel_id=1, replica_groups=mesh['pair'=2,'core'=2,'half'=2,'quad'=2,'side'=2,'rest'=1] {'quad','side'}, dimensions={0} | all-to-all | bytes 1769472 | tf_op jit(solution)/shard_map/all_to_all | solution.py:519
  109.5 9.8 shard_map.178
  138.6 38.6 %all-gather.9.cloned.1.call-done.w_ref.w_out_ref.w_up_ref.refs_1_ = bf16[768,6144]{1,0:T(8,128)(2,1)} async-done(((bf16[96,6144]{1,0:T(8,128)(2,1)}), bf16[768,6144]{1,0:T(8,128)(2,1)}) %all-gather.9.cloned.1.call-update) | async-done | bytes 9437200 | tf_op jit(solution)/shard_map/all_gather | solution.py:575
  182.3 23.1 %all_to_all.101 = bf16[4,192,576]{2,1,0:T(8,128)(2,1)S(1)} all-to-all(bf16[4,192,576]{2,1,0:T(8,128)(2,1)} %get-tuple-element.79), channel_id=1, replica_groups=mesh['pair'=2,'core'=2,'half'=2,'quad'=2,'side'=2,'rest'=1] {'quad','side'}, dimensions={0} | all-to-all | bytes 1769472 | tf_op jit(solution)/shard_map/all_to_all | solution.py:519
  209.8 9.8 shard_map.181
  254.2 16.4 %all_to_all.102 = bf16[4,192,576]{2,1,0:T(8,128)(2,1)S(1)} all-to-all(bf16[4,192,576]{2,1,0:T(8,128)(2,1)} %get-tuple-element.81), channel_id=1, replica_groups=mesh['pair'=2,'core'=2,'half'=2,'quad'=2,'side'=2,'rest'=1] {'quad','side'}, dimensions={0} | all-to-all | bytes 1769472 | tf_op jit(solution)/shard_map/all_to_all | solution.py:519
  275.0 9.8 shard_map.184
  284.8 11.9 %all_to_all.103.att_ref = bf16[4,192,192]{2,1,0:T(8,128)(2,1)} all-to-all(bf16[4,192,192]{2,1,0:T(8,128)(2,1)} %bitcast.229), channel_id=1, replica_groups=mesh['pair'=2,'core'=2,'half'=2,'quad'=2,'side'=2,'rest'=1] {'quad','side'}, dimensions={0} | all-to-all | bytes 589824 | tf_op jit(solution)/shard_map/all_to_all | solution.py:519
  311.0 16.5 %all_to_all.104 = bf16[4,192,576]{2,1,0:T(8,128)(2,1)S(1)} all-to-all(bf16[4,192,576]{2,1,0:T(8,128)(2,1)} %get-tuple-element.84), channel_id=1, replica_groups=mesh['pair'=2,'core'=2,'half'=2,'quad'=2,'side'=2,'rest'=1] {'quad','side'}, dimensions={0} | all-to-all | bytes 1769472 | tf_op jit(solution)/shard_map/all_to_all | solution.py:519
  331.9 9.8 shard_map.187
  361.4 10.0 shard_map.189
  371.4 11.4 %all_to_all.105 = bf16[4,192,192]{2,1,0:T(8,128)(2,1)} all-to-all(bf16[4,192,192]{2,1,0:T(8,128)(2,1)} %get-tuple-element.89), channel_id=1, replica_groups=mesh['pair'=2,'core'=2,'half'=2,'quad'=2,'side'=2,'rest'=1] {'quad','side'}, dimensions={0} | all-to-all | bytes 589824 | tf_op jit(solution)/shard_map/all_to_all | solution.py:519
  382.8 17.7 %shard_map.190 = (bf16[1,768,192]{2,1,0:T(8,128)(2,1)}, f32[1,768,384]{2,1,0:T(8,128)}, bf16[1,768,384]{2,1,0:T(8,128)(2,1)}) custom-call(bf16[1,768,576]{2,1,0:T(8,128)(2,1)} %bitcast.204, bf16[1,768,576]{2,1,0:T(8,128)(2,1)} %bitcast.205, bf16[1,768,576]{2,1,0:T(8,128)(2,1)} %copy.29.refs_2_, bf16[1,768,192]{2,1,0:T(8,128)(2,1)} %bitcast.227, ...), custom_call_target="tpu_custom_call" | custom-call | flops 9059696640 | bytes 7077888 | tf_op jit(solution)/shard_map/pallas_call | solution.py:242
  405.4 17.7 %all_to_all.106.refs_0_ = bf16[4,192,576]{2,1,0:T(8,128)(2,1)} all-to-all(bf16[4,192,576]{2,1,0:T(8,128)(2,1)S(1)} %bitcast.216), channel_id=1, replica_groups=mesh['pair'=2,'core'=2,'half'=2,'quad'=2,'side'=2,'rest'=1] {'quad','side'}, dimensions={0} | all-to-all | bytes 1769472 | tf_op jit(solution)/shard_map/all_to_all | solution.py:519
  428.7 10.0 shard_map.192
  438.7 11.1 %all_to_all.107 = bf16[4,192,192]{2,1,0:T(8,128)(2,1)} all-to-all(bf16[4,192,192]{2,1,0:T(8,128)(2,1)} %get-tuple-element.98), channel_id=1, replica_groups=mesh['pair'=2,'core'=2,'half'=2,'quad'=2,'side'=2,'rest'=1] {'quad','side'}, dimensions={0} | all-to-all | bytes 589824 | tf_op jit(solution)/shard_map/all_to_all | solution.py:519
  449.9 17.7 %shard_map.193 = (bf16[1,768,192]{2,1,0:T(8,128)(2,1)}, f32[1,768,384]{2,1,0:T(8,128)}, bf16[1,768,384]{2,1,0:T(8,128)(2,1)}) custom-call(bf16[1,768,576]{2,1,0:T(8,128)(2,1)} %bitcast.197, bf16[1,768,576]{2,1,0:T(8,128)(2,1)} %bitcast.198, bf16[1,768,576]{2,1,0:T(8,128)(2,1)} %copy.27.refs_2_, bf16[1,768,192]{2,1,0:T(8,128)(2,1)} %bitcast.228, ...), custom_call_target="tpu_custom_call" | custom-call | flops 9059696640 | bytes 7077888 | tf_op jit(solution)/shard_map/pallas_call | solution.py:242
  478.3 11.4 %all-to-all-done.13.refs_0_ = bf16[4,192,576]{2,1,0:T(8,128)(2,1)S(1)} async-done(((bf16[4,192,576]{2,1,0:T(8,128)(2,1)}), bf16[4,192,576]{2,1,0:T(8,128)(2,1)S(1)}, u32[]{:S(2)}, u32[]{:S(2)}) %all-to-all-start.13) | async-done | bytes 884768 | tf_op jit(solution)/shard_map/all_to_all | solution.py:519
  509.2 9.9 shard_map.195
  535.9 17.8 %shard_map.196 = (bf16[1,768,192]{2,1,0:T(8,128)(2,1)}, f32[1,768,384]{2,1,0:T(8,128)}, bf16[1,768,384]{2,1,0:T(8,128)(2,1)}) custom-call(bf16[1,768,576]{2,1,0:T(8,128)(2,1)} %bitcast.206, bf16[1,768,576]{2,1,0:T(8,128)(2,1)} %bitcast.207, bf16[1,768,576]{2,1,0:T(8,128)(2,1)} %copy.29.refs_2_, bf16[1,768,192]{2,1,0:T(8,128)(2,1)} %bitcast.223, ...), custom_call_target="tpu_custom_call" | custom-call | flops 9059696640 | bytes 7077888 | tf_op jit(solution)/shard_map/pallas_call | solution.py:242
  570.8 51.6 %collective-permute-done.30 = bf16[192,768]{1,0:T(8,128)(2,1)S(1)} collective-permute-done((bf16[192,768]{1,0:T(8,128)(2,1)S(1)}, bf16[192,768]{1,0:T(8,128)(2,1)S(1)}, u32[]{:S(2)}, u32[]{:S(2)}) %collective-permute-start.30) | collective-permute-done | bytes 294944 | tf_op jit(solution)/shard_map/ppermute | solution.py:510
  638.4 9.9 shard_map.198
  670.3 17.8 %shard_map.199 = (bf16[1,768,192]{2,1,0:T(8,128)(2,1)}, f32[1,768,384]{2,1,0:T(8,128)}, bf16[1,768,384]{2,1,0:T(8,128)(2,1)}) custom-call(bf16[1,768,576]{2,1,0:T(8,128)(2,1)} %bitcast.199, bf16[1,768,576]{2,1,0:T(8,128)(2,1)} %bitcast.200, bf16[1,768,576]{2,1,0:T(8,128)(2,1)} %copy.27.refs_2_, bf16[1,768,192]{2,1,0:T(8,128)(2,1)} %bitcast.222, ...), custom_call_target="tpu_custom_call" | custom-call | flops 9059696640 | bytes 7077888 | tf_op jit(solution)/shard_map/pallas_call | solution.py:242
  707.6 9.9 collective-permute-done.31
  721.0 25.7 %collective-permute-done.28 = bf16[768,768]{1,0:T(8,128)(2,1)} collective-permute-done((bf16[768,768]{1,0:T(8,128)(2,1)S(1)}, bf16[768,768]{1,0:T(8,128)(2,1)}, u32[]{:S(2)}, u32[]{:S(2)}) %collective-permute-start.28) | collective-permute-done | bytes 1179680 | tf_op jit(solution)/shard_map/ppermute | solution.py:510
  750.3 21.7 %collective-permute-done.29 = bf16[192,3072]{1,0:T(8,128)(2,1)} collective-permute-done((bf16[192,3072]{1,0:T(8,128)(2,1)}, bf16[192,3072]{1,0:T(8,128)(2,1)}, u32[]{:S(2)}, u32[]{:S(2)}) %collective-permute-start.29) | collective-permute-done | bytes 1179680 | tf_op jit(solution)/shard_map/ppermute | solution.py:510
  790.5 52.5 %all-reduce.11.cloned.1.call-done = bf16[192,3072]{1,0:T(8,128)(2,1)} async-done(((bf16[192,3072]{1,0:T(8,128)(2,1)}), bf16[192,3072]{1,0:T(8,128)(2,1)}) %all-reduce.11.cloned.1.call-update) | async-done | bytes 1179664 | tf_op jit(solution)/shard_map/psum | solution.py:625
  850.9 43.5 %all-reduce.13.cloned.1.call-done = bf16[208,2304]{1,0:T(8,128)(2,1)} async-done(((bf16[208,2304]{1,0:T(8,128)(2,1)}), bf16[208,2304]{1,0:T(8,128)(2,1)}) %all-reduce.13.cloned.1.call-update) | async-done | bytes 958480 | tf_op jit(solution)/shard_map/psum | solution.py:625
  908.7 56.2 %all-reduce.15.cloned.1.call-done = bf16[192,3072]{1,0:T(8,128)(2,1)} async-done(((bf16[192,3072]{1,0:T(8,128)(2,1)}), bf16[192,3072]{1,0:T(8,128)(2,1)}) %all-reduce.15.cloned.1.call-update) | async-done | bytes 1179664 | tf_op jit(solution)/shard_map/psum | solution.py:625
  978.9 34.7 %all-to-all-done.19 = bf16[2,192,768]{2,1,0:T(8,128)(2,1)} async-done(((bf16[2,192,768]{2,1,0:T(8,128)(2,1)}), bf16[2,192,768]{2,1,0:T(8,128)(2,1)}, u32[]{:S(2)}, u32[]{:S(2)}) %all-to-all-start.19) | async-done | bytes 589856 | tf_op jit(solution)/shard_map/all_to_all | solution.py:649
  1017.8 71.1 %all-reduce.17.cloned.1.call-done = (bf16[208,2304]{1,0:T(8,128)(2,1)}, bf16[192,768]{1,0:T(8,128)(2,1)}, bf16[192,768]{1,0:T(8,128)(2,1)}, bf16[768,768]{1,0:T(8,128)(2,1)}) async-done(((bf16[208,2304]{1,0:T(8,128)(2,1)}, bf16[192,768]{1,0:T(8,128)(2,1)}, bf16[192,768]{1,0:T(8,128)(2,1)}, bf16[768,768]{1,0:T(8,128)(2,1)}), (bf16[208,2304]{1,0:T(8,128)(2,1)}, bf16[192,768]{1,0:T(8,128)(2,1)}, ...) | async-done | bytes 2727952 | tf_op jit(solution)/shard_map/psum | solution.py:625
  (467 shorter events, 354.1 us)
Async XLA Ops:
  7.2 70.5 %all-gather.5.cloned.1.call-start = ((), (), s32[]{:S(2)}) async-start(), calls=%async_computation.20 | async-start | bytes 10616832 | tf_op jit(solution)/shard_map/all_gather | solution.py:575
  18.4 108.5 %all-gather.7.cloned.1.call-start = ((), (), s32[]{:S(2)}) async-start(), calls=%async_computation.21 | async-start | bytes 5308416 | tf_op jit(solution)/shard_map/all_gather | solution.py:575
  23.1 154.2 %all-gather.9.cloned.1.call-start = ((), (), s32[]{:S(2)}) async-start(), calls=%async_computation.22 | async-start | bytes 10616832 | tf_op jit(solution)/shard_map/all_gather | solution.py:575
  23.8 202.4 %all-gather.11.cloned.1.call-start = ((), (), s32[]{:S(2)}) async-start(), calls=%async_computation.23 | async-start | bytes 5308416 | tf_op jit(solution)/shard_map/all_gather | solution.py:575
  472.6 17.1 %all-to-all-start.13 = ((bf16[4,192,576]{2,1,0:T(8,128)(2,1)}), bf16[4,192,576]{2,1,0:T(8,128)(2,1)S(1)}, u32[]{:S(2)}, u32[]{:S(2)}) async-start(bf16[4,192,576]{2,1,0:T(8,128)(2,1)} %bitcast.28), calls=%async_computation.13 | async-start | bytes 1966080 | tf_op jit(solution)/shard_map/all_to_all | solution.py:519
  509.2 44.6 %collective-permute-start.15 = (bf16[1536,768]{1,0:T(8,128)(2,1)}, bf16[1536,768]{1,0:T(8,128)(2,1)}, u32[]{:S(2)}, u32[]{:S(2)}) collective-permute-start(bf16[1536,768]{1,0:T(8,128)(2,1)} %convolution_convert_fusion.11.refs_5_), channel_id=1, source_target_pairs={{0,8},{8,0},{1,9},{9,1},{2,10},{10,2},{3,11},{11,3},{4,12},{12,4},... | collective-permute-start | bytes 7077896 | tf_op jit(solution)/shard_map/ppermute | solution.py:510
  522.8 34.9 %collective-permute-start.16 = (bf16[384,3072]{1,0:T(8,128)(2,1)}, bf16[384,3072]{1,0:T(8,128)(2,1)}, u32[]{:S(2)}, u32[]{:S(2)}) collective-permute-start(bf16[384,3072]{1,0:T(8,128)(2,1)} %convolution_convert_fusion.7.refs_7_), channel_id=1, source_target_pairs={{0,8},{8,0},{1,9},{9,1},{2,10},{10,2},{3,11},{11,3},{4,12},{12,4},... | collective-permute-start | bytes 7077896 | tf_op jit(solution)/shard_map/ppermute | solution.py:510
  528.2 33.1 %collective-permute-start.20 = (bf16[384,768]{1,0:T(8,128)(2,1)S(1)}, bf16[384,768]{1,0:T(8,128)(2,1)}, u32[]{:S(2)}, u32[]{:S(2)}) collective-permute-start(bf16[384,768]{1,0:T(8,128)(2,1)S(1)} %convolution_convert_fusion.15.refs_9_), channel_id=1, source_target_pairs={{0,8},{8,0},{1,9},{9,1},{2,10},{10,2},{3,11},{11,3},{4,12},{12,4},... | collective-permute-start | bytes 1769480 | tf_op jit(solution)/shard_map/ppermute | solution.py:510
  556.5 67.8 %collective-permute-start.17 = (bf16[768,768]{1,0:T(8,128)(2,1)}, bf16[768,768]{1,0:T(8,128)(2,1)}, u32[]{:S(2)}, u32[]{:S(2)}) collective-permute-start(bf16[768,768]{1,0:T(8,128)(2,1)} %add_convert_fusion.11.refs_5_), channel_id=1, source_target_pairs={{0,1},{1,0},{2,3},{3,2},{4,5},{5,4},{6,7},{7,6},{8,9},{9,8},{10,11... | collective-permute-start | bytes 3538952 | tf_op jit(solution)/shard_map/ppermute | solution.py:510
  560.3 67.8 %collective-permute-start.19 = (bf16[192,3072]{1,0:T(8,128)(2,1)}, bf16[192,3072]{1,0:T(8,128)(2,1)}, u32[]{:S(2)}, u32[]{:S(2)}) collective-permute-start(bf16[192,3072]{1,0:T(8,128)(2,1)} %add_convert_fusion.9.refs_7_), channel_id=1, source_target_pairs={{0,1},{1,0},{2,3},{3,2},{4,5},{5,4},{6,7},{7,6},{8,9},{9,8},{10,11... | collective-permute-start | bytes 3538952 | tf_op jit(solution)/shard_map/ppermute | solution.py:510
  562.3 60.1 %collective-permute-start.30 = (bf16[192,768]{1,0:T(8,128)(2,1)S(1)}, bf16[192,768]{1,0:T(8,128)(2,1)S(1)}, u32[]{:S(2)}, u32[]{:S(2)}) collective-permute-start(bf16[192,768]{1,0:T(8,128)(2,1)S(1)} %add_convert_fusion.27.refs_6_), channel_id=1, source_target_pairs={{0,1},{1,0},{2,3},{3,2},{4,5},{5,4},{6,7},{7,6},{8,9},{9,8},{10,11... | collective-permute-start | bytes 884744 | tf_op jit(solution)/shard_map/ppermute | solution.py:510
  565.0 67.0 %all-to-all-start.15 = ((bf16[4,192,576]{2,1,0:T(8,128)(2,1)}), bf16[4,192,576]{2,1,0:T(8,128)(2,1)}, u32[]{:S(2)}, u32[]{:S(2)}) async-start(bf16[4,192,576]{2,1,0:T(8,128)(2,1)} %bitcast.214), calls=%async_computation.15 | async-start | bytes 1966080 | tf_op jit(solution)/shard_map/all_to_all | solution.py:519
  648.3 21.2 %all-to-all-start.16 = ((bf16[4,192,192]{2,1,0:T(8,128)(2,1)}), bf16[4,192,192]{2,1,0:T(8,128)(2,1)S(1)}, u32[]{:S(2)}, u32[]{:S(2)}) async-start(bf16[4,192,192]{2,1,0:T(8,128)(2,1)} %get-tuple-element.116), calls=%async_computation.16 | async-start | bytes 786432 | tf_op jit(solution)/shard_map/all_to_all | solution.py:519
  654.7 34.5 %collective-permute-start.21 = (bf16[416,2304]{1,0:T(8,128)(2,1)}, bf16[416,2304]{1,0:T(8,128)(2,1)}, u32[]{:S(2)}, u32[]{:S(2)}) collective-permute-start(bf16[416,2304]{1,0:T(8,128)(2,1)} %bitcast.37.refs_5_), channel_id=1, source_target_pairs={{0,8},{8,0},{1,9},{9,1},{2,10},{10,2},{3,11},{11,3},{4,12},{12,4},... | collective-permute-start | bytes 5750792 | tf_op jit(solution)/shard_map/ppermute | solution.py:510
  657.0 38.0 %collective-permute-start.22 = (bf16[1536,768]{1,0:T(8,128)(2,1)}, bf16[1536,768]{1,0:T(8,128)(2,1)}, u32[]{:S(2)}, u32[]{:S(2)}) collective-permute-start(bf16[1536,768]{1,0:T(8,128)(2,1)} %convolution_convert_fusion.9.refs_7_), channel_id=1, source_target_pairs={{0,8},{8,0},{1,9},{9,1},{2,10},{10,2},{3,11},{11,3},{4,12},{12,4},... | collective-permute-start | bytes 7077896 | tf_op jit(solution)/shard_map/ppermute | solution.py:510
  659.8 37.5 %collective-permute-start.23 = (bf16[384,3072]{1,0:T(8,128)(2,1)}, bf16[384,3072]{1,0:T(8,128)(2,1)}, u32[]{:S(2)}, u32[]{:S(2)}) collective-permute-start(bf16[384,3072]{1,0:T(8,128)(2,1)} %convolution_convert_fusion.3.refs_9_), channel_id=1, source_target_pairs={{0,8},{8,0},{1,9},{9,1},{2,10},{10,2},{3,11},{11,3},{4,12},{12,4},... | collective-permute-start | bytes 7077896 | tf_op jit(solution)/shard_map/ppermute | solution.py:510
  688.1 98.8 %all-reduce.9.cloned.1.call-start = ((), (), s32[]{:S(2)}) async-start(), calls=%async_computation.24 | async-start | bytes 2359296 | tf_op jit(solution)/shard_map/psum | solution.py:625
  691.8 25.8 %collective-permute-start.31 = (bf16[208,2304]{1,0:T(8,128)(2,1)}, bf16[208,2304]{1,0:T(8,128)(2,1)}, u32[]{:S(2)}, u32[]{:S(2)}) collective-permute-start(bf16[208,2304]{1,0:T(8,128)(2,1)} %add_convert_fusion.17.refs_8_), channel_id=1, source_target_pairs={{0,1},{1,0},{2,3},{3,2},{4,5},{5,4},{6,7},{7,6},{8,9},{9,8},{10,11... | collective-permute-start | bytes 2875400 | tf_op jit(solution)/shard_map/ppermute | solution.py:510
  697.1 49.5 %collective-permute-start.28 = (bf16[768,768]{1,0:T(8,128)(2,1)S(1)}, bf16[768,768]{1,0:T(8,128)(2,1)}, u32[]{:S(2)}, u32[]{:S(2)}) collective-permute-start(bf16[768,768]{1,0:T(8,128)(2,1)S(1)} %add_convert_fusion.5.refs_10_), channel_id=1, source_target_pairs={{0,1},{1,0},{2,3},{3,2},{4,5},{5,4},{6,7},{7,6},{8,9},{9,8},{10,11... | collective-permute-start | bytes 3538952 | tf_op jit(solution)/shard_map/ppermute | solution.py:510
  700.4 71.6 %collective-permute-start.29 = (bf16[192,3072]{1,0:T(8,128)(2,1)}, bf16[192,3072]{1,0:T(8,128)(2,1)}, u32[]{:S(2)}, u32[]{:S(2)}) collective-permute-start(bf16[192,3072]{1,0:T(8,128)(2,1)} %add_convert_fusion.3.refs_12_), channel_id=1, source_target_pairs={{0,1},{1,0},{2,3},{3,2},{4,5},{5,4},{6,7},{7,6},{8,9},{9,8},{10,11... | collective-permute-start | bytes 3538952 | tf_op jit(solution)/shard_map/ppermute | solution.py:510
  703.4 73.4 %all-to-all-start.17 = ((bf16[4,192,576]{2,1,0:T(8,128)(2,1)}), bf16[4,192,576]{2,1,0:T(8,128)(2,1)}, u32[]{:S(2)}, u32[]{:S(2)}) async-start(bf16[4,192,576]{2,1,0:T(8,128)(2,1)} %bitcast.215), calls=%async_computation.17 | async-start | bytes 1966080 | tf_op jit(solution)/shard_map/all_to_all | solution.py:519
  782.4 60.6 %all-reduce.11.cloned.1.call-start = ((), (), s32[]{:S(2)}) async-start(), calls=%async_computation.25 | async-start | bytes 2359296 | tf_op jit(solution)/shard_map/psum | solution.py:625
  787.0 57.7 %collective-permute-start.26 = (bf16[416,2304]{1,0:T(8,128)(2,1)}, bf16[416,2304]{1,0:T(8,128)(2,1)}, u32[]{:S(2)}, u32[]{:S(2)}) collective-permute-start(bf16[416,2304]{1,0:T(8,128)(2,1)} %bitcast.53), channel_id=1, source_target_pairs={{0,8},{8,0},{1,9},{9,1},{2,10},{10,2},{3,11},{11,3},{4,12},{12,4},... | collective-permute-start | bytes 5750792 | tf_op jit(solution)/shard_map/ppermute | solution.py:510
  787.0 107.5 %all-reduce.13.cloned.1.call-start = ((), (), s32[]{:S(2)}) async-start(), calls=%async_computation.26 | async-start | bytes 1916928 | tf_op jit(solution)/shard_map/psum | solution.py:625
  787.0 61.6 %collective-permute-start.24 = (bf16[384,768]{1,0:T(8,128)(2,1)S(1)}, bf16[384,768]{1,0:T(8,128)(2,1)}, u32[]{:S(2)}, u32[]{:S(2)}) collective-permute-start(bf16[384,768]{1,0:T(8,128)(2,1)S(1)} %copy-done.31), channel_id=1, source_target_pairs={{0,8},{8,0},{1,9},{9,1},{2,10},{10,2},{3,11},{11,3},{4,12},{12,4},... | collective-permute-start | bytes 1769480 | tf_op jit(solution)/shard_map/ppermute | solution.py:510
  843.0 121.9 %all-reduce.15.cloned.1.call-start = ((), (), s32[]{:S(2)}) async-start(), calls=%async_computation.27 | async-start | bytes 2359296 | tf_op jit(solution)/shard_map/psum | solution.py:625
  847.2 58.8 %collective-permute-start.27 = (bf16[208,2304]{1,0:T(8,128)(2,1)}, bf16[208,2304]{1,0:T(8,128)(2,1)}, u32[]{:S(2)}, u32[]{:S(2)}) collective-permute-start(bf16[208,2304]{1,0:T(8,128)(2,1)} %add_convert_fusion.14), channel_id=1, source_target_pairs={{0,1},{1,0},{2,3},{3,2},{4,5},{5,4},{6,7},{7,6},{8,9},{9,8},{10,11... | collective-permute-start | bytes 2875400 | tf_op jit(solution)/shard_map/ppermute | solution.py:510
  850.4 53.7 %collective-permute-start.25 = (bf16[192,768]{1,0:T(8,128)(2,1)}, bf16[192,768]{1,0:T(8,128)(2,1)}, u32[]{:S(2)}, u32[]{:S(2)}) collective-permute-start(bf16[192,768]{1,0:T(8,128)(2,1)} %add_convert_fusion.24), channel_id=1, source_target_pairs={{0,1},{1,0},{2,3},{3,2},{4,5},{5,4},{6,7},{7,6},{8,9},{9,8},{10,11... | collective-permute-start | bytes 884744 | tf_op jit(solution)/shard_map/ppermute | solution.py:510
  900.5 67.7 %all-to-all-start.9 = ((bf16[2,192,768]{2,1,0:T(8,128)(2,1)}), bf16[2,192,768]{2,1,0:T(8,128)(2,1)S(1)}, u32[]{:S(2)}, u32[]{:S(2)}) async-start(bf16[2,192,768]{2,1,0:T(8,128)(2,1)} %all_to_all.108), calls=%async_computation.9 | async-start | bytes 1179648 | tf_op jit(solution)/shard_map/all_to_all | solution.py:649
  904.0 184.9 %all-reduce.17.cloned.1.call-start = ((), (), s32[]{:S(2)}) async-start(), calls=%async_computation.28 | async-start | bytes 5455872 | tf_op jit(solution)/shard_map/psum | solution.py:625
  967.3 46.3 %collective-permute-start.34 = (bf16[192,3072]{1,0:T(8,128)(2,1)}, bf16[192,3072]{1,0:T(8,128)(2,1)}, u32[]{:S(2)}, u32[]{:S(2)}) collective-permute-start(bf16[192,3072]{1,0:T(8,128)(2,1)} %broadcast_select_fusion.2), channel_id=1, source_target_pairs={{0,8},{8,0},{1,9},{9,1},{2,10},{10,2},{3,11},{11,3},{4,12},{12,4},... | collective-permute-start | bytes 3538952 | tf_op jit(solution)/shard_map/ppermute | solution.py:510
  974.4 39.2 %all-to-all-start.19 = ((bf16[2,192,768]{2,1,0:T(8,128)(2,1)}), bf16[2,192,768]{2,1,0:T(8,128)(2,1)}, u32[]{:S(2)}, u32[]{:S(2)}) async-start(bf16[2,192,768]{2,1,0:T(8,128)(2,1)} %all_to_all.109), calls=%async_computation.19 | async-start | bytes 1179648 | tf_op jit(solution)/shard_map/all_to_all | solution.py:649
  (116 other events, 968.3 us)
Sparse Core Ops, SparseCore 0:
  18.6 59.0 all-gather.4
  79.8 41.5 all-gather.6
  123.5 53.6 all-gather.8
  179.3 41.7 all-gather.10
  693.9 65.0 all-reduce.8
  787.1 55.8 all-reduce.10
  845.4 49.0 all-reduce.12
  897.0 67.8 all-reduce.14
  968.3 120.5 all-reduce.16

commit v3 on v2

--- a/solution.py
+++ b/solution.py
@@ -506,6 +506,25 @@
     )(grads, joined, x, dx1, gain, *after)
 
 
+def add_body(one_ref, two_ref, *rest):
+    rest[-1][...] = (one_ref[...].astype(F32) + two_ref[...].astype(F32)).astype(BF16)
+
+
+def add_after(one, two, after):
+    rows, wide = one.shape
+    block = next((n for n in (256, 208, 192, 128, 96, 64, 48) if rows % n == 0), rows)
+    spec = pl.BlockSpec((block, wide), lambda i: (i, 0))
+    return call(
+        add_body,
+        jax.ShapeDtypeStruct((rows, wide), BF16),
+        grid=(rows // block,),
+        in_specs=[spec, spec] + [pl.BlockSpec(memory_space=pl.ANY)] * len(after),
+        out_specs=spec,
+        flops=one.size,
+        moved=6 * one.size,
+    )(one, two, *after)
+
+
 def swap(block, axis):
     return lax.ppermute(block, axis, [(0, 1), (1, 0)])
 
@@ -558,14 +577,17 @@
     return jnp.where(flag, one, two)
 
 
-def gather_weight(block):
+def gather_weight(*blocks):
     core = lax.axis_index("core")
     quads = lax.axis_size("quad")
-    part = block.shape[0] // (2 * quads)
+    part = blocks[0].shape[0] // (2 * quads)
     quad = lax.axis_index("quad")
 
     def cut(which):
-        return lax.dynamic_slice_in_dim(block, (which * quads + quad) * part, part, 0)
+        start = (which * quads + quad) * part
+        return jnp.concatenate(
+            [lax.dynamic_slice_in_dim(block, start, part, 0) for block in blocks], axis=1
+        )
 
     own = cut(core)
     came = swap(cut(1 - core), "core")
@@ -575,6 +597,34 @@
         lax.all_gather(item, ("side", "rest", "core", "quad"), axis=0, tiled=True)
         for item in (first, second)
     ]
+
+
+def in_order(second, mine, other):
+    return pick(second, other, mine), pick(second, mine, other)
+
+
+def gather_by_swaps(block):
+    if lax.axis_size("rest") > 1 or lax.axis_size("quad") != 2:
+        return gather_weight(block)
+    core, quad, side = (lax.axis_index(name) for name in ("core", "quad", "side"))
+    part = block.shape[0] // 4
+    layers = in_order(core == 1, block, swap(block, "core"))
+    start = (core * 2 + quad) * part
+    near = jnp.stack([lax.dynamic_slice_in_dim(item, start, part, 0) for item in layers])
+    near = swap(near, "side")
+    both = jnp.stack([near, swap(near, "quad")])
+    far = swap(both, "core")
+    here = in_order(quad == 1, both[0], both[1])
+    there = in_order(quad == 1, far[0], far[1])
+    rows = [
+        *(pick(core == 1, b, a) for a, b in zip(here, there)),
+        *(pick(core == 1, a, b) for a, b in zip(here, there)),
+    ]
+    result = []
+    for layer in range(2):
+        other = jnp.concatenate([row[layer] for row in rows], axis=0)
+        result.append(jnp.concatenate(in_order(side == 1, layers[layer], other), axis=0))
+    return result
 
 
 def add(one, two):
@@ -614,15 +664,15 @@
     return cut(1 - side), cut(side)
 
 
-def side_sum(sent, kept):
-    total = add(kept, swap(sent, "side"))
+def side_sum(sent, kept, *after):
+    total = add_after(kept, swap(sent, "side"), after)
     if lax.axis_size("rest") > 1:
         total = lax.psum_scatter(total, "rest", scatter_dimension=0, tiled=True)
     return total
 
 
-def line_sum(*items):
-    return lax.psum(items, ("half", "quad"))
+def line_sum(*items, turned=False):
+    return lax.psum(items, ("quad", "half") if turned else ("half", "quad"))
 
 
 def join_cores(first, second):
@@ -644,10 +694,12 @@
 
 def swap_out(first, second, micro):
     rows, wide = first.shape
-    both = jnp.stack([first, second])
-    both = lax.all_to_all(both, "core", 0, 0, tiled=True)
-    both = lax.all_to_all(both, "half", 0, 0, tiled=True)
-    return both.reshape(micro, 2 * rows // micro, wide)
+    second_core, second_half = lax.axis_index("core") == 1, lax.axis_index("half") == 1
+    mine, sent = in_order(second_core, first, second)
+    parts = in_order(second_core, mine, swap(sent, "core"))
+    mine, sent = in_order(second_half, *parts)
+    clips = in_order(second_half, mine, swap(sent, "half"))
+    return jnp.stack(clips).reshape(micro, 2 * rows // micro, wide)
 
 
 def forward_layer(x, weights, clips, head, keep):
@@ -668,14 +720,14 @@
     d_heads = to_clips(spread(d_att), clips)
     dq, kept_kv, sent_kv = attend_backward(own, other, d_heads, log_total, head, after)
     dkv = return_keys(kept_kv, sent_kv).astype(BF16)
-    return spread(to_tokens(jnp.concatenate([dq, dkv], axis=2)))
+    return spread(to_tokens(jnp.concatenate([dq, dkv], axis=2))), dq
 
 
 def backward_lean(kept, g, weights, clips, head):
     x, _, _, _, _, x1, _, slope, _, _ = kept
     joined, w_down, gains = weights[:3]
     _, dx1, _, d_att, _, _ = feed_backward(g, slope, w_down, joined, x1, gains[1:2])
-    d_tokens = attention_grads(kept, d_att, clips, head, ())
+    d_tokens, _ = attention_grads(kept, d_att, clips, head, ())
     return qkv_backward(d_tokens, joined, x, dx1, gains[0:1])[0]
 
 
@@ -721,7 +773,7 @@
     )
     down = weight_halves(lifted, g)
     up = weight_halves(normed_two, d_upper)
-    d_tokens = attention_grads(kept_second, d_att, clips, head, (*down, *up))
+    d_tokens, _ = attention_grads(kept_second, d_att, clips, head, (*down, *up))
     down, up = side_parts(*down), side_parts(*up)
     out = weight_halves(att, branch)
     d_second, flat, sums_one = qkv_backward(
@@ -734,32 +786,34 @@
     d_upper, dx1, branch, d_att, sums_two, up_sum = feed_backward(
         d_second, slope, w_down, joined, x1, gains[1:2]
     )
-    down_two = side_sum(*down)
     down_one = weight_halves(lifted, d_second)
     up_one = weight_halves(normed_two, d_upper)
-    d_tokens = attention_grads(
-        kept_first, d_att, clips, head, (*qkv, *down_one, *up_one, down_two)
-    )
-    (down_two,) = line_sum(down_two)
-    up_two = side_sum(*up)
+    d_tokens, marker = attention_grads(
+        kept_first, d_att, clips, head, (*qkv, *down_one, *up_one)
+    )
+    down_two, up_two = side_sum(*down, marker), side_sum(*up, marker)
     out, qkv = side_parts(*out), side_parts(*qkv)
     down_one, up_one = side_parts(*down_one), side_parts(*up_one)
     out_one = weight_halves(att, branch)
     d_first, flat, sums_one = qkv_backward(
-        d_tokens, joined, x, dx1, gains[0:1], (up_two, *out, *qkv, *down_one, *up_one, *out_one)
-    )
-    up_two, held = lax.optimization_barrier((up_two, down_two))
-    (up_two,) = line_sum(up_two)
+        d_tokens,
+        joined,
+        x,
+        dx1,
+        gains[0:1],
+        (down_two, up_two, *out, *qkv, *down_one, *up_one, *out_one),
+    )
+    down_two, up_two = line_sum(down_two, up_two)
     qkv_one = qkv_halves(normed_one, flat, sums_one, sums_two, up_sum, shards)
-    out_two, qkv_two, _ = lax.optimization_barrier((side_sum(*out), side_sum(*qkv), up_two))
-    out_two, qkv_two = line_sum(out_two, qkv_two)
+    out_two, qkv_two = side_sum(*out, *qkv_one), side_sum(*qkv, *qkv_one)
     out_one, qkv_one = side_parts(*out_one), side_parts(*qkv_one)
-    down_one, up_one, _ = lax.optimization_barrier(
-        (side_sum(*down_one), side_sum(*up_one), qkv_two)
-    )
+    out_two, qkv_two = line_sum(out_two, qkv_two, turned=True)
+    late = (down_two, up_two, out_one[0], qkv_one[0])
+    down_one, up_one = side_sum(*down_one, *late), side_sum(*up_one, *late)
     down_one, up_one = line_sum(down_one, up_one)
-    out_one, qkv_one, _ = lax.optimization_barrier((side_sum(*out_one), side_sum(*qkv_one), up_one))
-    out_one, qkv_one = line_sum(out_one, qkv_one)
+    late = (out_two, qkv_two)
+    out_one, qkv_one = side_sum(*out_one, *late), side_sum(*qkv_one, *late)
+    out_one, qkv_one = line_sum(out_one, qkv_one, turned=True)
     firsts = (qkv_one, out_one, up_one, down_one)
     seconds = (qkv_two, out_two, up_two, down_two)
     return d_first, d_second, [join_cores(a, b) for a, b in zip(firsts, seconds)]
@@ -787,8 +841,8 @@
     head = width // HEADS
     part = width // shards
 
-    joined = gather_weight(jnp.concatenate([w_qkv[0], w_out[0], w_up[0]], axis=1))
-    downs = gather_weight(w_down[0])
+    joined = gather_weight(w_qkv[0], w_out[0], w_up[0])
+    downs = gather_by_swaps(w_down[0])
     small = jnp.concatenate(
         [norm_gain.reshape(-1), norm_bias.reshape(-1), proj_bias.reshape(-1), up_bias.reshape(-1)]
     )

time: 1120 us -> 1120 us (level)
  waiting for transfers between devices: 508 us -> 474 us
  Pallas kernels: 227 us -> 250 us
  blocking collectives: 142 us -> 120 us
  local copies, waits for them, and re-layouts: 40.3 us -> 54.6 us
    all_gather x4 -> x2, waiting for transfers between devices: 83.6 us -> 0.01 us  [gather_weight(): lax.all_gather(item, ('side', 'rest', 'core', 'quad'), axis=0, tiled=True)]
    ppermute x32 -> x39, waiting for transfers between devices: 127 us -> 208 us  [swap(): return lax.ppermute(block, axis, [(0, 1), (1, 0)])]
    all_to_all x2 -> x0, waiting for transfers between devices: 34.7 us -> none  [swap_out(): both = lax.all_to_all(both, 'half', 0, 0, tiled=True)]
    pallas_call x0 -> x8, Pallas kernels: none -> 22.2 us  [add_after(): call(add_body, jax.ShapeDtypeStruct((rows, wide), BF16), grid=(rows // bl...]
    convert_element_type x16 -> x8, other arithmetic: 43.2 us -> 24.2 us  [add(): return (one.astype(F32) + two.astype(F32)).astype(one.dtype)]
    select_n x12 -> x18, other arithmetic: 10.5 us -> 28 us  [pick(): return jnp.where(flag, one, two)]
    ppermute x32 -> x39, starting transfers between devices: 18.8 us -> 33.7 us  [swap(): return lax.ppermute(block, axis, [(0, 1), (1, 0)])]
    psum x5 -> x4, waiting for transfers between devices: 223 us -> 224 us  [line_sum(): return lax.psum(items, ('quad', 'half') if turned else ('half', 'quad'))]
  transfers between devices with their start and end apart: 55 -> 57, of which waited for: 29 -> 24; matrix products, arithmetic and copies ran while one was open for 11% -> 14% of each run, Pallas kernels for 9% -> 10%
where the time goes in v3:
time: 1120 us; the launch traced here: 1110 us
  waiting for transfers between devices  474 us (42%)
  Pallas kernels  250 us (22%)
  blocking collectives  120 us (11%)
  other arithmetic  93.8 us (8%)
  starting transfers between devices  73.7 us (7%)
  local copies, waits for them, and re-layouts  54.6 us (5%)
  matrix products  28.1 us (3%)
  between operations  15.8 us (1%)
    psum x4, waiting for transfers between devices, line_sum(): return lax.psum(items, ('quad', 'half') if turned else ('half', 'quad'))  224 us
    ppermute x39, waiting for transfers between devices, swap(): return lax.ppermute(block, axis, [(0, 1), (1, 0)])  208 us
    all_to_all x8, blocking collectives, spread(): return lax.all_to_all(block, ('quad', 'side'), 0, 0, tiled=True)  120 us
    pallas_call x4, Pallas kernels, attend_backward(): call(body, (jax.ShapeDtypeStruct((clips, queries, span), BF16), jax.Shape...  71.1 us
    pallas_call x4, Pallas kernels, feed_backward(): call(feed_back_body, (jax.ShapeDtypeStruct((rows, hidden), BF16), jax.Sha...  39.8 us
    pallas_call x4, Pallas kernels, attend_forward(): call(body, (jax.ShapeDtypeStruct((clips, queries, span), BF16), jax.Shape...  39.4 us
    pallas_call x4, Pallas kernels, feed_forward(): call(feed_body, tuple(shapes), grid=(hidden // width,), in_specs=[full, w...  34.3 us
    ppermute x39, starting transfers between devices, swap(): return lax.ppermute(block, axis, [(0, 1), (1, 0)])  33.7 us
  transfers between devices with their start and end apart: 57, of which 24 were waited for; matrix products, arithmetic and copies ran while one was open for 14% of the time, Pallas kernels for 10%

profile of v3, /device:TPU:0, one launch (start us, length us, event | category | flops | bytes accessed | tf_op | source)
XLA Modules:
  0.0 1109.8 jit_solution(12761537309227889426)
XLA Ops:
  27.8 39.2 %collective-permute-done.6 = bf16[2,384,768]{2,1,0:T(8,128)(2,1)S(1)} collective-permute-done((bf16[2,384,768]{2,1,0:T(8,128)(2,1)S(1)}, bf16[2,384,768]{2,1,0:T(8,128)(2,1)S(1)}, u32[]{:S(2)}, u32[]{:S(2)}) %collective-permute-start.6) | collective-permute-done | bytes 1179680 | tf_op jit(solution)/shard_map/ppermute | solution.py:529
  79.7 30.9 %collective-permute-done.7 = bf16[2,384,768]{2,1,0:T(8,128)(2,1)} collective-permute-done((bf16[2,384,768]{2,1,0:T(8,128)(2,1)S(1)}, bf16[2,384,768]{2,1,0:T(8,128)(2,1)}, u32[]{:S(2)}, u32[]{:S(2)}) %collective-permute-start.7) | collective-permute-done | bytes 1179680 | tf_op jit(solution)/shard_map/ppermute | solution.py:529
  136.5 13.6 %all-to-all-done = bf16[4,192,576]{2,1,0:T(8,128)(2,1)} async-done(((bf16[4,192,576]{2,1,0:T(8,128)(2,1)}), bf16[4,192,576]{2,1,0:T(8,128)(2,1)}, u32[]{:S(2)}, u32[]{:S(2)}) %all-to-all-start) | async-done | bytes 884768 | tf_op jit(solution)/shard_map/all_to_all | solution.py:538
  161.9 10.0 shard_map.178
  198.6 17.4 %all_to_all.80 = bf16[4,192,576]{2,1,0:T(8,128)(2,1)S(1)} all-to-all(bf16[4,192,576]{2,1,0:T(8,128)(2,1)} %get-tuple-element.72), channel_id=1, replica_groups=mesh['pair'=2,'core'=2,'half'=2,'quad'=2,'side'=2,'rest'=1] {'quad','side'}, dimensions={0} | all-to-all | bytes 1769472 | tf_op jit(solution)/shard_map/all_to_all | solution.py:538
  220.9 9.9 shard_map.181
  266.4 16.3 %all_to_all.81 = bf16[4,192,576]{2,1,0:T(8,128)(2,1)S(1)} all-to-all(bf16[4,192,576]{2,1,0:T(8,128)(2,1)} %get-tuple-element.74), channel_id=1, replica_groups=mesh['pair'=2,'core'=2,'half'=2,'quad'=2,'side'=2,'rest'=1] {'quad','side'}, dimensions={0} | all-to-all | bytes 1769472 | tf_op jit(solution)/shard_map/all_to_all | solution.py:538
  287.1 9.8 shard_map.184
  296.9 11.9 %all_to_all.82.att_ref = bf16[4,192,192]{2,1,0:T(8,128)(2,1)} all-to-all(bf16[4,192,192]{2,1,0:T(8,128)(2,1)} %bitcast.266), channel_id=1, replica_groups=mesh['pair'=2,'core'=2,'half'=2,'quad'=2,'side'=2,'rest'=1] {'quad','side'}, dimensions={0} | all-to-all | bytes 589824 | tf_op jit(solution)/shard_map/all_to_all | solution.py:538
  323.1 16.6 %all_to_all.83 = bf16[4,192,576]{2,1,0:T(8,128)(2,1)S(1)} all-to-all(bf16[4,192,576]{2,1,0:T(8,128)(2,1)} %get-tuple-element.77), channel_id=1, replica_groups=mesh['pair'=2,'core'=2,'half'=2,'quad'=2,'side'=2,'rest'=1] {'quad','side'}, dimensions={0} | all-to-all | bytes 1769472 | tf_op jit(solution)/shard_map/all_to_all | solution.py:538
  344.3 9.8 shard_map.187
  373.4 10.0 shard_map.189
  383.4 11.1 all_to_all.84
  394.5 17.7 %shard_map.190 = (bf16[1,768,192]{2,1,0:T(8,128)(2,1)}, f32[1,768,384]{2,1,0:T(8,128)}, bf16[1,768,384]{2,1,0:T(8,128)(2,1)}) custom-call(bf16[1,768,576]{2,1,0:T(8,128)(2,1)} %bitcast.247, bf16[1,768,576]{2,1,0:T(8,128)(2,1)} %bitcast.248, bf16[1,768,576]{2,1,0:T(8,128)(2,1)} %copy.29.refs_2_, bf16[1,768,192]{2,1,0:T(8,128)(2,1)} %bitcast.264, ...), custom_call_target="tpu_custom_call" | custom-call | flops 9059696640 | bytes 7077888 | tf_op jit(solution)/shard_map/pallas_call | solution.py:242
  417.4 17.7 %all_to_all.85.refs_0_ = bf16[4,192,576]{2,1,0:T(8,128)(2,1)} all-to-all(bf16[4,192,576]{2,1,0:T(8,128)(2,1)S(1)} %bitcast.255), channel_id=1, replica_groups=mesh['pair'=2,'core'=2,'half'=2,'quad'=2,'side'=2,'rest'=1] {'quad','side'}, dimensions={0} | all-to-all | bytes 1769472 | tf_op jit(solution)/shard_map/all_to_all | solution.py:538
  440.8 9.9 shard_map.192
  450.7 11.1 %all_to_all.86 = bf16[4,192,192]{2,1,0:T(8,128)(2,1)} all-to-all(bf16[4,192,192]{2,1,0:T(8,128)(2,1)} %get-tuple-element.91), channel_id=1, replica_groups=mesh['pair'=2,'core'=2,'half'=2,'quad'=2,'side'=2,'rest'=1] {'quad','side'}, dimensions={0} | all-to-all | bytes 589824 | tf_op jit(solution)/shard_map/all_to_all | solution.py:538
  461.9 17.7 %shard_map.193 = (bf16[1,768,192]{2,1,0:T(8,128)(2,1)}, f32[1,768,384]{2,1,0:T(8,128)}, bf16[1,768,384]{2,1,0:T(8,128)(2,1)}) custom-call(bf16[1,768,576]{2,1,0:T(8,128)(2,1)} %bitcast.240, bf16[1,768,576]{2,1,0:T(8,128)(2,1)} %bitcast.241, bf16[1,768,576]{2,1,0:T(8,128)(2,1)} %copy.27.refs_2_, bf16[1,768,192]{2,1,0:T(8,128)(2,1)} %bitcast.265, ...), custom_call_target="tpu_custom_call" | custom-call | flops 9059696640 | bytes 7077888 | tf_op jit(solution)/shard_map/pallas_call | solution.py:242
  483.7 17.3 %all_to_all.87.refs_0_ = bf16[4,192,576]{2,1,0:T(8,128)(2,1)} all-to-all(bf16[4,192,576]{2,1,0:T(8,128)(2,1)S(1)} %bitcast.256), channel_id=1, replica_groups=mesh['pair'=2,'core'=2,'half'=2,'quad'=2,'side'=2,'rest'=1] {'quad','side'}, dimensions={0} | all-to-all | bytes 1769472 | tf_op jit(solution)/shard_map/all_to_all | solution.py:538
  517.8 10.0 shard_map.195
  541.8 17.7 %shard_map.196 = (bf16[1,768,192]{2,1,0:T(8,128)(2,1)}, f32[1,768,384]{2,1,0:T(8,128)}, bf16[1,768,384]{2,1,0:T(8,128)(2,1)}) custom-call(bf16[1,768,576]{2,1,0:T(8,128)(2,1)} %bitcast.249, bf16[1,768,576]{2,1,0:T(8,128)(2,1)} %bitcast.250, bf16[1,768,576]{2,1,0:T(8,128)(2,1)} %copy.29.refs_2_, bf16[1,768,192]{2,1,0:T(8,128)(2,1)} %bitcast.260, ...), custom_call_target="tpu_custom_call" | custom-call | flops 9059696640 | bytes 7077888 | tf_op jit(solution)/shard_map/pallas_call | solution.py:242
  591.3 9.9 shard_map.198
  621.0 17.9 %shard_map.199 = (bf16[1,768,192]{2,1,0:T(8,128)(2,1)}, f32[1,768,384]{2,1,0:T(8,128)}, bf16[1,768,384]{2,1,0:T(8,128)(2,1)}) custom-call(bf16[1,768,576]{2,1,0:T(8,128)(2,1)} %bitcast.242, bf16[1,768,576]{2,1,0:T(8,128)(2,1)} %bitcast.243, bf16[1,768,576]{2,1,0:T(8,128)(2,1)} %copy.27.refs_2_, bf16[1,768,192]{2,1,0:T(8,128)(2,1)} %bitcast.259, ...), custom_call_target="tpu_custom_call" | custom-call | flops 9059696640 | bytes 7077888 | tf_op jit(solution)/shard_map/pallas_call | solution.py:242
  654.4 22.5 %collective-permute-done.23.two_ref = bf16[768,768]{1,0:T(8,128)(2,1)} collective-permute-done((bf16[768,768]{1,0:T(8,128)(2,1)S(1)}, bf16[768,768]{1,0:T(8,128)(2,1)}, u32[]{:S(2)}, u32[]{:S(2)}) %collective-permute-start.23) | collective-permute-done | bytes 1179680 | tf_op jit(solution)/shard_map/ppermute | solution.py:529
  682.3 19.9 %collective-permute-done.24.two_ref = bf16[192,3072]{1,0:T(8,128)(2,1)} collective-permute-done((bf16[192,3072]{1,0:T(8,128)(2,1)}, bf16[192,3072]{1,0:T(8,128)(2,1)}, u32[]{:S(2)}, u32[]{:S(2)}) %collective-permute-start.24) | collective-permute-done | bytes 1179680 | tf_op jit(solution)/shard_map/ppermute | solution.py:529
  746.9 26.7 %collective-permute-done.37.two_ref = bf16[192,768]{1,0:T(8,128)(2,1)S(1)} collective-permute-done((bf16[192,768]{1,0:T(8,128)(2,1)S(1)}, bf16[192,768]{1,0:T(8,128)(2,1)S(1)}, u32[]{:S(2)}, u32[]{:S(2)}) %collective-permute-start.37) | collective-permute-done | bytes 294944 | tf_op jit(solution)/shard_map/ppermute | solution.py:529
  773.6 22.6 %all-reduce.17.cloned.1.call-done = (bf16[208,2304]{1,0:T(8,128)(2,1)}, bf16[192,768]{1,0:T(8,128)(2,1)}) async-done(((bf16[208,2304]{1,0:T(8,128)(2,1)}, bf16[192,768]{1,0:T(8,128)(2,1)}), (bf16[208,2304]{1,0:T(8,128)(2,1)}, bf16[192,768]{1,0:T(8,128)(2,1)})) %all-reduce.17.cloned.1.call-update) | async-done | bytes 1253392 | tf_op jit(solution)/shard_map/psum | solution.py:675
  811.9 18.9 %collective-permute-done.39.two_ref = bf16[192,3072]{1,0:T(8,128)(2,1)} collective-permute-done((bf16[192,3072]{1,0:T(8,128)(2,1)S(1)}, bf16[192,3072]{1,0:T(8,128)(2,1)}, u32[]{:S(2)}, u32[]{:S(2)}) %collective-permute-start.39) | collective-permute-done | bytes 1179680 | tf_op jit(solution)/shard_map/ppermute | solution.py:529
  830.9 76.2 %all-reduce.13.cloned.1.call-done = (bf16[192,3072]{1,0:T(8,128)(2,1)}, bf16[768,768]{1,0:T(8,128)(2,1)}) async-done(((bf16[192,3072]{1,0:T(8,128)(2,1)}, bf16[768,768]{1,0:T(8,128)(2,1)}), (bf16[192,3072]{1,0:T(8,128)(2,1)}, bf16[768,768]{1,0:T(8,128)(2,1)})) %all-reduce.13.cloned.1.call-update) | async-done | bytes 2359312 | tf_op jit(solution)/shard_map/psum | solution.py:675
  918.2 29.4 %collective-permute-done.30 = bf16[192,768]{1,0:T(8,128)(2,1)S(1)} collective-permute-done((bf16[192,768]{1,0:T(8,128)(2,1)S(1)}, bf16[192,768]{1,0:T(8,128)(2,1)S(1)}, u32[]{:S(2)}, u32[]{:S(2)}) %collective-permute-start.30) | collective-permute-done | bytes 294944 | tf_op jit(solution)/shard_map/ppermute | solution.py:529
  948.5 31.0 %all-reduce.15.cloned.1.call-done = (bf16[208,2304]{1,0:T(8,128)(2,1)}, bf16[192,768]{1,0:T(8,128)(2,1)}) async-done(((bf16[208,2304]{1,0:T(8,128)(2,1)}, bf16[192,768]{1,0:T(8,128)(2,1)}), (bf16[208,2304]{1,0:T(8,128)(2,1)}, bf16[192,768]{1,0:T(8,128)(2,1)})) %all-reduce.15.cloned.1.call-update) | async-done | bytes 1253392 | tf_op jit(solution)/shard_map/psum | solution.py:675
  984.2 93.9 %all-reduce.11.cloned.1.call-done = (bf16[192,3072]{1,0:T(8,128)(2,1)}, bf16[768,768]{1,0:T(8,128)(2,1)}) async-done(((bf16[192,3072]{1,0:T(8,128)(2,1)}, bf16[768,768]{1,0:T(8,128)(2,1)}), (bf16[192,3072]{1,0:T(8,128)(2,1)}, bf16[768,768]{1,0:T(8,128)(2,1)})) %all-reduce.11.cloned.1.call-update) | async-done | bytes 2359312 | tf_op jit(solution)/shard_map/psum | solution.py:675
  (485 shorter events, 399.3 us)
Async XLA Ops:
  7.2 113.9 %all-gather.3.cloned.1.call-start = ((), (), s32[]{:S(2)}) async-start(), calls=%async_computation.16 | async-start | bytes 10616832 | tf_op jit(solution)/shard_map/all_gather | solution.py:597
  14.2 179.3 %all-gather.5.cloned.1.call-start = ((), (), s32[]{:S(2)}) async-start(), calls=%async_computation.17 | async-start | bytes 10616832 | tf_op jit(solution)/shard_map/all_gather | solution.py:597
  24.6 42.3 %collective-permute-start.6 = (bf16[2,384,768]{2,1,0:T(8,128)(2,1)S(1)}, bf16[2,384,768]{2,1,0:T(8,128)(2,1)S(1)}, u32[]{:S(2)}, u32[]{:S(2)}) collective-permute-start(bf16[2,384,768]{2,1,0:T(8,128)(2,1)S(1)} %pad_maximum_fusion.12), channel_id=1, source_target_pairs={{0,1},{1,0},{2,3},{3,2},{4,5},{5,4},{6,7},{7,6},{8,9},{9,8},{10,11... | collective-permute-start | bytes 3538952 | tf_op jit(solution)/shard_map/ppermute | solution.py:529
  66.9 43.7 %collective-permute-start.7 = (bf16[2,384,768]{2,1,0:T(8,128)(2,1)S(1)}, bf16[2,384,768]{2,1,0:T(8,128)(2,1)}, u32[]{:S(2)}, u32[]{:S(2)}) collective-permute-start(bf16[2,384,768]{2,1,0:T(8,128)(2,1)S(1)} %collective-permute-done.6), channel_id=1, source_target_pairs={{0,2},{2,0},{1,3},{3,1},{4,6},{6,4},{5,7},{7,5},{8,10},{10,8},{9,1... | collective-permute-start | bytes 3538952 | tf_op jit(solution)/shard_map/ppermute | solution.py:529
  74.2 46.2 %collective-permute-start = (bf16[192,768]{1,0:T(8,128)(2,1)}, bf16[192,768]{1,0:T(8,128)(2,1)}, u32[]{:S(2)}, u32[]{:S(2)}) collective-permute-start(bf16[192,768]{1,0:T(8,128)(2,1)} %dynamic-slice_bitcast_fusion.7), channel_id=1, source_target_pairs={{4,8},{8,4},{5,9},{9,5},{6,10},{10,6},{7,11},{11,7},{20,24},{24,20... | collective-permute-start | bytes 884744 | tf_op jit(solution)/shard_map/ppermute | solution.py:691
  76.4 37.2 %collective-permute-start.2 = (bf16[2,4608]{1,0:T(2,128)(2,1)S(1)}, bf16[2,4608]{1,0:T(2,128)(2,1)S(1)}, u32[]{:S(2)}, u32[]{:S(2)}) collective-permute-start(bf16[2,4608]{1,0:T(2,128)(2,1)S(1)} %pad_maximum_fusion.17), channel_id=1, source_target_pairs={{0,8},{8,0},{1,9},{9,1},{2,10},{10,2},{3,11},{11,3},{4,12},{12,4},... | collective-permute-start | bytes 55304 | tf_op jit(solution)/shard_map/ppermute | solution.py:529
  126.4 23.7 %all-to-all-start = ((bf16[4,192,576]{2,1,0:T(8,128)(2,1)}), bf16[4,192,576]{2,1,0:T(8,128)(2,1)}, u32[]{:S(2)}, u32[]{:S(2)}) async-start(bf16[4,192,576]{2,1,0:T(8,128)(2,1)} %get-tuple-element.70), calls=%async_computation | async-start | bytes 1966080 | tf_op jit(solution)/shard_map/all_to_all | solution.py:538
  533.7 42.6 %collective-permute-start.20 = (bf16[1536,768]{1,0:T(8,128)(2,1)}, bf16[1536,768]{1,0:T(8,128)(2,1)}, u32[]{:S(2)}, u32[]{:S(2)}) collective-permute-start(bf16[1536,768]{1,0:T(8,128)(2,1)} %convolution_convert_fusion.11.refs_5_), channel_id=1, source_target_pairs={{0,8},{8,0},{1,9},{9,1},{2,10},{10,2},{3,11},{11,3},{4,12},{12,4},... | collective-permute-start | bytes 7077896 | tf_op jit(solution)/shard_map/ppermute | solution.py:529
  536.0 44.1 %collective-permute-start.21 = (bf16[384,3072]{1,0:T(8,128)(2,1)}, bf16[384,3072]{1,0:T(8,128)(2,1)}, u32[]{:S(2)}, u32[]{:S(2)}) collective-permute-start(bf16[384,3072]{1,0:T(8,128)(2,1)} %convolution_convert_fusion.7.refs_7_), channel_id=1, source_target_pairs={{0,8},{8,0},{1,9},{9,1},{2,10},{10,2},{3,11},{11,3},{4,12},{12,4},... | collective-permute-start | bytes 7077896 | tf_op jit(solution)/shard_map/ppermute | solution.py:529
  565.0 19.0 %all-to-all-start.13 = ((bf16[4,192,576]{2,1,0:T(8,128)(2,1)}), bf16[4,192,576]{2,1,0:T(8,128)(2,1)S(1)}, u32[]{:S(2)}, u32[]{:S(2)}) async-start(bf16[4,192,576]{2,1,0:T(8,128)(2,1)} %bitcast.254), calls=%async_computation.13 | async-start | bytes 1966080 | tf_op jit(solution)/shard_map/all_to_all | solution.py:538
  573.3 67.4 %collective-permute-start.25 = (bf16[384,768]{1,0:T(8,128)(2,1)}, bf16[384,768]{1,0:T(8,128)(2,1)}, u32[]{:S(2)}, u32[]{:S(2)}) collective-permute-start(bf16[384,768]{1,0:T(8,128)(2,1)} %convolution_convert_fusion.15.refs_9_), channel_id=1, source_target_pairs={{0,8},{8,0},{1,9},{9,1},{2,10},{10,2},{3,11},{11,3},{4,12},{12,4},... | collective-permute-start | bytes 1769480 | tf_op jit(solution)/shard_map/ppermute | solution.py:529
  601.3 18.9 %all-to-all-start.14 = ((bf16[4,192,192]{2,1,0:T(8,128)(2,1)}), bf16[4,192,192]{2,1,0:T(8,128)(2,1)S(1)}, u32[]{:S(2)}, u32[]{:S(2)}) async-start(bf16[4,192,192]{2,1,0:T(8,128)(2,1)} %get-tuple-element.109), calls=%async_computation.14 | async-start | bytes 786432 | tf_op jit(solution)/shard_map/all_to_all | solution.py:538
  608.2 96.9 %collective-permute-start.26 = (bf16[416,2304]{1,0:T(8,128)(2,1)}, bf16[416,2304]{1,0:T(8,128)(2,1)}, u32[]{:S(2)}, u32[]{:S(2)}) collective-permute-start(bf16[416,2304]{1,0:T(8,128)(2,1)} %bitcast.53.refs_5_), channel_id=1, source_target_pairs={{0,8},{8,0},{1,9},{9,1},{2,10},{10,2},{3,11},{11,3},{4,12},{12,4},... | collective-permute-start | bytes 5750792 | tf_op jit(solution)/shard_map/ppermute | solution.py:529
  610.7 99.4 %collective-permute-start.27 = (bf16[1536,768]{1,0:T(8,128)(2,1)}, bf16[1536,768]{1,0:T(8,128)(2,1)}, u32[]{:S(2)}, u32[]{:S(2)}) collective-permute-start(bf16[1536,768]{1,0:T(8,128)(2,1)} %convolution_convert_fusion.9.refs_7_), channel_id=1, source_target_pairs={{0,8},{8,0},{1,9},{9,1},{2,10},{10,2},{3,11},{11,3},{4,12},{12,4},... | collective-permute-start | bytes 7077896 | tf_op jit(solution)/shard_map/ppermute | solution.py:529
  639.3 74.4 %collective-permute-start.28 = (bf16[384,3072]{1,0:T(8,128)(2,1)}, bf16[384,3072]{1,0:T(8,128)(2,1)}, u32[]{:S(2)}, u32[]{:S(2)}) collective-permute-start(bf16[384,3072]{1,0:T(8,128)(2,1)} %convolution_convert_fusion.3.refs_9_), channel_id=1, source_target_pairs={{0,8},{8,0},{1,9},{9,1},{2,10},{10,2},{3,11},{11,3},{4,12},{12,4},... | collective-permute-start | bytes 7077896 | tf_op jit(solution)/shard_map/ppermute | solution.py:529
  642.7 34.2 %collective-permute-start.23 = (bf16[768,768]{1,0:T(8,128)(2,1)S(1)}, bf16[768,768]{1,0:T(8,128)(2,1)}, u32[]{:S(2)}, u32[]{:S(2)}) collective-permute-start(bf16[768,768]{1,0:T(8,128)(2,1)S(1)} %copy-done.19), channel_id=1, source_target_pairs={{0,1},{1,0},{2,3},{3,2},{4,5},{5,4},{6,7},{7,6},{8,9},{9,8},{10,11... | collective-permute-start | bytes 3538952 | tf_op jit(solution)/shard_map/ppermute | solution.py:529
  644.7 57.5 %collective-permute-start.24 = (bf16[192,3072]{1,0:T(8,128)(2,1)}, bf16[192,3072]{1,0:T(8,128)(2,1)}, u32[]{:S(2)}, u32[]{:S(2)}) collective-permute-start(bf16[192,3072]{1,0:T(8,128)(2,1)} %get-tuple-element.149.refs_7_), channel_id=1, source_target_pairs={{0,1},{1,0},{2,3},{3,2},{4,5},{5,4},{6,7},{7,6},{8,9},{9,8},{10,11... | collective-permute-start | bytes 3538952 | tf_op jit(solution)/shard_map/ppermute | solution.py:529
  648.8 69.0 %all-to-all-start.15 = ((bf16[4,192,576]{2,1,0:T(8,128)(2,1)}), bf16[4,192,576]{2,1,0:T(8,128)(2,1)}, u32[]{:S(2)}, u32[]{:S(2)}) async-start(bf16[4,192,576]{2,1,0:T(8,128)(2,1)} %bitcast.57), calls=%async_computation.15 | async-start | bytes 1966080 | tf_op jit(solution)/shard_map/all_to_all | solution.py:538
  653.0 143.2 %all-reduce.17.cloned.1.call-start = ((), (), s32[]{:S(2)}) async-start(), calls=%async_computation.21 | async-start | bytes 2506752 | tf_op jit(solution)/shard_map/psum | solution.py:675
  676.9 52.1 %collective-permute-start.33 = (bf16[192,768]{1,0:T(8,128)(2,1)S(1)}, bf16[192,768]{1,0:T(8,128)(2,1)}, u32[]{:S(2)}, u32[]{:S(2)}) collective-permute-start(bf16[192,768]{1,0:T(8,128)(2,1)S(1)} %get-tuple-element.181.refs_7_), channel_id=1, source_target_pairs={{0,1},{1,0},{2,3},{3,2},{4,5},{5,4},{6,7},{7,6},{8,9},{9,8},{10,11... | collective-permute-start | bytes 884744 | tf_op jit(solution)/shard_map/ppermute | solution.py:529
  708.2 25.8 %collective-permute-start.34 = (bf16[208,2304]{1,0:T(8,128)(2,1)S(1)}, bf16[208,2304]{1,0:T(8,128)(2,1)}, u32[]{:S(2)}, u32[]{:S(2)}) collective-permute-start(bf16[208,2304]{1,0:T(8,128)(2,1)S(1)} %get-tuple-element.165.refs_9_), channel_id=1, source_target_pairs={{0,1},{1,0},{2,3},{3,2},{4,5},{5,4},{6,7},{7,6},{8,9},{9,8},{10,11... | collective-permute-start | bytes 2875400 | tf_op jit(solution)/shard_map/ppermute | solution.py:529
  736.7 170.4 %all-reduce.13.cloned.1.call-start = ((), (), s32[]{:S(2)}) async-start(), calls=%async_computation.19 | async-start | bytes 4718592 | tf_op jit(solution)/shard_map/psum | solution.py:675
  737.3 242.3 %all-reduce.15.cloned.1.call-start = ((), (), s32[]{:S(2)}) async-start(), calls=%async_computation.20 | async-start | bytes 2506752 | tf_op jit(solution)/shard_map/psum | solution.py:675
  744.0 54.1 %collective-permute-start.32 = (bf16[208,2304]{1,0:T(8,128)(2,1)S(1)}, bf16[208,2304]{1,0:T(8,128)(2,1)S(1)}, u32[]{:S(2)}, u32[]{:S(2)}) collective-permute-start(bf16[208,2304]{1,0:T(8,128)(2,1)S(1)} %get-tuple-element.162.rest_3_), channel_id=1, source_target_pairs={{0,1},{1,0},{2,3},{3,2},{4,5},{5,4},{6,7},{7,6},{8,9},{9,8},{10,11... | collective-permute-start | bytes 2875400 | tf_op jit(solution)/shard_map/ppermute | solution.py:529
  746.6 27.0 %collective-permute-start.37 = (bf16[192,768]{1,0:T(8,128)(2,1)S(1)}, bf16[192,768]{1,0:T(8,128)(2,1)S(1)}, u32[]{:S(2)}, u32[]{:S(2)}) collective-permute-start(bf16[192,768]{1,0:T(8,128)(2,1)S(1)} %get-tuple-element.178.rest_2_), channel_id=1, source_target_pairs={{0,1},{1,0},{2,3},{3,2},{4,5},{5,4},{6,7},{7,6},{8,9},{9,8},{10,11... | collective-permute-start | bytes 884744 | tf_op jit(solution)/shard_map/ppermute | solution.py:529
  801.8 276.3 %all-reduce.11.cloned.1.call-start = ((), (), s32[]{:S(2)}) async-start(), calls=%async_computation.18 | async-start | bytes 4718592 | tf_op jit(solution)/shard_map/psum | solution.py:675
  801.9 29.0 %collective-permute-start.39 = (bf16[192,3072]{1,0:T(8,128)(2,1)S(1)}, bf16[192,3072]{1,0:T(8,128)(2,1)}, u32[]{:S(2)}, u32[]{:S(2)}) collective-permute-start(bf16[192,3072]{1,0:T(8,128)(2,1)S(1)} %copy-done.20), channel_id=1, source_target_pairs={{0,1},{1,0},{2,3},{3,2},{4,5},{5,4},{6,7},{7,6},{8,9},{9,8},{10,11... | collective-permute-start | bytes 3538952 | tf_op jit(solution)/shard_map/ppermute | solution.py:529
  803.4 106.6 %collective-permute-start.41 = (bf16[768,768]{1,0:T(8,128)(2,1)S(1)}, bf16[768,768]{1,0:T(8,128)(2,1)}, u32[]{:S(2)}, u32[]{:S(2)}) collective-permute-start(bf16[768,768]{1,0:T(8,128)(2,1)S(1)} %copy-done.18), channel_id=1, source_target_pairs={{0,1},{1,0},{2,3},{3,2},{4,5},{5,4},{6,7},{7,6},{8,9},{9,8},{10,11... | collective-permute-start | bytes 3538952 | tf_op jit(solution)/shard_map/ppermute | solution.py:529
  806.5 107.3 %collective-permute-start.29 = (bf16[192,768]{1,0:T(8,128)(2,1)}, bf16[192,768]{1,0:T(8,128)(2,1)}, u32[]{:S(2)}, u32[]{:S(2)}) collective-permute-start(bf16[192,768]{1,0:T(8,128)(2,1)} %broadcast_select_fusion.27), channel_id=1, source_target_pairs={{0,8},{8,0},{1,9},{9,1},{2,10},{10,2},{3,11},{11,3},{4,12},{12,4},... | collective-permute-start | bytes 884744 | tf_op jit(solution)/shard_map/ppermute | solution.py:529
  809.9 107.4 %collective-permute-start.14 = (bf16[192,768]{1,0:T(8,128)(2,1)}, bf16[192,768]{1,0:T(8,128)(2,1)S(1)}, u32[]{:S(2)}, u32[]{:S(2)}) collective-permute-start(bf16[192,768]{1,0:T(8,128)(2,1)} %get-tuple-element.141), channel_id=1, source_target_pairs={{0,4},{4,0},{1,5},{5,1},{2,6},{6,2},{3,7},{7,3},{8,12},{12,8},{9,1... | collective-permute-start | bytes 884744 | tf_op jit(solution)/shard_map/ppermute | solution.py:529
  915.7 31.9 %collective-permute-start.30 = (bf16[192,768]{1,0:T(8,128)(2,1)S(1)}, bf16[192,768]{1,0:T(8,128)(2,1)S(1)}, u32[]{:S(2)}, u32[]{:S(2)}) collective-permute-start(bf16[192,768]{1,0:T(8,128)(2,1)S(1)} %get-tuple-element.138), channel_id=1, source_target_pairs={{0,4},{4,0},{1,5},{5,1},{2,6},{6,2},{3,7},{7,3},{8,12},{12,8},{9,1... | collective-permute-start | bytes 884744 | tf_op jit(solution)/shard_map/ppermute | solution.py:529
  981.8 99.8 %collective-permute-start.35 = (bf16[208,2304]{1,0:T(8,128)(2,1)}, bf16[208,2304]{1,0:T(8,128)(2,1)}, u32[]{:S(2)}, u32[]{:S(2)}) collective-permute-start(bf16[208,2304]{1,0:T(8,128)(2,1)} %broadcast_select_fusion.18), channel_id=1, source_target_pairs={{0,8},{8,0},{1,9},{9,1},{2,10},{10,2},{3,11},{11,3},{4,12},{12,4},... | collective-permute-start | bytes 2875400 | tf_op jit(solution)/shard_map/ppermute | solution.py:529
  (118 other events, 1269.0 us)
Sparse Core Ops, SparseCore 0:
  14.3 101.1 all-gather.2
  117.7 67.9 all-gather.4
  736.8 59.3 all-reduce.16
  799.1 107.9 all-reduce.12
  909.6 69.9 all-reduce.14
  982.4 95.6 all-reduce.10

commit v4 on v3

--- a/solution.py
+++ b/solution.py
@@ -525,6 +525,48 @@
     )(one, two, *after)
 
 
+def copy_body(one_ref, *rest):
+    rest[-1][...] = one_ref[...]
+
+
+def copy_after(one, after):
+    spec = pl.BlockSpec(one.shape, lambda i: (0, 0))
+    return call(
+        copy_body,
+        jax.ShapeDtypeStruct(one.shape, one.dtype),
+        grid=(1,),
+        in_specs=[spec] + [pl.BlockSpec(memory_space=pl.ANY)] * len(after),
+        out_specs=spec,
+        flops=one.size,
+        moved=4 * one.size,
+    )(one, *after)
+
+
+def join_body(dq_ref, kept_ref, back_ref, *rest):
+    out_ref = rest[-1]
+    span = dq_ref.shape[2]
+    out_ref[:, :, :span] = dq_ref[...]
+    out_ref[:, :, span:] = (kept_ref[...] + back_ref[...].astype(F32)).astype(BF16)
+
+
+def join_grads(dq, kept, back, after):
+    clips, rows, span = dq.shape
+
+    def spec(wide):
+        return pl.BlockSpec((1, rows, wide), lambda i: (i, 0, 0))
+
+    return call(
+        join_body,
+        jax.ShapeDtypeStruct((clips, rows, 3 * span), BF16),
+        grid=(clips,),
+        in_specs=[spec(span), spec(2 * span), spec(2 * span)]
+        + [pl.BlockSpec(memory_space=pl.ANY)] * len(after),
+        out_specs=spec(3 * span),
+        flops=kept.size,
+        moved=8 * kept.size,
+    )(dq, kept, back, *after)
+
+
 def swap(block, axis):
     return lax.ppermute(block, axis, [(0, 1), (1, 0)])
 
@@ -554,23 +596,25 @@
     return jnp.swapaxes(block, 0, 1).reshape(HEAD_GROUPS, -1, wide)
 
 
-def other_keys(own):
+def other_keys(grouped, own, clips):
+    if lax.axis_size("rest") == 1:
+        return to_clips(swap(grouped, "core"), clips)
     near = [shift(own, k) for k in range(1, lax.axis_size("rest"))]
-    far = swap(jnp.concatenate([own] + near, axis=1) if near else own, "core")
-    return jnp.concatenate(near + [far], axis=1) if near else far
+    far = swap(jnp.concatenate([own] + near, axis=1), "core")
+    return jnp.concatenate(near + [far], axis=1)
 
 
 def return_keys(kept, sent):
     queries = kept.shape[1]
     count = lax.axis_size("rest")
     near = (count - 1) * queries
-    back = swap(sent[:, near:], "core").astype(F32)
-    total = kept + back[:, :queries]
+    back = swap(sent[:, near:], "core")
+    total = kept
     for k in range(1, count):
         part = sent[:, (k - 1) * queries : k * queries].astype(F32)
-        part = part + back[:, k * queries : (k + 1) * queries]
+        part = part + back[:, k * queries : (k + 1) * queries].astype(F32)
         total = total + shift(part.astype(BF16), -k).astype(F32)
-    return total
+    return total, back[:, :queries]
 
 
 def pick(flag, one, two):
@@ -603,15 +647,17 @@
     return pick(second, other, mine), pick(second, mine, other)
 
 
-def gather_by_swaps(block):
+def gather_downs(block, after):
     if lax.axis_size("rest") > 1 or lax.axis_size("quad") != 2:
         return gather_weight(block)
     core, quad, side = (lax.axis_index(name) for name in ("core", "quad", "side"))
     part = block.shape[0] // 4
-    layers = in_order(core == 1, block, swap(block, "core"))
     start = (core * 2 + quad) * part
-    near = jnp.stack([lax.dynamic_slice_in_dim(item, start, part, 0) for item in layers])
-    near = swap(near, "side")
+    came = swap(block, "core")
+    mine, second = in_order(core == 1, block, came)
+    near, line = (lax.dynamic_slice_in_dim(item, start, part, 0) for item in (mine, second))
+    second = lax.all_gather(line, ("side", "rest", "core", "quad"), axis=0, tiled=True)
+    near = swap(copy_after(near, after), "side")
     both = jnp.stack([near, swap(near, "quad")])
     far = swap(both, "core")
     here = in_order(quad == 1, both[0], both[1])
@@ -620,11 +666,8 @@
         *(pick(core == 1, b, a) for a, b in zip(here, there)),
         *(pick(core == 1, a, b) for a, b in zip(here, there)),
     ]
-    result = []
-    for layer in range(2):
-        other = jnp.concatenate([row[layer] for row in rows], axis=0)
-        result.append(jnp.concatenate(in_order(side == 1, layers[layer], other), axis=0))
-    return result
+    other = jnp.concatenate(rows, axis=0)
+    return [jnp.concatenate(in_order(side == 1, mine, other), axis=0), second]
 
 
 def add(one, two):
@@ -705,8 +748,9 @@
 def forward_layer(x, weights, clips, head, keep):
     joined, w_down, gains, shifts, b_qkv, b_out, b_down, b_up = weights
     grouped, normed_one = qkv_forward(x, gains[0:1], shifts[0:1], joined, b_qkv)
-    own = to_clips(spread(grouped), clips)
-    other = other_keys(own)
+    grouped = spread(grouped)
+    own = to_clips(grouped, clips)
+    other = other_keys(grouped, own, clips)
     att, log_total = attend_forward(own, other, head)
     att = spread(to_tokens(att))
     y, *kept = feed_forward(
@@ -719,15 +763,18 @@
     own, other, log_total = kept[2:5]
     d_heads = to_clips(spread(d_att), clips)
     dq, kept_kv, sent_kv = attend_backward(own, other, d_heads, log_total, head, after)
-    dkv = return_keys(kept_kv, sent_kv).astype(BF16)
-    return spread(to_tokens(jnp.concatenate([dq, dkv], axis=2))), dq
+    return (dq, *return_keys(kept_kv, sent_kv))
+
+
+def spread_grads(grads, after=()):
+    return spread(to_tokens(join_grads(*grads, after)))
 
 
 def backward_lean(kept, g, weights, clips, head):
     x, _, _, _, _, x1, _, slope, _, _ = kept
     joined, w_down, gains = weights[:3]
     _, dx1, _, d_att, _, _ = feed_backward(g, slope, w_down, joined, x1, gains[1:2])
-    d_tokens, _ = attention_grads(kept, d_att, clips, head, ())
+    d_tokens = spread_grads(attention_grads(kept, d_att, clips, head, ()))
     return qkv_backward(d_tokens, joined, x, dx1, gains[0:1])[0]
 
 
@@ -773,12 +820,11 @@
     )
     down = weight_halves(lifted, g)
     up = weight_halves(normed_two, d_upper)
-    d_tokens, _ = attention_grads(kept_second, d_att, clips, head, (*down, *up))
+    grads = attention_grads(kept_second, d_att, clips, head, (*down, *up))
     down, up = side_parts(*down), side_parts(*up)
+    d_tokens = spread_grads(grads, (*down, *up))
     out = weight_halves(att, branch)
-    d_second, flat, sums_one = qkv_backward(
-        d_tokens, joined, x, dx1, gains[0:1], (*down, *up, *out)
-    )
+    d_second, flat, sums_one = qkv_backward(d_tokens, joined, x, dx1, gains[0:1], out)
     qkv = qkv_halves(normed_one, flat, sums_one, sums_two, up_sum, shards)
 
     x, normed_one, _, _, _, x1, normed_two, slope, lifted, att = kept_first
@@ -788,32 +834,27 @@
     )
     down_one = weight_halves(lifted, d_second)
     up_one = weight_halves(normed_two, d_upper)
-    d_tokens, marker = attention_grads(
-        kept_first, d_att, clips, head, (*qkv, *down_one, *up_one)
-    )
-    down_two, up_two = side_sum(*down, marker), side_sum(*up, marker)
+    grads = attention_grads(kept_first, d_att, clips, head, (*qkv, *down_one, *up_one))
+    down_two, up_two = side_sum(*down, grads[0]), side_sum(*up, grads[0])
     out, qkv = side_parts(*out), side_parts(*qkv)
+    d_tokens = spread_grads(grads, (down_two, up_two, *out, *qkv))
+    down_two, up_two = line_sum(down_two, up_two)
     down_one, up_one = side_parts(*down_one), side_parts(*up_one)
     out_one = weight_halves(att, branch)
     d_first, flat, sums_one = qkv_backward(
-        d_tokens,
-        joined,
-        x,
-        dx1,
-        gains[0:1],
-        (down_two, up_two, *out, *qkv, *down_one, *up_one, *out_one),
-    )
-    down_two, up_two = line_sum(down_two, up_two)
+        d_tokens, joined, x, dx1, gains[0:1], (*down_one, *up_one, *out_one)
+    )
     qkv_one = qkv_halves(normed_one, flat, sums_one, sums_two, up_sum, shards)
     out_two, qkv_two = side_sum(*out, *qkv_one), side_sum(*qkv, *qkv_one)
     out_one, qkv_one = side_parts(*out_one), side_parts(*qkv_one)
-    out_two, qkv_two = line_sum(out_two, qkv_two, turned=True)
-    late = (down_two, up_two, out_one[0], qkv_one[0])
+    late = (out_one[0], qkv_one[0], out_two, qkv_two)
     down_one, up_one = side_sum(*down_one, *late), side_sum(*up_one, *late)
-    down_one, up_one = line_sum(down_one, up_one)
-    late = (out_two, qkv_two)
+    late = (down_two, up_two, down_one, up_one)
+    out_two, qkv_two, down_one, up_one = line_sum(
+        out_two, qkv_two, down_one, up_one, turned=True
+    )
     out_one, qkv_one = side_sum(*out_one, *late), side_sum(*qkv_one, *late)
-    out_one, qkv_one = line_sum(out_one, qkv_one, turned=True)
+    out_one, qkv_one = line_sum(out_one, qkv_one)
     firsts = (qkv_one, out_one, up_one, down_one)
     seconds = (qkv_two, out_two, up_two, down_two)
     return d_first, d_second, [join_cores(a, b) for a, b in zip(firsts, seconds)]
@@ -842,7 +883,7 @@
     part = width // shards
 
     joined = gather_weight(w_qkv[0], w_out[0], w_up[0])
-    downs = gather_by_swaps(w_down[0])
+    downs = gather_downs(w_down[0], joined[:1])
     small = jnp.concatenate(
         [norm_gain.reshape(-1), norm_bias.reshape(-1), proj_bias.reshape(-1), up_bias.reshape(-1)]
     )

time: 1120 us -> 1080 us (0.964)
  other arithmetic: 93.8 us -> 64.3 us
  Pallas kernels: 250 us -> 262 us
  starting transfers between devices: 73.7 us -> 61.8 us
    psum x4 -> x3, waiting for transfers between devices: 224 us -> 166 us  [line_sum(): return lax.psum(items, ('quad', 'half') if turned else ('half', 'quad'))]
    all_gather x2, waiting for transfers between devices: 0.01 us -> 43.7 us  [gather_weight(): lax.all_gather(item, ('side', 'rest', 'core', 'quad'), axis=0, tiled=True)]
    pallas_call x0 -> x5, Pallas kernels: none -> 13.1 us  [the longest x4 11.2 us: join_grads(): call(join_body, jax.ShapeDtypeStruct((clips, rows, 3 * span), BF16), grid...]
    select_n x18 -> x19, other arithmetic: 28 us -> 15.6 us  [pick(): return jnp.where(flag, one, two)]
    all_to_all x8, waiting for transfers between devices: 27.4 us -> 39.7 us  [spread(): return lax.all_to_all(block, ('quad', 'side'), 0, 0, tiled=True)]
    ppermute x39, starting transfers between devices: 33.7 us -> 22.2 us  [swap(): return lax.ppermute(block, axis, [(0, 1), (1, 0)])]
    unnamed x209 -> x227, local copies, waits for them, and re-layouts: 18.7 us -> 25.7 us
  transfers between devices with their start and end apart: 57 -> 57, of which waited for: 24 -> 26; matrix products, arithmetic and copies ran while one was open for 14% -> 11% of each run, Pallas kernels for 10% -> 12%
where the time goes in v4:
time: 1080 us; the launch traced here: 1070 us
  waiting for transfers between devices  464 us (43%)
  Pallas kernels  262 us (24%)
  blocking collectives  125 us (12%)
  other arithmetic  64.3 us (6%)
  starting transfers between devices  61.8 us (6%)
  local copies, waits for them, and re-layouts  48.1 us (4%)
  matrix products  29.6 us (3%)
  between operations  16 us (1%)
    ppermute x39, waiting for transfers between devices, swap(): return lax.ppermute(block, axis, [(0, 1), (1, 0)])  200 us
    psum x3, waiting for transfers between devices, line_sum(): return lax.psum(items, ('quad', 'half') if turned else ('half', 'quad'))  166 us
    all_to_all x8, blocking collectives, spread(): return lax.all_to_all(block, ('quad', 'side'), 0, 0, tiled=True)  125 us
    pallas_call x4, Pallas kernels, attend_backward(): call(body, (jax.ShapeDtypeStruct((clips, queries, span), BF16), jax.Shape...  71.2 us
    all_gather x2, waiting for transfers between devices, gather_weight(): lax.all_gather(item, ('side', 'rest', 'core', 'quad'), axis=0, tiled=True)  43.7 us
    pallas_call x4, Pallas kernels, feed_backward(): call(feed_back_body, (jax.ShapeDtypeStruct((rows, hidden), BF16), jax.Sha...  39.9 us
    all_to_all x8, waiting for transfers between devices, spread(): return lax.all_to_all(block, ('quad', 'side'), 0, 0, tiled=True)  39.7 us
    pallas_call x4, Pallas kernels, attend_forward(): call(body, (jax.ShapeDtypeStruct((clips, queries, span), BF16), jax.Shape...  39.1 us
  transfers between devices with their start and end apart: 57, of which 26 were waited for; matrix products, arithmetic and copies ran while one was open for 11% of the time, Pallas kernels for 12%

profile of v4, /device:TPU:0, one launch (start us, length us, event | category | flops | bytes accessed | tf_op | source)
XLA Modules:
  0.0 1070.9 jit_solution(9902064869395794042)
XLA Ops:
  29.8 43.7 %all-gather.4.cloned.1.call-done.w_ref.rest_0_.w_out_ref.w_up_ref.refs_1_ = bf16[768,6144]{1,0:T(8,128)(2,1)} async-done(((bf16[96,6144]{1,0:T(8,128)(2,1)}), bf16[768,6144]{1,0:T(8,128)(2,1)}) %all-gather.4.cloned.1.call-update) | async-done | bytes 9437200 | tf_op jit(solution)/shard_map/all_gather | solution.py:641
  89.4 27.8 %collective-permute-done.6 = bf16[384,768]{1,0:T(8,128)(2,1)S(1)} collective-permute-done((bf16[384,768]{1,0:T(8,128)(2,1)}, bf16[384,768]{1,0:T(8,128)(2,1)S(1)}, u32[]{:S(2)}, u32[]{:S(2)}) %collective-permute-start.6) | collective-permute-done | bytes 589856 | tf_op jit(solution)/shard_map/ppermute | solution.py:571
  118.5 20.0 %collective-permute-done.7 = bf16[384,768]{1,0:T(8,128)(2,1)S(1)} collective-permute-done((bf16[384,768]{1,0:T(8,128)(2,1)S(1)}, bf16[384,768]{1,0:T(8,128)(2,1)S(1)}, u32[]{:S(2)}, u32[]{:S(2)}) %collective-permute-start.7) | collective-permute-done | bytes 589856 | tf_op jit(solution)/shard_map/ppermute | solution.py:571
  146.6 9.8 shard_map.178
  169.1 7.9 shard_map.180.x_ref
  182.2 19.2 %all_to_all.80 = bf16[4,192,576]{2,1,0:T(8,128)(2,1)S(1)} all-to-all(bf16[4,192,576]{2,1,0:T(8,128)(2,1)} %get-tuple-element.72), channel_id=1, replica_groups=mesh['pair'=2,'core'=2,'half'=2,'quad'=2,'side'=2,'rest'=1] {'quad','side'}, dimensions={0} | all-to-all | bytes 1769472 | tf_op jit(solution)/shard_map/all_to_all | solution.py:580
  204.9 9.8 shard_map.182
  249.2 16.4 %all_to_all.81 = bf16[4,192,576]{2,1,0:T(8,128)(2,1)S(1)} all-to-all(bf16[4,192,576]{2,1,0:T(8,128)(2,1)} %get-tuple-element.74), channel_id=1, replica_groups=mesh['pair'=2,'core'=2,'half'=2,'quad'=2,'side'=2,'rest'=1] {'quad','side'}, dimensions={0} | all-to-all | bytes 1769472 | tf_op jit(solution)/shard_map/all_to_all | solution.py:580
  269.1 9.7 shard_map.185
  278.9 11.9 %all_to_all.82.att_ref = bf16[4,192,192]{2,1,0:T(8,128)(2,1)} all-to-all(bf16[4,192,192]{2,1,0:T(8,128)(2,1)} %bitcast.248), channel_id=1, replica_groups=mesh['pair'=2,'core'=2,'half'=2,'quad'=2,'side'=2,'rest'=1] {'quad','side'}, dimensions={0} | all-to-all | bytes 589824 | tf_op jit(solution)/shard_map/all_to_all | solution.py:580
  290.8 9.2 shard_map.186
  305.1 16.6 %all_to_all.83 = bf16[4,192,576]{2,1,0:T(8,128)(2,1)S(1)} all-to-all(bf16[4,192,576]{2,1,0:T(8,128)(2,1)} %get-tuple-element.77), channel_id=1, replica_groups=mesh['pair'=2,'core'=2,'half'=2,'quad'=2,'side'=2,'rest'=1] {'quad','side'}, dimensions={0} | all-to-all | bytes 1769472 | tf_op jit(solution)/shard_map/all_to_all | solution.py:580
  325.2 9.8 shard_map.188
  345.8 9.3 shard_map.189
  355.1 10.0 shard_map.190
  365.0 12.4 %all_to_all.84 = bf16[4,192,192]{2,1,0:T(8,128)(2,1)} all-to-all(bf16[4,192,192]{2,1,0:T(8,128)(2,1)} %get-tuple-element.82), channel_id=1, replica_groups=mesh['pair'=2,'core'=2,'half'=2,'quad'=2,'side'=2,'rest'=1] {'quad','side'}, dimensions={0} | all-to-all | bytes 589824 | tf_op jit(solution)/shard_map/all_to_all | solution.py:580
  377.4 17.8 %shard_map.191 = (bf16[1,768,192]{2,1,0:T(8,128)(2,1)}, f32[1,768,384]{2,1,0:T(8,128)}, bf16[1,768,384]{2,1,0:T(8,128)(2,1)}) custom-call(bf16[1,768,576]{2,1,0:T(8,128)(2,1)} %bitcast.236, bf16[1,768,576]{2,1,0:T(8,128)(2,1)} %bitcast.237, bf16[1,768,576]{2,1,0:T(8,128)(2,1)} %bitcast.301, bf16[1,768,192]{2,1,0:T(8,128)(2,1)} %bitcast.246, ...), custom_call_target="tpu_custom_call" | custom-call | flops 9059696640 | bytes 7077888 | tf_op jit(solution)/shard_map/pallas_call | solution.py:242
  401.1 18.6 %all_to_all.85.refs_0_ = bf16[4,192,576]{2,1,0:T(8,128)(2,1)} all-to-all(bf16[4,192,576]{2,1,0:T(8,128)(2,1)} %bitcast.221), channel_id=1, replica_groups=mesh['pair'=2,'core'=2,'half'=2,'quad'=2,'side'=2,'rest'=1] {'quad','side'}, dimensions={0} | all-to-all | bytes 1769472 | tf_op jit(solution)/shard_map/all_to_all | solution.py:580
  425.4 10.0 shard_map.194
  435.4 10.9 %all_to_all.86 = bf16[4,192,192]{2,1,0:T(8,128)(2,1)} all-to-all(bf16[4,192,192]{2,1,0:T(8,128)(2,1)} %get-tuple-element.91), channel_id=1, replica_groups=mesh['pair'=2,'core'=2,'half'=2,'quad'=2,'side'=2,'rest'=1] {'quad','side'}, dimensions={0} | all-to-all | bytes 589824 | tf_op jit(solution)/shard_map/all_to_all | solution.py:580
  446.2 17.8 %shard_map.195 = (bf16[1,768,192]{2,1,0:T(8,128)(2,1)}, f32[1,768,384]{2,1,0:T(8,128)}, bf16[1,768,384]{2,1,0:T(8,128)(2,1)}) custom-call(bf16[1,768,576]{2,1,0:T(8,128)(2,1)} %bitcast.230, bf16[1,768,576]{2,1,0:T(8,128)(2,1)} %bitcast.231, bf16[1,768,576]{2,1,0:T(8,128)(2,1)} %bitcast.298, bf16[1,768,192]{2,1,0:T(8,128)(2,1)} %bitcast.247, ...), custom_call_target="tpu_custom_call" | custom-call | flops 9059696640 | bytes 7077888 | tf_op jit(solution)/shard_map/pallas_call | solution.py:242
  469.9 18.5 %all_to_all.87.refs_0_ = bf16[4,192,576]{2,1,0:T(8,128)(2,1)} all-to-all(bf16[4,192,576]{2,1,0:T(8,128)(2,1)} %bitcast.222), channel_id=1, replica_groups=mesh['pair'=2,'core'=2,'half'=2,'quad'=2,'side'=2,'rest'=1] {'quad','side'}, dimensions={0} | all-to-all | bytes 1769472 | tf_op jit(solution)/shard_map/all_to_all | solution.py:580
  506.7 10.0 shard_map.198
  532.3 17.8 %shard_map.199 = (bf16[1,768,192]{2,1,0:T(8,128)(2,1)}, f32[1,768,384]{2,1,0:T(8,128)}, bf16[1,768,384]{2,1,0:T(8,128)(2,1)}) custom-call(bf16[1,768,576]{2,1,0:T(8,128)(2,1)} %bitcast.238, bf16[1,768,576]{2,1,0:T(8,128)(2,1)} %bitcast.239, bf16[1,768,576]{2,1,0:T(8,128)(2,1)} %bitcast.302, bf16[1,768,192]{2,1,0:T(8,128)(2,1)} %bitcast.244, ...), custom_call_target="tpu_custom_call" | custom-call | flops 9059696640 | bytes 7077888 | tf_op jit(solution)/shard_map/pallas_call | solution.py:242
  586.5 10.0 shard_map.202
  618.3 16.2 %all-to-all-done.14 = bf16[4,192,192]{2,1,0:T(8,128)(2,1)} async-done(((bf16[4,192,192]{2,1,0:T(8,128)(2,1)}), bf16[4,192,192]{2,1,0:T(8,128)(2,1)}, u32[]{:S(2)}, u32[]{:S(2)}) %all-to-all-start.14) | async-done | bytes 294944 | tf_op jit(solution)/shard_map/all_to_all | solution.py:580
  634.6 17.8 %shard_map.203 = (bf16[1,768,192]{2,1,0:T(8,128)(2,1)}, f32[1,768,384]{2,1,0:T(8,128)}, bf16[1,768,384]{2,1,0:T(8,128)(2,1)}) custom-call(bf16[1,768,576]{2,1,0:T(8,128)(2,1)} %bitcast.232, bf16[1,768,576]{2,1,0:T(8,128)(2,1)} %bitcast.233, bf16[1,768,576]{2,1,0:T(8,128)(2,1)} %bitcast.299, bf16[1,768,192]{2,1,0:T(8,128)(2,1)} %bitcast.41.refs_3_, ...), custom_call_target="tpu_custom_call" | custom-call | flops 9059696640 | bytes 7077888 | tf_op jit(solution)/shard_map/pallas_call | solution.py:242
  707.7 88.4 %collective-permute-done.35.two_ref = bf16[192,768]{1,0:T(8,128)(2,1)S(1)} collective-permute-done((bf16[192,768]{1,0:T(8,128)(2,1)S(1)}, bf16[192,768]{1,0:T(8,128)(2,1)S(1)}, u32[]{:S(2)}, u32[]{:S(2)}) %collective-permute-start.35) | collective-permute-done | bytes 294944 | tf_op jit(solution)/shard_map/ppermute | solution.py:571
  822.6 35.0 %collective-permute-done.14 = bf16[192,768]{1,0:T(8,128)(2,1)S(1)} collective-permute-done((bf16[192,768]{1,0:T(8,128)(2,1)S(1)}, bf16[192,768]{1,0:T(8,128)(2,1)S(1)}, u32[]{:S(2)}, u32[]{:S(2)}) %collective-permute-start.14) | collective-permute-done | bytes 294944 | tf_op jit(solution)/shard_map/ppermute | solution.py:571
  858.5 10.5 collective-permute-done.30
  869.9 25.7 %all-reduce.9.cloned.1.call-done = (bf16[208,2304]{1,0:T(8,128)(2,1)}, bf16[192,768]{1,0:T(8,128)(2,1)}) async-done(((bf16[208,2304]{1,0:T(8,128)(2,1)}, bf16[192,768]{1,0:T(8,128)(2,1)}), (bf16[208,2304]{1,0:T(8,128)(2,1)}, bf16[192,768]{1,0:T(8,128)(2,1)})) %all-reduce.9.cloned.1.call-update) | async-done | bytes 1253392 | tf_op jit(solution)/shard_map/psum | solution.py:718
  895.6 140.4 %all-reduce.13.cloned.1.call-done = (bf16[208,2304]{1,0:T(8,128)(2,1)}, bf16[192,768]{1,0:T(8,128)(2,1)}, bf16[192,3072]{1,0:T(8,128)(2,1)}, bf16[768,768]{1,0:T(8,128)(2,1)}) async-done(((bf16[208,2304]{1,0:T(8,128)(2,1)}, bf16[192,768]{1,0:T(8,128)(2,1)}, bf16[192,3072]{1,0:T(8,128)(2,1)}, bf16[768,768]{1,0:T(8,128)(2,1)}), (bf16[208,2304]{1,0:T(8,128)(2,1)}, bf16[192,768]{1,0:T(8,128)(2,1)}, ...) | async-done | bytes 3612688 | tf_op jit(solution)/shard_map/psum | solution.py:718
  (484 shorter events, 345.9 us)
Async XLA Ops:
  7.2 66.3 %all-gather.4.cloned.1.call-start = ((), (), s32[]{:S(2)}) async-start(), calls=%async_computation.16 | async-start | bytes 10616832 | tf_op jit(solution)/shard_map/all_gather | solution.py:641
  14.2 162.8 %all-gather.6.cloned.1.call-start = ((), (), s32[]{:S(2)}) async-start(), calls=%async_computation.17 | async-start | bytes 10616832 | tf_op jit(solution)/shard_map/all_gather | solution.py:641
  15.0 206.1 %all-gather.8.cloned.1.call-start = ((), (), s32[]{:S(2)}) async-start(), calls=%async_computation.18 | async-start | bytes 5308416 | tf_op jit(solution)/shard_map/all_gather | solution.py:659
  78.5 40.0 %all-to-all-start = ((bf16[4,192,576]{2,1,0:T(8,128)(2,1)}), bf16[4,192,576]{2,1,0:T(8,128)(2,1)}, u32[]{:S(2)}, u32[]{:S(2)}) async-start(bf16[4,192,576]{2,1,0:T(8,128)(2,1)} %get-tuple-element.70), calls=%async_computation | async-start | bytes 1966080 | tf_op jit(solution)/shard_map/all_to_all | solution.py:580
  87.5 29.8 %collective-permute-start.6 = (bf16[384,768]{1,0:T(8,128)(2,1)}, bf16[384,768]{1,0:T(8,128)(2,1)S(1)}, u32[]{:S(2)}, u32[]{:S(2)}) collective-permute-start(bf16[384,768]{1,0:T(8,128)(2,1)} %shard_map.179), channel_id=1, source_target_pairs={{0,1},{1,0},{2,3},{3,2},{4,5},{5,4},{6,7},{7,6},{8,9},{9,8},{10,11... | collective-permute-start | bytes 1769480 | tf_op jit(solution)/shard_map/ppermute | solution.py:571
  117.3 21.3 %collective-permute-start.7 = (bf16[384,768]{1,0:T(8,128)(2,1)S(1)}, bf16[384,768]{1,0:T(8,128)(2,1)S(1)}, u32[]{:S(2)}, u32[]{:S(2)}) collective-permute-start(bf16[384,768]{1,0:T(8,128)(2,1)S(1)} %collective-permute-done.6), channel_id=1, source_target_pairs={{0,2},{2,0},{1,3},{3,1},{4,6},{6,4},{5,7},{7,5},{8,10},{10,8},{9,1... | collective-permute-start | bytes 1769480 | tf_op jit(solution)/shard_map/ppermute | solution.py:571
  118.5 28.1 %collective-permute-start.4 = (bf16[4,192,576]{2,1,0:T(8,128)(2,1)}, bf16[4,192,576]{2,1,0:T(8,128)(2,1)}, u32[]{:S(2)}, u32[]{:S(2)}) collective-permute-start(bf16[4,192,576]{2,1,0:T(8,128)(2,1)} %all-to-all-done), channel_id=1, source_target_pairs={{0,8},{8,0},{1,9},{9,1},{2,10},{10,2},{3,11},{11,3},{4,12},{12,4},... | collective-permute-start | bytes 2654216 | tf_op jit(solution)/shard_map/ppermute | solution.py:571
  139.7 20.9 %collective-permute-start.8 = (bf16[2,384,768]{2,1,0:T(8,128)(2,1)}, bf16[2,384,768]{2,1,0:T(8,128)(2,1)}, u32[]{:S(2)}, u32[]{:S(2)}) collective-permute-start(bf16[2,384,768]{2,1,0:T(8,128)(2,1)} %pad_maximum_fusion.9), channel_id=1, source_target_pairs={{0,8},{8,0},{1,9},{9,1},{2,10},{10,2},{3,11},{11,3},{4,12},{12,4},... | collective-permute-start | bytes 3538952 | tf_op jit(solution)/shard_map/ppermute | solution.py:571
  321.7 16.7 %collective-permute-start.15 = (bf16[192,768]{1,0:T(8,128)(2,1)S(1)}, bf16[192,768]{1,0:T(8,128)(2,1)S(1)}, u32[]{:S(2)}, u32[]{:S(2)}) collective-permute-start(bf16[192,768]{1,0:T(8,128)(2,1)S(1)} %dynamic-slice_bitcast_fusion.4), channel_id=1, source_target_pairs={{4,8},{8,4},{5,9},{9,5},{6,10},{10,6},{7,11},{11,7},{20,24},{24,20... | collective-permute-start | bytes 884744 | tf_op jit(solution)/shard_map/ppermute | solution.py:734
  506.7 43.4 %collective-permute-start.20 = (bf16[1536,768]{1,0:T(8,128)(2,1)}, bf16[1536,768]{1,0:T(8,128)(2,1)}, u32[]{:S(2)}, u32[]{:S(2)}) collective-permute-start(bf16[1536,768]{1,0:T(8,128)(2,1)} %convolution_convert_fusion.11.refs_5_), channel_id=1, source_target_pairs={{0,8},{8,0},{1,9},{9,1},{2,10},{10,2},{3,11},{11,3},{4,12},{12,4},... | collective-permute-start | bytes 7077896 | tf_op jit(solution)/shard_map/ppermute | solution.py:571
  520.4 33.5 %collective-permute-start.21 = (bf16[384,3072]{1,0:T(8,128)(2,1)}, bf16[384,3072]{1,0:T(8,128)(2,1)}, u32[]{:S(2)}, u32[]{:S(2)}) collective-permute-start(bf16[384,3072]{1,0:T(8,128)(2,1)} %convolution_convert_fusion.7.refs_7_), channel_id=1, source_target_pairs={{0,8},{8,0},{1,9},{9,1},{2,10},{10,2},{3,11},{11,3},{4,12},{12,4},... | collective-permute-start | bytes 7077896 | tf_op jit(solution)/shard_map/ppermute | solution.py:571
  561.4 18.8 %all-to-all-start.13 = ((bf16[4,192,576]{2,1,0:T(8,128)(2,1)}), bf16[4,192,576]{2,1,0:T(8,128)(2,1)}, u32[]{:S(2)}, u32[]{:S(2)}) async-start(bf16[4,192,576]{2,1,0:T(8,128)(2,1)} %bitcast.219), calls=%async_computation.13 | async-start | bytes 1966080 | tf_op jit(solution)/shard_map/all_to_all | solution.py:580
  572.0 46.3 %collective-permute-start.25 = (bf16[384,768]{1,0:T(8,128)(2,1)}, bf16[384,768]{1,0:T(8,128)(2,1)}, u32[]{:S(2)}, u32[]{:S(2)}) collective-permute-start(bf16[384,768]{1,0:T(8,128)(2,1)} %convolution_convert_fusion.15.refs_5_), channel_id=1, source_target_pairs={{0,8},{8,0},{1,9},{9,1},{2,10},{10,2},{3,11},{11,3},{4,12},{12,4},... | collective-permute-start | bytes 1769480 | tf_op jit(solution)/shard_map/ppermute | solution.py:571
  574.3 78.0 %collective-permute-start.23 = (bf16[768,768]{1,0:T(8,128)(2,1)S(1)}, bf16[768,768]{1,0:T(8,128)(2,1)}, u32[]{:S(2)}, u32[]{:S(2)}) collective-permute-start(bf16[768,768]{1,0:T(8,128)(2,1)S(1)} %copy-done.22), channel_id=1, source_target_pairs={{0,1},{1,0},{2,3},{3,2},{4,5},{5,4},{6,7},{7,6},{8,9},{9,8},{10,11... | collective-permute-start | bytes 3538952 | tf_op jit(solution)/shard_map/ppermute | solution.py:571
  576.1 83.0 %collective-permute-start.24 = (bf16[192,3072]{1,0:T(8,128)(2,1)S(1)}, bf16[192,3072]{1,0:T(8,128)(2,1)}, u32[]{:S(2)}, u32[]{:S(2)}) collective-permute-start(bf16[192,3072]{1,0:T(8,128)(2,1)S(1)} %copy-done.21), channel_id=1, source_target_pairs={{0,1},{1,0},{2,3},{3,2},{4,5},{5,4},{6,7},{7,6},{8,9},{9,8},{10,11... | collective-permute-start | bytes 3538952 | tf_op jit(solution)/shard_map/ppermute | solution.py:571
  596.5 38.0 %all-to-all-start.14 = ((bf16[4,192,192]{2,1,0:T(8,128)(2,1)}), bf16[4,192,192]{2,1,0:T(8,128)(2,1)}, u32[]{:S(2)}, u32[]{:S(2)}) async-start(bf16[4,192,192]{2,1,0:T(8,128)(2,1)} %get-tuple-element.109), calls=%async_computation.14 | async-start | bytes 786432 | tf_op jit(solution)/shard_map/all_to_all | solution.py:580
  606.1 56.0 %collective-permute-start.26 = (bf16[416,2304]{1,0:T(8,128)(2,1)}, bf16[416,2304]{1,0:T(8,128)(2,1)}, u32[]{:S(2)}, u32[]{:S(2)}) collective-permute-start(bf16[416,2304]{1,0:T(8,128)(2,1)} %bitcast.47.refs_5_), channel_id=1, source_target_pairs={{0,8},{8,0},{1,9},{9,1},{2,10},{10,2},{3,11},{11,3},{4,12},{12,4},... | collective-permute-start | bytes 5750792 | tf_op jit(solution)/shard_map/ppermute | solution.py:571
  608.4 67.1 %collective-permute-start.27 = (bf16[1536,768]{1,0:T(8,128)(2,1)}, bf16[1536,768]{1,0:T(8,128)(2,1)}, u32[]{:S(2)}, u32[]{:S(2)}) collective-permute-start(bf16[1536,768]{1,0:T(8,128)(2,1)} %convolution_convert_fusion.9.refs_7_), channel_id=1, source_target_pairs={{0,8},{8,0},{1,9},{9,1},{2,10},{10,2},{3,11},{11,3},{4,12},{12,4},... | collective-permute-start | bytes 7077896 | tf_op jit(solution)/shard_map/ppermute | solution.py:571
  618.3 60.9 %collective-permute-start.28 = (bf16[384,3072]{1,0:T(8,128)(2,1)}, bf16[384,3072]{1,0:T(8,128)(2,1)}, u32[]{:S(2)}, u32[]{:S(2)}) collective-permute-start(bf16[384,3072]{1,0:T(8,128)(2,1)} %convolution_convert_fusion.3.refs_9_), channel_id=1, source_target_pairs={{0,8},{8,0},{1,9},{9,1},{2,10},{10,2},{3,11},{11,3},{4,12},{12,4},... | collective-permute-start | bytes 7077896 | tf_op jit(solution)/shard_map/ppermute | solution.py:571
  668.2 18.4 %all-to-all-start.15 = ((bf16[4,192,576]{2,1,0:T(8,128)(2,1)}), bf16[4,192,576]{2,1,0:T(8,128)(2,1)}, u32[]{:S(2)}, u32[]{:S(2)}) async-start(bf16[4,192,576]{2,1,0:T(8,128)(2,1)} %bitcast.220), calls=%async_computation.15 | async-start | bytes 1966080 | tf_op jit(solution)/shard_map/all_to_all | solution.py:580
  672.8 138.7 %all-reduce.11.cloned.1.call-start = ((), (), s32[]{:S(2)}) async-start(), calls=%async_computation.20 | async-start | bytes 4718592 | tf_op jit(solution)/shard_map/psum | solution.py:718
  694.7 201.0 %all-reduce.9.cloned.1.call-start = ((), (), s32[]{:S(2)}) async-start(), calls=%async_computation.19 | async-start | bytes 2506752 | tf_op jit(solution)/shard_map/psum | solution.py:718
  695.3 104.2 %collective-permute-start.36 = (bf16[208,2304]{1,0:T(8,128)(2,1)}, bf16[208,2304]{1,0:T(8,128)(2,1)S(1)}, u32[]{:S(2)}, u32[]{:S(2)}) collective-permute-start(bf16[208,2304]{1,0:T(8,128)(2,1)} %get-tuple-element.157.rest_4_), channel_id=1, source_target_pairs={{0,1},{1,0},{2,3},{3,2},{4,5},{5,4},{6,7},{7,6},{8,9},{9,8},{10,11... | collective-permute-start | bytes 2875400 | tf_op jit(solution)/shard_map/ppermute | solution.py:571
  696.7 106.3 %collective-permute-start.33 = (bf16[768,768]{1,0:T(8,128)(2,1)S(1)}, bf16[768,768]{1,0:T(8,128)(2,1)S(1)}, u32[]{:S(2)}, u32[]{:S(2)}) collective-permute-start(bf16[768,768]{1,0:T(8,128)(2,1)S(1)} %copy-done.14), channel_id=1, source_target_pairs={{0,1},{1,0},{2,3},{3,2},{4,5},{5,4},{6,7},{7,6},{8,9},{9,8},{10,11... | collective-permute-start | bytes 3538952 | tf_op jit(solution)/shard_map/ppermute | solution.py:571
  698.0 109.6 %collective-permute-start.37 = (bf16[192,3072]{1,0:T(8,128)(2,1)}, bf16[192,3072]{1,0:T(8,128)(2,1)S(1)}, u32[]{:S(2)}, u32[]{:S(2)}) collective-permute-start(bf16[192,3072]{1,0:T(8,128)(2,1)} %get-tuple-element.145.refs_7_), channel_id=1, source_target_pairs={{0,1},{1,0},{2,3},{3,2},{4,5},{5,4},{6,7},{7,6},{8,9},{9,8},{10,11... | collective-permute-start | bytes 3538952 | tf_op jit(solution)/shard_map/ppermute | solution.py:571
  704.8 109.3 %collective-permute-start.32 = (bf16[208,2304]{1,0:T(8,128)(2,1)S(1)}, bf16[208,2304]{1,0:T(8,128)(2,1)}, u32[]{:S(2)}, u32[]{:S(2)}) collective-permute-start(bf16[208,2304]{1,0:T(8,128)(2,1)S(1)} %get-tuple-element.155.rest_1_), channel_id=1, source_target_pairs={{0,1},{1,0},{2,3},{3,2},{4,5},{5,4},{6,7},{7,6},{8,9},{9,8},{10,11... | collective-permute-start | bytes 2875400 | tf_op jit(solution)/shard_map/ppermute | solution.py:571
  706.1 90.0 %collective-permute-start.35 = (bf16[192,768]{1,0:T(8,128)(2,1)S(1)}, bf16[192,768]{1,0:T(8,128)(2,1)S(1)}, u32[]{:S(2)}, u32[]{:S(2)}) collective-permute-start(bf16[192,768]{1,0:T(8,128)(2,1)S(1)} %copy-done.33), channel_id=1, source_target_pairs={{0,1},{1,0},{2,3},{3,2},{4,5},{5,4},{6,7},{7,6},{8,9},{9,8},{10,11... | collective-permute-start | bytes 884744 | tf_op jit(solution)/shard_map/ppermute | solution.py:571
  796.1 15.4 %collective-permute-start.39 = (bf16[192,768]{1,0:T(8,128)(2,1)S(1)}, bf16[192,768]{1,0:T(8,128)(2,1)S(1)}, u32[]{:S(2)}, u32[]{:S(2)}) collective-permute-start(bf16[192,768]{1,0:T(8,128)(2,1)S(1)} %get-tuple-element.175.rest_0_), channel_id=1, source_target_pairs={{0,1},{1,0},{2,3},{3,2},{4,5},{5,4},{6,7},{7,6},{8,9},{9,8},{10,11... | collective-permute-start | bytes 884744 | tf_op jit(solution)/shard_map/ppermute | solution.py:571
  816.7 219.3 %all-reduce.13.cloned.1.call-start = ((), (), s32[]{:S(2)}) async-start(), calls=%async_computation.21 | async-start | bytes 7225344 | tf_op jit(solution)/shard_map/psum | solution.py:718
  819.5 38.1 %collective-permute-start.14 = (bf16[192,768]{1,0:T(8,128)(2,1)S(1)}, bf16[192,768]{1,0:T(8,128)(2,1)S(1)}, u32[]{:S(2)}, u32[]{:S(2)}) collective-permute-start(bf16[192,768]{1,0:T(8,128)(2,1)S(1)} %get-tuple-element.141), channel_id=1, source_target_pairs={{0,4},{4,0},{1,5},{5,1},{2,6},{6,2},{3,7},{7,3},{8,12},{12,8},{9,1... | collective-permute-start | bytes 884744 | tf_op jit(solution)/shard_map/ppermute | solution.py:571
  821.0 48.1 %collective-permute-start.30 = (bf16[192,768]{1,0:T(8,128)(2,1)S(1)}, bf16[192,768]{1,0:T(8,128)(2,1)S(1)}, u32[]{:S(2)}, u32[]{:S(2)}) collective-permute-start(bf16[192,768]{1,0:T(8,128)(2,1)S(1)} %get-tuple-element.138), channel_id=1, source_target_pairs={{0,4},{4,0},{1,5},{5,1},{2,6},{6,2},{3,7},{7,3},{8,12},{12,8},{9,1... | collective-permute-start | bytes 884744 | tf_op jit(solution)/shard_map/ppermute | solution.py:571
  1041.8 17.8 %collective-permute-start.42 = (bf16[768,768]{1,0:T(8,128)(2,1)}, bf16[768,768]{1,0:T(8,128)(2,1)}, u32[]{:S(2)}, u32[]{:S(2)}) collective-permute-start(bf16[768,768]{1,0:T(8,128)(2,1)} %broadcast_select_fusion.3), channel_id=1, source_target_pairs={{0,8},{8,0},{1,9},{9,1},{2,10},{10,2},{3,11},{11,3},{4,12},{12,4},... | collective-permute-start | bytes 3538952 | tf_op jit(solution)/shard_map/ppermute | solution.py:571
  (127 other events, 1234.7 us)
Sparse Core Ops, SparseCore 0:
  14.4 59.0 all-gather.3
  75.6 80.7 all-gather.5
  158.6 36.8 all-gather.7
  694.8 94.1 all-reduce.10
  816.8 78.7 all-reduce.8
  898.9 137.0 all-reduce.12

commit v5 on v4

--- a/solution.py
+++ b/solution.py
@@ -512,7 +512,7 @@
 
 def add_after(one, two, after):
     rows, wide = one.shape
-    block = next((n for n in (256, 208, 192, 128, 96, 64, 48) if rows % n == 0), rows)
+    block = next((n for n in (272, 256, 192, 128, 96, 80, 64, 48) if rows % n == 0), rows)
     spec = pl.BlockSpec((block, wide), lambda i: (i, 0))
     return call(
         add_body,
@@ -647,27 +647,26 @@
     return pick(second, other, mine), pick(second, mine, other)
 
 
-def gather_downs(block, after):
+def start_downs(block, after):
     if lax.axis_size("rest") > 1 or lax.axis_size("quad") != 2:
-        return gather_weight(block)
-    core, quad, side = (lax.axis_index(name) for name in ("core", "quad", "side"))
+        first, second = gather_weight(block)
+        return None, first, second
+    core, quad = lax.axis_index("core"), lax.axis_index("quad")
     part = block.shape[0] // 4
-    start = (core * 2 + quad) * part
-    came = swap(block, "core")
-    mine, second = in_order(core == 1, block, came)
-    near, line = (lax.dynamic_slice_in_dim(item, start, part, 0) for item in (mine, second))
+    mine, other = in_order(core == 1, block, swap(block, "core"))
+    line = lax.dynamic_slice_in_dim(other, (core * 2 + quad) * part, part, 0)
     second = lax.all_gather(line, ("side", "rest", "core", "quad"), axis=0, tiled=True)
-    near = swap(copy_after(near, after), "side")
-    both = jnp.stack([near, swap(near, "quad")])
-    far = swap(both, "core")
-    here = in_order(quad == 1, both[0], both[1])
-    there = in_order(quad == 1, far[0], far[1])
-    rows = [
-        *(pick(core == 1, b, a) for a, b in zip(here, there)),
-        *(pick(core == 1, a, b) for a, b in zip(here, there)),
-    ]
-    other = jnp.concatenate(rows, axis=0)
-    return [jnp.concatenate(in_order(side == 1, mine, other), axis=0), second]
+    near = lax.dynamic_slice_in_dim(mine, core * 2 * part, 2 * part, 0)
+    return swap(copy_after(near, after), "side"), mine, second
+
+
+def finish_down(near, mine, after):
+    if near is None:
+        return mine
+    core, side = lax.axis_index("core"), lax.axis_index("side")
+    near = copy_after(near, after)
+    other = jnp.concatenate(in_order(core == 1, near, swap(near, "core")), axis=0)
+    return jnp.concatenate(in_order(side == 1, mine, other), axis=0)
 
 
 def add(one, two):
@@ -714,8 +713,31 @@
     return total
 
 
-def line_sum(*items, turned=False):
-    return lax.psum(items, ("quad", "half") if turned else ("half", "quad"))
+def line_sum(*items):
+    return lax.psum(items, ("half", "quad"))
+
+
+def line_hop(block, pairs):
+    return lax.ppermute(block, ("half", "quad"), pairs)
+
+
+def line_sums(sides):
+    inward, across, outward = [(0, 1), (3, 2)], [(1, 2), (2, 1)], [(1, 0), (2, 3)]
+    inner = lax.axis_index("half") != lax.axis_index("quad")
+    count = len(sides)
+    totals, mark = [None] * count, ()
+    results = []
+    for turn in range(count + 2):
+        if turn < count:
+            totals[turn] = sides[turn](*mark)
+            mark = (totals[turn],)
+        for hops, at in ((inward, turn - 1), (across, turn - 2)):
+            if 0 <= at < count:
+                totals[at] = add_after(totals[at], line_hop(totals[at], hops), mark)
+                mark = (totals[at],)
+                if hops is across:
+                    results.append(pick(inner, totals[at], line_hop(totals[at], outward)))
+    return results
 
 
 def join_cores(first, second):
@@ -752,11 +774,14 @@
     own = to_clips(grouped, clips)
     other = other_keys(grouped, own, clips)
     att, log_total = attend_forward(own, other, head)
+    if callable(w_down):
+        w_down = w_down(log_total)
+        weights = (joined, w_down, *weights[2:])
     att = spread(to_tokens(att))
     y, *kept = feed_forward(
         x, att, joined, b_out, gains[1:2], shifts[1:2], b_up, w_down, b_down, keep
     )
-    return y, (x, normed_one, own, other, log_total, *kept)
+    return y, (x, normed_one, own, other, log_total, *kept), weights
 
 
 def attention_grads(kept, d_att, clips, head, after):
@@ -798,17 +823,22 @@
     return packed.reshape(shards, 2, -1, wide)
 
 
-def beside(weight, rows):
-    shards, _, wide = rows.shape
-    return jnp.concatenate([weight.reshape(shards, -1, wide), rows], axis=1).reshape(-1, wide)
-
-
-def qkv_halves(normed_one, flat, sums_one, sums_two, up_sum, shards):
+def beside(weight, *rows):
+    shards, _, wide = rows[0].shape
+    return jnp.concatenate([weight.reshape(shards, -1, wide), *rows], axis=1).reshape(-1, wide)
+
+
+def rest_halves(normed_one, flat, out, sums_one, sums_two, up_sum, shards):
     core = lax.axis_index("core")
-    rows = small_rows(sums_one, sums_two, up_sum, shards, flat.shape[1])
+    wide = flat.shape[1]
+    rows = small_rows(sums_one, sums_two, up_sum, shards, wide)
     return [
-        beside(item, lax.dynamic_index_in_dim(rows, which, 1, keepdims=False))
-        for item, which in zip(weight_halves(normed_one, flat), (1 - core, core))
+        beside(
+            item,
+            lax.dynamic_index_in_dim(rows, which, 1, keepdims=False),
+            outs.reshape(shards, -1, wide),
+        )
+        for item, outs, which in zip(weight_halves(normed_one, flat), out, (1 - core, core))
     ]
 
 
@@ -825,7 +855,7 @@
     d_tokens = spread_grads(grads, (*down, *up))
     out = weight_halves(att, branch)
     d_second, flat, sums_one = qkv_backward(d_tokens, joined, x, dx1, gains[0:1], out)
-    qkv = qkv_halves(normed_one, flat, sums_one, sums_two, up_sum, shards)
+    rest = rest_halves(normed_one, flat, out, sums_one, sums_two, up_sum, shards)
 
     x, normed_one, _, _, _, x1, normed_two, slope, lifted, att = kept_first
     joined, w_down, gains = layers[0][:3]
@@ -834,29 +864,27 @@
     )
     down_one = weight_halves(lifted, d_second)
     up_one = weight_halves(normed_two, d_upper)
-    grads = attention_grads(kept_first, d_att, clips, head, (*qkv, *down_one, *up_one))
-    down_two, up_two = side_sum(*down, grads[0]), side_sum(*up, grads[0])
-    out, qkv = side_parts(*out), side_parts(*qkv)
-    d_tokens = spread_grads(grads, (down_two, up_two, *out, *qkv))
-    down_two, up_two = line_sum(down_two, up_two)
+    rest = side_parts(*rest)
+    grads = attention_grads(kept_first, d_att, clips, head, (*rest, *down_one, *up_one))
+    down_two, up_two, rest_two = (side_sum(*item, grads[0]) for item in (down, up, rest))
+    d_tokens = spread_grads(grads, (down_two, up_two, rest_two))
+    seconds = line_sum(rest_two, up_two, down_two)
     down_one, up_one = side_parts(*down_one), side_parts(*up_one)
     out_one = weight_halves(att, branch)
     d_first, flat, sums_one = qkv_backward(
         d_tokens, joined, x, dx1, gains[0:1], (*down_one, *up_one, *out_one)
     )
-    qkv_one = qkv_halves(normed_one, flat, sums_one, sums_two, up_sum, shards)
-    out_two, qkv_two = side_sum(*out, *qkv_one), side_sum(*qkv, *qkv_one)
-    out_one, qkv_one = side_parts(*out_one), side_parts(*qkv_one)
-    late = (out_one[0], qkv_one[0], out_two, qkv_two)
-    down_one, up_one = side_sum(*down_one, *late), side_sum(*up_one, *late)
-    late = (down_two, up_two, down_one, up_one)
-    out_two, qkv_two, down_one, up_one = line_sum(
-        out_two, qkv_two, down_one, up_one, turned=True
-    )
-    out_one, qkv_one = side_sum(*out_one, *late), side_sum(*qkv_one, *late)
-    out_one, qkv_one = line_sum(out_one, qkv_one)
-    firsts = (qkv_one, out_one, up_one, down_one)
-    seconds = (qkv_two, out_two, up_two, down_two)
+    rest_one = rest_halves(normed_one, flat, out_one, sums_one, sums_two, up_sum, shards)
+    rest_one = side_parts(*rest_one)
+    sides = [
+        lambda *after, item=item: side_sum(*item, *after, rest_one[0])
+        for item in (down_one, up_one, rest_one)
+    ]
+    if lax.axis_size("quad") == 2:
+        firsts = line_sums(sides)
+    else:
+        firsts = line_sum(*(item() for item in sides))
+    firsts = (firsts[2], firsts[1], firsts[0])
     return d_first, d_second, [join_cores(a, b) for a, b in zip(firsts, seconds)]
 
 
@@ -883,7 +911,8 @@
     part = width // shards
 
     joined = gather_weight(w_qkv[0], w_out[0], w_up[0])
-    downs = gather_downs(w_down[0], joined[:1])
+    near, mine, second_down = start_downs(w_down[0], joined[:1])
+    downs = [lambda *after: finish_down(near, mine, after), lambda *after: second_down]
     small = jnp.concatenate(
         [norm_gain.reshape(-1), norm_bias.reshape(-1), proj_bias.reshape(-1), up_bias.reshape(-1)]
     )
@@ -906,8 +935,8 @@
             came = lax.ppermute(second, "pair", [(i, i + 1) for i in range(pairs - 1)])
             x = pick(pair == 0, x_start, came)
         keep = phase == pairs - 1
-        first, kept_first = forward_layer(x, layers[0], clips, head, keep)
-        second, kept_second = forward_layer(first, layers[1], clips, head, keep)
+        first, kept_first, layers[0] = forward_layer(x, layers[0], clips, head, keep)
+        second, kept_second, layers[1] = forward_layer(first, layers[1], clips, head, keep)
     hidden = swap_out(first, second, micro)
 
     g_start = swap_in(out_grad)
@@ -917,22 +946,25 @@
         d_first = backward_lean(kept_first, d_second, layers[0], clips, head)
         came = lax.ppermute(d_first, "pair", [(i + 1, i) for i in range(pairs - 1)])
         g = pick(pair == pairs - 1, g_start, came)
-    d_first, d_second, (qkv, out, up, down) = backward_all(
+    d_first, d_second, (rest, up, down) = backward_all(
         kept_first, kept_second, g, layers, clips, head, shards
     )
     input_grads = swap_out(d_first, d_second, micro)
 
     own_rows = part // 2
-    qkv = qkv.reshape(2, -1, 3 * width).astype(F32)
-    packed = qkv[:, own_rows:].reshape(2, -1)[:, : (8 * part + up_bias.shape[1]) // 2].reshape(-1)
+    rest = rest.reshape(2, -1, 3 * width)
+    out_rows = own_rows // 3
+    qkv = rest[:, :own_rows].reshape(-1, 3 * width)
+    out = rest[:, rest.shape[1] - out_rows :].reshape(-1, width)
+    packed = rest[:, own_rows : rest.shape[1] - out_rows].astype(F32)
+    packed = packed.reshape(2, -1)[:, : (8 * part + up_bias.shape[1]) // 2].reshape(-1)
     heads = packed[: 8 * part].reshape(8, part)
-    qkv = qkv[:, :own_rows].reshape(-1, 3 * width)
     return (
         hidden[None],
         input_grads[None],
         heads[0:2][None],
         heads[2:4][None],
-        qkv[None],
+        qkv.astype(F32)[None],
         out.astype(F32)[None],
         up.astype(F32)[None],
         down.astype(F32)[None],

time: 1080 us -> 1040 us (0.963)
  waiting for transfers between devices: 464 us -> 369 us
  starting transfers between devices: 61.8 us -> 96.9 us
  Pallas kernels: 262 us -> 281 us
    psum x3 -> x1, waiting for transfers between devices: 166 us -> 0.02 us  [line_sum(): return lax.psum(items, ('half', 'quad'))]
    ppermute x0 -> x9, waiting for transfers between devices: none -> 94.3 us  [line_hop(): return lax.ppermute(block, ('half', 'quad'), pairs)]
    ppermute x39 -> x33, waiting for transfers between devices: 200 us -> 151 us  [swap(): return lax.ppermute(block, axis, [(0, 1), (1, 0)])]
    all_to_all x8, waiting for transfers between devices: 39.7 us -> 66 us  [spread(): return lax.all_to_all(block, ('quad', 'side'), 0, 0, tiled=True)]
    ppermute x0 -> x9, starting transfers between devices: none -> 21.7 us  [line_hop(): return lax.ppermute(block, ('half', 'quad'), pairs)]
    pallas_call x8 -> x12, Pallas kernels: 22.1 us -> 38 us  [add_after(): call(add_body, jax.ShapeDtypeStruct((rows, wide), BF16), grid=(rows // bl...]
    ppermute x39 -> x33, starting transfers between devices: 22.2 us -> 38 us  [swap(): return lax.ppermute(block, axis, [(0, 1), (1, 0)])]
    convert_element_type x8 -> x6, other arithmetic: 25.3 us -> 23 us  [add(): return (one.astype(F32) + two.astype(F32)).astype(one.dtype)]
  transfers between devices with their start and end apart: 57 -> 58, of which waited for: 26 -> 28; matrix products, arithmetic and copies ran while one was open for 11% -> 9% of each run, Pallas kernels for 12% -> 14%
where the time goes in v5:
time: 1040 us; the launch traced here: 1030 us
  waiting for transfers between devices  369 us (35%)
  Pallas kernels  281 us (27%)
  blocking collectives  129 us (12%)
  starting transfers between devices  96.9 us (9%)
  other arithmetic  61.2 us (6%)
  local copies, waits for them, and re-layouts  46.1 us (4%)
  matrix products  28.8 us (3%)
  between operations  15.7 us (2%)
    ppermute x33, waiting for transfers between devices, swap(): return lax.ppermute(block, axis, [(0, 1), (1, 0)])  151 us
    all_to_all x8, blocking collectives, spread(): return lax.all_to_all(block, ('quad', 'side'), 0, 0, tiled=True)  129 us
    ppermute x9, waiting for transfers between devices, line_hop(): return lax.ppermute(block, ('half', 'quad'), pairs)  94.3 us
    pallas_call x4, Pallas kernels, attend_backward(): call(body, (jax.ShapeDtypeStruct((clips, queries, span), BF16), jax.Shape...  71.2 us
    all_to_all x8, waiting for transfers between devices, spread(): return lax.all_to_all(block, ('quad', 'side'), 0, 0, tiled=True)  66 us
    all_gather x2, waiting for transfers between devices, gather_weight(): lax.all_gather(item, ('side', 'rest', 'core', 'quad'), axis=0, tiled=True)  43 us
    pallas_call x4, Pallas kernels, feed_backward(): call(feed_back_body, (jax.ShapeDtypeStruct((rows, hidden), BF16), jax.Sha...  39.9 us
    pallas_call x4, Pallas kernels, attend_forward(): call(body, (jax.ShapeDtypeStruct((clips, queries, span), BF16), jax.Shape...  39.1 us
  transfers between devices with their start and end apart: 58, of which 28 were waited for; matrix products, arithmetic and copies ran while one was open for 9% of the time, Pallas kernels for 14%

profile of v5, /device:TPU:0, one launch (start us, length us, event | category | flops | bytes accessed | tf_op | source)
XLA Modules:
  0.0 1026.8 jit_solution(12145256372099103117)
XLA Ops:
  30.5 43.0 %all-gather.4.cloned.1.call-done.w_ref.rest_0_.w_out_ref.w_up_ref.refs_1_ = bf16[768,6144]{1,0:T(8,128)(2,1)} async-done(((bf16[96,6144]{1,0:T(8,128)(2,1)}), bf16[768,6144]{1,0:T(8,128)(2,1)}) %all-gather.4.cloned.1.call-update) | async-done | bytes 9437200 | tf_op jit(solution)/shard_map/all_gather | solution.py:641
  86.1 14.5 %all-to-all-done = bf16[4,192,576]{2,1,0:T(8,128)(2,1)S(1)} async-done(((bf16[4,192,576]{2,1,0:T(8,128)(2,1)}), bf16[4,192,576]{2,1,0:T(8,128)(2,1)S(1)}, u32[]{:S(2)}, u32[]{:S(2)}) %all-to-all-start) | async-done | bytes 884768 | tf_op jit(solution)/shard_map/all_to_all | solution.py:580
  106.4 9.8 shard_map.178
  116.2 29.3 %collective-permute-done.6.one_ref = bf16[768,768]{1,0:T(8,128)(2,1)S(1)} collective-permute-done((bf16[768,768]{1,0:T(8,128)(2,1)}, bf16[768,768]{1,0:T(8,128)(2,1)S(1)}, u32[]{:S(2)}, u32[]{:S(2)}) %collective-permute-start.6) | collective-permute-done | bytes 1179680 | tf_op jit(solution)/shard_map/ppermute | solution.py:571
  178.9 23.1 %all_to_all.80 = bf16[4,192,576]{2,1,0:T(8,128)(2,1)S(1)} all-to-all(bf16[4,192,576]{2,1,0:T(8,128)(2,1)} %get-tuple-element.74), channel_id=1, replica_groups=mesh['pair'=2,'core'=2,'half'=2,'quad'=2,'side'=2,'rest'=1] {'quad','side'}, dimensions={0} | all-to-all | bytes 1769472 | tf_op jit(solution)/shard_map/all_to_all | solution.py:580
  205.6 9.8 shard_map.183
  249.8 16.4 %all_to_all.81 = bf16[4,192,576]{2,1,0:T(8,128)(2,1)S(1)} all-to-all(bf16[4,192,576]{2,1,0:T(8,128)(2,1)} %get-tuple-element.76), channel_id=1, replica_groups=mesh['pair'=2,'core'=2,'half'=2,'quad'=2,'side'=2,'rest'=1] {'quad','side'}, dimensions={0} | all-to-all | bytes 1769472 | tf_op jit(solution)/shard_map/all_to_all | solution.py:580
  279.5 11.9 %all_to_all.82.att_ref = bf16[4,192,192]{2,1,0:T(8,128)(2,1)} all-to-all(bf16[4,192,192]{2,1,0:T(8,128)(2,1)} %bitcast.232), channel_id=1, replica_groups=mesh['pair'=2,'core'=2,'half'=2,'quad'=2,'side'=2,'rest'=1] {'quad','side'}, dimensions={0} | all-to-all | bytes 589824 | tf_op jit(solution)/shard_map/all_to_all | solution.py:580
  305.7 16.6 %all_to_all.83 = bf16[4,192,576]{2,1,0:T(8,128)(2,1)S(1)} all-to-all(bf16[4,192,576]{2,1,0:T(8,128)(2,1)} %get-tuple-element.79), channel_id=1, replica_groups=mesh['pair'=2,'core'=2,'half'=2,'quad'=2,'side'=2,'rest'=1] {'quad','side'}, dimensions={0} | all-to-all | bytes 1769472 | tf_op jit(solution)/shard_map/all_to_all | solution.py:580
  355.7 10.0 shard_map.191
  365.6 12.5 %all_to_all.84 = bf16[4,192,192]{2,1,0:T(8,128)(2,1)} all-to-all(bf16[4,192,192]{2,1,0:T(8,128)(2,1)} %get-tuple-element.84), channel_id=1, replica_groups=mesh['pair'=2,'core'=2,'half'=2,'quad'=2,'side'=2,'rest'=1] {'quad','side'}, dimensions={0} | all-to-all | bytes 589824 | tf_op jit(solution)/shard_map/all_to_all | solution.py:580
  378.1 17.8 %shard_map.192 = (bf16[1,768,192]{2,1,0:T(8,128)(2,1)}, f32[1,768,384]{2,1,0:T(8,128)}, bf16[1,768,384]{2,1,0:T(8,128)(2,1)}) custom-call(bf16[1,768,576]{2,1,0:T(8,128)(2,1)} %bitcast.219, bf16[1,768,576]{2,1,0:T(8,128)(2,1)} %bitcast.220, bf16[1,768,576]{2,1,0:T(8,128)(2,1)} %bitcast.285, bf16[1,768,192]{2,1,0:T(8,128)(2,1)} %bitcast.230, ...), custom_call_target="tpu_custom_call" | custom-call | flops 9059696640 | bytes 7077888 | tf_op jit(solution)/shard_map/pallas_call | solution.py:242
  401.8 18.7 %all_to_all.85.refs_0_ = bf16[4,192,576]{2,1,0:T(8,128)(2,1)} all-to-all(bf16[4,192,576]{2,1,0:T(8,128)(2,1)} %bitcast.207), channel_id=1, replica_groups=mesh['pair'=2,'core'=2,'half'=2,'quad'=2,'side'=2,'rest'=1] {'quad','side'}, dimensions={0} | all-to-all | bytes 1769472 | tf_op jit(solution)/shard_map/all_to_all | solution.py:580
  426.1 10.0 shard_map.195
  436.1 10.9 %all_to_all.86 = bf16[4,192,192]{2,1,0:T(8,128)(2,1)} all-to-all(bf16[4,192,192]{2,1,0:T(8,128)(2,1)} %get-tuple-element.93), channel_id=1, replica_groups=mesh['pair'=2,'core'=2,'half'=2,'quad'=2,'side'=2,'rest'=1] {'quad','side'}, dimensions={0} | all-to-all | bytes 589824 | tf_op jit(solution)/shard_map/all_to_all | solution.py:580
  447.0 17.8 %shard_map.196 = (bf16[1,768,192]{2,1,0:T(8,128)(2,1)}, f32[1,768,384]{2,1,0:T(8,128)}, bf16[1,768,384]{2,1,0:T(8,128)(2,1)}) custom-call(bf16[1,768,576]{2,1,0:T(8,128)(2,1)} %bitcast.213, bf16[1,768,576]{2,1,0:T(8,128)(2,1)} %bitcast.214, bf16[1,768,576]{2,1,0:T(8,128)(2,1)} %bitcast.282, bf16[1,768,192]{2,1,0:T(8,128)(2,1)} %bitcast.231, ...), custom_call_target="tpu_custom_call" | custom-call | flops 9059696640 | bytes 7077888 | tf_op jit(solution)/shard_map/pallas_call | solution.py:242
  470.6 18.5 %all_to_all.87.refs_0_ = bf16[4,192,576]{2,1,0:T(8,128)(2,1)} all-to-all(bf16[4,192,576]{2,1,0:T(8,128)(2,1)} %bitcast.208), channel_id=1, replica_groups=mesh['pair'=2,'core'=2,'half'=2,'quad'=2,'side'=2,'rest'=1] {'quad','side'}, dimensions={0} | all-to-all | bytes 1769472 | tf_op jit(solution)/shard_map/all_to_all | solution.py:580
  507.5 10.0 shard_map.199
  532.9 17.8 %shard_map.200 = (bf16[1,768,192]{2,1,0:T(8,128)(2,1)}, f32[1,768,384]{2,1,0:T(8,128)}, bf16[1,768,384]{2,1,0:T(8,128)(2,1)}) custom-call(bf16[1,768,576]{2,1,0:T(8,128)(2,1)} %bitcast.221, bf16[1,768,576]{2,1,0:T(8,128)(2,1)} %bitcast.222, bf16[1,768,576]{2,1,0:T(8,128)(2,1)} %bitcast.286, bf16[1,768,192]{2,1,0:T(8,128)(2,1)} %bitcast.228, ...), custom_call_target="tpu_custom_call" | custom-call | flops 9059696640 | bytes 7077888 | tf_op jit(solution)/shard_map/pallas_call | solution.py:242
  569.1 10.7 %all-to-all-done.13.refs_0_ = bf16[4,192,576]{2,1,0:T(8,128)(2,1)S(1)} async-done(((bf16[4,192,576]{2,1,0:T(8,128)(2,1)}), bf16[4,192,576]{2,1,0:T(8,128)(2,1)S(1)}, u32[]{:S(2)}, u32[]{:S(2)}) %all-to-all-start.13) | async-done | bytes 884768 | tf_op jit(solution)/shard_map/all_to_all | solution.py:580
  597.7 10.0 shard_map.203
  629.4 24.9 %all-to-all-done.14 = bf16[4,192,192]{2,1,0:T(8,128)(2,1)} async-done(((bf16[4,192,192]{2,1,0:T(8,128)(2,1)}), bf16[4,192,192]{2,1,0:T(8,128)(2,1)}, u32[]{:S(2)}, u32[]{:S(2)}) %all-to-all-start.14) | async-done | bytes 294944 | tf_op jit(solution)/shard_map/all_to_all | solution.py:580
  654.2 17.7 %shard_map.204 = (bf16[1,768,192]{2,1,0:T(8,128)(2,1)}, f32[1,768,384]{2,1,0:T(8,128)}, bf16[1,768,384]{2,1,0:T(8,128)(2,1)}) custom-call(bf16[1,768,576]{2,1,0:T(8,128)(2,1)} %bitcast.215, bf16[1,768,576]{2,1,0:T(8,128)(2,1)} %bitcast.216, bf16[1,768,576]{2,1,0:T(8,128)(2,1)} %bitcast.283, bf16[1,768,192]{2,1,0:T(8,128)(2,1)} %bitcast.37.refs_3_, ...), custom_call_target="tpu_custom_call" | custom-call | flops 9059696640 | bytes 7077888 | tf_op jit(solution)/shard_map/pallas_call | solution.py:242
  725.4 20.3 %collective-permute-done.32.two_ref = bf16[768,768]{1,0:T(8,128)(2,1)} collective-permute-done((bf16[768,768]{1,0:T(8,128)(2,1)}, bf16[768,768]{1,0:T(8,128)(2,1)}, u32[]{:S(2)}, u32[]{:S(2)}) %collective-permute-start.32) | collective-permute-done | bytes 1179680 | tf_op jit(solution)/shard_map/ppermute | solution.py:571
  754.6 16.4 %collective-permute-done.34.two_ref = bf16[192,3072]{1,0:T(8,128)(2,1)} collective-permute-done((bf16[192,3072]{1,0:T(8,128)(2,1)S(1)}, bf16[192,3072]{1,0:T(8,128)(2,1)}, u32[]{:S(2)}, u32[]{:S(2)}) %collective-permute-start.34) | collective-permute-done | bytes 1179680 | tf_op jit(solution)/shard_map/ppermute | solution.py:571
  777.7 27.4 %collective-permute-done.33.two_ref = bf16[768,768]{1,0:T(8,128)(2,1)S(1)} collective-permute-done((bf16[768,768]{1,0:T(8,128)(2,1)}, bf16[768,768]{1,0:T(8,128)(2,1)S(1)}, u32[]{:S(2)}, u32[]{:S(2)}) %collective-permute-start.33) | collective-permute-done | bytes 1179680 | tf_op jit(solution)/shard_map/ppermute | solution.py:721
  820.2 20.9 %collective-permute-done.37.two_ref = bf16[192,3072]{1,0:T(8,128)(2,1)S(1)} collective-permute-done((bf16[192,3072]{1,0:T(8,128)(2,1)}, bf16[192,3072]{1,0:T(8,128)(2,1)S(1)}, u32[]{:S(2)}, u32[]{:S(2)}) %collective-permute-start.37) | collective-permute-done | bytes 1179680 | tf_op jit(solution)/shard_map/ppermute | solution.py:721
  852.9 19.3 %collective-permute-start.13 = (bf16[192,768]{1,0:T(8,128)(2,1)S(1)}, bf16[192,768]{1,0:T(8,128)(2,1)S(1)}, u32[]{:S(2)}, u32[]{:S(2)}) collective-permute-start(bf16[192,768]{1,0:T(8,128)(2,1)S(1)} %get-tuple-element.144), channel_id=1, source_target_pairs={{0,4},{4,0},{1,5},{5,1},{2,6},{6,2},{3,7},{7,3},{8,12},{12,8},{9,1... | collective-permute-start | bytes 884744 | tf_op jit(solution)/shard_map/ppermute | solution.py:571
  872.3 22.6 %collective-permute-done.35.two_ref = bf16[272,2304]{1,0:T(8,128)(2,1)S(1)} collective-permute-done((bf16[272,2304]{1,0:T(8,128)(2,1)}, bf16[272,2304]{1,0:T(8,128)(2,1)S(1)}, u32[]{:S(2)}, u32[]{:S(2)}) %collective-permute-start.35) | collective-permute-done | bytes 1253408 | tf_op jit(solution)/shard_map/ppermute | solution.py:721
  904.8 36.8 %collective-permute-done.13 = bf16[192,768]{1,0:T(8,128)(2,1)S(1)} collective-permute-done((bf16[192,768]{1,0:T(8,128)(2,1)S(1)}, bf16[192,768]{1,0:T(8,128)(2,1)S(1)}, u32[]{:S(2)}, u32[]{:S(2)}) %collective-permute-start.13) | collective-permute-done | bytes 294944 | tf_op jit(solution)/shard_map/ppermute | solution.py:571
  945.1 30.4 %collective-permute-done.29 = bf16[192,768]{1,0:T(8,128)(2,1)S(1)} collective-permute-done((bf16[192,768]{1,0:T(8,128)(2,1)S(1)}, bf16[192,768]{1,0:T(8,128)(2,1)S(1)}, u32[]{:S(2)}, u32[]{:S(2)}) %collective-permute-start.29) | collective-permute-done | bytes 294944 | tf_op jit(solution)/shard_map/ppermute | solution.py:571
  987.3 23.3 %collective-permute-done.40 = bf16[272,2304]{1,0:T(8,128)(2,1)S(1)} collective-permute-done((bf16[272,2304]{1,0:T(8,128)(2,1)}, bf16[272,2304]{1,0:T(8,128)(2,1)S(1)}, u32[]{:S(2)}, u32[]{:S(2)}) %collective-permute-start.40) | collective-permute-done | bytes 1253408 | tf_op jit(solution)/shard_map/ppermute | solution.py:721
  (489 shorter events, 412.1 us)
Async XLA Ops:
  7.2 66.3 %all-gather.4.cloned.1.call-start = ((), (), s32[]{:S(2)}) async-start(), calls=%async_computation.16 | async-start | bytes 10616832 | tf_op jit(solution)/shard_map/all_gather | solution.py:641
  14.2 159.6 %all-gather.6.cloned.1.call-start = ((), (), s32[]{:S(2)}) async-start(), calls=%async_computation.17 | async-start | bytes 10616832 | tf_op jit(solution)/shard_map/all_gather | solution.py:641
  21.2 60.8 %collective-permute-start.5 = (bf16[1536,768]{1,0:T(8,128)(2,1)S(1)}, bf16[1536,768]{1,0:T(8,128)(2,1)}, u32[]{:S(2)}, u32[]{:S(2)}) collective-permute-start(bf16[1536,768]{1,0:T(8,128)(2,1)S(1)} %bitcast.209), channel_id=1, source_target_pairs={{0,8},{8,0},{1,9},{9,1},{2,10},{10,2},{3,11},{11,3},{4,12},{12,4},... | collective-permute-start | bytes 7077896 | tf_op jit(solution)/shard_map/ppermute | solution.py:571
  82.0 139.8 %all-gather.8.cloned.1.call-start = ((), (), s32[]{:S(2)}) async-start(), calls=%async_computation.18 | async-start | bytes 5308416 | tf_op jit(solution)/shard_map/all_gather | solution.py:658
  104.1 41.4 %collective-permute-start.6 = (bf16[768,768]{1,0:T(8,128)(2,1)}, bf16[768,768]{1,0:T(8,128)(2,1)S(1)}, u32[]{:S(2)}, u32[]{:S(2)}) collective-permute-start(bf16[768,768]{1,0:T(8,128)(2,1)} %shard_map.179), channel_id=1, source_target_pairs={{0,1},{1,0},{2,3},{3,2},{4,5},{5,4},{6,7},{7,6},{8,9},{9,8},{10,11... | collective-permute-start | bytes 3538952 | tf_op jit(solution)/shard_map/ppermute | solution.py:571
  507.4 43.3 %collective-permute-start.19 = (bf16[1536,768]{1,0:T(8,128)(2,1)}, bf16[1536,768]{1,0:T(8,128)(2,1)}, u32[]{:S(2)}, u32[]{:S(2)}) collective-permute-start(bf16[1536,768]{1,0:T(8,128)(2,1)} %convolution_convert_fusion.11.refs_5_), channel_id=1, source_target_pairs={{0,8},{8,0},{1,9},{9,1},{2,10},{10,2},{3,11},{11,3},{4,12},{12,4},... | collective-permute-start | bytes 7077896 | tf_op jit(solution)/shard_map/ppermute | solution.py:571
  521.1 33.4 %collective-permute-start.20 = (bf16[384,3072]{1,0:T(8,128)(2,1)}, bf16[384,3072]{1,0:T(8,128)(2,1)}, u32[]{:S(2)}, u32[]{:S(2)}) collective-permute-start(bf16[384,3072]{1,0:T(8,128)(2,1)} %convolution_convert_fusion.7.refs_7_), channel_id=1, source_target_pairs={{0,8},{8,0},{1,9},{9,1},{2,10},{10,2},{3,11},{11,3},{4,12},{12,4},... | collective-permute-start | bytes 7077896 | tf_op jit(solution)/shard_map/ppermute | solution.py:571
  591.6 31.9 %collective-permute-start.21 = (bf16[544,2304]{1,0:T(8,128)(2,1)}, bf16[544,2304]{1,0:T(8,128)(2,1)}, u32[]{:S(2)}, u32[]{:S(2)}) collective-permute-start(bf16[544,2304]{1,0:T(8,128)(2,1)} %bitcast.46), channel_id=1, source_target_pairs={{0,8},{8,0},{1,9},{9,1},{2,10},{10,2},{3,11},{11,3},{4,12},{12,4},... | collective-permute-start | bytes 7520264 | tf_op jit(solution)/shard_map/ppermute | solution.py:571
  595.6 76.4 %collective-permute-start.23 = (bf16[768,768]{1,0:T(8,128)(2,1)}, bf16[768,768]{1,0:T(8,128)(2,1)}, u32[]{:S(2)}, u32[]{:S(2)}) collective-permute-start(bf16[768,768]{1,0:T(8,128)(2,1)} %get-tuple-element.158.rest_0_), channel_id=1, source_target_pairs={{0,1},{1,0},{2,3},{3,2},{4,5},{5,4},{6,7},{7,6},{8,9},{9,8},{10,11... | collective-permute-start | bytes 3538952 | tf_op jit(solution)/shard_map/ppermute | solution.py:571
  597.1 79.4 %collective-permute-start.24 = (bf16[192,3072]{1,0:T(8,128)(2,1)S(1)}, bf16[192,3072]{1,0:T(8,128)(2,1)}, u32[]{:S(2)}, u32[]{:S(2)}) collective-permute-start(bf16[192,3072]{1,0:T(8,128)(2,1)S(1)} %copy-done.22), channel_id=1, source_target_pairs={{0,1},{1,0},{2,3},{3,2},{4,5},{5,4},{6,7},{7,6},{8,9},{9,8},{10,11... | collective-permute-start | bytes 3538952 | tf_op jit(solution)/shard_map/ppermute | solution.py:571
  607.7 46.5 %all-to-all-start.14 = ((bf16[4,192,192]{2,1,0:T(8,128)(2,1)}), bf16[4,192,192]{2,1,0:T(8,128)(2,1)}, u32[]{:S(2)}, u32[]{:S(2)}) async-start(bf16[4,192,192]{2,1,0:T(8,128)(2,1)} %get-tuple-element.111), calls=%async_computation.14 | async-start | bytes 786432 | tf_op jit(solution)/shard_map/all_to_all | solution.py:580
  614.3 84.5 %collective-permute-start.26 = (bf16[1536,768]{1,0:T(8,128)(2,1)}, bf16[1536,768]{1,0:T(8,128)(2,1)}, u32[]{:S(2)}, u32[]{:S(2)}) collective-permute-start(bf16[1536,768]{1,0:T(8,128)(2,1)} %convolution_convert_fusion.9.refs_7_), channel_id=1, source_target_pairs={{0,8},{8,0},{1,9},{9,1},{2,10},{10,2},{3,11},{11,3},{4,12},{12,4},... | collective-permute-start | bytes 7077896 | tf_op jit(solution)/shard_map/ppermute | solution.py:571
  616.6 85.9 %collective-permute-start.27 = (bf16[384,3072]{1,0:T(8,128)(2,1)}, bf16[384,3072]{1,0:T(8,128)(2,1)}, u32[]{:S(2)}, u32[]{:S(2)}) collective-permute-start(bf16[384,3072]{1,0:T(8,128)(2,1)} %convolution_convert_fusion.3.refs_9_), channel_id=1, source_target_pairs={{0,8},{8,0},{1,9},{9,1},{2,10},{10,2},{3,11},{11,3},{4,12},{12,4},... | collective-permute-start | bytes 7077896 | tf_op jit(solution)/shard_map/ppermute | solution.py:571
  627.4 53.3 %collective-permute-start.25 = (bf16[272,2304]{1,0:T(8,128)(2,1)}, bf16[272,2304]{1,0:T(8,128)(2,1)}, u32[]{:S(2)}, u32[]{:S(2)}) collective-permute-start(bf16[272,2304]{1,0:T(8,128)(2,1)} %get-tuple-element.150.refs_5_), channel_id=1, source_target_pairs={{0,1},{1,0},{2,3},{3,2},{4,5},{5,4},{6,7},{7,6},{8,9},{9,8},{10,11... | collective-permute-start | bytes 3760136 | tf_op jit(solution)/shard_map/ppermute | solution.py:571
  691.7 251.1 %all-reduce.5.cloned.1.call-start = ((), (), s32[]{:S(2)}) async-start(), calls=%async_computation.19 | async-start | bytes 7225344 | tf_op jit(solution)/shard_map/psum | solution.py:717
  716.6 29.2 %collective-permute-start.32 = (bf16[768,768]{1,0:T(8,128)(2,1)}, bf16[768,768]{1,0:T(8,128)(2,1)}, u32[]{:S(2)}, u32[]{:S(2)}) collective-permute-start(bf16[768,768]{1,0:T(8,128)(2,1)} %get-tuple-element.154.refs_5_), channel_id=1, source_target_pairs={{0,1},{1,0},{2,3},{3,2},{4,5},{5,4},{6,7},{7,6},{8,9},{9,8},{10,11... | collective-permute-start | bytes 3538952 | tf_op jit(solution)/shard_map/ppermute | solution.py:571
  718.8 52.2 %collective-permute-start.34 = (bf16[192,3072]{1,0:T(8,128)(2,1)S(1)}, bf16[192,3072]{1,0:T(8,128)(2,1)}, u32[]{:S(2)}, u32[]{:S(2)}) collective-permute-start(bf16[192,3072]{1,0:T(8,128)(2,1)S(1)} %copy-done.15), channel_id=1, source_target_pairs={{0,1},{1,0},{2,3},{3,2},{4,5},{5,4},{6,7},{7,6},{8,9},{9,8},{10,11... | collective-permute-start | bytes 3538952 | tf_op jit(solution)/shard_map/ppermute | solution.py:571
  749.3 55.8 %collective-permute-start.33 = (bf16[768,768]{1,0:T(8,128)(2,1)}, bf16[768,768]{1,0:T(8,128)(2,1)S(1)}, u32[]{:S(2)}, u32[]{:S(2)}) collective-permute-start(bf16[768,768]{1,0:T(8,128)(2,1)} %shard_map.210.rest_0_.one_ref), channel_id=1, source_target_pairs={{0,2},{6,4},{1,3},{7,5},{8,10},{14,12},{9,11},{15,13},{16,18},{22,... | collective-permute-start | bytes 3538952 | tf_op jit(solution)/shard_map/ppermute | solution.py:721
  753.1 58.2 %collective-permute-start.31 = (bf16[272,2304]{1,0:T(8,128)(2,1)S(1)}, bf16[272,2304]{1,0:T(8,128)(2,1)S(1)}, u32[]{:S(2)}, u32[]{:S(2)}) collective-permute-start(bf16[272,2304]{1,0:T(8,128)(2,1)S(1)} %copy-done), channel_id=1, source_target_pairs={{0,1},{1,0},{2,3},{3,2},{4,5},{5,4},{6,7},{7,6},{8,9},{9,8},{10,11... | collective-permute-start | bytes 3760136 | tf_op jit(solution)/shard_map/ppermute | solution.py:571
  773.9 67.3 %collective-permute-start.37 = (bf16[192,3072]{1,0:T(8,128)(2,1)}, bf16[192,3072]{1,0:T(8,128)(2,1)S(1)}, u32[]{:S(2)}, u32[]{:S(2)}) collective-permute-start(bf16[192,3072]{1,0:T(8,128)(2,1)} %shard_map.211.rest_0_.one_ref), channel_id=1, source_target_pairs={{0,2},{6,4},{1,3},{7,5},{8,10},{14,12},{9,11},{15,13},{16,18},{22,... | collective-permute-start | bytes 3538952 | tf_op jit(solution)/shard_map/ppermute | solution.py:721
  809.7 37.2 %collective-permute-start.36 = (bf16[768,768]{1,0:T(8,128)(2,1)}, bf16[768,768]{1,0:T(8,128)(2,1)}, u32[]{:S(2)}, u32[]{:S(2)}) collective-permute-start(bf16[768,768]{1,0:T(8,128)(2,1)} %shard_map.212.rest_0_.one_ref), channel_id=1, source_target_pairs={{2,4},{4,2},{3,5},{5,3},{10,12},{12,10},{11,13},{13,11},{18,20},{2... | collective-permute-start | bytes 3538952 | tf_op jit(solution)/shard_map/ppermute | solution.py:721
  815.4 79.5 %collective-permute-start.35 = (bf16[272,2304]{1,0:T(8,128)(2,1)}, bf16[272,2304]{1,0:T(8,128)(2,1)S(1)}, u32[]{:S(2)}, u32[]{:S(2)}) collective-permute-start(bf16[272,2304]{1,0:T(8,128)(2,1)} %shard_map.213.rest_0_.one_ref), channel_id=1, source_target_pairs={{0,2},{6,4},{1,3},{7,5},{8,10},{14,12},{9,11},{15,13},{16,18},{22,... | collective-permute-start | bytes 3760136 | tf_op jit(solution)/shard_map/ppermute | solution.py:721
  845.1 55.5 %collective-permute-start.39 = (bf16[192,3072]{1,0:T(8,128)(2,1)}, bf16[192,3072]{1,0:T(8,128)(2,1)}, u32[]{:S(2)}, u32[]{:S(2)}) collective-permute-start(bf16[192,3072]{1,0:T(8,128)(2,1)} %shard_map.214.rest_0_.one_ref), channel_id=1, source_target_pairs={{2,4},{4,2},{3,5},{5,3},{10,12},{12,10},{11,13},{13,11},{18,20},{2... | collective-permute-start | bytes 3538952 | tf_op jit(solution)/shard_map/ppermute | solution.py:721
  850.4 92.4 %collective-permute-start.44 = (bf16[768,768]{1,0:T(8,128)(2,1)}, bf16[768,768]{1,0:T(8,128)(2,1)}, u32[]{:S(2)}, u32[]{:S(2)}) collective-permute-start(bf16[768,768]{1,0:T(8,128)(2,1)} %shard_map.215.rest_0_), channel_id=1, source_target_pairs={{2,0},{4,6},{3,1},{5,7},{10,8},{12,14},{11,9},{13,15},{18,16},{20,... | collective-permute-start | bytes 3538952 | tf_op jit(solution)/shard_map/ppermute | solution.py:721
  852.9 88.8 %collective-permute-start.13 = (bf16[192,768]{1,0:T(8,128)(2,1)S(1)}, bf16[192,768]{1,0:T(8,128)(2,1)S(1)}, u32[]{:S(2)}, u32[]{:S(2)}) collective-permute-start(bf16[192,768]{1,0:T(8,128)(2,1)S(1)} %get-tuple-element.144), channel_id=1, source_target_pairs={{0,4},{4,0},{1,5},{5,1},{2,6},{6,2},{3,7},{7,3},{8,12},{12,8},{9,1... | collective-permute-start | bytes 884744 | tf_op jit(solution)/shard_map/ppermute | solution.py:571
  872.3 70.3 %collective-permute-start.28 = (bf16[192,768]{1,0:T(8,128)(2,1)S(1)}, bf16[192,768]{1,0:T(8,128)(2,1)S(1)}, u32[]{:S(2)}, u32[]{:S(2)}) collective-permute-start(bf16[192,768]{1,0:T(8,128)(2,1)S(1)} %broadcast_select_fusion.23), channel_id=1, source_target_pairs={{0,8},{8,0},{1,9},{9,1},{2,10},{10,2},{3,11},{11,3},{4,12},{12,4},... | collective-permute-start | bytes 884744 | tf_op jit(solution)/shard_map/ppermute | solution.py:571
  898.9 79.2 %collective-permute-start.38 = (bf16[272,2304]{1,0:T(8,128)(2,1)}, bf16[272,2304]{1,0:T(8,128)(2,1)}, u32[]{:S(2)}, u32[]{:S(2)}) collective-permute-start(bf16[272,2304]{1,0:T(8,128)(2,1)} %shard_map.216.rest_0_.one_ref), channel_id=1, source_target_pairs={{2,4},{4,2},{3,5},{5,3},{10,12},{12,10},{11,13},{13,11},{18,20},{2... | collective-permute-start | bytes 3760136 | tf_op jit(solution)/shard_map/ppermute | solution.py:721
  903.6 79.2 %collective-permute-start.42 = (bf16[192,3072]{1,0:T(8,128)(2,1)}, bf16[192,3072]{1,0:T(8,128)(2,1)}, u32[]{:S(2)}, u32[]{:S(2)}) collective-permute-start(bf16[192,3072]{1,0:T(8,128)(2,1)} %shard_map.217.rest_0_), channel_id=1, source_target_pairs={{2,0},{4,6},{3,1},{5,7},{10,8},{12,14},{11,9},{13,15},{18,16},{20,... | collective-permute-start | bytes 3538952 | tf_op jit(solution)/shard_map/ppermute | solution.py:721
  942.7 32.8 %collective-permute-start.29 = (bf16[192,768]{1,0:T(8,128)(2,1)S(1)}, bf16[192,768]{1,0:T(8,128)(2,1)S(1)}, u32[]{:S(2)}, u32[]{:S(2)}) collective-permute-start(bf16[192,768]{1,0:T(8,128)(2,1)S(1)} %get-tuple-element.141), channel_id=1, source_target_pairs={{0,4},{4,0},{1,5},{5,1},{2,6},{6,2},{3,7},{7,3},{8,12},{12,8},{9,1... | collective-permute-start | bytes 884744 | tf_op jit(solution)/shard_map/ppermute | solution.py:571
  945.0 39.4 %collective-permute-start.45 = (bf16[768,768]{1,0:T(8,128)(2,1)S(1)}, bf16[768,768]{1,0:T(8,128)(2,1)S(1)}, u32[]{:S(2)}, u32[]{:S(2)}) collective-permute-start(bf16[768,768]{1,0:T(8,128)(2,1)S(1)} %get-tuple-element.135), channel_id=1, source_target_pairs={{0,8},{8,0},{1,9},{9,1},{2,10},{10,2},{3,11},{11,3},{4,12},{12,4},... | collective-permute-start | bytes 3538952 | tf_op jit(solution)/shard_map/ppermute | solution.py:571
  981.2 29.4 %collective-permute-start.40 = (bf16[272,2304]{1,0:T(8,128)(2,1)}, bf16[272,2304]{1,0:T(8,128)(2,1)S(1)}, u32[]{:S(2)}, u32[]{:S(2)}) collective-permute-start(bf16[272,2304]{1,0:T(8,128)(2,1)} %shard_map.218), channel_id=1, source_target_pairs={{2,0},{4,6},{3,1},{5,7},{10,8},{12,14},{11,9},{13,15},{18,16},{20,... | collective-permute-start | bytes 3760136 | tf_op jit(solution)/shard_map/ppermute | solution.py:721
  984.4 26.5 %collective-permute-start.43 = (bf16[192,3072]{1,0:T(8,128)(2,1)S(1)}, bf16[192,3072]{1,0:T(8,128)(2,1)S(1)}, u32[]{:S(2)}, u32[]{:S(2)}) collective-permute-start(bf16[192,3072]{1,0:T(8,128)(2,1)S(1)} %get-tuple-element.137), channel_id=1, source_target_pairs={{0,8},{8,0},{1,9},{9,1},{2,10},{10,2},{3,11},{11,3},{4,12},{12,4},... | collective-permute-start | bytes 3538952 | tf_op jit(solution)/shard_map/ppermute | solution.py:571
  (128 other events, 975.5 us)
Sparse Core Ops, SparseCore 0:
  14.4 59.0 all-gather.3
  75.6 84.4 all-gather.5
  162.2 50.4 all-gather.7
  719.2 205.7 all-reduce.4

commit v6 on v5

--- a/solution.py
+++ b/solution.py
@@ -15,6 +15,7 @@
 VMEM_LIMIT = 56 * 1024 * 1024
 AXES = ("pair", "core", "half", "quad", "side", "rest")
 HEAD_GROUPS = 4
+ROW_BLOCKS = (272, 256, 192, 128, 96, 80, 64, 48)
 
 
 def call(body, out_shapes, grid=None, in_specs=None, out_specs=None, scratch=(), flops=0, moved=0):
@@ -57,19 +58,16 @@
 
 
 def qkv_body(x_ref, gain_ref, shift_ref, w_ref, bias_ref, out_ref, normed_ref):
-    @pl.when(pl.program_id(0) == 0)
-    def _():
-        scaled, _ = norm_parts(x_ref[...].astype(F32))
-        normed_ref[...] = (scaled * gain_ref[...] + shift_ref[...]).astype(BF16)
-
+    scaled, _ = norm_parts(x_ref[...].astype(F32))
+    normed = (scaled * gain_ref[...] + shift_ref[...]).astype(BF16)
+    normed_ref[...] = normed
     span = out_ref.shape[2] // 3
-    piece = (dot(normed_ref[...], w_ref[...]) + bias_ref[...]).astype(BF16)
+    width = x_ref.shape[1]
     for part in range(3):
-
-        @pl.when(pl.program_id(0) == part)
-        def _(part=part):
-            for g in range(HEAD_GROUPS):
-                out_ref[g, :, part * span : (part + 1) * span] = piece[:, g * span : (g + 1) * span]
+        cols = slice(part * width, (part + 1) * width)
+        piece = (dot(normed, w_ref[:, cols]) + bias_ref[:, cols]).astype(BF16)
+        for g in range(HEAD_GROUPS):
+            out_ref[g, :, part * span : (part + 1) * span] = piece[:, g * span : (g + 1) * span]
 
 
 def qkv_forward(x, gain, shift, joined, bias):
@@ -81,13 +79,13 @@
             jax.ShapeDtypeStruct((HEAD_GROUPS, rows, 3 * span), BF16),
             jax.ShapeDtypeStruct((rows, width), BF16),
         ),
-        grid=(3,),
+        grid=(1,),
         in_specs=[
             whole((rows, width)),
             whole((1, width)),
             whole((1, width)),
-            pl.BlockSpec((width, width), lambda i: (0, i)),
-            pl.BlockSpec((1, width), lambda i: (0, i)),
+            whole((width, 3 * width)),
+            whole((1, 3 * width)),
         ],
         out_specs=(whole((HEAD_GROUPS, rows, 3 * span)), whole((rows, width))),
         flops=2 * rows * width * 3 * width,
@@ -447,34 +445,22 @@
     )(g, slope, w_down, joined, joined, x1, gain)
 
 
-def qkv_back_body(
-    grads_ref, w_ref, x_ref, dx1_ref, gain_ref, dx_ref, flat_ref, sums_ref, acc
-):
+def qkv_back_body(grads_ref, w_ref, x_ref, dx1_ref, gain_ref, dx_ref, flat_ref, sums_ref):
     width = x_ref.shape[1]
     span = grads_ref.shape[2] // 3
-    step = pl.program_id(0)
-    for part in range(3):
-
-        @pl.when(step == part)
-        def _(part=part):
-            cols = slice(part * width, (part + 1) * width)
-            for g in range(HEAD_GROUPS):
-                flat_ref[:, part * width + g * span : part * width + (g + 1) * span] = grads_ref[
-                    g, :, part * span : (part + 1) * span
-                ]
-            came = dot_t(flat_ref[:, cols], w_ref[...])
-            acc[...] = came if part == 0 else acc[...] + came
-
-    @pl.when(step == 2)
-    def _():
-        d_normed = acc[...]
-        scaled, inverse = norm_parts(x_ref[...].astype(F32))
-        dx = dx1_ref[...] + norm_back(d_normed, scaled, inverse, gain_ref[...])
-        dx_ref[...] = dx.astype(BF16)
-        sums_ref[0:1, :] = jnp.sum(d_normed * scaled, axis=0, keepdims=True)
-        sums_ref[1:2, :] = jnp.sum(d_normed, axis=0, keepdims=True)
-        sums_ref[2:3, :] = jnp.sum(flat_ref[:, :width].astype(F32), axis=0, keepdims=True)
-        sums_ref[3:4, :] = jnp.sum(flat_ref[:, 2 * width :].astype(F32), axis=0, keepdims=True)
+    for g in range(HEAD_GROUPS):
+        for part in range(3):
+            flat_ref[:, part * width + g * span : part * width + (g + 1) * span] = grads_ref[
+                g, :, part * span : (part + 1) * span
+            ]
+    d_normed = dot_t(flat_ref[...], w_ref[...])
+    scaled, inverse = norm_parts(x_ref[...].astype(F32))
+    dx = dx1_ref[...] + norm_back(d_normed, scaled, inverse, gain_ref[...])
+    dx_ref[...] = dx.astype(BF16)
+    sums_ref[0:1, :] = jnp.sum(d_normed * scaled, axis=0, keepdims=True)
+    sums_ref[1:2, :] = jnp.sum(d_normed, axis=0, keepdims=True)
+    sums_ref[2:3, :] = jnp.sum(flat_ref[:, :width].astype(F32), axis=0, keepdims=True)
+    sums_ref[3:4, :] = jnp.sum(flat_ref[:, 2 * width :].astype(F32), axis=0, keepdims=True)
 
 
 def qkv_backward(grads, joined, x, dx1, gain, after=()):
@@ -490,17 +476,16 @@
             jax.ShapeDtypeStruct((rows, 3 * width), BF16),
             jax.ShapeDtypeStruct((4, width), F32),
         ),
-        grid=(3,),
+        grid=(1,),
         in_specs=[
             whole(grads.shape),
-            pl.BlockSpec((width, width), lambda i: (0, i)),
+            whole((width, 3 * width)),
             whole((rows, width)),
             whole((rows, width)),
             whole((1, width)),
         ]
         + [pl.BlockSpec(memory_space=pl.ANY)] * len(after),
         out_specs=(whole((rows, width)), whole((rows, 3 * width)), whole((4, width))),
-        scratch=[pltpu.VMEM((rows, width), F32)],
         flops=2 * rows * width * 3 * width,
         moved=6 * width * width + 20 * x.size,
     )(grads, joined, x, dx1, gain, *after)
@@ -512,7 +497,7 @@
 
 def add_after(one, two, after):
     rows, wide = one.shape
-    block = next((n for n in (272, 256, 192, 128, 96, 80, 64, 48) if rows % n == 0), rows)
+    block = next((n for n in ROW_BLOCKS if rows % n == 0), rows)
     spec = pl.BlockSpec((block, wide), lambda i: (i, 0))
     return call(
         add_body,
@@ -692,18 +677,37 @@
     ]
 
 
-def side_parts(sent, kept):
-    side = lax.axis_index("side")
+def parts_body(side_ref, *refs):
+    far_one, far_two, near_one, near_two = refs[:4]
+    sent_ref, kept_ref = refs[-2:]
+    sent_ref[...] = (far_one[...].astype(F32) + far_two[...].astype(F32)).astype(BF16)
+    kept_ref[...] = (near_one[...].astype(F32) + near_two[...].astype(F32)).astype(BF16)
+
+
+def side_parts(sent, kept, *after):
     came = swap(sent, "core")
-    half = kept.shape[0] // 2
-
-    def cut(which):
-        return add(
-            lax.dynamic_slice_in_dim(kept, which * half, half, 0),
-            lax.dynamic_slice_in_dim(came, which * half, half, 0),
-        )
-
-    return cut(1 - side), cut(side)
+    rows, wide = kept.shape
+    half = rows // 2
+    block = next((n for n in ROW_BLOCKS if half % n == 0), half)
+    steps = half // block
+    far = pl.BlockSpec((block, wide), lambda i, side: ((1 - side[0]) * steps + i, 0))
+    near = pl.BlockSpec((block, wide), lambda i, side: (side[0] * steps + i, 0))
+    out = pl.BlockSpec((block, wide), lambda i, side: (i, 0))
+    return pl.pallas_call(
+        parts_body,
+        out_shape=(jax.ShapeDtypeStruct((half, wide), BF16),) * 2,
+        grid_spec=pltpu.PrefetchScalarGridSpec(
+            num_scalar_prefetch=1,
+            grid=(steps,),
+            in_specs=[far, far, near, near]
+            + [pl.BlockSpec(memory_space=pl.ANY)] * len(after),
+            out_specs=(out, out),
+        ),
+        compiler_params=pltpu.CompilerParams(vmem_limit_bytes=VMEM_LIMIT),
+        cost_estimate=pl.CostEstimate(
+            flops=kept.size, bytes_accessed=6 * kept.size, transcendentals=0
+        ),
+    )(lax.axis_index("side").astype(jnp.int32).reshape(1), kept, came, kept, came, *after)
 
 
 def side_sum(sent, kept, *after):
@@ -721,7 +725,7 @@
     return lax.ppermute(block, ("half", "quad"), pairs)
 
 
-def line_sums(sides):
+def line_sums(sides, last):
     inward, across, outward = [(0, 1), (3, 2)], [(1, 2), (2, 1)], [(1, 0), (2, 3)]
     inner = lax.axis_index("half") != lax.axis_index("quad")
     count = len(sides)
@@ -733,11 +737,13 @@
             mark = (totals[turn],)
         for hops, at in ((inward, turn - 1), (across, turn - 2)):
             if 0 <= at < count:
+                if turn == count + 1:
+                    mark = (*mark, *last)
                 totals[at] = add_after(totals[at], line_hop(totals[at], hops), mark)
                 mark = (totals[at],)
                 if hops is across:
                     results.append(pick(inner, totals[at], line_hop(totals[at], outward)))
-    return results
+    return results, mark[0]
 
 
 def join_cores(first, second):
@@ -757,13 +763,16 @@
     return pick(core == half, own, came)
 
 
-def swap_out(first, second, micro):
+def swap_out(first, second, micro, *after):
     rows, wide = first.shape
     second_core, second_half = lax.axis_index("core") == 1, lax.axis_index("half") == 1
     mine, sent = in_order(second_core, first, second)
     parts = in_order(second_core, mine, swap(sent, "core"))
     mine, sent = in_order(second_half, *parts)
-    clips = in_order(second_half, mine, swap(sent, "half"))
+    came = swap(sent, "half")
+    if after:
+        came = copy_after(came, after)
+    clips = in_order(second_half, mine, came)
     return jnp.stack(clips).reshape(micro, 2 * rows // micro, wide)
 
 
@@ -785,8 +794,11 @@
 
 
 def attention_grads(kept, d_att, clips, head, after):
+    return heads_back(kept, to_clips(spread(d_att), clips), head, after)
+
+
+def heads_back(kept, d_heads, head, after):
     own, other, log_total = kept[2:5]
-    d_heads = to_clips(spread(d_att), clips)
     dq, kept_kv, sent_kv = attend_backward(own, other, d_heads, log_total, head, after)
     return (dq, *return_keys(kept_kv, sent_kv))
 
@@ -795,11 +807,11 @@
     return spread(to_tokens(join_grads(*grads, after)))
 
 
-def backward_lean(kept, g, weights, clips, head):
+def backward_lean(kept, g, weights, clips, head, *after):
     x, _, _, _, _, x1, _, slope, _, _ = kept
     joined, w_down, gains = weights[:3]
     _, dx1, _, d_att, _, _ = feed_backward(g, slope, w_down, joined, x1, gains[1:2])
-    d_tokens = spread_grads(attention_grads(kept, d_att, clips, head, ()))
+    d_tokens = spread_grads(attention_grads(kept, d_att, clips, head, after))
     return qkv_backward(d_tokens, joined, x, dx1, gains[0:1])[0]
 
 
@@ -851,10 +863,12 @@
     down = weight_halves(lifted, g)
     up = weight_halves(normed_two, d_upper)
     grads = attention_grads(kept_second, d_att, clips, head, (*down, *up))
-    down, up = side_parts(*down), side_parts(*up)
-    d_tokens = spread_grads(grads, (*down, *up))
+    d_tokens = spread_grads(grads)
     out = weight_halves(att, branch)
-    d_second, flat, sums_one = qkv_backward(d_tokens, joined, x, dx1, gains[0:1], out)
+    down = side_parts(*down, d_tokens)
+    d_second, flat, sums_one = qkv_backward(
+        d_tokens, joined, x, dx1, gains[0:1], (*down, *out)
+    )
     rest = rest_halves(normed_one, flat, out, sums_one, sums_two, up_sum, shards)
 
     x, normed_one, _, _, _, x1, normed_two, slope, lifted, att = kept_first
@@ -864,16 +878,22 @@
     )
     down_one = weight_halves(lifted, d_second)
     up_one = weight_halves(normed_two, d_upper)
-    rest = side_parts(*rest)
-    grads = attention_grads(kept_first, d_att, clips, head, (*rest, *down_one, *up_one))
-    down_two, up_two, rest_two = (side_sum(*item, grads[0]) for item in (down, up, rest))
-    d_tokens = spread_grads(grads, (down_two, up_two, rest_two))
-    seconds = line_sum(rest_two, up_two, down_two)
+    d_heads = to_clips(spread(d_att), clips)
+    up = side_parts(*up, d_heads)
+    down_two = side_sum(*down)
+    grads = heads_back(
+        kept_first, d_heads, head, (down_two, *up, *rest, *down_one, *up_one)
+    )
+    rest = side_parts(*rest, grads[0])
+    up_two = side_sum(*up, grads[0])
+    d_tokens = spread_grads(grads, (up_two, *rest))
+    rest_two = side_sum(*rest)
     down_one, up_one = side_parts(*down_one), side_parts(*up_one)
     out_one = weight_halves(att, branch)
     d_first, flat, sums_one = qkv_backward(
-        d_tokens, joined, x, dx1, gains[0:1], (*down_one, *up_one, *out_one)
-    )
+        d_tokens, joined, x, dx1, gains[0:1], (rest_two, *down_one, *up_one, *out_one)
+    )
+    seconds = line_sum(rest_two, up_two, down_two)
     rest_one = rest_halves(normed_one, flat, out_one, sums_one, sums_two, up_sum, shards)
     rest_one = side_parts(*rest_one)
     sides = [
@@ -881,11 +901,12 @@
         for item in (down_one, up_one, rest_one)
     ]
     if lax.axis_size("quad") == 2:
-        firsts = line_sums(sides)
+        firsts, mark = line_sums(sides, seconds)
     else:
         firsts = line_sum(*(item() for item in sides))
+        mark = firsts[2]
     firsts = (firsts[2], firsts[1], firsts[0])
-    return d_first, d_second, [join_cores(a, b) for a, b in zip(firsts, seconds)]
+    return d_first, d_second, mark, [join_cores(a, b) for a, b in zip(firsts, seconds)]
 
 
 def gather_small(block):
@@ -942,14 +963,14 @@
     g_start = swap_in(out_grad)
     g = g_start
     for phase in range(pairs - 1):
-        d_second = backward_lean(kept_second, g, layers[1], clips, head)
+        d_second = backward_lean(kept_second, g, layers[1], clips, head, hidden)
         d_first = backward_lean(kept_first, d_second, layers[0], clips, head)
         came = lax.ppermute(d_first, "pair", [(i + 1, i) for i in range(pairs - 1)])
         g = pick(pair == pairs - 1, g_start, came)
-    d_first, d_second, (rest, up, down) = backward_all(
+    d_first, d_second, mark, (rest, up, down) = backward_all(
         kept_first, kept_second, g, layers, clips, head, shards
     )
-    input_grads = swap_out(d_first, d_second, micro)
+    input_grads = swap_out(d_first, d_second, micro, mark)
 
     own_rows = part // 2
     rest = rest.reshape(2, -1, 3 * width)

time: 1040 us -> 1040 us (level)
  waiting for transfers between devices: 369 us -> 325 us
  starting transfers between devices: 96.9 us -> 121 us
  Pallas kernels: 281 us -> 301 us
  other arithmetic: 61.2 us -> 46.1 us
  local copies, waits for them, and re-layouts: 46.1 us -> 59.1 us
    all_to_all x8, waiting for transfers between devices: 66 us -> 22.5 us  [spread(): return lax.all_to_all(block, ('quad', 'side'), 0, 0, tiled=True)]
    ppermute x33, starting transfers between devices: 38 us -> 64.5 us  [swap(): return lax.ppermute(block, axis, [(0, 1), (1, 0)])]
    pallas_call x0 -> x6, Pallas kernels: none -> 25.4 us  [side_parts(): pl.pallas_call(parts_body, out_shape=(jax.ShapeDtypeStruct((half, wide),...]
    convert_element_type x6 -> x0, other arithmetic: 23 us -> none  [add(): return (one.astype(F32) + two.astype(F32)).astype(one.dtype)]
    ppermute x9, waiting for transfers between devices: 94.3 us -> 116 us  [line_hop(): return lax.ppermute(block, ('half', 'quad'), pairs)]
    ppermute x33, waiting for transfers between devices: 151 us -> 129 us  [swap(): return lax.ppermute(block, axis, [(0, 1), (1, 0)])]
    unnamed x227 -> x239, local copies, waits for them, and re-layouts: 29.2 us -> 37.5 us
  transfers between devices with their start and end apart: 58 -> 58, of which waited for: 28 -> 29; matrix products, arithmetic and copies ran while one was open for 9% -> 9% of each run, Pallas kernels for 14% -> 17%
where the time goes in v6:
time: 1040 us; the launch traced here: 1020 us
  waiting for transfers between devices  325 us (31%)
  Pallas kernels  301 us (29%)
  blocking collectives  129 us (12%)
  starting transfers between devices  121 us (12%)
  local copies, waits for them, and re-layouts  59.1 us (6%)
  other arithmetic  46.1 us (4%)
  matrix products  27.7 us (3%)
  between operations  15.6 us (2%)
    ppermute x33, waiting for transfers between devices, swap(): return lax.ppermute(block, axis, [(0, 1), (1, 0)])  129 us
    all_to_all x8, blocking collectives, spread(): return lax.all_to_all(block, ('quad', 'side'), 0, 0, tiled=True)  129 us
    ppermute x9, waiting for transfers between devices, line_hop(): return lax.ppermute(block, ('half', 'quad'), pairs)  116 us
    pallas_call x4, Pallas kernels, attend_backward(): call(body, (jax.ShapeDtypeStruct((clips, queries, span), BF16), jax.Shape...  71.3 us
    ppermute x33, starting transfers between devices, swap(): return lax.ppermute(block, axis, [(0, 1), (1, 0)])  64.5 us
    all_gather x2, waiting for transfers between devices, gather_weight(): lax.all_gather(item, ('side', 'rest', 'core', 'quad'), axis=0, tiled=True)  43 us
    pallas_call x4, Pallas kernels, feed_backward(): call(feed_back_body, (jax.ShapeDtypeStruct((rows, hidden), BF16), jax.Sha...  39.8 us
    pallas_call x4, Pallas kernels, attend_forward(): call(body, (jax.ShapeDtypeStruct((clips, queries, span), BF16), jax.Shape...  39.2 us
  transfers between devices with their start and end apart: 58, of which 29 were waited for; matrix products, arithmetic and copies ran while one was open for 9% of the time, Pallas kernels for 17%

profile of v6, /device:TPU:0, one launch (start us, length us, event | category | flops | bytes accessed | tf_op | source)
XLA Modules:
  0.0 1024.3 jit_solution(17494156612445716963)
XLA Ops:
  30.6 43.0 %all-gather.4.cloned.1.call-done.w_ref.rest_0_.w_out_ref.w_up_ref.refs_1_ = bf16[768,6144]{1,0:T(8,128)(2,1)} async-done(((bf16[96,6144]{1,0:T(8,128)(2,1)}), bf16[768,6144]{1,0:T(8,128)(2,1)}) %all-gather.4.cloned.1.call-update) | async-done | bytes 9437200 | tf_op jit(solution)/shard_map/all_gather | solution.py:626
  85.3 13.9 %all-to-all-done = bf16[4,192,576]{2,1,0:T(8,128)(2,1)S(1)} async-done(((bf16[4,192,576]{2,1,0:T(8,128)(2,1)}), bf16[4,192,576]{2,1,0:T(8,128)(2,1)S(1)}, u32[]{:S(2)}, u32[]{:S(2)}) %all-to-all-start) | async-done | bytes 884768 | tf_op jit(solution)/shard_map/all_to_all | solution.py:565
  105.0 9.8 shard_map.178
  114.9 29.3 %collective-permute-done.6.one_ref = bf16[768,768]{1,0:T(8,128)(2,1)S(1)} collective-permute-done((bf16[768,768]{1,0:T(8,128)(2,1)}, bf16[768,768]{1,0:T(8,128)(2,1)S(1)}, u32[]{:S(2)}, u32[]{:S(2)}) %collective-permute-start.6) | collective-permute-done | bytes 1179680 | tf_op jit(solution)/shard_map/ppermute | solution.py:556
  176.7 23.1 %all_to_all.80 = bf16[4,192,576]{2,1,0:T(8,128)(2,1)S(1)} all-to-all(bf16[4,192,576]{2,1,0:T(8,128)(2,1)} %get-tuple-element.86), channel_id=1, replica_groups=mesh['pair'=2,'core'=2,'half'=2,'quad'=2,'side'=2,'rest'=1] {'quad','side'}, dimensions={0} | all-to-all | bytes 1769472 | tf_op jit(solution)/shard_map/all_to_all | solution.py:565
  203.4 9.8 shard_map.183
  246.7 16.4 %all_to_all.81 = bf16[4,192,576]{2,1,0:T(8,128)(2,1)S(1)} all-to-all(bf16[4,192,576]{2,1,0:T(8,128)(2,1)} %get-tuple-element.88), channel_id=1, replica_groups=mesh['pair'=2,'core'=2,'half'=2,'quad'=2,'side'=2,'rest'=1] {'quad','side'}, dimensions={0} | all-to-all | bytes 1769472 | tf_op jit(solution)/shard_map/all_to_all | solution.py:565
  266.7 9.8 shard_map.186
  276.5 11.9 %all_to_all.82.att_ref = bf16[4,192,192]{2,1,0:T(8,128)(2,1)} all-to-all(bf16[4,192,192]{2,1,0:T(8,128)(2,1)} %bitcast.236), channel_id=1, replica_groups=mesh['pair'=2,'core'=2,'half'=2,'quad'=2,'side'=2,'rest'=1] {'quad','side'}, dimensions={0} | all-to-all | bytes 589824 | tf_op jit(solution)/shard_map/all_to_all | solution.py:565
  301.8 16.9 %all_to_all.83 = bf16[4,192,576]{2,1,0:T(8,128)(2,1)S(1)} all-to-all(bf16[4,192,576]{2,1,0:T(8,128)(2,1)} %get-tuple-element.91), channel_id=1, replica_groups=mesh['pair'=2,'core'=2,'half'=2,'quad'=2,'side'=2,'rest'=1] {'quad','side'}, dimensions={0} | all-to-all | bytes 1769472 | tf_op jit(solution)/shard_map/all_to_all | solution.py:565
  322.2 9.7 shard_map.189
  332.0 11.9 %all_to_all.84.att_ref = bf16[4,192,192]{2,1,0:T(8,128)(2,1)} all-to-all(bf16[4,192,192]{2,1,0:T(8,128)(2,1)} %bitcast.237), channel_id=1, replica_groups=mesh['pair'=2,'core'=2,'half'=2,'quad'=2,'side'=2,'rest'=1] {'quad','side'}, dimensions={0} | all-to-all | bytes 589824 | tf_op jit(solution)/shard_map/all_to_all | solution.py:565
  360.1 9.9 shard_map.191
  382.6 17.7 %shard_map.192 = (bf16[1,768,192]{2,1,0:T(8,128)(2,1)}, f32[1,768,384]{2,1,0:T(8,128)}, bf16[1,768,384]{2,1,0:T(8,128)(2,1)}) custom-call(bf16[1,768,576]{2,1,0:T(8,128)(2,1)} %bitcast.225, bf16[1,768,576]{2,1,0:T(8,128)(2,1)} %bitcast.226, bf16[1,768,576]{2,1,0:T(8,128)(2,1)} %bitcast.290, bf16[1,768,192]{2,1,0:T(8,128)(2,1)} %bitcast.233, ...), custom_call_target="tpu_custom_call" | custom-call | flops 9059696640 | bytes 7077888 | tf_op jit(solution)/shard_map/pallas_call | solution.py:240
  400.3 12.9 %collective-permute-start.15 = (bf16[1,768,384]{2,1,0:T(8,128)(2,1)}, bf16[1,768,384]{2,1,0:T(8,128)(2,1)S(1)}, u32[]{:S(2)}, u32[]{:S(2)}) collective-permute-start(bf16[1,768,384]{2,1,0:T(8,128)(2,1)} %get-tuple-element.100), channel_id=1, source_target_pairs={{0,8},{8,0},{1,9},{9,1},{2,10},{10,2},{3,11},{11,3},{4,12},{12,4},... | collective-permute-start | bytes 1769480 | tf_op jit(solution)/shard_map/ppermute | solution.py:556
  418.6 18.9 %all_to_all.85.refs_0_ = bf16[4,192,576]{2,1,0:T(8,128)(2,1)} all-to-all(bf16[4,192,576]{2,1,0:T(8,128)(2,1)} %bitcast.211), channel_id=1, replica_groups=mesh['pair'=2,'core'=2,'half'=2,'quad'=2,'side'=2,'rest'=1] {'quad','side'}, dimensions={0} | all-to-all | bytes 1769472 | tf_op jit(solution)/shard_map/all_to_all | solution.py:565
  442.2 9.9 shard_map.195
  452.2 11.1 %all_to_all.86 = bf16[4,192,192]{2,1,0:T(8,128)(2,1)} all-to-all(bf16[4,192,192]{2,1,0:T(8,128)(2,1)} %get-tuple-element.105), channel_id=1, replica_groups=mesh['pair'=2,'core'=2,'half'=2,'quad'=2,'side'=2,'rest'=1] {'quad','side'}, dimensions={0} | all-to-all | bytes 589824 | tf_op jit(solution)/shard_map/all_to_all | solution.py:565
  463.3 17.9 %shard_map.196 = (bf16[1,768,192]{2,1,0:T(8,128)(2,1)}, f32[1,768,384]{2,1,0:T(8,128)}, bf16[1,768,384]{2,1,0:T(8,128)(2,1)}) custom-call(bf16[1,768,576]{2,1,0:T(8,128)(2,1)} %bitcast.219, bf16[1,768,576]{2,1,0:T(8,128)(2,1)} %bitcast.220, bf16[1,768,576]{2,1,0:T(8,128)(2,1)} %bitcast.287, bf16[1,768,192]{2,1,0:T(8,128)(2,1)} %bitcast.235, ...), custom_call_target="tpu_custom_call" | custom-call | flops 9059696640 | bytes 7077888 | tf_op jit(solution)/shard_map/pallas_call | solution.py:240
  487.0 18.5 %all_to_all.87.refs_0_ = bf16[4,192,576]{2,1,0:T(8,128)(2,1)} all-to-all(bf16[4,192,576]{2,1,0:T(8,128)(2,1)} %bitcast.212), channel_id=1, replica_groups=mesh['pair'=2,'core'=2,'half'=2,'quad'=2,'side'=2,'rest'=1] {'quad','side'}, dimensions={0} | all-to-all | bytes 1769472 | tf_op jit(solution)/shard_map/all_to_all | solution.py:565
  521.3 10.0 shard_map.199
  544.9 17.7 %shard_map.200 = (bf16[1,768,192]{2,1,0:T(8,128)(2,1)}, f32[1,768,384]{2,1,0:T(8,128)}, bf16[1,768,384]{2,1,0:T(8,128)(2,1)}) custom-call(bf16[1,768,576]{2,1,0:T(8,128)(2,1)} %bitcast.227, bf16[1,768,576]{2,1,0:T(8,128)(2,1)} %bitcast.228, bf16[1,768,576]{2,1,0:T(8,128)(2,1)} %bitcast.291, bf16[1,768,192]{2,1,0:T(8,128)(2,1)} %bitcast.35.refs_3_, ...), custom_call_target="tpu_custom_call" | custom-call | flops 9059696640 | bytes 7077888 | tf_op jit(solution)/shard_map/pallas_call | solution.py:240
  603.0 10.0 shard_map.204
  642.6 17.9 %shard_map.207 = (bf16[1,768,192]{2,1,0:T(8,128)(2,1)}, f32[1,768,384]{2,1,0:T(8,128)}, bf16[1,768,384]{2,1,0:T(8,128)(2,1)}) custom-call(bf16[1,768,576]{2,1,0:T(8,128)(2,1)} %bitcast.221, bf16[1,768,576]{2,1,0:T(8,128)(2,1)} %bitcast.222, bf16[1,768,576]{2,1,0:T(8,128)(2,1)} %bitcast.288, bf16[1,768,192]{2,1,0:T(8,128)(2,1)} %bitcast.216, ...), custom_call_target="tpu_custom_call" | custom-call | flops 9059696640 | bytes 7077888 | tf_op jit(solution)/shard_map/pallas_call | solution.py:240
  696.9 26.2 %collective-permute-done.25.two_ref = bf16[272,2304]{1,0:T(8,128)(2,1)} collective-permute-done((bf16[272,2304]{1,0:T(8,128)(2,1)}, bf16[272,2304]{1,0:T(8,128)(2,1)}, u32[]{:S(2)}, u32[]{:S(2)}) %collective-permute-start.25) | collective-permute-done | bytes 1253408 | tf_op jit(solution)/shard_map/ppermute | solution.py:556
  748.6 15.8 %collective-permute-done.32.two_ref = bf16[768,768]{1,0:T(8,128)(2,1)} collective-permute-done((bf16[768,768]{1,0:T(8,128)(2,1)}, bf16[768,768]{1,0:T(8,128)(2,1)}, u32[]{:S(2)}, u32[]{:S(2)}) %collective-permute-start.32) | collective-permute-done | bytes 1179680 | tf_op jit(solution)/shard_map/ppermute | solution.py:556
  771.9 17.9 %collective-permute-done.34.two_ref = bf16[192,3072]{1,0:T(8,128)(2,1)} collective-permute-done((bf16[192,3072]{1,0:T(8,128)(2,1)}, bf16[192,3072]{1,0:T(8,128)(2,1)}, u32[]{:S(2)}, u32[]{:S(2)}) %collective-permute-start.34) | collective-permute-done | bytes 1179680 | tf_op jit(solution)/shard_map/ppermute | solution.py:556
  796.1 27.4 %collective-permute-done.33.two_ref = bf16[768,768]{1,0:T(8,128)(2,1)S(1)} collective-permute-done((bf16[768,768]{1,0:T(8,128)(2,1)}, bf16[768,768]{1,0:T(8,128)(2,1)S(1)}, u32[]{:S(2)}, u32[]{:S(2)}) %collective-permute-start.33) | collective-permute-done | bytes 1179680 | tf_op jit(solution)/shard_map/ppermute | solution.py:725
  839.2 19.6 %collective-permute-done.37.two_ref = bf16[192,3072]{1,0:T(8,128)(2,1)S(1)} collective-permute-done((bf16[192,3072]{1,0:T(8,128)(2,1)}, bf16[192,3072]{1,0:T(8,128)(2,1)S(1)}, u32[]{:S(2)}, u32[]{:S(2)}) %collective-permute-start.37) | collective-permute-done | bytes 1179680 | tf_op jit(solution)/shard_map/ppermute | solution.py:725
  869.2 42.7 %collective-permute-done.35.two_ref = bf16[272,2304]{1,0:T(8,128)(2,1)S(1)} collective-permute-done((bf16[272,2304]{1,0:T(8,128)(2,1)}, bf16[272,2304]{1,0:T(8,128)(2,1)S(1)}, u32[]{:S(2)}, u32[]{:S(2)}) %collective-permute-start.35) | collective-permute-done | bytes 1253408 | tf_op jit(solution)/shard_map/ppermute | solution.py:725
  926.1 28.8 %collective-permute-start.29 = (bf16[192,768]{1,0:T(8,128)(2,1)}, bf16[192,768]{1,0:T(8,128)(2,1)S(1)}, u32[]{:S(2)}, u32[]{:S(2)}) collective-permute-start(bf16[192,768]{1,0:T(8,128)(2,1)} %get-tuple-element.165), channel_id=1, source_target_pairs={{0,4},{4,0},{1,5},{5,1},{2,6},{6,2},{3,7},{7,3},{8,12},{12,8},{9,1... | collective-permute-start | bytes 884744 | tf_op jit(solution)/shard_map/ppermute | solution.py:556
  989.8 18.3 %collective-permute-done.40 = bf16[272,2304]{1,0:T(8,128)(2,1)S(1)} collective-permute-done((bf16[272,2304]{1,0:T(8,128)(2,1)}, bf16[272,2304]{1,0:T(8,128)(2,1)S(1)}, u32[]{:S(2)}, u32[]{:S(2)}) %collective-permute-start.40) | collective-permute-done | bytes 1253408 | tf_op jit(solution)/shard_map/ppermute | solution.py:725
  (502 shorter events, 433.9 us)
Async XLA Ops:
  7.2 66.4 %all-gather.4.cloned.1.call-start = ((), (), s32[]{:S(2)}) async-start(), calls=%async_computation.16 | async-start | bytes 10616832 | tf_op jit(solution)/shard_map/all_gather | solution.py:626
  14.3 158.2 %all-gather.6.cloned.1.call-start = ((), (), s32[]{:S(2)}) async-start(), calls=%async_computation.17 | async-start | bytes 10616832 | tf_op jit(solution)/shard_map/all_gather | solution.py:626
  21.3 59.9 %collective-permute-start.5 = (bf16[1536,768]{1,0:T(8,128)(2,1)S(1)}, bf16[1536,768]{1,0:T(8,128)(2,1)}, u32[]{:S(2)}, u32[]{:S(2)}) collective-permute-start(bf16[1536,768]{1,0:T(8,128)(2,1)S(1)} %bitcast.213), channel_id=1, source_target_pairs={{0,8},{8,0},{1,9},{9,1},{2,10},{10,2},{3,11},{11,3},{4,12},{12,4},... | collective-permute-start | bytes 7077896 | tf_op jit(solution)/shard_map/ppermute | solution.py:556
  77.7 21.6 %all-to-all-start = ((bf16[4,192,576]{2,1,0:T(8,128)(2,1)}), bf16[4,192,576]{2,1,0:T(8,128)(2,1)S(1)}, u32[]{:S(2)}, u32[]{:S(2)}) async-start(bf16[4,192,576]{2,1,0:T(8,128)(2,1)} %get-tuple-element.83), calls=%async_computation | async-start | bytes 1966080 | tf_op jit(solution)/shard_map/all_to_all | solution.py:565
  81.2 138.4 %all-gather.8.cloned.1.call-start = ((), (), s32[]{:S(2)}) async-start(), calls=%async_computation.18 | async-start | bytes 5308416 | tf_op jit(solution)/shard_map/all_gather | solution.py:643
  102.8 41.4 %collective-permute-start.6 = (bf16[768,768]{1,0:T(8,128)(2,1)}, bf16[768,768]{1,0:T(8,128)(2,1)S(1)}, u32[]{:S(2)}, u32[]{:S(2)}) collective-permute-start(bf16[768,768]{1,0:T(8,128)(2,1)} %shard_map.179), channel_id=1, source_target_pairs={{0,1},{1,0},{2,3},{3,2},{4,5},{5,4},{6,7},{7,6},{8,9},{9,8},{10,11... | collective-permute-start | bytes 3538952 | tf_op jit(solution)/shard_map/ppermute | solution.py:556
  355.9 23.9 %collective-permute-start.13 = (bf16[192,768]{1,0:T(8,128)(2,1)S(1)}, bf16[192,768]{1,0:T(8,128)(2,1)S(1)}, u32[]{:S(2)}, u32[]{:S(2)}) collective-permute-start(bf16[192,768]{1,0:T(8,128)(2,1)S(1)} %get-tuple-element.168), channel_id=1, source_target_pairs={{0,4},{4,0},{1,5},{5,1},{2,6},{6,2},{3,7},{7,3},{8,12},{12,8},{9,1... | collective-permute-start | bytes 884744 | tf_op jit(solution)/shard_map/ppermute | solution.py:556
  538.1 51.1 %collective-permute-start.19 = (bf16[1536,768]{1,0:T(8,128)(2,1)}, bf16[1536,768]{1,0:T(8,128)(2,1)S(1)}, u32[]{:S(2)}, u32[]{:S(2)}) collective-permute-start(bf16[1536,768]{1,0:T(8,128)(2,1)} %convolution_convert_fusion.11.refs_5_), channel_id=1, source_target_pairs={{0,8},{8,0},{1,9},{9,1},{2,10},{10,2},{3,11},{11,3},{4,12},{12,4},... | collective-permute-start | bytes 7077896 | tf_op jit(solution)/shard_map/ppermute | solution.py:556
  578.5 53.9 %collective-permute-start.21 = (bf16[384,3072]{1,0:T(8,128)(2,1)}, bf16[384,3072]{1,0:T(8,128)(2,1)}, u32[]{:S(2)}, u32[]{:S(2)}) collective-permute-start(bf16[384,3072]{1,0:T(8,128)(2,1)} %convolution_convert_fusion.7.refs_7_), channel_id=1, source_target_pairs={{0,8},{8,0},{1,9},{9,1},{2,10},{10,2},{3,11},{11,3},{4,12},{12,4},... | collective-permute-start | bytes 7077896 | tf_op jit(solution)/shard_map/ppermute | solution.py:556
  595.4 43.7 %collective-permute-start.20 = (bf16[768,768]{1,0:T(8,128)(2,1)}, bf16[768,768]{1,0:T(8,128)(2,1)}, u32[]{:S(2)}, u32[]{:S(2)}) collective-permute-start(bf16[768,768]{1,0:T(8,128)(2,1)} %get-tuple-element.120.refs_5_), channel_id=1, source_target_pairs={{0,1},{1,0},{2,3},{3,2},{4,5},{5,4},{6,7},{7,6},{8,9},{9,8},{10,11... | collective-permute-start | bytes 3538952 | tf_op jit(solution)/shard_map/ppermute | solution.py:556
  620.0 49.9 %collective-permute-start.24 = (bf16[544,2304]{1,0:T(8,128)(2,1)}, bf16[544,2304]{1,0:T(8,128)(2,1)S(1)}, u32[]{:S(2)}, u32[]{:S(2)}) collective-permute-start(bf16[544,2304]{1,0:T(8,128)(2,1)} %bitcast.44.refs_8_), channel_id=1, source_target_pairs={{0,8},{8,0},{1,9},{9,1},{2,10},{10,2},{3,11},{11,3},{4,12},{12,4},... | collective-permute-start | bytes 7520264 | tf_op jit(solution)/shard_map/ppermute | solution.py:556
  622.3 66.0 %collective-permute-start.26 = (bf16[1536,768]{1,0:T(8,128)(2,1)}, bf16[1536,768]{1,0:T(8,128)(2,1)}, u32[]{:S(2)}, u32[]{:S(2)}) collective-permute-start(bf16[1536,768]{1,0:T(8,128)(2,1)} %convolution_convert_fusion.9.refs_10_), channel_id=1, source_target_pairs={{0,8},{8,0},{1,9},{9,1},{2,10},{10,2},{3,11},{11,3},{4,12},{12,4},... | collective-permute-start | bytes 7077896 | tf_op jit(solution)/shard_map/ppermute | solution.py:556
  625.1 67.8 %collective-permute-start.27 = (bf16[384,3072]{1,0:T(8,128)(2,1)}, bf16[384,3072]{1,0:T(8,128)(2,1)}, u32[]{:S(2)}, u32[]{:S(2)}) collective-permute-start(bf16[384,3072]{1,0:T(8,128)(2,1)} %convolution_convert_fusion.3.refs_12_), channel_id=1, source_target_pairs={{0,8},{8,0},{1,9},{9,1},{2,10},{10,2},{3,11},{11,3},{4,12},{12,4},... | collective-permute-start | bytes 7077896 | tf_op jit(solution)/shard_map/ppermute | solution.py:556
  637.1 28.8 %collective-permute-start.23 = (bf16[192,3072]{1,0:T(8,128)(2,1)}, bf16[192,3072]{1,0:T(8,128)(2,1)S(1)}, u32[]{:S(2)}, u32[]{:S(2)}) collective-permute-start(bf16[192,3072]{1,0:T(8,128)(2,1)} %get-tuple-element.126.refs_6_), channel_id=1, source_target_pairs={{0,1},{1,0},{2,3},{3,2},{4,5},{5,4},{6,7},{7,6},{8,9},{9,8},{10,11... | collective-permute-start | bytes 3538952 | tf_op jit(solution)/shard_map/ppermute | solution.py:556
  679.2 46.8 %all-to-all-start.15 = ((bf16[4,192,576]{2,1,0:T(8,128)(2,1)}), bf16[4,192,576]{2,1,0:T(8,128)(2,1)S(1)}, u32[]{:S(2)}, u32[]{:S(2)}) async-start(bf16[4,192,576]{2,1,0:T(8,128)(2,1)} %bitcast.210), calls=%async_computation.15 | async-start | bytes 1966080 | tf_op jit(solution)/shard_map/all_to_all | solution.py:565
  683.3 39.7 %collective-permute-start.25 = (bf16[272,2304]{1,0:T(8,128)(2,1)}, bf16[272,2304]{1,0:T(8,128)(2,1)}, u32[]{:S(2)}, u32[]{:S(2)}) collective-permute-start(bf16[272,2304]{1,0:T(8,128)(2,1)} %get-tuple-element.139.rest_1_), channel_id=1, source_target_pairs={{0,1},{1,0},{2,3},{3,2},{4,5},{5,4},{6,7},{7,6},{8,9},{9,8},{10,11... | collective-permute-start | bytes 3760136 | tf_op jit(solution)/shard_map/ppermute | solution.py:556
  731.7 223.2 %all-reduce.5.cloned.1.call-start = ((), (), s32[]{:S(2)}) async-start(), calls=%async_computation.19 | async-start | bytes 7225344 | tf_op jit(solution)/shard_map/psum | solution.py:721
  735.4 29.1 %collective-permute-start.32 = (bf16[768,768]{1,0:T(8,128)(2,1)}, bf16[768,768]{1,0:T(8,128)(2,1)}, u32[]{:S(2)}, u32[]{:S(2)}) collective-permute-start(bf16[768,768]{1,0:T(8,128)(2,1)} %get-tuple-element.142.refs_6_), channel_id=1, source_target_pairs={{0,1},{1,0},{2,3},{3,2},{4,5},{5,4},{6,7},{7,6},{8,9},{9,8},{10,11... | collective-permute-start | bytes 3538952 | tf_op jit(solution)/shard_map/ppermute | solution.py:556
  735.7 54.1 %collective-permute-start.34 = (bf16[192,3072]{1,0:T(8,128)(2,1)}, bf16[192,3072]{1,0:T(8,128)(2,1)}, u32[]{:S(2)}, u32[]{:S(2)}) collective-permute-start(bf16[192,3072]{1,0:T(8,128)(2,1)} %get-tuple-element.144.refs_8_), channel_id=1, source_target_pairs={{0,1},{1,0},{2,3},{3,2},{4,5},{5,4},{6,7},{7,6},{8,9},{9,8},{10,11... | collective-permute-start | bytes 3538952 | tf_op jit(solution)/shard_map/ppermute | solution.py:556
  768.1 55.5 %collective-permute-start.33 = (bf16[768,768]{1,0:T(8,128)(2,1)}, bf16[768,768]{1,0:T(8,128)(2,1)S(1)}, u32[]{:S(2)}, u32[]{:S(2)}) collective-permute-start(bf16[768,768]{1,0:T(8,128)(2,1)} %shard_map.216.rest_0_.one_ref), channel_id=1, source_target_pairs={{0,2},{6,4},{1,3},{7,5},{8,10},{14,12},{9,11},{15,13},{16,18},{22,... | collective-permute-start | bytes 3538952 | tf_op jit(solution)/shard_map/ppermute | solution.py:725
  771.5 57.3 %collective-permute-start.31 = (bf16[272,2304]{1,0:T(8,128)(2,1)S(1)}, bf16[272,2304]{1,0:T(8,128)(2,1)S(1)}, u32[]{:S(2)}, u32[]{:S(2)}) collective-permute-start(bf16[272,2304]{1,0:T(8,128)(2,1)S(1)} %copy-done.2), channel_id=1, source_target_pairs={{0,1},{1,0},{2,3},{3,2},{4,5},{5,4},{6,7},{7,6},{8,9},{9,8},{10,11... | collective-permute-start | bytes 3760136 | tf_op jit(solution)/shard_map/ppermute | solution.py:556
  792.7 66.1 %collective-permute-start.37 = (bf16[192,3072]{1,0:T(8,128)(2,1)}, bf16[192,3072]{1,0:T(8,128)(2,1)S(1)}, u32[]{:S(2)}, u32[]{:S(2)}) collective-permute-start(bf16[192,3072]{1,0:T(8,128)(2,1)} %shard_map.217.rest_0_.one_ref), channel_id=1, source_target_pairs={{0,2},{6,4},{1,3},{7,5},{8,10},{14,12},{9,11},{15,13},{16,18},{22,... | collective-permute-start | bytes 3538952 | tf_op jit(solution)/shard_map/ppermute | solution.py:725
  828.1 35.3 %collective-permute-start.36 = (bf16[768,768]{1,0:T(8,128)(2,1)}, bf16[768,768]{1,0:T(8,128)(2,1)S(1)}, u32[]{:S(2)}, u32[]{:S(2)}) collective-permute-start(bf16[768,768]{1,0:T(8,128)(2,1)} %shard_map.218.rest_0_.one_ref), channel_id=1, source_target_pairs={{2,4},{4,2},{3,5},{5,3},{10,12},{12,10},{11,13},{13,11},{18,20},{2... | collective-permute-start | bytes 3538952 | tf_op jit(solution)/shard_map/ppermute | solution.py:725
  832.9 79.0 %collective-permute-start.35 = (bf16[272,2304]{1,0:T(8,128)(2,1)}, bf16[272,2304]{1,0:T(8,128)(2,1)S(1)}, u32[]{:S(2)}, u32[]{:S(2)}) collective-permute-start(bf16[272,2304]{1,0:T(8,128)(2,1)} %shard_map.219.rest_0_.one_ref), channel_id=1, source_target_pairs={{0,2},{6,4},{1,3},{7,5},{8,10},{14,12},{9,11},{15,13},{16,18},{22,... | collective-permute-start | bytes 3760136 | tf_op jit(solution)/shard_map/ppermute | solution.py:725
  862.7 54.2 %collective-permute-start.39 = (bf16[192,3072]{1,0:T(8,128)(2,1)}, bf16[192,3072]{1,0:T(8,128)(2,1)S(1)}, u32[]{:S(2)}, u32[]{:S(2)}) collective-permute-start(bf16[192,3072]{1,0:T(8,128)(2,1)} %shard_map.220.rest_0_.one_ref), channel_id=1, source_target_pairs={{2,4},{4,2},{3,5},{5,3},{10,12},{12,10},{11,13},{13,11},{18,20},{2... | collective-permute-start | bytes 3538952 | tf_op jit(solution)/shard_map/ppermute | solution.py:725
  867.9 87.0 %collective-permute-start.44 = (bf16[768,768]{1,0:T(8,128)(2,1)}, bf16[768,768]{1,0:T(8,128)(2,1)}, u32[]{:S(2)}, u32[]{:S(2)}) collective-permute-start(bf16[768,768]{1,0:T(8,128)(2,1)} %shard_map.221.rest_0_), channel_id=1, source_target_pairs={{2,0},{4,6},{3,1},{5,7},{10,8},{12,14},{11,9},{13,15},{18,16},{20,... | collective-permute-start | bytes 3538952 | tf_op jit(solution)/shard_map/ppermute | solution.py:725
  916.0 41.7 %collective-permute-start.38 = (bf16[272,2304]{1,0:T(8,128)(2,1)}, bf16[272,2304]{1,0:T(8,128)(2,1)S(1)}, u32[]{:S(2)}, u32[]{:S(2)}) collective-permute-start(bf16[272,2304]{1,0:T(8,128)(2,1)} %shard_map.222.rest_0_.one_ref), channel_id=1, source_target_pairs={{2,4},{4,2},{3,5},{5,3},{10,12},{12,10},{11,13},{13,11},{18,20},{2... | collective-permute-start | bytes 3760136 | tf_op jit(solution)/shard_map/ppermute | solution.py:725
  920.8 50.9 %collective-permute-start.42 = (bf16[192,3072]{1,0:T(8,128)(2,1)}, bf16[192,3072]{1,0:T(8,128)(2,1)}, u32[]{:S(2)}, u32[]{:S(2)}) collective-permute-start(bf16[192,3072]{1,0:T(8,128)(2,1)} %shard_map.223.rest_0_), channel_id=1, source_target_pairs={{2,0},{4,6},{3,1},{5,7},{10,8},{12,14},{11,9},{13,15},{18,16},{20,... | collective-permute-start | bytes 3538952 | tf_op jit(solution)/shard_map/ppermute | solution.py:725
  926.1 55.3 %collective-permute-start.29 = (bf16[192,768]{1,0:T(8,128)(2,1)}, bf16[192,768]{1,0:T(8,128)(2,1)S(1)}, u32[]{:S(2)}, u32[]{:S(2)}) collective-permute-start(bf16[192,768]{1,0:T(8,128)(2,1)} %get-tuple-element.165), channel_id=1, source_target_pairs={{0,4},{4,0},{1,5},{5,1},{2,6},{6,2},{3,7},{7,3},{8,12},{12,8},{9,1... | collective-permute-start | bytes 884744 | tf_op jit(solution)/shard_map/ppermute | solution.py:556
  957.7 28.0 %collective-permute-start.45 = (bf16[768,768]{1,0:T(8,128)(2,1)}, bf16[768,768]{1,0:T(8,128)(2,1)}, u32[]{:S(2)}, u32[]{:S(2)}) collective-permute-start(bf16[768,768]{1,0:T(8,128)(2,1)} %get-tuple-element.159), channel_id=1, source_target_pairs={{0,8},{8,0},{1,9},{9,1},{2,10},{10,2},{3,11},{11,3},{4,12},{12,4},... | collective-permute-start | bytes 3538952 | tf_op jit(solution)/shard_map/ppermute | solution.py:556
  961.9 46.2 %collective-permute-start.40 = (bf16[272,2304]{1,0:T(8,128)(2,1)}, bf16[272,2304]{1,0:T(8,128)(2,1)S(1)}, u32[]{:S(2)}, u32[]{:S(2)}) collective-permute-start(bf16[272,2304]{1,0:T(8,128)(2,1)} %shard_map.224.rest_0_), channel_id=1, source_target_pairs={{2,0},{4,6},{3,1},{5,7},{10,8},{12,14},{11,9},{13,15},{18,16},{20,... | collective-permute-start | bytes 3760136 | tf_op jit(solution)/shard_map/ppermute | solution.py:725
  973.2 35.2 %collective-permute-start.43 = (bf16[192,3072]{1,0:T(8,128)(2,1)S(1)}, bf16[192,3072]{1,0:T(8,128)(2,1)S(1)}, u32[]{:S(2)}, u32[]{:S(2)}) collective-permute-start(bf16[192,3072]{1,0:T(8,128)(2,1)S(1)} %get-tuple-element.161), channel_id=1, source_target_pairs={{0,8},{8,0},{1,9},{9,1},{2,10},{10,2},{3,11},{11,3},{4,12},{12,4},... | collective-permute-start | bytes 3538952 | tf_op jit(solution)/shard_map/ppermute | solution.py:556
  (134 other events, 894.6 us)
Sparse Core Ops, SparseCore 0:
  14.5 59.0 all-gather.3
  75.7 83.4 all-gather.5
  161.4 50.4 all-gather.7
  738.7 198.6 all-reduce.4

commit v7 on v6

--- a/solution.py
+++ b/solution.py
@@ -632,7 +632,7 @@
     return pick(second, other, mine), pick(second, mine, other)
 
 
-def start_downs(block, after):
+def start_downs(block):
     if lax.axis_size("rest") > 1 or lax.axis_size("quad") != 2:
         first, second = gather_weight(block)
         return None, first, second
@@ -642,14 +642,13 @@
     line = lax.dynamic_slice_in_dim(other, (core * 2 + quad) * part, part, 0)
     second = lax.all_gather(line, ("side", "rest", "core", "quad"), axis=0, tiled=True)
     near = lax.dynamic_slice_in_dim(mine, core * 2 * part, 2 * part, 0)
-    return swap(copy_after(near, after), "side"), mine, second
-
-
-def finish_down(near, mine, after):
+    return swap(near, "side"), mine, second
+
+
+def finish_down(near, mine):
     if near is None:
         return mine
     core, side = lax.axis_index("core"), lax.axis_index("side")
-    near = copy_after(near, after)
     other = jnp.concatenate(in_order(core == 1, near, swap(near, "core")), axis=0)
     return jnp.concatenate(in_order(side == 1, mine, other), axis=0)
 
@@ -725,25 +724,24 @@
     return lax.ppermute(block, ("half", "quad"), pairs)
 
 
-def line_sums(sides, last):
+def line_sums(sides, ties):
     inward, across, outward = [(0, 1), (3, 2)], [(1, 2), (2, 1)], [(1, 0), (2, 3)]
     inner = lax.axis_index("half") != lax.axis_index("quad")
     count = len(sides)
     totals, mark = [None] * count, ()
     results = []
     for turn in range(count + 2):
+        mark = (*mark, *ties.get(turn, ()))
         if turn < count:
             totals[turn] = sides[turn](*mark)
             mark = (totals[turn],)
         for hops, at in ((inward, turn - 1), (across, turn - 2)):
             if 0 <= at < count:
-                if turn == count + 1:
-                    mark = (*mark, *last)
                 totals[at] = add_after(totals[at], line_hop(totals[at], hops), mark)
                 mark = (totals[at],)
                 if hops is across:
                     results.append(pick(inner, totals[at], line_hop(totals[at], outward)))
-    return results, mark[0]
+    return results
 
 
 def join_cores(first, second):
@@ -763,16 +761,17 @@
     return pick(core == half, own, came)
 
 
-def swap_out(first, second, micro, *after):
-    rows, wide = first.shape
+def start_out(first, second):
     second_core, second_half = lax.axis_index("core") == 1, lax.axis_index("half") == 1
     mine, sent = in_order(second_core, first, second)
     parts = in_order(second_core, mine, swap(sent, "core"))
     mine, sent = in_order(second_half, *parts)
-    came = swap(sent, "half")
-    if after:
-        came = copy_after(came, after)
-    clips = in_order(second_half, mine, came)
+    return mine, swap(sent, "half")
+
+
+def finish_out(mine, came, micro):
+    rows, wide = mine.shape
+    clips = in_order(lax.axis_index("half") == 1, mine, came)
     return jnp.stack(clips).reshape(micro, 2 * rows // micro, wide)
 
 
@@ -784,7 +783,7 @@
     other = other_keys(grouped, own, clips)
     att, log_total = attend_forward(own, other, head)
     if callable(w_down):
-        w_down = w_down(log_total)
+        w_down = w_down()
         weights = (joined, w_down, *weights[2:])
     att = spread(to_tokens(att))
     y, *kept = feed_forward(
@@ -887,26 +886,33 @@
     rest = side_parts(*rest, grads[0])
     up_two = side_sum(*up, grads[0])
     d_tokens = spread_grads(grads, (up_two, *rest))
-    rest_two = side_sum(*rest)
     down_one, up_one = side_parts(*down_one), side_parts(*up_one)
     out_one = weight_halves(att, branch)
     d_first, flat, sums_one = qkv_backward(
-        d_tokens, joined, x, dx1, gains[0:1], (rest_two, *down_one, *up_one, *out_one)
-    )
-    seconds = line_sum(rest_two, up_two, down_two)
-    rest_one = rest_halves(normed_one, flat, out_one, sums_one, sums_two, up_sum, shards)
-    rest_one = side_parts(*rest_one)
+        d_tokens, joined, x, dx1, gains[0:1], (*down_one, *up_one, *out_one)
+    )
+    placed = start_out(d_first, d_second)
+    halves = rest_halves(normed_one, flat, out_one, sums_one, sums_two, up_sum, shards)
+    rest_one = side_parts(*halves)
+    blocks = (
+        (rest, halves[0]),
+        (down_one, rest_one[0]),
+        (up_one, rest_one[0]),
+        (rest_one, placed[1]),
+    )
     sides = [
-        lambda *after, item=item: side_sum(*item, *after, rest_one[0])
-        for item in (down_one, up_one, rest_one)
+        lambda *after, item=item, mark=mark: side_sum(*item, *after, mark)
+        for item, mark in blocks
     ]
+    up_two, down_two = line_sum(up_two, down_two)
     if lax.axis_size("quad") == 2:
-        firsts, mark = line_sums(sides, seconds)
+        sums = line_sums(sides, {1: (up_two, down_two)})
     else:
-        firsts = line_sum(*(item() for item in sides))
-        mark = firsts[2]
-    firsts = (firsts[2], firsts[1], firsts[0])
-    return d_first, d_second, mark, [join_cores(a, b) for a, b in zip(firsts, seconds)]
+        sums = line_sum(*(item() for item in sides))
+    rest_two, down_one, up_one, rest_one = sums
+    firsts = (rest_one, up_one, down_one)
+    seconds = (rest_two, up_two, down_two)
+    return placed, [join_cores(a, b) for a, b in zip(firsts, seconds)]
 
 
 def gather_small(block):
@@ -932,8 +938,8 @@
     part = width // shards
 
     joined = gather_weight(w_qkv[0], w_out[0], w_up[0])
-    near, mine, second_down = start_downs(w_down[0], joined[:1])
-    downs = [lambda *after: finish_down(near, mine, after), lambda *after: second_down]
+    near, mine, second_down = start_downs(w_down[0])
+    downs = [lambda: finish_down(near, mine), lambda: second_down]
     small = jnp.concatenate(
         [norm_gain.reshape(-1), norm_bias.reshape(-1), proj_bias.reshape(-1), up_bias.reshape(-1)]
     )
@@ -950,7 +956,7 @@
             (joined[layer], downs[layer], r[0:2], r[2:4], b_qkv, r[6:7], r[7:8], ups[layer])
         )
 
-    x = x_start
+    x = x_start if near is None else copy_after(x_start, (near,))
     for phase in range(pairs):
         if phase > 0:
             came = lax.ppermute(second, "pair", [(i, i + 1) for i in range(pairs - 1)])
@@ -958,7 +964,7 @@
         keep = phase == pairs - 1
         first, kept_first, layers[0] = forward_layer(x, layers[0], clips, head, keep)
         second, kept_second, layers[1] = forward_layer(first, layers[1], clips, head, keep)
-    hidden = swap_out(first, second, micro)
+    hidden = finish_out(*start_out(first, second), micro)
 
     g_start = swap_in(out_grad)
     g = g_start
@@ -967,10 +973,10 @@
         d_first = backward_lean(kept_first, d_second, layers[0], clips, head)
         came = lax.ppermute(d_first, "pair", [(i + 1, i) for i in range(pairs - 1)])
         g = pick(pair == pairs - 1, g_start, came)
-    d_first, d_second, mark, (rest, up, down) = backward_all(
+    placed, (rest, up, down) = backward_all(
         kept_first, kept_second, g, layers, clips, head, shards
     )
-    input_grads = swap_out(d_first, d_second, micro, mark)
+    input_grads = finish_out(*placed, micro)
 
     own_rows = part // 2
     rest = rest.reshape(2, -1, 3 * width)

time: 1040 us -> 1040 us (level)
  waiting for transfers between devices: 325 us -> 340 us
  starting transfers between devices: 121 us -> 107 us
    psum x1, waiting for transfers between devices: 0.01 us -> 51.9 us  [line_sum(): return lax.psum(items, ('half', 'quad'))]
    ppermute x33, starting transfers between devices: 64.5 us -> 39.4 us  [swap(): return lax.ppermute(block, axis, [(0, 1), (1, 0)])]
    ppermute x9 -> x12, waiting for transfers between devices: 116 us -> 92.6 us  [line_hop(): return lax.ppermute(block, ('half', 'quad'), pairs)]
    all_gather x2, waiting for transfers between devices: 43 us -> 25 us  [gather_weight(): lax.all_gather(item, ('side', 'rest', 'core', 'quad'), axis=0, tiled=True)]
    ppermute x9 -> x12, starting transfers between devices: 19.6 us -> 25.9 us  [line_hop(): return lax.ppermute(block, ('half', 'quad'), pairs)]
    pallas_call x12 -> x14, Pallas kernels: 38 us -> 43.7 us  [add_after(): call(add_body, jax.ShapeDtypeStruct((rows, wide), BF16), grid=(rows // bl...]
    unnamed x239 -> x241, local copies, waits for them, and re-layouts: 37.5 us -> 39.1 us
  transfers between devices with their start and end apart: 58 -> 61, of which waited for: 29 -> 31; matrix products, arithmetic and copies ran while one was open for 9% -> 9% of each run, Pallas kernels for 17% -> 17%
where the time goes in v7:
time: 1040 us; the launch traced here: 1030 us
  waiting for transfers between devices  340 us (33%)
  Pallas kernels  302 us (29%)
  blocking collectives  129 us (12%)
  starting transfers between devices  107 us (10%)
  local copies, waits for them, and re-layouts  60.3 us (6%)
  other arithmetic  48.7 us (5%)
  matrix products  26.4 us (3%)
  between operations  15.6 us (2%)
    ppermute x33, waiting for transfers between devices, swap(): return lax.ppermute(block, axis, [(0, 1), (1, 0)])  133 us
    all_to_all x8, blocking collectives, spread(): return lax.all_to_all(block, ('quad', 'side'), 0, 0, tiled=True)  129 us
    ppermute x12, waiting for transfers between devices, line_hop(): return lax.ppermute(block, ('half', 'quad'), pairs)  92.6 us
    pallas_call x4, Pallas kernels, attend_backward(): call(body, (jax.ShapeDtypeStruct((clips, queries, span), BF16), jax.Shape...  71 us
    psum x1, waiting for transfers between devices, line_sum(): return lax.psum(items, ('half', 'quad'))  51.9 us
    pallas_call x14, Pallas kernels, add_after(): call(add_body, jax.ShapeDtypeStruct((rows, wide), BF16), grid=(rows // bl...  43.7 us
    pallas_call x4, Pallas kernels, feed_backward(): call(feed_back_body, (jax.ShapeDtypeStruct((rows, hidden), BF16), jax.Sha...  40 us
    ppermute x33, starting transfers between devices, swap(): return lax.ppermute(block, axis, [(0, 1), (1, 0)])  39.4 us
  transfers between devices with their start and end apart: 61, of which 31 were waited for; matrix products, arithmetic and copies ran while one was open for 9% of the time, Pallas kernels for 17%

profile of v7, /device:TPU:0, one launch (start us, length us, event | category | flops | bytes accessed | tf_op | source)
XLA Modules:
  0.0 1028.8 jit_solution(4832086973559181042)
XLA Ops:
  33.4 34.4 %collective-permute-done.2.rest_0_ = bf16[768,768]{1,0:T(8,128)(2,1)S(1)} collective-permute-done((bf16[768,768]{1,0:T(8,128)(2,1)S(1)}, bf16[768,768]{1,0:T(8,128)(2,1)S(1)}, u32[]{:S(2)}, u32[]{:S(2)}) %collective-permute-start.2) | collective-permute-done | bytes 1179680 | tf_op jit(solution)/shard_map/ppermute | solution.py:556
  70.5 20.3 %all-gather.4.cloned.1.call-done.w_ref.w_out_ref.w_up_ref.refs_1_ = bf16[768,6144]{1,0:T(8,128)(2,1)} async-done(((bf16[96,6144]{1,0:T(8,128)(2,1)}), bf16[768,6144]{1,0:T(8,128)(2,1)}) %all-gather.4.cloned.1.call-update) | async-done | bytes 9437200 | tf_op jit(solution)/shard_map/all_gather | solution.py:626
  111.4 11.7 %all-to-all-done = bf16[4,192,576]{2,1,0:T(8,128)(2,1)} async-done(((bf16[4,192,576]{2,1,0:T(8,128)(2,1)}), bf16[4,192,576]{2,1,0:T(8,128)(2,1)}, u32[]{:S(2)}, u32[]{:S(2)}) %all-to-all-start) | async-done | bytes 884768 | tf_op jit(solution)/shard_map/all_to_all | solution.py:565
  128.6 10.0 shard_map.179
  169.4 23.1 %all_to_all.80 = bf16[4,192,576]{2,1,0:T(8,128)(2,1)S(1)} all-to-all(bf16[4,192,576]{2,1,0:T(8,128)(2,1)} %get-tuple-element.84), channel_id=1, replica_groups=mesh['pair'=2,'core'=2,'half'=2,'quad'=2,'side'=2,'rest'=1] {'quad','side'}, dimensions={0} | all-to-all | bytes 1769472 | tf_op jit(solution)/shard_map/all_to_all | solution.py:565
  196.0 9.8 shard_map.182
  239.4 16.4 %all_to_all.81 = bf16[4,192,576]{2,1,0:T(8,128)(2,1)S(1)} all-to-all(bf16[4,192,576]{2,1,0:T(8,128)(2,1)} %get-tuple-element.86), channel_id=1, replica_groups=mesh['pair'=2,'core'=2,'half'=2,'quad'=2,'side'=2,'rest'=1] {'quad','side'}, dimensions={0} | all-to-all | bytes 1769472 | tf_op jit(solution)/shard_map/all_to_all | solution.py:565
  259.3 9.8 shard_map.185
  269.1 11.9 %all_to_all.82.att_ref = bf16[4,192,192]{2,1,0:T(8,128)(2,1)} all-to-all(bf16[4,192,192]{2,1,0:T(8,128)(2,1)} %bitcast.235), channel_id=1, replica_groups=mesh['pair'=2,'core'=2,'half'=2,'quad'=2,'side'=2,'rest'=1] {'quad','side'}, dimensions={0} | all-to-all | bytes 589824 | tf_op jit(solution)/shard_map/all_to_all | solution.py:565
  294.3 16.9 %all_to_all.83 = bf16[4,192,576]{2,1,0:T(8,128)(2,1)S(1)} all-to-all(bf16[4,192,576]{2,1,0:T(8,128)(2,1)} %get-tuple-element.89), channel_id=1, replica_groups=mesh['pair'=2,'core'=2,'half'=2,'quad'=2,'side'=2,'rest'=1] {'quad','side'}, dimensions={0} | all-to-all | bytes 1769472 | tf_op jit(solution)/shard_map/all_to_all | solution.py:565
  314.7 9.7 shard_map.188
  324.5 11.9 %all_to_all.84.att_ref = bf16[4,192,192]{2,1,0:T(8,128)(2,1)} all-to-all(bf16[4,192,192]{2,1,0:T(8,128)(2,1)} %bitcast.236), channel_id=1, replica_groups=mesh['pair'=2,'core'=2,'half'=2,'quad'=2,'side'=2,'rest'=1] {'quad','side'}, dimensions={0} | all-to-all | bytes 589824 | tf_op jit(solution)/shard_map/all_to_all | solution.py:565
  352.7 9.9 shard_map.190
  375.1 17.7 %shard_map.191 = (bf16[1,768,192]{2,1,0:T(8,128)(2,1)}, f32[1,768,384]{2,1,0:T(8,128)}, bf16[1,768,384]{2,1,0:T(8,128)(2,1)}) custom-call(bf16[1,768,576]{2,1,0:T(8,128)(2,1)} %bitcast.225, bf16[1,768,576]{2,1,0:T(8,128)(2,1)} %bitcast.226, bf16[1,768,576]{2,1,0:T(8,128)(2,1)} %bitcast.289, bf16[1,768,192]{2,1,0:T(8,128)(2,1)} %bitcast.231, ...), custom_call_target="tpu_custom_call" | custom-call | flops 9059696640 | bytes 7077888 | tf_op jit(solution)/shard_map/pallas_call | solution.py:240
  392.8 12.9 %collective-permute-start.15 = (bf16[1,768,384]{2,1,0:T(8,128)(2,1)}, bf16[1,768,384]{2,1,0:T(8,128)(2,1)S(1)}, u32[]{:S(2)}, u32[]{:S(2)}) collective-permute-start(bf16[1,768,384]{2,1,0:T(8,128)(2,1)} %get-tuple-element.98), channel_id=1, source_target_pairs={{0,8},{8,0},{1,9},{9,1},{2,10},{10,2},{3,11},{11,3},{4,12},{12,4},... | collective-permute-start | bytes 1769480 | tf_op jit(solution)/shard_map/ppermute | solution.py:556
  411.1 18.9 %all_to_all.85.refs_0_ = bf16[4,192,576]{2,1,0:T(8,128)(2,1)} all-to-all(bf16[4,192,576]{2,1,0:T(8,128)(2,1)} %bitcast.211), channel_id=1, replica_groups=mesh['pair'=2,'core'=2,'half'=2,'quad'=2,'side'=2,'rest'=1] {'quad','side'}, dimensions={0} | all-to-all | bytes 1769472 | tf_op jit(solution)/shard_map/all_to_all | solution.py:565
  434.7 10.0 shard_map.194
  444.7 11.1 %all_to_all.86 = bf16[4,192,192]{2,1,0:T(8,128)(2,1)} all-to-all(bf16[4,192,192]{2,1,0:T(8,128)(2,1)} %get-tuple-element.103), channel_id=1, replica_groups=mesh['pair'=2,'core'=2,'half'=2,'quad'=2,'side'=2,'rest'=1] {'quad','side'}, dimensions={0} | all-to-all | bytes 589824 | tf_op jit(solution)/shard_map/all_to_all | solution.py:565
  455.9 17.7 %shard_map.195 = (bf16[1,768,192]{2,1,0:T(8,128)(2,1)}, f32[1,768,384]{2,1,0:T(8,128)}, bf16[1,768,384]{2,1,0:T(8,128)(2,1)}) custom-call(bf16[1,768,576]{2,1,0:T(8,128)(2,1)} %bitcast.219, bf16[1,768,576]{2,1,0:T(8,128)(2,1)} %bitcast.220, bf16[1,768,576]{2,1,0:T(8,128)(2,1)} %bitcast.286, bf16[1,768,192]{2,1,0:T(8,128)(2,1)} %bitcast.234, ...), custom_call_target="tpu_custom_call" | custom-call | flops 9059696640 | bytes 7077888 | tf_op jit(solution)/shard_map/pallas_call | solution.py:240
  479.4 18.5 %all_to_all.87.refs_0_ = bf16[4,192,576]{2,1,0:T(8,128)(2,1)} all-to-all(bf16[4,192,576]{2,1,0:T(8,128)(2,1)} %bitcast.212), channel_id=1, replica_groups=mesh['pair'=2,'core'=2,'half'=2,'quad'=2,'side'=2,'rest'=1] {'quad','side'}, dimensions={0} | all-to-all | bytes 1769472 | tf_op jit(solution)/shard_map/all_to_all | solution.py:565
  513.7 10.0 shard_map.198
  537.4 17.7 %shard_map.199 = (bf16[1,768,192]{2,1,0:T(8,128)(2,1)}, f32[1,768,384]{2,1,0:T(8,128)}, bf16[1,768,384]{2,1,0:T(8,128)(2,1)}) custom-call(bf16[1,768,576]{2,1,0:T(8,128)(2,1)} %bitcast.227, bf16[1,768,576]{2,1,0:T(8,128)(2,1)} %bitcast.228, bf16[1,768,576]{2,1,0:T(8,128)(2,1)} %bitcast.290, bf16[1,768,192]{2,1,0:T(8,128)(2,1)} %bitcast.35.refs_3_, ...), custom_call_target="tpu_custom_call" | custom-call | flops 9059696640 | bytes 7077888 | tf_op jit(solution)/shard_map/pallas_call | solution.py:240
  595.3 10.1 shard_map.203
  635.0 17.9 %shard_map.206 = (bf16[1,768,192]{2,1,0:T(8,128)(2,1)}, f32[1,768,384]{2,1,0:T(8,128)}, bf16[1,768,384]{2,1,0:T(8,128)(2,1)}) custom-call(bf16[1,768,576]{2,1,0:T(8,128)(2,1)} %bitcast.221, bf16[1,768,576]{2,1,0:T(8,128)(2,1)} %bitcast.222, bf16[1,768,576]{2,1,0:T(8,128)(2,1)} %bitcast.287, bf16[1,768,192]{2,1,0:T(8,128)(2,1)} %bitcast.216, ...), custom_call_target="tpu_custom_call" | custom-call | flops 9059696640 | bytes 7077888 | tf_op jit(solution)/shard_map/pallas_call | solution.py:240
  700.9 27.5 %collective-permute-done.31.two_ref = bf16[272,2304]{1,0:T(8,128)(2,1)} collective-permute-done((bf16[272,2304]{1,0:T(8,128)(2,1)}, bf16[272,2304]{1,0:T(8,128)(2,1)}, u32[]{:S(2)}, u32[]{:S(2)}) %collective-permute-start.31) | collective-permute-done | bytes 1253408 | tf_op jit(solution)/shard_map/ppermute | solution.py:556
  753.7 51.9 %all-reduce.5.cloned.1.call-done = (bf16[192,3072]{1,0:T(8,128)(2,1)}, bf16[768,768]{1,0:T(8,128)(2,1)}) async-done(((bf16[192,3072]{1,0:T(8,128)(2,1)}, bf16[768,768]{1,0:T(8,128)(2,1)}), (bf16[192,3072]{1,0:T(8,128)(2,1)}, bf16[768,768]{1,0:T(8,128)(2,1)})) %all-reduce.5.cloned.1.call-update) | async-done | bytes 2359312 | tf_op jit(solution)/shard_map/psum | solution.py:720
  827.7 13.5 %collective-permute-done.35.two_ref = bf16[768,768]{1,0:T(8,128)(2,1)S(1)} collective-permute-done((bf16[768,768]{1,0:T(8,128)(2,1)}, bf16[768,768]{1,0:T(8,128)(2,1)S(1)}, u32[]{:S(2)}, u32[]{:S(2)}) %collective-permute-start.35) | collective-permute-done | bytes 1179680 | tf_op jit(solution)/shard_map/ppermute | solution.py:724
  856.4 32.4 %collective-permute-done.28.rest_1_ = bf16[192,768]{1,0:T(8,128)(2,1)S(1)} collective-permute-done((bf16[192,768]{1,0:T(8,128)(2,1)S(1)}, bf16[192,768]{1,0:T(8,128)(2,1)S(1)}, u32[]{:S(2)}, u32[]{:S(2)}) %collective-permute-start.28) | collective-permute-done | bytes 294944 | tf_op jit(solution)/shard_map/ppermute | solution.py:556
  905.4 14.0 %collective-permute-done.37.two_ref = bf16[272,2304]{1,0:T(8,128)(2,1)S(1)} collective-permute-done((bf16[272,2304]{1,0:T(8,128)(2,1)}, bf16[272,2304]{1,0:T(8,128)(2,1)S(1)}, u32[]{:S(2)}, u32[]{:S(2)}) %collective-permute-start.37) | collective-permute-done | bytes 1253408 | tf_op jit(solution)/shard_map/ppermute | solution.py:724
  940.9 20.8 %collective-permute-done.45 = bf16[192,3072]{1,0:T(8,128)(2,1)} collective-permute-done((bf16[192,3072]{1,0:T(8,128)(2,1)}, bf16[192,3072]{1,0:T(8,128)(2,1)}, u32[]{:S(2)}, u32[]{:S(2)}) %collective-permute-start.45) | collective-permute-done | bytes 1179680 | tf_op jit(solution)/shard_map/ppermute | solution.py:724
  967.3 21.3 %collective-permute-done.43 = bf16[272,2304]{1,0:T(8,128)(2,1)} collective-permute-done((bf16[272,2304]{1,0:T(8,128)(2,1)S(1)}, bf16[272,2304]{1,0:T(8,128)(2,1)}, u32[]{:S(2)}, u32[]{:S(2)}) %collective-permute-start.43) | collective-permute-done | bytes 1253408 | tf_op jit(solution)/shard_map/ppermute | solution.py:724
  988.6 22.5 %collective-permute-done.42 = bf16[272,2304]{1,0:T(8,128)(2,1)S(1)} collective-permute-done((bf16[272,2304]{1,0:T(8,128)(2,1)}, bf16[272,2304]{1,0:T(8,128)(2,1)S(1)}, u32[]{:S(2)}, u32[]{:S(2)}) %collective-permute-start.42) | collective-permute-done | bytes 1253408 | tf_op jit(solution)/shard_map/ppermute | solution.py:724
  (510 shorter events, 451.3 us)
Async XLA Ops:
  7.2 83.6 %all-gather.4.cloned.1.call-start = ((), (), s32[]{:S(2)}) async-start(), calls=%async_computation.16 | async-start | bytes 10616832 | tf_op jit(solution)/shard_map/all_gather | solution.py:626
  14.3 151.0 %all-gather.6.cloned.1.call-start = ((), (), s32[]{:S(2)}) async-start(), calls=%async_computation.17 | async-start | bytes 10616832 | tf_op jit(solution)/shard_map/all_gather | solution.py:626
  15.1 197.2 %all-gather.8.cloned.1.call-start = ((), (), s32[]{:S(2)}) async-start(), calls=%async_computation.18 | async-start | bytes 5308416 | tf_op jit(solution)/shard_map/all_gather | solution.py:643
  27.9 39.8 %collective-permute-start.2 = (bf16[768,768]{1,0:T(8,128)(2,1)S(1)}, bf16[768,768]{1,0:T(8,128)(2,1)S(1)}, u32[]{:S(2)}, u32[]{:S(2)}) collective-permute-start(bf16[768,768]{1,0:T(8,128)(2,1)S(1)} %constant_dynamic-slice_fusion.32), channel_id=1, source_target_pairs={{0,1},{1,0},{2,3},{3,2},{4,5},{5,4},{6,7},{7,6},{8,9},{9,8},{10,11... | collective-permute-start | bytes 3538952 | tf_op jit(solution)/shard_map/ppermute | solution.py:556
  94.9 28.2 %all-to-all-start = ((bf16[4,192,576]{2,1,0:T(8,128)(2,1)}), bf16[4,192,576]{2,1,0:T(8,128)(2,1)}, u32[]{:S(2)}, u32[]{:S(2)}) async-start(bf16[4,192,576]{2,1,0:T(8,128)(2,1)} %get-tuple-element.82), calls=%async_computation | async-start | bytes 1966080 | tf_op jit(solution)/shard_map/all_to_all | solution.py:565
  530.6 51.0 %collective-permute-start.19 = (bf16[1536,768]{1,0:T(8,128)(2,1)}, bf16[1536,768]{1,0:T(8,128)(2,1)S(1)}, u32[]{:S(2)}, u32[]{:S(2)}) collective-permute-start(bf16[1536,768]{1,0:T(8,128)(2,1)} %convolution_convert_fusion.11.refs_5_), channel_id=1, source_target_pairs={{0,8},{8,0},{1,9},{9,1},{2,10},{10,2},{3,11},{11,3},{4,12},{12,4},... | collective-permute-start | bytes 7077896 | tf_op jit(solution)/shard_map/ppermute | solution.py:556
  570.8 53.9 %collective-permute-start.21 = (bf16[384,3072]{1,0:T(8,128)(2,1)}, bf16[384,3072]{1,0:T(8,128)(2,1)}, u32[]{:S(2)}, u32[]{:S(2)}) collective-permute-start(bf16[384,3072]{1,0:T(8,128)(2,1)} %convolution_convert_fusion.7.refs_7_), channel_id=1, source_target_pairs={{0,8},{8,0},{1,9},{9,1},{2,10},{10,2},{3,11},{11,3},{4,12},{12,4},... | collective-permute-start | bytes 7077896 | tf_op jit(solution)/shard_map/ppermute | solution.py:556
  587.8 43.7 %collective-permute-start.20 = (bf16[768,768]{1,0:T(8,128)(2,1)}, bf16[768,768]{1,0:T(8,128)(2,1)}, u32[]{:S(2)}, u32[]{:S(2)}) collective-permute-start(bf16[768,768]{1,0:T(8,128)(2,1)} %get-tuple-element.118.refs_5_), channel_id=1, source_target_pairs={{0,1},{1,0},{2,3},{3,2},{4,5},{5,4},{6,7},{7,6},{8,9},{9,8},{10,11... | collective-permute-start | bytes 3538952 | tf_op jit(solution)/shard_map/ppermute | solution.py:556
  612.4 49.8 %collective-permute-start.24 = (bf16[544,2304]{1,0:T(8,128)(2,1)}, bf16[544,2304]{1,0:T(8,128)(2,1)S(1)}, u32[]{:S(2)}, u32[]{:S(2)}) collective-permute-start(bf16[544,2304]{1,0:T(8,128)(2,1)} %bitcast.44.refs_8_), channel_id=1, source_target_pairs={{0,8},{8,0},{1,9},{9,1},{2,10},{10,2},{3,11},{11,3},{4,12},{12,4},... | collective-permute-start | bytes 7520264 | tf_op jit(solution)/shard_map/ppermute | solution.py:556
  614.7 63.9 %collective-permute-start.25 = (bf16[1536,768]{1,0:T(8,128)(2,1)}, bf16[1536,768]{1,0:T(8,128)(2,1)}, u32[]{:S(2)}, u32[]{:S(2)}) collective-permute-start(bf16[1536,768]{1,0:T(8,128)(2,1)} %convolution_convert_fusion.9.refs_10_), channel_id=1, source_target_pairs={{0,8},{8,0},{1,9},{9,1},{2,10},{10,2},{3,11},{11,3},{4,12},{12,4},... | collective-permute-start | bytes 7077896 | tf_op jit(solution)/shard_map/ppermute | solution.py:556
  617.5 65.6 %collective-permute-start.26 = (bf16[384,3072]{1,0:T(8,128)(2,1)}, bf16[384,3072]{1,0:T(8,128)(2,1)}, u32[]{:S(2)}, u32[]{:S(2)}) collective-permute-start(bf16[384,3072]{1,0:T(8,128)(2,1)} %convolution_convert_fusion.3.refs_12_), channel_id=1, source_target_pairs={{0,8},{8,0},{1,9},{9,1},{2,10},{10,2},{3,11},{11,3},{4,12},{12,4},... | collective-permute-start | bytes 7077896 | tf_op jit(solution)/shard_map/ppermute | solution.py:556
  629.6 28.8 %collective-permute-start.23 = (bf16[192,3072]{1,0:T(8,128)(2,1)}, bf16[192,3072]{1,0:T(8,128)(2,1)S(1)}, u32[]{:S(2)}, u32[]{:S(2)}) collective-permute-start(bf16[192,3072]{1,0:T(8,128)(2,1)} %get-tuple-element.124.refs_6_), channel_id=1, source_target_pairs={{0,1},{1,0},{2,3},{3,2},{4,5},{5,4},{6,7},{7,6},{8,9},{9,8},{10,11... | collective-permute-start | bytes 3538952 | tf_op jit(solution)/shard_map/ppermute | solution.py:556
  675.5 130.1 %all-reduce.5.cloned.1.call-start = ((), (), s32[]{:S(2)}) async-start(), calls=%async_computation.19 | async-start | bytes 4718592 | tf_op jit(solution)/shard_map/psum | solution.py:720
  697.7 41.8 %collective-permute-start.29 = (bf16[544,2304]{1,0:T(8,128)(2,1)}, bf16[544,2304]{1,0:T(8,128)(2,1)S(1)}, u32[]{:S(2)}, u32[]{:S(2)}) collective-permute-start(bf16[544,2304]{1,0:T(8,128)(2,1)} %bitcast.60.rest_0_), channel_id=1, source_target_pairs={{0,8},{8,0},{1,9},{9,1},{2,10},{10,2},{3,11},{11,3},{4,12},{12,4},... | collective-permute-start | bytes 7520264 | tf_op jit(solution)/shard_map/ppermute | solution.py:556
  697.7 30.7 %collective-permute-start.31 = (bf16[272,2304]{1,0:T(8,128)(2,1)}, bf16[272,2304]{1,0:T(8,128)(2,1)}, u32[]{:S(2)}, u32[]{:S(2)}) collective-permute-start(bf16[272,2304]{1,0:T(8,128)(2,1)} %get-tuple-element.137.rest_1_), channel_id=1, source_target_pairs={{0,1},{1,0},{2,3},{3,2},{4,5},{5,4},{6,7},{7,6},{8,9},{9,8},{10,11... | collective-permute-start | bytes 3760136 | tf_op jit(solution)/shard_map/ppermute | solution.py:556
  699.3 54.5 %collective-permute-start.33 = (bf16[768,768]{1,0:T(8,128)(2,1)}, bf16[768,768]{1,0:T(8,128)(2,1)}, u32[]{:S(2)}, u32[]{:S(2)}) collective-permute-start(bf16[768,768]{1,0:T(8,128)(2,1)} %get-tuple-element.140.refs_5_), channel_id=1, source_target_pairs={{0,1},{1,0},{2,3},{3,2},{4,5},{5,4},{6,7},{7,6},{8,9},{9,8},{10,11... | collective-permute-start | bytes 3538952 | tf_op jit(solution)/shard_map/ppermute | solution.py:556
  731.6 83.0 %collective-permute-start.32 = (bf16[272,2304]{1,0:T(8,128)(2,1)}, bf16[272,2304]{1,0:T(8,128)(2,1)}, u32[]{:S(2)}, u32[]{:S(2)}) collective-permute-start(bf16[272,2304]{1,0:T(8,128)(2,1)} %shard_map.214.rest_0_.one_ref), channel_id=1, source_target_pairs={{0,2},{6,4},{1,3},{7,5},{8,10},{14,12},{9,11},{15,13},{16,18},{22,... | collective-permute-start | bytes 3760136 | tf_op jit(solution)/shard_map/ppermute | solution.py:724
  736.0 84.0 %collective-permute-start.36 = (bf16[192,3072]{1,0:T(8,128)(2,1)}, bf16[192,3072]{1,0:T(8,128)(2,1)}, u32[]{:S(2)}, u32[]{:S(2)}) collective-permute-start(bf16[192,3072]{1,0:T(8,128)(2,1)} %get-tuple-element.142.refs_7_), channel_id=1, source_target_pairs={{0,1},{1,0},{2,3},{3,2},{4,5},{5,4},{6,7},{7,6},{8,9},{9,8},{10,11... | collective-permute-start | bytes 3538952 | tf_op jit(solution)/shard_map/ppermute | solution.py:556
  809.1 32.0 %collective-permute-start.35 = (bf16[768,768]{1,0:T(8,128)(2,1)}, bf16[768,768]{1,0:T(8,128)(2,1)S(1)}, u32[]{:S(2)}, u32[]{:S(2)}) collective-permute-start(bf16[768,768]{1,0:T(8,128)(2,1)} %shard_map.215.rest_0_.one_ref), channel_id=1, source_target_pairs={{0,2},{6,4},{1,3},{7,5},{8,10},{14,12},{9,11},{15,13},{16,18},{22,... | collective-permute-start | bytes 3538952 | tf_op jit(solution)/shard_map/ppermute | solution.py:724
  817.6 34.8 %collective-permute-start.34 = (bf16[272,2304]{1,0:T(8,128)(2,1)}, bf16[272,2304]{1,0:T(8,128)(2,1)S(1)}, u32[]{:S(2)}, u32[]{:S(2)}) collective-permute-start(bf16[272,2304]{1,0:T(8,128)(2,1)} %shard_map.216.rest_0_.one_ref), channel_id=1, source_target_pairs={{2,4},{4,2},{3,5},{5,3},{10,12},{12,10},{11,13},{13,11},{18,20},{2... | collective-permute-start | bytes 3760136 | tf_op jit(solution)/shard_map/ppermute | solution.py:724
  818.4 70.3 %collective-permute-start.30 = (bf16[272,2304]{1,0:T(8,128)(2,1)S(1)}, bf16[272,2304]{1,0:T(8,128)(2,1)S(1)}, u32[]{:S(2)}, u32[]{:S(2)}) collective-permute-start(bf16[272,2304]{1,0:T(8,128)(2,1)S(1)} %copy-done.14), channel_id=1, source_target_pairs={{0,1},{1,0},{2,3},{3,2},{4,5},{5,4},{6,7},{7,6},{8,9},{9,8},{10,11... | collective-permute-start | bytes 3760136 | tf_op jit(solution)/shard_map/ppermute | solution.py:556
  822.9 71.8 %collective-permute-start.39 = (bf16[192,3072]{1,0:T(8,128)(2,1)}, bf16[192,3072]{1,0:T(8,128)(2,1)S(1)}, u32[]{:S(2)}, u32[]{:S(2)}) collective-permute-start(bf16[192,3072]{1,0:T(8,128)(2,1)} %shard_map.217.rest_0_.one_ref), channel_id=1, source_target_pairs={{0,2},{6,4},{1,3},{7,5},{8,10},{14,12},{9,11},{15,13},{16,18},{22,... | collective-permute-start | bytes 3538952 | tf_op jit(solution)/shard_map/ppermute | solution.py:724
  845.6 53.7 %collective-permute-start.38 = (bf16[768,768]{1,0:T(8,128)(2,1)}, bf16[768,768]{1,0:T(8,128)(2,1)S(1)}, u32[]{:S(2)}, u32[]{:S(2)}) collective-permute-start(bf16[768,768]{1,0:T(8,128)(2,1)} %shard_map.218.rest_0_.one_ref), channel_id=1, source_target_pairs={{2,4},{4,2},{3,5},{5,3},{10,12},{12,10},{11,13},{13,11},{18,20},{2... | collective-permute-start | bytes 3538952 | tf_op jit(solution)/shard_map/ppermute | solution.py:724
  847.2 41.5 %collective-permute-start.28 = (bf16[192,768]{1,0:T(8,128)(2,1)S(1)}, bf16[192,768]{1,0:T(8,128)(2,1)S(1)}, u32[]{:S(2)}, u32[]{:S(2)}) collective-permute-start(bf16[192,768]{1,0:T(8,128)(2,1)S(1)} %get-tuple-element.163), channel_id=1, source_target_pairs={{0,4},{4,0},{1,5},{5,1},{2,6},{6,2},{3,7},{7,3},{8,12},{12,8},{9,1... | collective-permute-start | bytes 884744 | tf_op jit(solution)/shard_map/ppermute | solution.py:556
  892.9 26.5 %collective-permute-start.37 = (bf16[272,2304]{1,0:T(8,128)(2,1)}, bf16[272,2304]{1,0:T(8,128)(2,1)S(1)}, u32[]{:S(2)}, u32[]{:S(2)}) collective-permute-start(bf16[272,2304]{1,0:T(8,128)(2,1)} %shard_map.220.rest_0_.one_ref), channel_id=1, source_target_pairs={{0,2},{6,4},{1,3},{7,5},{8,10},{14,12},{9,11},{15,13},{16,18},{22,... | collective-permute-start | bytes 3760136 | tf_op jit(solution)/shard_map/ppermute | solution.py:724
  898.6 26.8 %collective-permute-start.41 = (bf16[192,3072]{1,0:T(8,128)(2,1)}, bf16[192,3072]{1,0:T(8,128)(2,1)S(1)}, u32[]{:S(2)}, u32[]{:S(2)}) collective-permute-start(bf16[192,3072]{1,0:T(8,128)(2,1)} %shard_map.221.rest_0_.one_ref), channel_id=1, source_target_pairs={{2,4},{4,2},{3,5},{5,3},{10,12},{12,10},{11,13},{13,11},{18,20},{2... | collective-permute-start | bytes 3538952 | tf_op jit(solution)/shard_map/ppermute | solution.py:724
  903.9 27.3 %collective-permute-start.47 = (bf16[768,768]{1,0:T(8,128)(2,1)}, bf16[768,768]{1,0:T(8,128)(2,1)}, u32[]{:S(2)}, u32[]{:S(2)}) collective-permute-start(bf16[768,768]{1,0:T(8,128)(2,1)} %shard_map.222.rest_0_), channel_id=1, source_target_pairs={{2,0},{4,6},{3,1},{5,7},{10,8},{12,14},{11,9},{13,15},{18,16},{20,... | collective-permute-start | bytes 3538952 | tf_op jit(solution)/shard_map/ppermute | solution.py:724
  929.3 32.4 %collective-permute-start.45 = (bf16[192,3072]{1,0:T(8,128)(2,1)}, bf16[192,3072]{1,0:T(8,128)(2,1)}, u32[]{:S(2)}, u32[]{:S(2)}) collective-permute-start(bf16[192,3072]{1,0:T(8,128)(2,1)} %shard_map.224.rest_0_), channel_id=1, source_target_pairs={{2,0},{4,6},{3,1},{5,7},{10,8},{12,14},{11,9},{13,15},{18,16},{20,... | collective-permute-start | bytes 3538952 | tf_op jit(solution)/shard_map/ppermute | solution.py:724
  933.7 29.6 %collective-permute-start.48 = (bf16[768,768]{1,0:T(8,128)(2,1)}, bf16[768,768]{1,0:T(8,128)(2,1)}, u32[]{:S(2)}, u32[]{:S(2)}) collective-permute-start(bf16[768,768]{1,0:T(8,128)(2,1)} %get-tuple-element.156), channel_id=1, source_target_pairs={{0,8},{8,0},{1,9},{9,1},{2,10},{10,2},{3,11},{11,3},{4,12},{12,4},... | collective-permute-start | bytes 3538952 | tf_op jit(solution)/shard_map/ppermute | solution.py:556
  935.2 53.4 %collective-permute-start.43 = (bf16[272,2304]{1,0:T(8,128)(2,1)S(1)}, bf16[272,2304]{1,0:T(8,128)(2,1)}, u32[]{:S(2)}, u32[]{:S(2)}) collective-permute-start(bf16[272,2304]{1,0:T(8,128)(2,1)S(1)} %copy-done), channel_id=1, source_target_pairs={{2,0},{4,6},{3,1},{5,7},{10,8},{12,14},{11,9},{13,15},{18,16},{20,... | collective-permute-start | bytes 3760136 | tf_op jit(solution)/shard_map/ppermute | solution.py:724
  939.6 71.4 %collective-permute-start.42 = (bf16[272,2304]{1,0:T(8,128)(2,1)}, bf16[272,2304]{1,0:T(8,128)(2,1)S(1)}, u32[]{:S(2)}, u32[]{:S(2)}) collective-permute-start(bf16[272,2304]{1,0:T(8,128)(2,1)} %shard_map.225), channel_id=1, source_target_pairs={{2,0},{4,6},{3,1},{5,7},{10,8},{12,14},{11,9},{13,15},{18,16},{20,... | collective-permute-start | bytes 3760136 | tf_op jit(solution)/shard_map/ppermute | solution.py:724
  963.2 49.6 %collective-permute-start.46 = (bf16[192,3072]{1,0:T(8,128)(2,1)S(1)}, bf16[192,3072]{1,0:T(8,128)(2,1)S(1)}, u32[]{:S(2)}, u32[]{:S(2)}) collective-permute-start(bf16[192,3072]{1,0:T(8,128)(2,1)S(1)} %get-tuple-element.158), channel_id=1, source_target_pairs={{0,8},{8,0},{1,9},{9,1},{2,10},{10,2},{3,11},{11,3},{4,12},{12,4},... | collective-permute-start | bytes 3538952 | tf_op jit(solution)/shard_map/ppermute | solution.py:556
  (138 other events, 910.4 us)
Sparse Core Ops, SparseCore 0:
  14.4 76.2 all-gather.3
  92.3 72.9 all-gather.5
  167.5 41.7 all-gather.7
  697.9 107.7 all-reduce.4

commit v8 on v7

--- a/solution.py
+++ b/solution.py
@@ -15,6 +15,7 @@
 VMEM_LIMIT = 56 * 1024 * 1024
 AXES = ("pair", "core", "half", "quad", "side", "rest")
 HEAD_GROUPS = 4
+INWARD, ACROSS, OUTWARD = [(0, 1), (3, 2)], [(1, 2), (2, 1)], [(1, 0), (2, 3)]
 ROW_BLOCKS = (272, 256, 192, 128, 96, 80, 64, 48)
 
 
@@ -724,23 +725,24 @@
     return lax.ppermute(block, ("half", "quad"), pairs)
 
 
-def line_sums(sides, ties):
-    inward, across, outward = [(0, 1), (3, 2)], [(1, 2), (2, 1)], [(1, 0), (2, 3)]
+def line_sums(begun, sides, ties):
     inner = lax.axis_index("half") != lax.axis_index("quad")
-    count = len(sides)
-    totals, mark = [None] * count, ()
+    count = len(begun) + len(sides)
+    totals, mark = [*begun, *sides], ()
     results = []
-    for turn in range(count + 2):
+    for turn in range(2, count + 2):
         mark = (*mark, *ties.get(turn, ()))
         if turn < count:
-            totals[turn] = sides[turn](*mark)
+            totals[turn] = totals[turn](*mark)
             mark = (totals[turn],)
-        for hops, at in ((inward, turn - 1), (across, turn - 2)):
+        for hops, at in ((INWARD, turn - 1), (ACROSS, turn - 2)):
             if 0 <= at < count:
+                if hops is ACROSS:
+                    mark = (*mark, *results[-1:])
                 totals[at] = add_after(totals[at], line_hop(totals[at], hops), mark)
                 mark = (totals[at],)
-                if hops is across:
-                    results.append(pick(inner, totals[at], line_hop(totals[at], outward)))
+                if hops is ACROSS:
+                    results.append(pick(inner, totals[at], line_hop(totals[at], OUTWARD)))
     return results
 
 
@@ -885,7 +887,10 @@
     )
     rest = side_parts(*rest, grads[0])
     up_two = side_sum(*up, grads[0])
-    d_tokens = spread_grads(grads, (up_two, *rest))
+    line = lax.axis_size("quad") == 2
+    if line:
+        down_two = add_after(down_two, line_hop(down_two, INWARD), (grads[0],))
+    d_tokens = spread_grads(grads, (down_two, up_two, *rest))
     down_one, up_one = side_parts(*down_one), side_parts(*up_one)
     out_one = weight_halves(att, branch)
     d_first, flat, sums_one = qkv_backward(
@@ -898,18 +903,17 @@
         (rest, halves[0]),
         (down_one, rest_one[0]),
         (up_one, rest_one[0]),
-        (rest_one, placed[1]),
+        (rest_one, rest_one[0]),
     )
     sides = [
         lambda *after, item=item, mark=mark: side_sum(*item, *after, mark)
         for item, mark in blocks
     ]
-    up_two, down_two = line_sum(up_two, down_two)
-    if lax.axis_size("quad") == 2:
-        sums = line_sums(sides, {1: (up_two, down_two)})
+    if line:
+        sums = line_sums((down_two, up_two), sides, {3: placed[1:]})
     else:
-        sums = line_sum(*(item() for item in sides))
-    rest_two, down_one, up_one, rest_one = sums
+        sums = line_sum(down_two, up_two, *(item() for item in sides))
+    down_two, up_two, rest_two, down_one, up_one, rest_one = sums
     firsts = (rest_one, up_one, down_one)
     seconds = (rest_two, up_two, down_two)
     return placed, [join_cores(a, b) for a, b in zip(firsts, seconds)]

time: 1040 us -> 977 us (0.939)
  waiting for transfers between devices: 340 us -> 241 us
  starting transfers between devices: 107 us -> 122 us
  Pallas kernels: 302 us -> 315 us
    psum x1 -> x0, waiting for transfers between devices: 51.9 us -> none  [line_sum(): return lax.psum(items, ('half', 'quad'))]
    ppermute x33, waiting for transfers between devices: 133 us -> 86.4 us  [swap(): return lax.ppermute(block, axis, [(0, 1), (1, 0)])]
    ppermute x12 -> x18, starting transfers between devices: 25.9 us -> 46.5 us  [line_hop(): return lax.ppermute(block, ('half', 'quad'), pairs)]
    pallas_call x14 -> x18, Pallas kernels: 43.7 us -> 57.1 us  [add_after(): call(add_body, jax.ShapeDtypeStruct((rows, wide), BF16), grid=(rows // bl...]
    select_n x18 -> x21, other arithmetic: 21.3 us -> 25.6 us  [pick(): return jnp.where(flag, one, two)]
    unnamed x241 -> x263, local copies, waits for them, and re-layouts: 39.1 us -> 38.2 us
    ppermute x12 -> x18, waiting for transfers between devices: 92.6 us -> 91.9 us  [line_hop(): return lax.ppermute(block, ('half', 'quad'), pairs)]
  transfers between devices with their start and end apart: 61 -> 66, of which waited for: 31 -> 31; matrix products, arithmetic and copies ran while one was open for 9% -> 11% of each run, Pallas kernels for 17% -> 19%
where the time goes in v8:
time: 977 us; the launch traced here: 965 us
  Pallas kernels  315 us (32%)
  waiting for transfers between devices  241 us (25%)
  blocking collectives  129 us (13%)
  starting transfers between devices  122 us (12%)
  local copies, waits for them, and re-layouts  60.4 us (6%)
  other arithmetic  52.7 us (5%)
  matrix products  30 us (3%)
  between operations  15.5 us (2%)
    all_to_all x8, blocking collectives, spread(): return lax.all_to_all(block, ('quad', 'side'), 0, 0, tiled=True)  129 us
    ppermute x18, waiting for transfers between devices, line_hop(): return lax.ppermute(block, ('half', 'quad'), pairs)  91.9 us
    ppermute x33, waiting for transfers between devices, swap(): return lax.ppermute(block, axis, [(0, 1), (1, 0)])  86.4 us
    pallas_call x4, Pallas kernels, attend_backward(): call(body, (jax.ShapeDtypeStruct((clips, queries, span), BF16), jax.Shape...  70.9 us
    pallas_call x18, Pallas kernels, add_after(): call(add_body, jax.ShapeDtypeStruct((rows, wide), BF16), grid=(rows // bl...  57.1 us
    ppermute x18, starting transfers between devices, line_hop(): return lax.ppermute(block, ('half', 'quad'), pairs)  46.5 us
    pallas_call x4, Pallas kernels, feed_backward(): call(feed_back_body, (jax.ShapeDtypeStruct((rows, hidden), BF16), jax.Sha...  39.8 us
    pallas_call x4, Pallas kernels, attend_forward(): call(body, (jax.ShapeDtypeStruct((clips, queries, span), BF16), jax.Shape...  39.3 us
  transfers between devices with their start and end apart: 66, of which 31 were waited for; matrix products, arithmetic and copies ran while one was open for 11% of the time, Pallas kernels for 19%

profile of v8, /device:TPU:0, one launch (start us, length us, event | category | flops | bytes accessed | tf_op | source)
XLA Modules:
  0.0 965.3 jit_solution(14106120921220540651)
XLA Ops:
  33.4 34.4 %collective-permute-done.2.rest_0_ = bf16[768,768]{1,0:T(8,128)(2,1)S(1)} collective-permute-done((bf16[768,768]{1,0:T(8,128)(2,1)S(1)}, bf16[768,768]{1,0:T(8,128)(2,1)S(1)}, u32[]{:S(2)}, u32[]{:S(2)}) %collective-permute-start.2) | collective-permute-done | bytes 1179680 | tf_op jit(solution)/shard_map/ppermute | solution.py:557
  70.5 20.3 %all-gather.4.cloned.1.call-done.w_ref.w_out_ref.w_up_ref.refs_1_ = bf16[768,6144]{1,0:T(8,128)(2,1)} async-done(((bf16[96,6144]{1,0:T(8,128)(2,1)}), bf16[768,6144]{1,0:T(8,128)(2,1)}) %all-gather.4.cloned.1.call-update) | async-done | bytes 9437200 | tf_op jit(solution)/shard_map/all_gather | solution.py:627
  111.4 11.7 %all-to-all-done = bf16[4,192,576]{2,1,0:T(8,128)(2,1)} async-done(((bf16[4,192,576]{2,1,0:T(8,128)(2,1)}), bf16[4,192,576]{2,1,0:T(8,128)(2,1)}, u32[]{:S(2)}, u32[]{:S(2)}) %all-to-all-start) | async-done | bytes 884768 | tf_op jit(solution)/shard_map/all_to_all | solution.py:566
  128.7 10.0 %shard_map.179 = (bf16[1,768,192]{2,1,0:T(8,128)(2,1)}, f32[1,3,768]{2,1,0:T(4,128)}) custom-call(bf16[1,768,576]{2,1,0:T(8,128)(2,1)} %bitcast.14.refs_0_.refs_1_, bf16[1,768,576]{2,1,0:T(8,128)(2,1)} %bitcast.14.refs_0_.refs_1_, bf16[1,768,576]{2,1,0:T(8,128)(2,1)} %bitcast.291), custom_call_target="tpu_custom_call" | custom-call | flops 3623878656 | bytes 3538944 | tf_op jit(solution)/shard_map/pallas_call | solution.py:143
  169.4 23.1 %all_to_all.80 = bf16[4,192,576]{2,1,0:T(8,128)(2,1)S(1)} all-to-all(bf16[4,192,576]{2,1,0:T(8,128)(2,1)} %get-tuple-element.84), channel_id=1, replica_groups=mesh['pair'=2,'core'=2,'half'=2,'quad'=2,'side'=2,'rest'=1] {'quad','side'}, dimensions={0} | all-to-all | bytes 1769472 | tf_op jit(solution)/shard_map/all_to_all | solution.py:566
  196.0 9.8 %shard_map.182 = (bf16[1,768,192]{2,1,0:T(8,128)(2,1)}, f32[1,3,768]{2,1,0:T(4,128)}) custom-call(bf16[1,768,576]{2,1,0:T(8,128)(2,1)} %bitcast.229, bf16[1,768,576]{2,1,0:T(8,128)(2,1)} %bitcast.230, bf16[1,768,576]{2,1,0:T(8,128)(2,1)} %bitcast.292), custom_call_target="tpu_custom_call" | custom-call | flops 3623878656 | bytes 3538944 | tf_op jit(solution)/shard_map/pallas_call | solution.py:143
  239.3 16.4 %all_to_all.81 = bf16[4,192,576]{2,1,0:T(8,128)(2,1)S(1)} all-to-all(bf16[4,192,576]{2,1,0:T(8,128)(2,1)} %get-tuple-element.86), channel_id=1, replica_groups=mesh['pair'=2,'core'=2,'half'=2,'quad'=2,'side'=2,'rest'=1] {'quad','side'}, dimensions={0} | all-to-all | bytes 1769472 | tf_op jit(solution)/shard_map/all_to_all | solution.py:566
  259.3 9.8 %shard_map.185 = (bf16[1,768,192]{2,1,0:T(8,128)(2,1)}, f32[1,3,768]{2,1,0:T(4,128)}) custom-call(bf16[1,768,576]{2,1,0:T(8,128)(2,1)} %bitcast.217, bf16[1,768,576]{2,1,0:T(8,128)(2,1)} %bitcast.218, bf16[1,768,576]{2,1,0:T(8,128)(2,1)} %bitcast.285), custom_call_target="tpu_custom_call" | custom-call | flops 3623878656 | bytes 3538944 | tf_op jit(solution)/shard_map/pallas_call | solution.py:143
  269.1 11.9 %all_to_all.82.att_ref = bf16[4,192,192]{2,1,0:T(8,128)(2,1)} all-to-all(bf16[4,192,192]{2,1,0:T(8,128)(2,1)} %bitcast.235), channel_id=1, replica_groups=mesh['pair'=2,'core'=2,'half'=2,'quad'=2,'side'=2,'rest'=1] {'quad','side'}, dimensions={0} | all-to-all | bytes 589824 | tf_op jit(solution)/shard_map/all_to_all | solution.py:566
  294.3 16.7 %all_to_all.83 = bf16[4,192,576]{2,1,0:T(8,128)(2,1)S(1)} all-to-all(bf16[4,192,576]{2,1,0:T(8,128)(2,1)} %get-tuple-element.89), channel_id=1, replica_groups=mesh['pair'=2,'core'=2,'half'=2,'quad'=2,'side'=2,'rest'=1] {'quad','side'}, dimensions={0} | all-to-all | bytes 1769472 | tf_op jit(solution)/shard_map/all_to_all | solution.py:566
  314.5 9.8 %shard_map.188 = (bf16[1,768,192]{2,1,0:T(8,128)(2,1)}, f32[1,3,768]{2,1,0:T(4,128)}) custom-call(bf16[1,768,576]{2,1,0:T(8,128)(2,1)} %bitcast.223, bf16[1,768,576]{2,1,0:T(8,128)(2,1)} %bitcast.224, bf16[1,768,576]{2,1,0:T(8,128)(2,1)} %bitcast.288), custom_call_target="tpu_custom_call" | custom-call | flops 3623878656 | bytes 3538944 | tf_op jit(solution)/shard_map/pallas_call | solution.py:143
  324.2 11.9 %all_to_all.84.att_ref = bf16[4,192,192]{2,1,0:T(8,128)(2,1)} all-to-all(bf16[4,192,192]{2,1,0:T(8,128)(2,1)} %bitcast.236), channel_id=1, replica_groups=mesh['pair'=2,'core'=2,'half'=2,'quad'=2,'side'=2,'rest'=1] {'quad','side'}, dimensions={0} | all-to-all | bytes 589824 | tf_op jit(solution)/shard_map/all_to_all | solution.py:566
  352.5 9.9 %shard_map.190 = (bf16[192,3072]{1,0:T(8,128)(2,1)}, f32[192,768]{1,0:T(8,128)}, bf16[192,768]{1,0:T(8,128)(2,1)}, bf16[4,192,192]{2,1,0:T(8,128)(2,1)}, f32[4,768]{1,0:T(4,128)}, /*index=5*/f32[1,3072]{1,0:T(1,128)}) custom-call(bf16[192,768]{1,0:T(8,128)(2,1)} %bitcast_select_fusion.g_ref, f32[192,3072]{1,0:T(8,128)} %get-tuple-element.92.slope_ref, ...), custom_call_target="tpu_custom_call" | custom-call | flops 2038431744 | bytes 14155776 | tf_op jit(solution)/shard_map/pallas_call | solution.py:415
  374.9 17.7 %shard_map.191 = (bf16[1,768,192]{2,1,0:T(8,128)(2,1)}, f32[1,768,384]{2,1,0:T(8,128)}, bf16[1,768,384]{2,1,0:T(8,128)(2,1)}) custom-call(bf16[1,768,576]{2,1,0:T(8,128)(2,1)} %bitcast.225, bf16[1,768,576]{2,1,0:T(8,128)(2,1)} %bitcast.226, bf16[1,768,576]{2,1,0:T(8,128)(2,1)} %bitcast.289, bf16[1,768,192]{2,1,0:T(8,128)(2,1)} %bitcast.231, ...), custom_call_target="tpu_custom_call" | custom-call | flops 9059696640 | bytes 7077888 | tf_op jit(solution)/shard_map/pallas_call | solution.py:241
  392.6 12.9 %collective-permute-start.15 = (bf16[1,768,384]{2,1,0:T(8,128)(2,1)}, bf16[1,768,384]{2,1,0:T(8,128)(2,1)S(1)}, u32[]{:S(2)}, u32[]{:S(2)}) collective-permute-start(bf16[1,768,384]{2,1,0:T(8,128)(2,1)} %get-tuple-element.98), channel_id=1, source_target_pairs={{0,8},{8,0},{1,9},{9,1},{2,10},{10,2},{3,11},{11,3},{4,12},{12,4},... | collective-permute-start | bytes 1769480 | tf_op jit(solution)/shard_map/ppermute | solution.py:557
  410.9 19.1 %all_to_all.85.refs_0_ = bf16[4,192,576]{2,1,0:T(8,128)(2,1)} all-to-all(bf16[4,192,576]{2,1,0:T(8,128)(2,1)} %bitcast.211), channel_id=1, replica_groups=mesh['pair'=2,'core'=2,'half'=2,'quad'=2,'side'=2,'rest'=1] {'quad','side'}, dimensions={0} | all-to-all | bytes 1769472 | tf_op jit(solution)/shard_map/all_to_all | solution.py:566
  434.8 10.0 %shard_map.194 = (bf16[192,3072]{1,0:T(8,128)(2,1)}, f32[192,768]{1,0:T(8,128)}, bf16[192,768]{1,0:T(8,128)(2,1)}, bf16[4,192,192]{2,1,0:T(8,128)(2,1)}, f32[4,768]{1,0:T(4,128)}, /*index=5*/f32[1,3072]{1,0:T(1,128)}) custom-call(bf16[192,768]{1,0:T(8,128)(2,1)} %get-tuple-element.100.g_ref, f32[192,3072]{1,0:T(8,128)} %get-tuple-element.101.slope_ref, ...), custom_call_target="tpu_custom_call" | custom-call | flops 2038431744 | bytes 14155776 | tf_op jit(solution)/shard_map/pallas_call | solution.py:415
  444.8 11.1 %all_to_all.86 = bf16[4,192,192]{2,1,0:T(8,128)(2,1)} all-to-all(bf16[4,192,192]{2,1,0:T(8,128)(2,1)} %get-tuple-element.103), channel_id=1, replica_groups=mesh['pair'=2,'core'=2,'half'=2,'quad'=2,'side'=2,'rest'=1] {'quad','side'}, dimensions={0} | all-to-all | bytes 589824 | tf_op jit(solution)/shard_map/all_to_all | solution.py:566
  455.9 17.8 %shard_map.195 = (bf16[1,768,192]{2,1,0:T(8,128)(2,1)}, f32[1,768,384]{2,1,0:T(8,128)}, bf16[1,768,384]{2,1,0:T(8,128)(2,1)}) custom-call(bf16[1,768,576]{2,1,0:T(8,128)(2,1)} %bitcast.219, bf16[1,768,576]{2,1,0:T(8,128)(2,1)} %bitcast.220, bf16[1,768,576]{2,1,0:T(8,128)(2,1)} %bitcast.286, bf16[1,768,192]{2,1,0:T(8,128)(2,1)} %bitcast.234, ...), custom_call_target="tpu_custom_call" | custom-call | flops 9059696640 | bytes 7077888 | tf_op jit(solution)/shard_map/pallas_call | solution.py:241
  479.5 18.5 %all_to_all.87.refs_0_ = bf16[4,192,576]{2,1,0:T(8,128)(2,1)} all-to-all(bf16[4,192,576]{2,1,0:T(8,128)(2,1)} %bitcast.212), channel_id=1, replica_groups=mesh['pair'=2,'core'=2,'half'=2,'quad'=2,'side'=2,'rest'=1] {'quad','side'}, dimensions={0} | all-to-all | bytes 1769472 | tf_op jit(solution)/shard_map/all_to_all | solution.py:566
  513.9 10.0 %shard_map.198 = (bf16[192,3072]{1,0:T(8,128)(2,1)}, f32[192,768]{1,0:T(8,128)}, bf16[192,768]{1,0:T(8,128)(2,1)}, bf16[4,192,192]{2,1,0:T(8,128)(2,1)}, f32[4,768]{1,0:T(4,128)}, /*index=5*/f32[1,3072]{1,0:T(1,128)}) custom-call(bf16[192,768]{1,0:T(8,128)(2,1)} %broadcast_select_fusion.21.g_ref, f32[192,3072]{1,0:T(8,128)} %get-tuple-element.92.slope_ref, ...), custom_call_target="tpu_custom_call" | custom-call | flops 2038431744 | bytes 14155776 | tf_op jit(solution)/shard_map/pallas_call | solution.py:415
  537.3 17.7 %shard_map.199 = (bf16[1,768,192]{2,1,0:T(8,128)(2,1)}, f32[1,768,384]{2,1,0:T(8,128)}, bf16[1,768,384]{2,1,0:T(8,128)(2,1)}) custom-call(bf16[1,768,576]{2,1,0:T(8,128)(2,1)} %bitcast.227, bf16[1,768,576]{2,1,0:T(8,128)(2,1)} %bitcast.228, bf16[1,768,576]{2,1,0:T(8,128)(2,1)} %bitcast.290, bf16[1,768,192]{2,1,0:T(8,128)(2,1)} %bitcast.35.refs_3_, ...), custom_call_target="tpu_custom_call" | custom-call | flops 9059696640 | bytes 7077888 | tf_op jit(solution)/shard_map/pallas_call | solution.py:241
  595.5 10.0 %shard_map.203 = (bf16[192,3072]{1,0:T(8,128)(2,1)}, f32[192,768]{1,0:T(8,128)}, bf16[192,768]{1,0:T(8,128)(2,1)}, bf16[4,192,192]{2,1,0:T(8,128)(2,1)}, f32[4,768]{1,0:T(4,128)}, /*index=5*/f32[1,3072]{1,0:T(1,128)}) custom-call(bf16[192,768]{1,0:T(8,128)(2,1)} %get-tuple-element.122.g_ref, f32[192,3072]{1,0:T(8,128)} %get-tuple-element.101.slope_ref, ...), custom_call_target="tpu_custom_call" | custom-call | flops 2038431744 | bytes 14155776 | tf_op jit(solution)/shard_map/pallas_call | solution.py:415
  639.5 17.7 %shard_map.206 = (bf16[1,768,192]{2,1,0:T(8,128)(2,1)}, f32[1,768,384]{2,1,0:T(8,128)}, bf16[1,768,384]{2,1,0:T(8,128)(2,1)}) custom-call(bf16[1,768,576]{2,1,0:T(8,128)(2,1)} %bitcast.221, bf16[1,768,576]{2,1,0:T(8,128)(2,1)} %bitcast.222, bf16[1,768,576]{2,1,0:T(8,128)(2,1)} %bitcast.287, bf16[1,768,192]{2,1,0:T(8,128)(2,1)} %bitcast.216, ...), custom_call_target="tpu_custom_call" | custom-call | flops 9059696640 | bytes 7077888 | tf_op jit(solution)/shard_map/pallas_call | solution.py:241
  715.2 16.2 %collective-permute-done.32.two_ref = bf16[272,2304]{1,0:T(8,128)(2,1)} collective-permute-done((bf16[272,2304]{1,0:T(8,128)(2,1)}, bf16[272,2304]{1,0:T(8,128)(2,1)}, u32[]{:S(2)}, u32[]{:S(2)}) %collective-permute-start.32) | collective-permute-done | bytes 1253408 | tf_op jit(solution)/shard_map/ppermute | solution.py:557
  756.3 12.2 %collective-permute-done.41 = bf16[768,768]{1,0:T(8,128)(2,1)} collective-permute-done((bf16[768,768]{1,0:T(8,128)(2,1)}, bf16[768,768]{1,0:T(8,128)(2,1)}, u32[]{:S(2)}, u32[]{:S(2)}) %collective-permute-start.41) | collective-permute-done | bytes 1179680 | tf_op jit(solution)/shard_map/ppermute | solution.py:725
  776.4 11.1 %collective-permute-done.29.rest_1_ = bf16[192,768]{1,0:T(8,128)(2,1)S(1)} collective-permute-done((bf16[192,768]{1,0:T(8,128)(2,1)S(1)}, bf16[192,768]{1,0:T(8,128)(2,1)S(1)}, u32[]{:S(2)}, u32[]{:S(2)}) %collective-permute-start.29) | collective-permute-done | bytes 294944 | tf_op jit(solution)/shard_map/ppermute | solution.py:557
  801.0 9.5 collective-permute-start.38
  814.0 10.3 %collective-permute-done.42 = bf16[192,3072]{1,0:T(8,128)(2,1)} collective-permute-done((bf16[192,3072]{1,0:T(8,128)(2,1)}, bf16[192,3072]{1,0:T(8,128)(2,1)}, u32[]{:S(2)}, u32[]{:S(2)}) %collective-permute-start.42) | collective-permute-done | bytes 1179680 | tf_op jit(solution)/shard_map/ppermute | solution.py:725
  851.0 18.6 %collective-permute-done.45.two_ref = bf16[192,3072]{1,0:T(8,128)(2,1)} collective-permute-done((bf16[192,3072]{1,0:T(8,128)(2,1)S(1)}, bf16[192,3072]{1,0:T(8,128)(2,1)}, u32[]{:S(2)}, u32[]{:S(2)}) %collective-permute-start.45) | collective-permute-done | bytes 1179680 | tf_op jit(solution)/shard_map/ppermute | solution.py:725
  904.4 17.6 %collective-permute-done.50 = bf16[192,3072]{1,0:T(8,128)(2,1)S(1)} collective-permute-done((bf16[192,3072]{1,0:T(8,128)(2,1)}, bf16[192,3072]{1,0:T(8,128)(2,1)S(1)}, u32[]{:S(2)}, u32[]{:S(2)}) %collective-permute-start.50) | collective-permute-done | bytes 1179680 | tf_op jit(solution)/shard_map/ppermute | solution.py:725
  934.1 15.2 %collective-permute-done.51 = bf16[272,2304]{1,0:T(8,128)(2,1)S(1)} collective-permute-done((bf16[272,2304]{1,0:T(8,128)(2,1)}, bf16[272,2304]{1,0:T(8,128)(2,1)S(1)}, u32[]{:S(2)}, u32[]{:S(2)}) %collective-permute-start.51) | collective-permute-done | bytes 1253408 | tf_op jit(solution)/shard_map/ppermute | solution.py:725
  (548 shorter events, 481.2 us)
Async XLA Ops:
  7.2 83.6 %all-gather.4.cloned.1.call-start = ((), (), s32[]{:S(2)}) async-start(), calls=%async_computation.16 | async-start | bytes 10616832 | tf_op jit(solution)/shard_map/all_gather | solution.py:627
  14.3 151.0 %all-gather.6.cloned.1.call-start = ((), (), s32[]{:S(2)}) async-start(), calls=%async_computation.17 | async-start | bytes 10616832 | tf_op jit(solution)/shard_map/all_gather | solution.py:627
  15.1 197.2 %all-gather.8.cloned.1.call-start = ((), (), s32[]{:S(2)}) async-start(), calls=%async_computation.18 | async-start | bytes 5308416 | tf_op jit(solution)/shard_map/all_gather | solution.py:644
  27.9 39.8 %collective-permute-start.2 = (bf16[768,768]{1,0:T(8,128)(2,1)S(1)}, bf16[768,768]{1,0:T(8,128)(2,1)S(1)}, u32[]{:S(2)}, u32[]{:S(2)}) collective-permute-start(bf16[768,768]{1,0:T(8,128)(2,1)S(1)} %constant_dynamic-slice_fusion.32), channel_id=1, source_target_pairs={{0,1},{1,0},{2,3},{3,2},{4,5},{5,4},{6,7},{7,6},{8,9},{9,8},{10,11... | collective-permute-start | bytes 3538952 | tf_op jit(solution)/shard_map/ppermute | solution.py:557
  94.9 28.3 %all-to-all-start = ((bf16[4,192,576]{2,1,0:T(8,128)(2,1)}), bf16[4,192,576]{2,1,0:T(8,128)(2,1)}, u32[]{:S(2)}, u32[]{:S(2)}) async-start(bf16[4,192,576]{2,1,0:T(8,128)(2,1)} %get-tuple-element.82), calls=%async_computation | async-start | bytes 1966080 | tf_op jit(solution)/shard_map/all_to_all | solution.py:566
  530.5 51.3 %collective-permute-start.19 = (bf16[1536,768]{1,0:T(8,128)(2,1)}, bf16[1536,768]{1,0:T(8,128)(2,1)S(1)}, u32[]{:S(2)}, u32[]{:S(2)}) collective-permute-start(bf16[1536,768]{1,0:T(8,128)(2,1)} %convolution_convert_fusion.11.refs_5_), channel_id=1, source_target_pairs={{0,8},{8,0},{1,9},{9,1},{2,10},{10,2},{3,11},{11,3},{4,12},{12,4},... | collective-permute-start | bytes 7077896 | tf_op jit(solution)/shard_map/ppermute | solution.py:557
  571.2 49.0 %collective-permute-start.21 = (bf16[384,3072]{1,0:T(8,128)(2,1)}, bf16[384,3072]{1,0:T(8,128)(2,1)}, u32[]{:S(2)}, u32[]{:S(2)}) collective-permute-start(bf16[384,3072]{1,0:T(8,128)(2,1)} %convolution_convert_fusion.7.refs_7_), channel_id=1, source_target_pairs={{0,8},{8,0},{1,9},{9,1},{2,10},{10,2},{3,11},{11,3},{4,12},{12,4},... | collective-permute-start | bytes 7077896 | tf_op jit(solution)/shard_map/ppermute | solution.py:557
  588.0 44.2 %collective-permute-start.20 = (bf16[768,768]{1,0:T(8,128)(2,1)}, bf16[768,768]{1,0:T(8,128)(2,1)}, u32[]{:S(2)}, u32[]{:S(2)}) collective-permute-start(bf16[768,768]{1,0:T(8,128)(2,1)} %get-tuple-element.118.refs_5_), channel_id=1, source_target_pairs={{0,1},{1,0},{2,3},{3,2},{4,5},{5,4},{6,7},{7,6},{8,9},{9,8},{10,11... | collective-permute-start | bytes 3538952 | tf_op jit(solution)/shard_map/ppermute | solution.py:557
  612.3 56.6 %collective-permute-start.25 = (bf16[544,2304]{1,0:T(8,128)(2,1)}, bf16[544,2304]{1,0:T(8,128)(2,1)S(1)}, u32[]{:S(2)}, u32[]{:S(2)}) collective-permute-start(bf16[544,2304]{1,0:T(8,128)(2,1)} %bitcast.44.refs_8_), channel_id=1, source_target_pairs={{0,8},{8,0},{1,9},{9,1},{2,10},{10,2},{3,11},{11,3},{4,12},{12,4},... | collective-permute-start | bytes 7520264 | tf_op jit(solution)/shard_map/ppermute | solution.py:557
  614.7 79.9 %collective-permute-start.26 = (bf16[1536,768]{1,0:T(8,128)(2,1)}, bf16[1536,768]{1,0:T(8,128)(2,1)}, u32[]{:S(2)}, u32[]{:S(2)}) collective-permute-start(bf16[1536,768]{1,0:T(8,128)(2,1)} %convolution_convert_fusion.9.refs_10_), channel_id=1, source_target_pairs={{0,8},{8,0},{1,9},{9,1},{2,10},{10,2},{3,11},{11,3},{4,12},{12,4},... | collective-permute-start | bytes 7077896 | tf_op jit(solution)/shard_map/ppermute | solution.py:557
  617.4 81.8 %collective-permute-start.27 = (bf16[384,3072]{1,0:T(8,128)(2,1)}, bf16[384,3072]{1,0:T(8,128)(2,1)}, u32[]{:S(2)}, u32[]{:S(2)}) collective-permute-start(bf16[384,3072]{1,0:T(8,128)(2,1)} %convolution_convert_fusion.3.refs_12_), channel_id=1, source_target_pairs={{0,8},{8,0},{1,9},{9,1},{2,10},{10,2},{3,11},{11,3},{4,12},{12,4},... | collective-permute-start | bytes 7077896 | tf_op jit(solution)/shard_map/ppermute | solution.py:557
  625.9 31.4 %collective-permute-start.24 = (bf16[192,3072]{1,0:T(8,128)(2,1)}, bf16[192,3072]{1,0:T(8,128)(2,1)S(1)}, u32[]{:S(2)}, u32[]{:S(2)}) collective-permute-start(bf16[192,3072]{1,0:T(8,128)(2,1)} %get-tuple-element.124.refs_6_), channel_id=1, source_target_pairs={{0,1},{1,0},{2,3},{3,2},{4,5},{5,4},{6,7},{7,6},{8,9},{9,8},{10,11... | collective-permute-start | bytes 3538952 | tf_op jit(solution)/shard_map/ppermute | solution.py:557
  635.7 28.6 %collective-permute-start.23 = (bf16[768,768]{1,0:T(8,128)(2,1)}, bf16[768,768]{1,0:T(8,128)(2,1)S(1)}, u32[]{:S(2)}, u32[]{:S(2)}) collective-permute-start(bf16[768,768]{1,0:T(8,128)(2,1)} %shard_map.204.refs_5_.one_ref), channel_id=1, source_target_pairs={{0,2},{6,4},{1,3},{7,5},{8,10},{14,12},{9,11},{15,13},{16,18},{22,... | collective-permute-start | bytes 3538952 | tf_op jit(solution)/shard_map/ppermute | solution.py:725
  678.2 26.0 %all-to-all-start.15 = ((bf16[4,192,576]{2,1,0:T(8,128)(2,1)}), bf16[4,192,576]{2,1,0:T(8,128)(2,1)}, u32[]{:S(2)}, u32[]{:S(2)}) async-start(bf16[4,192,576]{2,1,0:T(8,128)(2,1)} %bitcast.210), calls=%async_computation.15 | async-start | bytes 1966080 | tf_op jit(solution)/shard_map/all_to_all | solution.py:566
  687.5 46.8 %collective-permute-start.36 = (bf16[192,3072]{1,0:T(8,128)(2,1)S(1)}, bf16[192,3072]{1,0:T(8,128)(2,1)}, u32[]{:S(2)}, u32[]{:S(2)}) collective-permute-start(bf16[192,3072]{1,0:T(8,128)(2,1)S(1)} %copy-done.8), channel_id=1, source_target_pairs={{0,2},{6,4},{1,3},{7,5},{8,10},{14,12},{9,11},{15,13},{16,18},{22,... | collective-permute-start | bytes 3538952 | tf_op jit(solution)/shard_map/ppermute | solution.py:725
  692.8 44.4 %collective-permute-start.35 = (bf16[768,768]{1,0:T(8,128)(2,1)S(1)}, bf16[768,768]{1,0:T(8,128)(2,1)}, u32[]{:S(2)}, u32[]{:S(2)}) collective-permute-start(bf16[768,768]{1,0:T(8,128)(2,1)S(1)} %copy-done.9), channel_id=1, source_target_pairs={{2,4},{4,2},{3,5},{5,3},{10,12},{12,10},{11,13},{13,11},{18,20},{2... | collective-permute-start | bytes 3538952 | tf_op jit(solution)/shard_map/ppermute | solution.py:725
  703.2 28.1 %collective-permute-start.32 = (bf16[272,2304]{1,0:T(8,128)(2,1)}, bf16[272,2304]{1,0:T(8,128)(2,1)}, u32[]{:S(2)}, u32[]{:S(2)}) collective-permute-start(bf16[272,2304]{1,0:T(8,128)(2,1)} %get-tuple-element.137.rest_2_), channel_id=1, source_target_pairs={{0,1},{1,0},{2,3},{3,2},{4,5},{5,4},{6,7},{7,6},{8,9},{9,8},{10,11... | collective-permute-start | bytes 3760136 | tf_op jit(solution)/shard_map/ppermute | solution.py:557
  713.9 57.1 %collective-permute-start.30 = (bf16[544,2304]{1,0:T(8,128)(2,1)}, bf16[544,2304]{1,0:T(8,128)(2,1)}, u32[]{:S(2)}, u32[]{:S(2)}) collective-permute-start(bf16[544,2304]{1,0:T(8,128)(2,1)} %bitcast.60.rest_0_), channel_id=1, source_target_pairs={{0,8},{8,0},{1,9},{9,1},{2,10},{10,2},{3,11},{11,3},{4,12},{12,4},... | collective-permute-start | bytes 7520264 | tf_op jit(solution)/shard_map/ppermute | solution.py:557
  714.7 35.0 %collective-permute-start.28 = (bf16[192,768]{1,0:T(8,128)(2,1)}, bf16[192,768]{1,0:T(8,128)(2,1)}, u32[]{:S(2)}, u32[]{:S(2)}) collective-permute-start(bf16[192,768]{1,0:T(8,128)(2,1)} %broadcast_select_fusion.26), channel_id=1, source_target_pairs={{0,8},{8,0},{1,9},{9,1},{2,10},{10,2},{3,11},{11,3},{4,12},{12,4},... | collective-permute-start | bytes 884744 | tf_op jit(solution)/shard_map/ppermute | solution.py:557
  740.9 27.5 %collective-permute-start.41 = (bf16[768,768]{1,0:T(8,128)(2,1)}, bf16[768,768]{1,0:T(8,128)(2,1)}, u32[]{:S(2)}, u32[]{:S(2)}) collective-permute-start(bf16[768,768]{1,0:T(8,128)(2,1)} %shard_map.217.rest_0_), channel_id=1, source_target_pairs={{2,0},{4,6},{3,1},{5,7},{10,8},{12,14},{11,9},{13,15},{18,16},{20,... | collective-permute-start | bytes 3538952 | tf_op jit(solution)/shard_map/ppermute | solution.py:725
  743.3 33.1 %collective-permute-start.34 = (bf16[768,768]{1,0:T(8,128)(2,1)}, bf16[768,768]{1,0:T(8,128)(2,1)S(1)}, u32[]{:S(2)}, u32[]{:S(2)}) collective-permute-start(bf16[768,768]{1,0:T(8,128)(2,1)} %get-tuple-element.140.refs_5_), channel_id=1, source_target_pairs={{0,1},{1,0},{2,3},{3,2},{4,5},{5,4},{6,7},{7,6},{8,9},{9,8},{10,11... | collective-permute-start | bytes 3538952 | tf_op jit(solution)/shard_map/ppermute | solution.py:557
  744.1 47.6 %collective-permute-start.33 = (bf16[272,2304]{1,0:T(8,128)(2,1)S(1)}, bf16[272,2304]{1,0:T(8,128)(2,1)S(1)}, u32[]{:S(2)}, u32[]{:S(2)}) collective-permute-start(bf16[272,2304]{1,0:T(8,128)(2,1)S(1)} %copy-done.3), channel_id=1, source_target_pairs={{0,2},{6,4},{1,3},{7,5},{8,10},{14,12},{9,11},{15,13},{16,18},{22,... | collective-permute-start | bytes 3760136 | tf_op jit(solution)/shard_map/ppermute | solution.py:725
  749.7 46.0 %collective-permute-start.40 = (bf16[192,3072]{1,0:T(8,128)(2,1)S(1)}, bf16[192,3072]{1,0:T(8,128)(2,1)}, u32[]{:S(2)}, u32[]{:S(2)}) collective-permute-start(bf16[192,3072]{1,0:T(8,128)(2,1)S(1)} %copy-done.10), channel_id=1, source_target_pairs={{2,4},{4,2},{3,5},{5,3},{10,12},{12,10},{11,13},{13,11},{18,20},{2... | collective-permute-start | bytes 3538952 | tf_op jit(solution)/shard_map/ppermute | solution.py:725
  771.0 40.1 %collective-permute-start.39 = (bf16[192,3072]{1,0:T(8,128)(2,1)}, bf16[192,3072]{1,0:T(8,128)(2,1)}, u32[]{:S(2)}, u32[]{:S(2)}) collective-permute-start(bf16[192,3072]{1,0:T(8,128)(2,1)} %get-tuple-element.142.refs_7_), channel_id=1, source_target_pairs={{0,1},{1,0},{2,3},{3,2},{4,5},{5,4},{6,7},{7,6},{8,9},{9,8},{10,11... | collective-permute-start | bytes 3538952 | tf_op jit(solution)/shard_map/ppermute | solution.py:557
  798.8 25.6 %collective-permute-start.42 = (bf16[192,3072]{1,0:T(8,128)(2,1)}, bf16[192,3072]{1,0:T(8,128)(2,1)}, u32[]{:S(2)}, u32[]{:S(2)}) collective-permute-start(bf16[192,3072]{1,0:T(8,128)(2,1)} %shard_map.220.rest_0_), channel_id=1, source_target_pairs={{2,0},{4,6},{3,1},{5,7},{10,8},{12,14},{11,9},{13,15},{18,16},{20,... | collective-permute-start | bytes 3538952 | tf_op jit(solution)/shard_map/ppermute | solution.py:725
  800.2 32.9 %collective-permute-start.37 = (bf16[272,2304]{1,0:T(8,128)(2,1)S(1)}, bf16[272,2304]{1,0:T(8,128)(2,1)S(1)}, u32[]{:S(2)}, u32[]{:S(2)}) collective-permute-start(bf16[272,2304]{1,0:T(8,128)(2,1)S(1)} %copy-done.5), channel_id=1, source_target_pairs={{2,4},{4,2},{3,5},{5,3},{10,12},{12,10},{11,13},{13,11},{18,20},{2... | collective-permute-start | bytes 3760136 | tf_op jit(solution)/shard_map/ppermute | solution.py:725
  801.0 28.7 %collective-permute-start.38 = (bf16[768,768]{1,0:T(8,128)(2,1)S(1)}, bf16[768,768]{1,0:T(8,128)(2,1)}, u32[]{:S(2)}, u32[]{:S(2)}) collective-permute-start(bf16[768,768]{1,0:T(8,128)(2,1)S(1)} %copy-done.14), channel_id=1, source_target_pairs={{0,2},{6,4},{1,3},{7,5},{8,10},{14,12},{9,11},{15,13},{16,18},{22,... | collective-permute-start | bytes 3538952 | tf_op jit(solution)/shard_map/ppermute | solution.py:725
  810.4 34.5 %collective-permute-start.31 = (bf16[272,2304]{1,0:T(8,128)(2,1)S(1)}, bf16[272,2304]{1,0:T(8,128)(2,1)S(1)}, u32[]{:S(2)}, u32[]{:S(2)}) collective-permute-start(bf16[272,2304]{1,0:T(8,128)(2,1)S(1)} %copy-done.4), channel_id=1, source_target_pairs={{0,1},{1,0},{2,3},{3,2},{4,5},{5,4},{6,7},{7,6},{8,9},{9,8},{10,11... | collective-permute-start | bytes 3760136 | tf_op jit(solution)/shard_map/ppermute | solution.py:557
  837.3 35.2 %collective-permute-start.46 = (bf16[272,2304]{1,0:T(8,128)(2,1)}, bf16[272,2304]{1,0:T(8,128)(2,1)S(1)}, u32[]{:S(2)}, u32[]{:S(2)}) collective-permute-start(bf16[272,2304]{1,0:T(8,128)(2,1)} %shard_map.223.rest_0_), channel_id=1, source_target_pairs={{2,0},{4,6},{3,1},{5,7},{10,8},{12,14},{11,9},{13,15},{18,16},{20,... | collective-permute-start | bytes 3760136 | tf_op jit(solution)/shard_map/ppermute | solution.py:725
  838.6 31.0 %collective-permute-start.45 = (bf16[192,3072]{1,0:T(8,128)(2,1)S(1)}, bf16[192,3072]{1,0:T(8,128)(2,1)}, u32[]{:S(2)}, u32[]{:S(2)}) collective-permute-start(bf16[192,3072]{1,0:T(8,128)(2,1)S(1)} %copy-done.15), channel_id=1, source_target_pairs={{0,2},{6,4},{1,3},{7,5},{8,10},{14,12},{9,11},{15,13},{16,18},{22,... | collective-permute-start | bytes 3538952 | tf_op jit(solution)/shard_map/ppermute | solution.py:725
  844.2 29.5 %collective-permute-start.44 = (bf16[768,768]{1,0:T(8,128)(2,1)S(1)}, bf16[768,768]{1,0:T(8,128)(2,1)S(1)}, u32[]{:S(2)}, u32[]{:S(2)}) collective-permute-start(bf16[768,768]{1,0:T(8,128)(2,1)S(1)} %copy-done.16), channel_id=1, source_target_pairs={{2,4},{4,2},{3,5},{5,3},{10,12},{12,10},{11,13},{13,11},{18,20},{2... | collective-permute-start | bytes 3538952 | tf_op jit(solution)/shard_map/ppermute | solution.py:725
  849.0 40.4 %collective-permute-start.43 = (bf16[272,2304]{1,0:T(8,128)(2,1)}, bf16[272,2304]{1,0:T(8,128)(2,1)S(1)}, u32[]{:S(2)}, u32[]{:S(2)}) collective-permute-start(bf16[272,2304]{1,0:T(8,128)(2,1)} %shard_map.224.rest_0_.one_ref), channel_id=1, source_target_pairs={{0,2},{6,4},{1,3},{7,5},{8,10},{14,12},{9,11},{15,13},{16,18},{22,... | collective-permute-start | bytes 3760136 | tf_op jit(solution)/shard_map/ppermute | solution.py:725
  (154 other events, 1065.3 us)
Sparse Core Ops, SparseCore 0:
  14.4 76.2 all-gather.3
  92.3 72.9 all-gather.5
  167.5 41.7 all-gather.7

commit v9 on v8

--- a/solution.py
+++ b/solution.py
@@ -910,7 +910,7 @@
         for item, mark in blocks
     ]
     if line:
-        sums = line_sums((down_two, up_two), sides, {3: placed[1:]})
+        sums = line_sums((down_two, up_two), sides, {4: placed[1:]})
     else:
         sums = line_sum(down_two, up_two, *(item() for item in sides))
     down_two, up_two, rest_two, down_one, up_one, rest_one = sums

time: 977 us -> 1010 us (1.034)
  waiting for transfers between devices: 241 us -> 278 us
    ppermute x33, waiting for transfers between devices: 86.4 us -> 116 us  [swap(): return lax.ppermute(block, axis, [(0, 1), (1, 0)])]
    unnamed x263 -> x261, local copies, waits for them, and re-layouts: 38.2 us -> 37.5 us
  transfers between devices with their start and end apart: 66 -> 66, of which waited for: 31 -> 31; matrix products, arithmetic and copies ran while one was open for 11% -> 10% of each run, Pallas kernels for 19% -> 19%
where the time goes in v9:
time: 1010 us; the launch traced here: 999 us
  Pallas kernels  315 us (31%)
  waiting for transfers between devices  278 us (28%)
  blocking collectives  129 us (13%)
  starting transfers between devices  122 us (12%)
  local copies, waits for them, and re-layouts  59.7 us (6%)
  other arithmetic  50.9 us (5%)
  matrix products  28.7 us (3%)
  between operations  15.5 us (2%)
    all_to_all x8, blocking collectives, spread(): return lax.all_to_all(block, ('quad', 'side'), 0, 0, tiled=True)  129 us
    ppermute x33, waiting for transfers between devices, swap(): return lax.ppermute(block, axis, [(0, 1), (1, 0)])  116 us
    ppermute x18, waiting for transfers between devices, line_hop(): return lax.ppermute(block, ('half', 'quad'), pairs)  99.9 us
    pallas_call x4, Pallas kernels, attend_backward(): call(body, (jax.ShapeDtypeStruct((clips, queries, span), BF16), jax.Shape...  70.9 us
    pallas_call x18, Pallas kernels, add_after(): call(add_body, jax.ShapeDtypeStruct((rows, wide), BF16), grid=(rows // bl...  57.2 us
    ppermute x18, starting transfers between devices, line_hop(): return lax.ppermute(block, ('half', 'quad'), pairs)  47.1 us
    pallas_call x4, Pallas kernels, feed_backward(): call(feed_back_body, (jax.ShapeDtypeStruct((rows, hidden), BF16), jax.Sha...  39.8 us
    pallas_call x4, Pallas kernels, attend_forward(): call(body, (jax.ShapeDtypeStruct((clips, queries, span), BF16), jax.Shape...  39.3 us
  transfers between devices with their start and end apart: 66, of which 31 were waited for; matrix products, arithmetic and copies ran while one was open for 10% of the time, Pallas kernels for 19%

profile of v9, /device:TPU:0, one launch (start us, length us, event | category | flops | bytes accessed | tf_op | source)
XLA Modules:
  0.0 999.1 jit_solution(7269087679954224985)
XLA Ops:
  33.4 34.4 %collective-permute-done.2.rest_0_ = bf16[768,768]{1,0:T(8,128)(2,1)S(1)} collective-permute-done((bf16[768,768]{1,0:T(8,128)(2,1)S(1)}, bf16[768,768]{1,0:T(8,128)(2,1)S(1)}, u32[]{:S(2)}, u32[]{:S(2)}) %collective-permute-start.2) | collective-permute-done | bytes 1179680 | tf_op jit(solution)/shard_map/ppermute | solution.py:557
  70.5 20.3 %all-gather.4.cloned.1.call-done.w_ref.w_out_ref.w_up_ref.refs_1_ = bf16[768,6144]{1,0:T(8,128)(2,1)} async-done(((bf16[96,6144]{1,0:T(8,128)(2,1)}), bf16[768,6144]{1,0:T(8,128)(2,1)}) %all-gather.4.cloned.1.call-update) | async-done | bytes 9437200 | tf_op jit(solution)/shard_map/all_gather | solution.py:627
  111.4 11.7 %all-to-all-done = bf16[4,192,576]{2,1,0:T(8,128)(2,1)} async-done(((bf16[4,192,576]{2,1,0:T(8,128)(2,1)}), bf16[4,192,576]{2,1,0:T(8,128)(2,1)}, u32[]{:S(2)}, u32[]{:S(2)}) %all-to-all-start) | async-done | bytes 884768 | tf_op jit(solution)/shard_map/all_to_all | solution.py:566
  128.7 10.0 shard_map.179
  169.4 23.1 %all_to_all.80 = bf16[4,192,576]{2,1,0:T(8,128)(2,1)S(1)} all-to-all(bf16[4,192,576]{2,1,0:T(8,128)(2,1)} %get-tuple-element.84), channel_id=1, replica_groups=mesh['pair'=2,'core'=2,'half'=2,'quad'=2,'side'=2,'rest'=1] {'quad','side'}, dimensions={0} | all-to-all | bytes 1769472 | tf_op jit(solution)/shard_map/all_to_all | solution.py:566
  196.0 9.8 shard_map.182
  239.4 16.4 %all_to_all.81 = bf16[4,192,576]{2,1,0:T(8,128)(2,1)S(1)} all-to-all(bf16[4,192,576]{2,1,0:T(8,128)(2,1)} %get-tuple-element.86), channel_id=1, replica_groups=mesh['pair'=2,'core'=2,'half'=2,'quad'=2,'side'=2,'rest'=1] {'quad','side'}, dimensions={0} | all-to-all | bytes 1769472 | tf_op jit(solution)/shard_map/all_to_all | solution.py:566
  259.3 9.8 shard_map.185
  269.1 11.9 %all_to_all.82.att_ref = bf16[4,192,192]{2,1,0:T(8,128)(2,1)} all-to-all(bf16[4,192,192]{2,1,0:T(8,128)(2,1)} %bitcast.235), channel_id=1, replica_groups=mesh['pair'=2,'core'=2,'half'=2,'quad'=2,'side'=2,'rest'=1] {'quad','side'}, dimensions={0} | all-to-all | bytes 589824 | tf_op jit(solution)/shard_map/all_to_all | solution.py:566
  294.3 16.7 %all_to_all.83 = bf16[4,192,576]{2,1,0:T(8,128)(2,1)S(1)} all-to-all(bf16[4,192,576]{2,1,0:T(8,128)(2,1)} %get-tuple-element.89), channel_id=1, replica_groups=mesh['pair'=2,'core'=2,'half'=2,'quad'=2,'side'=2,'rest'=1] {'quad','side'}, dimensions={0} | all-to-all | bytes 1769472 | tf_op jit(solution)/shard_map/all_to_all | solution.py:566
  314.5 9.7 shard_map.188
  324.2 11.9 %all_to_all.84.att_ref = bf16[4,192,192]{2,1,0:T(8,128)(2,1)} all-to-all(bf16[4,192,192]{2,1,0:T(8,128)(2,1)} %bitcast.236), channel_id=1, replica_groups=mesh['pair'=2,'core'=2,'half'=2,'quad'=2,'side'=2,'rest'=1] {'quad','side'}, dimensions={0} | all-to-all | bytes 589824 | tf_op jit(solution)/shard_map/all_to_all | solution.py:566
  336.1 9.3 shard_map.189
  352.5 9.9 shard_map.190
  374.9 17.7 %shard_map.191 = (bf16[1,768,192]{2,1,0:T(8,128)(2,1)}, f32[1,768,384]{2,1,0:T(8,128)}, bf16[1,768,384]{2,1,0:T(8,128)(2,1)}) custom-call(bf16[1,768,576]{2,1,0:T(8,128)(2,1)} %bitcast.225, bf16[1,768,576]{2,1,0:T(8,128)(2,1)} %bitcast.226, bf16[1,768,576]{2,1,0:T(8,128)(2,1)} %bitcast.289, bf16[1,768,192]{2,1,0:T(8,128)(2,1)} %bitcast.231, ...), custom_call_target="tpu_custom_call" | custom-call | flops 9059696640 | bytes 7077888 | tf_op jit(solution)/shard_map/pallas_call | solution.py:241
  392.7 12.9 %collective-permute-start.15 = (bf16[1,768,384]{2,1,0:T(8,128)(2,1)}, bf16[1,768,384]{2,1,0:T(8,128)(2,1)S(1)}, u32[]{:S(2)}, u32[]{:S(2)}) collective-permute-start(bf16[1,768,384]{2,1,0:T(8,128)(2,1)} %get-tuple-element.98), channel_id=1, source_target_pairs={{0,8},{8,0},{1,9},{9,1},{2,10},{10,2},{3,11},{11,3},{4,12},{12,4},... | collective-permute-start | bytes 1769480 | tf_op jit(solution)/shard_map/ppermute | solution.py:557
  411.0 19.1 %all_to_all.85.refs_0_ = bf16[4,192,576]{2,1,0:T(8,128)(2,1)} all-to-all(bf16[4,192,576]{2,1,0:T(8,128)(2,1)} %bitcast.211), channel_id=1, replica_groups=mesh['pair'=2,'core'=2,'half'=2,'quad'=2,'side'=2,'rest'=1] {'quad','side'}, dimensions={0} | all-to-all | bytes 1769472 | tf_op jit(solution)/shard_map/all_to_all | solution.py:566
  434.9 9.9 shard_map.194
  444.8 11.1 %all_to_all.86 = bf16[4,192,192]{2,1,0:T(8,128)(2,1)} all-to-all(bf16[4,192,192]{2,1,0:T(8,128)(2,1)} %get-tuple-element.103), channel_id=1, replica_groups=mesh['pair'=2,'core'=2,'half'=2,'quad'=2,'side'=2,'rest'=1] {'quad','side'}, dimensions={0} | all-to-all | bytes 589824 | tf_op jit(solution)/shard_map/all_to_all | solution.py:566
  455.9 17.8 %shard_map.195 = (bf16[1,768,192]{2,1,0:T(8,128)(2,1)}, f32[1,768,384]{2,1,0:T(8,128)}, bf16[1,768,384]{2,1,0:T(8,128)(2,1)}) custom-call(bf16[1,768,576]{2,1,0:T(8,128)(2,1)} %bitcast.219, bf16[1,768,576]{2,1,0:T(8,128)(2,1)} %bitcast.220, bf16[1,768,576]{2,1,0:T(8,128)(2,1)} %bitcast.286, bf16[1,768,192]{2,1,0:T(8,128)(2,1)} %bitcast.234, ...), custom_call_target="tpu_custom_call" | custom-call | flops 9059696640 | bytes 7077888 | tf_op jit(solution)/shard_map/pallas_call | solution.py:241
  479.5 18.5 %all_to_all.87.refs_0_ = bf16[4,192,576]{2,1,0:T(8,128)(2,1)} all-to-all(bf16[4,192,576]{2,1,0:T(8,128)(2,1)} %bitcast.212), channel_id=1, replica_groups=mesh['pair'=2,'core'=2,'half'=2,'quad'=2,'side'=2,'rest'=1] {'quad','side'}, dimensions={0} | all-to-all | bytes 1769472 | tf_op jit(solution)/shard_map/all_to_all | solution.py:566
  513.9 10.0 %shard_map.198 = (bf16[192,3072]{1,0:T(8,128)(2,1)}, f32[192,768]{1,0:T(8,128)}, bf16[192,768]{1,0:T(8,128)(2,1)}, bf16[4,192,192]{2,1,0:T(8,128)(2,1)}, f32[4,768]{1,0:T(4,128)}, /*index=5*/f32[1,3072]{1,0:T(1,128)}) custom-call(bf16[192,768]{1,0:T(8,128)(2,1)} %broadcast_select_fusion.21.g_ref, f32[192,3072]{1,0:T(8,128)} %get-tuple-element.92.slope_ref, ...), custom_call_target="tpu_custom_call" | custom-call | flops 2038431744 | bytes 14155776 | tf_op jit(solution)/shard_map/pallas_call | solution.py:415
  537.3 17.7 %shard_map.199 = (bf16[1,768,192]{2,1,0:T(8,128)(2,1)}, f32[1,768,384]{2,1,0:T(8,128)}, bf16[1,768,384]{2,1,0:T(8,128)(2,1)}) custom-call(bf16[1,768,576]{2,1,0:T(8,128)(2,1)} %bitcast.227, bf16[1,768,576]{2,1,0:T(8,128)(2,1)} %bitcast.228, bf16[1,768,576]{2,1,0:T(8,128)(2,1)} %bitcast.290, bf16[1,768,192]{2,1,0:T(8,128)(2,1)} %bitcast.35.refs_3_, ...), custom_call_target="tpu_custom_call" | custom-call | flops 9059696640 | bytes 7077888 | tf_op jit(solution)/shard_map/pallas_call | solution.py:241
  595.4 10.0 shard_map.203
  639.4 17.7 %shard_map.206 = (bf16[1,768,192]{2,1,0:T(8,128)(2,1)}, f32[1,768,384]{2,1,0:T(8,128)}, bf16[1,768,384]{2,1,0:T(8,128)(2,1)}) custom-call(bf16[1,768,576]{2,1,0:T(8,128)(2,1)} %bitcast.221, bf16[1,768,576]{2,1,0:T(8,128)(2,1)} %bitcast.222, bf16[1,768,576]{2,1,0:T(8,128)(2,1)} %bitcast.287, bf16[1,768,192]{2,1,0:T(8,128)(2,1)} %bitcast.216, ...), custom_call_target="tpu_custom_call" | custom-call | flops 9059696640 | bytes 7077888 | tf_op jit(solution)/shard_map/pallas_call | solution.py:241
  713.9 17.4 %collective-permute-done.32.two_ref = bf16[272,2304]{1,0:T(8,128)(2,1)} collective-permute-done((bf16[272,2304]{1,0:T(8,128)(2,1)}, bf16[272,2304]{1,0:T(8,128)(2,1)}, u32[]{:S(2)}, u32[]{:S(2)}) %collective-permute-start.32) | collective-permute-done | bytes 1253408 | tf_op jit(solution)/shard_map/ppermute | solution.py:557
  755.3 13.3 %collective-permute-done.41 = bf16[768,768]{1,0:T(8,128)(2,1)} collective-permute-done((bf16[768,768]{1,0:T(8,128)(2,1)}, bf16[768,768]{1,0:T(8,128)(2,1)}, u32[]{:S(2)}, u32[]{:S(2)}) %collective-permute-start.41) | collective-permute-done | bytes 1179680 | tf_op jit(solution)/shard_map/ppermute | solution.py:725
  800.6 36.2 %collective-permute-done.29.rest_1_ = bf16[192,768]{1,0:T(8,128)(2,1)S(1)} collective-permute-done((bf16[192,768]{1,0:T(8,128)(2,1)S(1)}, bf16[192,768]{1,0:T(8,128)(2,1)S(1)}, u32[]{:S(2)}, u32[]{:S(2)}) %collective-permute-start.29) | collective-permute-done | bytes 294944 | tf_op jit(solution)/shard_map/ppermute | solution.py:557
  864.7 18.2 %collective-permute-done.45.two_ref = bf16[192,3072]{1,0:T(8,128)(2,1)S(1)} collective-permute-done((bf16[192,3072]{1,0:T(8,128)(2,1)S(1)}, bf16[192,3072]{1,0:T(8,128)(2,1)S(1)}, u32[]{:S(2)}, u32[]{:S(2)}) %collective-permute-start.45) | collective-permute-done | bytes 1179680 | tf_op jit(solution)/shard_map/ppermute | solution.py:725
  893.8 14.3 %collective-permute-done.43.two_ref = bf16[272,2304]{1,0:T(8,128)(2,1)S(1)} collective-permute-done((bf16[272,2304]{1,0:T(8,128)(2,1)}, bf16[272,2304]{1,0:T(8,128)(2,1)S(1)}, u32[]{:S(2)}, u32[]{:S(2)}) %collective-permute-start.43) | collective-permute-done | bytes 1253408 | tf_op jit(solution)/shard_map/ppermute | solution.py:725
  926.3 23.5 %collective-permute-done.50 = bf16[192,3072]{1,0:T(8,128)(2,1)S(1)} collective-permute-done((bf16[192,3072]{1,0:T(8,128)(2,1)}, bf16[192,3072]{1,0:T(8,128)(2,1)S(1)}, u32[]{:S(2)}, u32[]{:S(2)}) %collective-permute-start.50) | collective-permute-done | bytes 1179680 | tf_op jit(solution)/shard_map/ppermute | solution.py:725
  962.0 21.1 %collective-permute-done.51 = bf16[272,2304]{1,0:T(8,128)(2,1)S(1)} collective-permute-done((bf16[272,2304]{1,0:T(8,128)(2,1)}, bf16[272,2304]{1,0:T(8,128)(2,1)S(1)}, u32[]{:S(2)}, u32[]{:S(2)}) %collective-permute-start.51) | collective-permute-done | bytes 1253408 | tf_op jit(solution)/shard_map/ppermute | solution.py:725
  (546 shorter events, 472.2 us)
Async XLA Ops:
  7.2 83.6 %all-gather.4.cloned.1.call-start = ((), (), s32[]{:S(2)}) async-start(), calls=%async_computation.16 | async-start | bytes 10616832 | tf_op jit(solution)/shard_map/all_gather | solution.py:627
  14.3 151.0 %all-gather.6.cloned.1.call-start = ((), (), s32[]{:S(2)}) async-start(), calls=%async_computation.17 | async-start | bytes 10616832 | tf_op jit(solution)/shard_map/all_gather | solution.py:627
  15.1 197.2 %all-gather.8.cloned.1.call-start = ((), (), s32[]{:S(2)}) async-start(), calls=%async_computation.18 | async-start | bytes 5308416 | tf_op jit(solution)/shard_map/all_gather | solution.py:644
  28.0 39.9 %collective-permute-start.2 = (bf16[768,768]{1,0:T(8,128)(2,1)S(1)}, bf16[768,768]{1,0:T(8,128)(2,1)S(1)}, u32[]{:S(2)}, u32[]{:S(2)}) collective-permute-start(bf16[768,768]{1,0:T(8,128)(2,1)S(1)} %constant_dynamic-slice_fusion.32), channel_id=1, source_target_pairs={{0,1},{1,0},{2,3},{3,2},{4,5},{5,4},{6,7},{7,6},{8,9},{9,8},{10,11... | collective-permute-start | bytes 3538952 | tf_op jit(solution)/shard_map/ppermute | solution.py:557
  94.9 28.3 %all-to-all-start = ((bf16[4,192,576]{2,1,0:T(8,128)(2,1)}), bf16[4,192,576]{2,1,0:T(8,128)(2,1)}, u32[]{:S(2)}, u32[]{:S(2)}) async-start(bf16[4,192,576]{2,1,0:T(8,128)(2,1)} %get-tuple-element.82), calls=%async_computation | async-start | bytes 1966080 | tf_op jit(solution)/shard_map/all_to_all | solution.py:566
  530.4 51.3 %collective-permute-start.19 = (bf16[1536,768]{1,0:T(8,128)(2,1)}, bf16[1536,768]{1,0:T(8,128)(2,1)S(1)}, u32[]{:S(2)}, u32[]{:S(2)}) collective-permute-start(bf16[1536,768]{1,0:T(8,128)(2,1)} %convolution_convert_fusion.11.refs_5_), channel_id=1, source_target_pairs={{0,8},{8,0},{1,9},{9,1},{2,10},{10,2},{3,11},{11,3},{4,12},{12,4},... | collective-permute-start | bytes 7077896 | tf_op jit(solution)/shard_map/ppermute | solution.py:557
  571.1 49.1 %collective-permute-start.21 = (bf16[384,3072]{1,0:T(8,128)(2,1)}, bf16[384,3072]{1,0:T(8,128)(2,1)}, u32[]{:S(2)}, u32[]{:S(2)}) collective-permute-start(bf16[384,3072]{1,0:T(8,128)(2,1)} %convolution_convert_fusion.7.refs_7_), channel_id=1, source_target_pairs={{0,8},{8,0},{1,9},{9,1},{2,10},{10,2},{3,11},{11,3},{4,12},{12,4},... | collective-permute-start | bytes 7077896 | tf_op jit(solution)/shard_map/ppermute | solution.py:557
  587.9 44.2 %collective-permute-start.20 = (bf16[768,768]{1,0:T(8,128)(2,1)}, bf16[768,768]{1,0:T(8,128)(2,1)}, u32[]{:S(2)}, u32[]{:S(2)}) collective-permute-start(bf16[768,768]{1,0:T(8,128)(2,1)} %get-tuple-element.118.refs_5_), channel_id=1, source_target_pairs={{0,1},{1,0},{2,3},{3,2},{4,5},{5,4},{6,7},{7,6},{8,9},{9,8},{10,11... | collective-permute-start | bytes 3538952 | tf_op jit(solution)/shard_map/ppermute | solution.py:557
  612.2 56.7 %collective-permute-start.25 = (bf16[544,2304]{1,0:T(8,128)(2,1)}, bf16[544,2304]{1,0:T(8,128)(2,1)S(1)}, u32[]{:S(2)}, u32[]{:S(2)}) collective-permute-start(bf16[544,2304]{1,0:T(8,128)(2,1)} %bitcast.44.refs_8_), channel_id=1, source_target_pairs={{0,8},{8,0},{1,9},{9,1},{2,10},{10,2},{3,11},{11,3},{4,12},{12,4},... | collective-permute-start | bytes 7520264 | tf_op jit(solution)/shard_map/ppermute | solution.py:557
  614.7 80.0 %collective-permute-start.26 = (bf16[1536,768]{1,0:T(8,128)(2,1)}, bf16[1536,768]{1,0:T(8,128)(2,1)}, u32[]{:S(2)}, u32[]{:S(2)}) collective-permute-start(bf16[1536,768]{1,0:T(8,128)(2,1)} %convolution_convert_fusion.9.refs_10_), channel_id=1, source_target_pairs={{0,8},{8,0},{1,9},{9,1},{2,10},{10,2},{3,11},{11,3},{4,12},{12,4},... | collective-permute-start | bytes 7077896 | tf_op jit(solution)/shard_map/ppermute | solution.py:557
  617.3 81.8 %collective-permute-start.27 = (bf16[384,3072]{1,0:T(8,128)(2,1)}, bf16[384,3072]{1,0:T(8,128)(2,1)}, u32[]{:S(2)}, u32[]{:S(2)}) collective-permute-start(bf16[384,3072]{1,0:T(8,128)(2,1)} %convolution_convert_fusion.3.refs_12_), channel_id=1, source_target_pairs={{0,8},{8,0},{1,9},{9,1},{2,10},{10,2},{3,11},{11,3},{4,12},{12,4},... | collective-permute-start | bytes 7077896 | tf_op jit(solution)/shard_map/ppermute | solution.py:557
  625.8 31.4 %collective-permute-start.24 = (bf16[192,3072]{1,0:T(8,128)(2,1)}, bf16[192,3072]{1,0:T(8,128)(2,1)S(1)}, u32[]{:S(2)}, u32[]{:S(2)}) collective-permute-start(bf16[192,3072]{1,0:T(8,128)(2,1)} %get-tuple-element.124.refs_6_), channel_id=1, source_target_pairs={{0,1},{1,0},{2,3},{3,2},{4,5},{5,4},{6,7},{7,6},{8,9},{9,8},{10,11... | collective-permute-start | bytes 3538952 | tf_op jit(solution)/shard_map/ppermute | solution.py:557
  635.6 28.6 %collective-permute-start.23 = (bf16[768,768]{1,0:T(8,128)(2,1)}, bf16[768,768]{1,0:T(8,128)(2,1)S(1)}, u32[]{:S(2)}, u32[]{:S(2)}) collective-permute-start(bf16[768,768]{1,0:T(8,128)(2,1)} %shard_map.204.refs_5_.one_ref), channel_id=1, source_target_pairs={{0,2},{6,4},{1,3},{7,5},{8,10},{14,12},{9,11},{15,13},{16,18},{22,... | collective-permute-start | bytes 3538952 | tf_op jit(solution)/shard_map/ppermute | solution.py:725
  687.5 46.9 %collective-permute-start.36 = (bf16[192,3072]{1,0:T(8,128)(2,1)S(1)}, bf16[192,3072]{1,0:T(8,128)(2,1)}, u32[]{:S(2)}, u32[]{:S(2)}) collective-permute-start(bf16[192,3072]{1,0:T(8,128)(2,1)S(1)} %copy-done.8), channel_id=1, source_target_pairs={{0,2},{6,4},{1,3},{7,5},{8,10},{14,12},{9,11},{15,13},{16,18},{22,... | collective-permute-start | bytes 3538952 | tf_op jit(solution)/shard_map/ppermute | solution.py:725
  692.8 44.5 %collective-permute-start.35 = (bf16[768,768]{1,0:T(8,128)(2,1)S(1)}, bf16[768,768]{1,0:T(8,128)(2,1)}, u32[]{:S(2)}, u32[]{:S(2)}) collective-permute-start(bf16[768,768]{1,0:T(8,128)(2,1)S(1)} %copy-done.9), channel_id=1, source_target_pairs={{2,4},{4,2},{3,5},{5,3},{10,12},{12,10},{11,13},{13,11},{18,20},{2... | collective-permute-start | bytes 3538952 | tf_op jit(solution)/shard_map/ppermute | solution.py:725
  703.2 28.2 %collective-permute-start.32 = (bf16[272,2304]{1,0:T(8,128)(2,1)}, bf16[272,2304]{1,0:T(8,128)(2,1)}, u32[]{:S(2)}, u32[]{:S(2)}) collective-permute-start(bf16[272,2304]{1,0:T(8,128)(2,1)} %get-tuple-element.137.rest_2_), channel_id=1, source_target_pairs={{0,1},{1,0},{2,3},{3,2},{4,5},{5,4},{6,7},{7,6},{8,9},{9,8},{10,11... | collective-permute-start | bytes 3760136 | tf_op jit(solution)/shard_map/ppermute | solution.py:557
  713.9 57.7 %collective-permute-start.30 = (bf16[544,2304]{1,0:T(8,128)(2,1)}, bf16[544,2304]{1,0:T(8,128)(2,1)}, u32[]{:S(2)}, u32[]{:S(2)}) collective-permute-start(bf16[544,2304]{1,0:T(8,128)(2,1)} %bitcast.60.rest_0_), channel_id=1, source_target_pairs={{0,8},{8,0},{1,9},{9,1},{2,10},{10,2},{3,11},{11,3},{4,12},{12,4},... | collective-permute-start | bytes 7520264 | tf_op jit(solution)/shard_map/ppermute | solution.py:557
  742.4 39.4 %collective-permute-start.33 = (bf16[272,2304]{1,0:T(8,128)(2,1)S(1)}, bf16[272,2304]{1,0:T(8,128)(2,1)}, u32[]{:S(2)}, u32[]{:S(2)}) collective-permute-start(bf16[272,2304]{1,0:T(8,128)(2,1)S(1)} %copy-done.4), channel_id=1, source_target_pairs={{0,2},{6,4},{1,3},{7,5},{8,10},{14,12},{9,11},{15,13},{16,18},{22,... | collective-permute-start | bytes 3760136 | tf_op jit(solution)/shard_map/ppermute | solution.py:725
  749.1 29.2 %collective-permute-start.34 = (bf16[768,768]{1,0:T(8,128)(2,1)}, bf16[768,768]{1,0:T(8,128)(2,1)}, u32[]{:S(2)}, u32[]{:S(2)}) collective-permute-start(bf16[768,768]{1,0:T(8,128)(2,1)} %get-tuple-element.140.refs_5_), channel_id=1, source_target_pairs={{0,1},{1,0},{2,3},{3,2},{4,5},{5,4},{6,7},{7,6},{8,9},{9,8},{10,11... | collective-permute-start | bytes 3538952 | tf_op jit(solution)/shard_map/ppermute | solution.py:557
  749.8 35.0 %collective-permute-start.40 = (bf16[192,3072]{1,0:T(8,128)(2,1)}, bf16[192,3072]{1,0:T(8,128)(2,1)}, u32[]{:S(2)}, u32[]{:S(2)}) collective-permute-start(bf16[192,3072]{1,0:T(8,128)(2,1)} %shard_map.216.rest_0_.one_ref), channel_id=1, source_target_pairs={{2,4},{4,2},{3,5},{5,3},{10,12},{12,10},{11,13},{13,11},{18,20},{2... | collective-permute-start | bytes 3538952 | tf_op jit(solution)/shard_map/ppermute | solution.py:725
  768.6 30.8 %collective-permute-start.39 = (bf16[192,3072]{1,0:T(8,128)(2,1)}, bf16[192,3072]{1,0:T(8,128)(2,1)}, u32[]{:S(2)}, u32[]{:S(2)}) collective-permute-start(bf16[192,3072]{1,0:T(8,128)(2,1)} %get-tuple-element.142.refs_7_), channel_id=1, source_target_pairs={{0,1},{1,0},{2,3},{3,2},{4,5},{5,4},{6,7},{7,6},{8,9},{9,8},{10,11... | collective-permute-start | bytes 3538952 | tf_op jit(solution)/shard_map/ppermute | solution.py:557
  787.8 52.6 %collective-permute-start.42 = (bf16[192,3072]{1,0:T(8,128)(2,1)}, bf16[192,3072]{1,0:T(8,128)(2,1)}, u32[]{:S(2)}, u32[]{:S(2)}) collective-permute-start(bf16[192,3072]{1,0:T(8,128)(2,1)} %shard_map.220.rest_0_), channel_id=1, source_target_pairs={{2,0},{4,6},{3,1},{5,7},{10,8},{12,14},{11,9},{13,15},{18,16},{20,... | collective-permute-start | bytes 3538952 | tf_op jit(solution)/shard_map/ppermute | solution.py:725
  789.3 57.2 %collective-permute-start.37 = (bf16[272,2304]{1,0:T(8,128)(2,1)S(1)}, bf16[272,2304]{1,0:T(8,128)(2,1)S(1)}, u32[]{:S(2)}, u32[]{:S(2)}) collective-permute-start(bf16[272,2304]{1,0:T(8,128)(2,1)S(1)} %copy-done.5), channel_id=1, source_target_pairs={{2,4},{4,2},{3,5},{5,3},{10,12},{12,10},{11,13},{13,11},{18,20},{2... | collective-permute-start | bytes 3760136 | tf_op jit(solution)/shard_map/ppermute | solution.py:725
  790.2 52.8 %collective-permute-start.38 = (bf16[768,768]{1,0:T(8,128)(2,1)S(1)}, bf16[768,768]{1,0:T(8,128)(2,1)}, u32[]{:S(2)}, u32[]{:S(2)}) collective-permute-start(bf16[768,768]{1,0:T(8,128)(2,1)S(1)} %copy-done.10), channel_id=1, source_target_pairs={{0,2},{6,4},{1,3},{7,5},{8,10},{14,12},{9,11},{15,13},{16,18},{22,... | collective-permute-start | bytes 3538952 | tf_op jit(solution)/shard_map/ppermute | solution.py:725
  798.7 38.1 %collective-permute-start.29 = (bf16[192,768]{1,0:T(8,128)(2,1)S(1)}, bf16[192,768]{1,0:T(8,128)(2,1)S(1)}, u32[]{:S(2)}, u32[]{:S(2)}) collective-permute-start(bf16[192,768]{1,0:T(8,128)(2,1)S(1)} %get-tuple-element.160), channel_id=1, source_target_pairs={{0,4},{4,0},{1,5},{5,1},{2,6},{6,2},{3,7},{7,3},{8,12},{12,8},{9,1... | collective-permute-start | bytes 884744 | tf_op jit(solution)/shard_map/ppermute | solution.py:557
  799.5 58.9 %collective-permute-start.31 = (bf16[272,2304]{1,0:T(8,128)(2,1)S(1)}, bf16[272,2304]{1,0:T(8,128)(2,1)S(1)}, u32[]{:S(2)}, u32[]{:S(2)}) collective-permute-start(bf16[272,2304]{1,0:T(8,128)(2,1)S(1)} %copy-done.3), channel_id=1, source_target_pairs={{0,1},{1,0},{2,3},{3,2},{4,5},{5,4},{6,7},{7,6},{8,9},{9,8},{10,11... | collective-permute-start | bytes 3760136 | tf_op jit(solution)/shard_map/ppermute | solution.py:557
  850.6 36.3 %collective-permute-start.46 = (bf16[272,2304]{1,0:T(8,128)(2,1)}, bf16[272,2304]{1,0:T(8,128)(2,1)S(1)}, u32[]{:S(2)}, u32[]{:S(2)}) collective-permute-start(bf16[272,2304]{1,0:T(8,128)(2,1)} %shard_map.223.rest_0_), channel_id=1, source_target_pairs={{2,0},{4,6},{3,1},{5,7},{10,8},{12,14},{11,9},{13,15},{18,16},{20,... | collective-permute-start | bytes 3760136 | tf_op jit(solution)/shard_map/ppermute | solution.py:725
  851.9 31.0 %collective-permute-start.45 = (bf16[192,3072]{1,0:T(8,128)(2,1)S(1)}, bf16[192,3072]{1,0:T(8,128)(2,1)S(1)}, u32[]{:S(2)}, u32[]{:S(2)}) collective-permute-start(bf16[192,3072]{1,0:T(8,128)(2,1)S(1)} %copy-done.15), channel_id=1, source_target_pairs={{0,2},{6,4},{1,3},{7,5},{8,10},{14,12},{9,11},{15,13},{16,18},{22,... | collective-permute-start | bytes 3538952 | tf_op jit(solution)/shard_map/ppermute | solution.py:725
  856.6 31.5 %collective-permute-start.44 = (bf16[768,768]{1,0:T(8,128)(2,1)S(1)}, bf16[768,768]{1,0:T(8,128)(2,1)}, u32[]{:S(2)}, u32[]{:S(2)}) collective-permute-start(bf16[768,768]{1,0:T(8,128)(2,1)S(1)} %copy-done.16), channel_id=1, source_target_pairs={{2,4},{4,2},{3,5},{5,3},{10,12},{12,10},{11,13},{13,11},{18,20},{2... | collective-permute-start | bytes 3538952 | tf_op jit(solution)/shard_map/ppermute | solution.py:725
  862.4 45.8 %collective-permute-start.43 = (bf16[272,2304]{1,0:T(8,128)(2,1)}, bf16[272,2304]{1,0:T(8,128)(2,1)S(1)}, u32[]{:S(2)}, u32[]{:S(2)}) collective-permute-start(bf16[272,2304]{1,0:T(8,128)(2,1)} %shard_map.224.rest_0_.one_ref), channel_id=1, source_target_pairs={{0,2},{6,4},{1,3},{7,5},{8,10},{14,12},{9,11},{15,13},{16,18},{22,... | collective-permute-start | bytes 3760136 | tf_op jit(solution)/shard_map/ppermute | solution.py:725
  926.2 31.2 %collective-permute-start.54 = (bf16[768,768]{1,0:T(8,128)(2,1)S(1)}, bf16[768,768]{1,0:T(8,128)(2,1)}, u32[]{:S(2)}, u32[]{:S(2)}) collective-permute-start(bf16[768,768]{1,0:T(8,128)(2,1)S(1)} %get-tuple-element.154), channel_id=1, source_target_pairs={{0,8},{8,0},{1,9},{9,1},{2,10},{10,2},{3,11},{11,3},{4,12},{12,4},... | collective-permute-start | bytes 3538952 | tf_op jit(solution)/shard_map/ppermute | solution.py:557
  955.2 27.9 %collective-permute-start.51 = (bf16[272,2304]{1,0:T(8,128)(2,1)}, bf16[272,2304]{1,0:T(8,128)(2,1)S(1)}, u32[]{:S(2)}, u32[]{:S(2)}) collective-permute-start(bf16[272,2304]{1,0:T(8,128)(2,1)} %shard_map.229), channel_id=1, source_target_pairs={{2,0},{4,6},{3,1},{5,7},{10,8},{12,14},{11,9},{13,15},{18,16},{20,... | collective-permute-start | bytes 3760136 | tf_op jit(solution)/shard_map/ppermute | solution.py:725
  (153 other events, 1176.4 us)
Sparse Core Ops, SparseCore 0:
  14.4 76.2 all-gather.3
  92.3 72.9 all-gather.5
  167.5 41.7 all-gather.7

commit v10 on v9

--- a/solution.py
+++ b/solution.py
@@ -910,7 +910,7 @@
         for item, mark in blocks
     ]
     if line:
-        sums = line_sums((down_two, up_two), sides, {4: placed[1:]})
+        sums = line_sums((down_two, up_two), sides, {2: placed[1:]})
     else:
         sums = line_sum(down_two, up_two, *(item() for item in sides))
     down_two, up_two, rest_two, down_one, up_one, rest_one = sums

time: 1010 us -> 983 us (0.973)
  waiting for transfers between devices: 278 us -> 251 us
    ppermute x33, waiting for transfers between devices: 116 us -> 83.8 us  [swap(): return lax.ppermute(block, axis, [(0, 1), (1, 0)])]
    unnamed x261 -> x265, local copies, waits for them, and re-layouts: 37.5 us -> 37.5 us
  transfers between devices with their start and end apart: 66 -> 66, of which waited for: 31 -> 34; matrix products, arithmetic and copies ran while one was open for 10% -> 10% of each run, Pallas kernels for 19% -> 19%
where the time goes in v10:
time: 983 us; the launch traced here: 972 us
  Pallas kernels  315 us (32%)
  waiting for transfers between devices  251 us (26%)
  blocking collectives  129 us (13%)
  starting transfers between devices  122 us (12%)
  local copies, waits for them, and re-layouts  59.6 us (6%)
  other arithmetic  51.7 us (5%)
  matrix products  28.7 us (3%)
  between operations  15.5 us (2%)
    all_to_all x8, blocking collectives, spread(): return lax.all_to_all(block, ('quad', 'side'), 0, 0, tiled=True)  129 us
    ppermute x18, waiting for transfers between devices, line_hop(): return lax.ppermute(block, ('half', 'quad'), pairs)  104 us
    ppermute x33, waiting for transfers between devices, swap(): return lax.ppermute(block, axis, [(0, 1), (1, 0)])  83.8 us
    pallas_call x4, Pallas kernels, attend_backward(): call(body, (jax.ShapeDtypeStruct((clips, queries, span), BF16), jax.Shape...  70.9 us
    pallas_call x18, Pallas kernels, add_after(): call(add_body, jax.ShapeDtypeStruct((rows, wide), BF16), grid=(rows // bl...  57.1 us
    ppermute x18, starting transfers between devices, line_hop(): return lax.ppermute(block, ('half', 'quad'), pairs)  47.6 us
    pallas_call x4, Pallas kernels, feed_backward(): call(feed_back_body, (jax.ShapeDtypeStruct((rows, hidden), BF16), jax.Sha...  39.8 us
    pallas_call x4, Pallas kernels, attend_forward(): call(body, (jax.ShapeDtypeStruct((clips, queries, span), BF16), jax.Shape...  39.3 us
  transfers between devices with their start and end apart: 66, of which 34 were waited for; matrix products, arithmetic and copies ran while one was open for 10% of the time, Pallas kernels for 19%

profile of v10, /device:TPU:0, one launch (start us, length us, event | category | flops | bytes accessed | tf_op | source)
XLA Modules:
  0.0 971.6 jit_solution(7991480018204472302)
XLA Ops:
  33.4 34.4 %collective-permute-done.2.rest_0_ = bf16[768,768]{1,0:T(8,128)(2,1)S(1)} collective-permute-done((bf16[768,768]{1,0:T(8,128)(2,1)S(1)}, bf16[768,768]{1,0:T(8,128)(2,1)S(1)}, u32[]{:S(2)}, u32[]{:S(2)}) %collective-permute-start.2) | collective-permute-done | bytes 1179680 | tf_op jit(solution)/shard_map/ppermute | solution.py:557
  70.5 20.3 %all-gather.4.cloned.1.call-done.w_ref.w_out_ref.w_up_ref.refs_1_ = bf16[768,6144]{1,0:T(8,128)(2,1)} async-done(((bf16[96,6144]{1,0:T(8,128)(2,1)}), bf16[768,6144]{1,0:T(8,128)(2,1)}) %all-gather.4.cloned.1.call-update) | async-done | bytes 9437200 | tf_op jit(solution)/shard_map/all_gather | solution.py:627
  111.4 11.7 %all-to-all-done = bf16[4,192,576]{2,1,0:T(8,128)(2,1)} async-done(((bf16[4,192,576]{2,1,0:T(8,128)(2,1)}), bf16[4,192,576]{2,1,0:T(8,128)(2,1)}, u32[]{:S(2)}, u32[]{:S(2)}) %all-to-all-start) | async-done | bytes 884768 | tf_op jit(solution)/shard_map/all_to_all | solution.py:566
  128.7 10.0 %shard_map.179 = (bf16[1,768,192]{2,1,0:T(8,128)(2,1)}, f32[1,3,768]{2,1,0:T(4,128)}) custom-call(bf16[1,768,576]{2,1,0:T(8,128)(2,1)} %bitcast.14.refs_0_.refs_1_, bf16[1,768,576]{2,1,0:T(8,128)(2,1)} %bitcast.14.refs_0_.refs_1_, bf16[1,768,576]{2,1,0:T(8,128)(2,1)} %bitcast.291), custom_call_target="tpu_custom_call" | custom-call | flops 3623878656 | bytes 3538944 | tf_op jit(solution)/shard_map/pallas_call | solution.py:143
  169.4 23.1 %all_to_all.80 = bf16[4,192,576]{2,1,0:T(8,128)(2,1)S(1)} all-to-all(bf16[4,192,576]{2,1,0:T(8,128)(2,1)} %get-tuple-element.84), channel_id=1, replica_groups=mesh['pair'=2,'core'=2,'half'=2,'quad'=2,'side'=2,'rest'=1] {'quad','side'}, dimensions={0} | all-to-all | bytes 1769472 | tf_op jit(solution)/shard_map/all_to_all | solution.py:566
  196.0 9.8 %shard_map.182 = (bf16[1,768,192]{2,1,0:T(8,128)(2,1)}, f32[1,3,768]{2,1,0:T(4,128)}) custom-call(bf16[1,768,576]{2,1,0:T(8,128)(2,1)} %bitcast.229, bf16[1,768,576]{2,1,0:T(8,128)(2,1)} %bitcast.230, bf16[1,768,576]{2,1,0:T(8,128)(2,1)} %bitcast.292), custom_call_target="tpu_custom_call" | custom-call | flops 3623878656 | bytes 3538944 | tf_op jit(solution)/shard_map/pallas_call | solution.py:143
  239.4 16.4 %all_to_all.81 = bf16[4,192,576]{2,1,0:T(8,128)(2,1)S(1)} all-to-all(bf16[4,192,576]{2,1,0:T(8,128)(2,1)} %get-tuple-element.86), channel_id=1, replica_groups=mesh['pair'=2,'core'=2,'half'=2,'quad'=2,'side'=2,'rest'=1] {'quad','side'}, dimensions={0} | all-to-all | bytes 1769472 | tf_op jit(solution)/shard_map/all_to_all | solution.py:566
  259.3 9.7 %shard_map.185 = (bf16[1,768,192]{2,1,0:T(8,128)(2,1)}, f32[1,3,768]{2,1,0:T(4,128)}) custom-call(bf16[1,768,576]{2,1,0:T(8,128)(2,1)} %bitcast.217, bf16[1,768,576]{2,1,0:T(8,128)(2,1)} %bitcast.218, bf16[1,768,576]{2,1,0:T(8,128)(2,1)} %bitcast.285), custom_call_target="tpu_custom_call" | custom-call | flops 3623878656 | bytes 3538944 | tf_op jit(solution)/shard_map/pallas_call | solution.py:143
  269.1 11.9 %all_to_all.82.att_ref = bf16[4,192,192]{2,1,0:T(8,128)(2,1)} all-to-all(bf16[4,192,192]{2,1,0:T(8,128)(2,1)} %bitcast.235), channel_id=1, replica_groups=mesh['pair'=2,'core'=2,'half'=2,'quad'=2,'side'=2,'rest'=1] {'quad','side'}, dimensions={0} | all-to-all | bytes 589824 | tf_op jit(solution)/shard_map/all_to_all | solution.py:566
  294.3 16.7 %all_to_all.83 = bf16[4,192,576]{2,1,0:T(8,128)(2,1)S(1)} all-to-all(bf16[4,192,576]{2,1,0:T(8,128)(2,1)} %get-tuple-element.89), channel_id=1, replica_groups=mesh['pair'=2,'core'=2,'half'=2,'quad'=2,'side'=2,'rest'=1] {'quad','side'}, dimensions={0} | all-to-all | bytes 1769472 | tf_op jit(solution)/shard_map/all_to_all | solution.py:566
  314.5 9.8 %shard_map.188 = (bf16[1,768,192]{2,1,0:T(8,128)(2,1)}, f32[1,3,768]{2,1,0:T(4,128)}) custom-call(bf16[1,768,576]{2,1,0:T(8,128)(2,1)} %bitcast.223, bf16[1,768,576]{2,1,0:T(8,128)(2,1)} %bitcast.224, bf16[1,768,576]{2,1,0:T(8,128)(2,1)} %bitcast.288), custom_call_target="tpu_custom_call" | custom-call | flops 3623878656 | bytes 3538944 | tf_op jit(solution)/shard_map/pallas_call | solution.py:143
  324.3 11.9 %all_to_all.84.att_ref = bf16[4,192,192]{2,1,0:T(8,128)(2,1)} all-to-all(bf16[4,192,192]{2,1,0:T(8,128)(2,1)} %bitcast.236), channel_id=1, replica_groups=mesh['pair'=2,'core'=2,'half'=2,'quad'=2,'side'=2,'rest'=1] {'quad','side'}, dimensions={0} | all-to-all | bytes 589824 | tf_op jit(solution)/shard_map/all_to_all | solution.py:566
  336.1 9.3 shard_map.189
  352.5 9.9 %shard_map.190 = (bf16[192,3072]{1,0:T(8,128)(2,1)}, f32[192,768]{1,0:T(8,128)}, bf16[192,768]{1,0:T(8,128)(2,1)}, bf16[4,192,192]{2,1,0:T(8,128)(2,1)}, f32[4,768]{1,0:T(4,128)}, /*index=5*/f32[1,3072]{1,0:T(1,128)}) custom-call(bf16[192,768]{1,0:T(8,128)(2,1)} %bitcast_select_fusion.g_ref, f32[192,3072]{1,0:T(8,128)} %get-tuple-element.92.slope_ref, ...), custom_call_target="tpu_custom_call" | custom-call | flops 2038431744 | bytes 14155776 | tf_op jit(solution)/shard_map/pallas_call | solution.py:415
  374.9 17.7 %shard_map.191 = (bf16[1,768,192]{2,1,0:T(8,128)(2,1)}, f32[1,768,384]{2,1,0:T(8,128)}, bf16[1,768,384]{2,1,0:T(8,128)(2,1)}) custom-call(bf16[1,768,576]{2,1,0:T(8,128)(2,1)} %bitcast.225, bf16[1,768,576]{2,1,0:T(8,128)(2,1)} %bitcast.226, bf16[1,768,576]{2,1,0:T(8,128)(2,1)} %bitcast.289, bf16[1,768,192]{2,1,0:T(8,128)(2,1)} %bitcast.231, ...), custom_call_target="tpu_custom_call" | custom-call | flops 9059696640 | bytes 7077888 | tf_op jit(solution)/shard_map/pallas_call | solution.py:241
  392.7 12.9 %collective-permute-start.15 = (bf16[1,768,384]{2,1,0:T(8,128)(2,1)}, bf16[1,768,384]{2,1,0:T(8,128)(2,1)S(1)}, u32[]{:S(2)}, u32[]{:S(2)}) collective-permute-start(bf16[1,768,384]{2,1,0:T(8,128)(2,1)} %get-tuple-element.98), channel_id=1, source_target_pairs={{0,8},{8,0},{1,9},{9,1},{2,10},{10,2},{3,11},{11,3},{4,12},{12,4},... | collective-permute-start | bytes 1769480 | tf_op jit(solution)/shard_map/ppermute | solution.py:557
  411.0 19.1 %all_to_all.85.refs_0_ = bf16[4,192,576]{2,1,0:T(8,128)(2,1)} all-to-all(bf16[4,192,576]{2,1,0:T(8,128)(2,1)} %bitcast.211), channel_id=1, replica_groups=mesh['pair'=2,'core'=2,'half'=2,'quad'=2,'side'=2,'rest'=1] {'quad','side'}, dimensions={0} | all-to-all | bytes 1769472 | tf_op jit(solution)/shard_map/all_to_all | solution.py:566
  434.8 9.9 %shard_map.194 = (bf16[192,3072]{1,0:T(8,128)(2,1)}, f32[192,768]{1,0:T(8,128)}, bf16[192,768]{1,0:T(8,128)(2,1)}, bf16[4,192,192]{2,1,0:T(8,128)(2,1)}, f32[4,768]{1,0:T(4,128)}, /*index=5*/f32[1,3072]{1,0:T(1,128)}) custom-call(bf16[192,768]{1,0:T(8,128)(2,1)} %get-tuple-element.100.g_ref, f32[192,3072]{1,0:T(8,128)} %get-tuple-element.101.slope_ref, ...), custom_call_target="tpu_custom_call" | custom-call | flops 2038431744 | bytes 14155776 | tf_op jit(solution)/shard_map/pallas_call | solution.py:415
  444.8 11.1 %all_to_all.86 = bf16[4,192,192]{2,1,0:T(8,128)(2,1)} all-to-all(bf16[4,192,192]{2,1,0:T(8,128)(2,1)} %get-tuple-element.103), channel_id=1, replica_groups=mesh['pair'=2,'core'=2,'half'=2,'quad'=2,'side'=2,'rest'=1] {'quad','side'}, dimensions={0} | all-to-all | bytes 589824 | tf_op jit(solution)/shard_map/all_to_all | solution.py:566
  455.9 17.8 %shard_map.195 = (bf16[1,768,192]{2,1,0:T(8,128)(2,1)}, f32[1,768,384]{2,1,0:T(8,128)}, bf16[1,768,384]{2,1,0:T(8,128)(2,1)}) custom-call(bf16[1,768,576]{2,1,0:T(8,128)(2,1)} %bitcast.219, bf16[1,768,576]{2,1,0:T(8,128)(2,1)} %bitcast.220, bf16[1,768,576]{2,1,0:T(8,128)(2,1)} %bitcast.286, bf16[1,768,192]{2,1,0:T(8,128)(2,1)} %bitcast.234, ...), custom_call_target="tpu_custom_call" | custom-call | flops 9059696640 | bytes 7077888 | tf_op jit(solution)/shard_map/pallas_call | solution.py:241
  479.5 18.5 %all_to_all.87.refs_0_ = bf16[4,192,576]{2,1,0:T(8,128)(2,1)} all-to-all(bf16[4,192,576]{2,1,0:T(8,128)(2,1)} %bitcast.212), channel_id=1, replica_groups=mesh['pair'=2,'core'=2,'half'=2,'quad'=2,'side'=2,'rest'=1] {'quad','side'}, dimensions={0} | all-to-all | bytes 1769472 | tf_op jit(solution)/shard_map/all_to_all | solution.py:566
  513.8 10.0 %shard_map.198 = (bf16[192,3072]{1,0:T(8,128)(2,1)}, f32[192,768]{1,0:T(8,128)}, bf16[192,768]{1,0:T(8,128)(2,1)}, bf16[4,192,192]{2,1,0:T(8,128)(2,1)}, f32[4,768]{1,0:T(4,128)}, /*index=5*/f32[1,3072]{1,0:T(1,128)}) custom-call(bf16[192,768]{1,0:T(8,128)(2,1)} %broadcast_select_fusion.21.g_ref, f32[192,3072]{1,0:T(8,128)} %get-tuple-element.92.slope_ref, ...), custom_call_target="tpu_custom_call" | custom-call | flops 2038431744 | bytes 14155776 | tf_op jit(solution)/shard_map/pallas_call | solution.py:415
  537.2 17.7 %shard_map.199 = (bf16[1,768,192]{2,1,0:T(8,128)(2,1)}, f32[1,768,384]{2,1,0:T(8,128)}, bf16[1,768,384]{2,1,0:T(8,128)(2,1)}) custom-call(bf16[1,768,576]{2,1,0:T(8,128)(2,1)} %bitcast.227, bf16[1,768,576]{2,1,0:T(8,128)(2,1)} %bitcast.228, bf16[1,768,576]{2,1,0:T(8,128)(2,1)} %bitcast.290, bf16[1,768,192]{2,1,0:T(8,128)(2,1)} %bitcast.35.refs_3_, ...), custom_call_target="tpu_custom_call" | custom-call | flops 9059696640 | bytes 7077888 | tf_op jit(solution)/shard_map/pallas_call | solution.py:241
  595.3 10.0 %shard_map.203 = (bf16[192,3072]{1,0:T(8,128)(2,1)}, f32[192,768]{1,0:T(8,128)}, bf16[192,768]{1,0:T(8,128)(2,1)}, bf16[4,192,192]{2,1,0:T(8,128)(2,1)}, f32[4,768]{1,0:T(4,128)}, /*index=5*/f32[1,3072]{1,0:T(1,128)}) custom-call(bf16[192,768]{1,0:T(8,128)(2,1)} %get-tuple-element.122.g_ref, f32[192,3072]{1,0:T(8,128)} %get-tuple-element.101.slope_ref, ...), custom_call_target="tpu_custom_call" | custom-call | flops 2038431744 | bytes 14155776 | tf_op jit(solution)/shard_map/pallas_call | solution.py:415
  639.3 17.7 %shard_map.206 = (bf16[1,768,192]{2,1,0:T(8,128)(2,1)}, f32[1,768,384]{2,1,0:T(8,128)}, bf16[1,768,384]{2,1,0:T(8,128)(2,1)}) custom-call(bf16[1,768,576]{2,1,0:T(8,128)(2,1)} %bitcast.221, bf16[1,768,576]{2,1,0:T(8,128)(2,1)} %bitcast.222, bf16[1,768,576]{2,1,0:T(8,128)(2,1)} %bitcast.287, bf16[1,768,192]{2,1,0:T(8,128)(2,1)} %bitcast.216, ...), custom_call_target="tpu_custom_call" | custom-call | flops 9059696640 | bytes 7077888 | tf_op jit(solution)/shard_map/pallas_call | solution.py:241
  719.5 11.7 %collective-permute-done.32.two_ref = bf16[272,2304]{1,0:T(8,128)(2,1)} collective-permute-done((bf16[272,2304]{1,0:T(8,128)(2,1)}, bf16[272,2304]{1,0:T(8,128)(2,1)}, u32[]{:S(2)}, u32[]{:S(2)}) %collective-permute-start.32) | collective-permute-done | bytes 1253408 | tf_op jit(solution)/shard_map/ppermute | solution.py:557
  759.8 16.6 %collective-permute-done.41 = bf16[768,768]{1,0:T(8,128)(2,1)} collective-permute-done((bf16[768,768]{1,0:T(8,128)(2,1)}, bf16[768,768]{1,0:T(8,128)(2,1)}, u32[]{:S(2)}, u32[]{:S(2)}) %collective-permute-start.41) | collective-permute-done | bytes 1179680 | tf_op jit(solution)/shard_map/ppermute | solution.py:725
  811.7 10.4 %collective-permute-done.42 = bf16[192,3072]{1,0:T(8,128)(2,1)} collective-permute-done((bf16[192,3072]{1,0:T(8,128)(2,1)}, bf16[192,3072]{1,0:T(8,128)(2,1)}, u32[]{:S(2)}, u32[]{:S(2)}) %collective-permute-start.42) | collective-permute-done | bytes 1179680 | tf_op jit(solution)/shard_map/ppermute | solution.py:725
  848.7 18.0 %collective-permute-done.45.two_ref = bf16[192,3072]{1,0:T(8,128)(2,1)} collective-permute-done((bf16[192,3072]{1,0:T(8,128)(2,1)S(1)}, bf16[192,3072]{1,0:T(8,128)(2,1)}, u32[]{:S(2)}, u32[]{:S(2)}) %collective-permute-start.45) | collective-permute-done | bytes 1179680 | tf_op jit(solution)/shard_map/ppermute | solution.py:725
  877.5 12.5 %collective-permute-done.43.two_ref = bf16[272,2304]{1,0:T(8,128)(2,1)S(1)} collective-permute-done((bf16[272,2304]{1,0:T(8,128)(2,1)}, bf16[272,2304]{1,0:T(8,128)(2,1)S(1)}, u32[]{:S(2)}, u32[]{:S(2)}) %collective-permute-start.43) | collective-permute-done | bytes 1253408 | tf_op jit(solution)/shard_map/ppermute | solution.py:725
  906.2 19.8 %collective-permute-done.50 = bf16[192,3072]{1,0:T(8,128)(2,1)S(1)} collective-permute-done((bf16[192,3072]{1,0:T(8,128)(2,1)}, bf16[192,3072]{1,0:T(8,128)(2,1)S(1)}, u32[]{:S(2)}, u32[]{:S(2)}) %collective-permute-start.50) | collective-permute-done | bytes 1179680 | tf_op jit(solution)/shard_map/ppermute | solution.py:725
  938.2 17.4 %collective-permute-done.51 = bf16[272,2304]{1,0:T(8,128)(2,1)S(1)} collective-permute-done((bf16[272,2304]{1,0:T(8,128)(2,1)}, bf16[272,2304]{1,0:T(8,128)(2,1)S(1)}, u32[]{:S(2)}, u32[]{:S(2)}) %collective-permute-start.51) | collective-permute-done | bytes 1253408 | tf_op jit(solution)/shard_map/ppermute | solution.py:725
  (550 shorter events, 482.5 us)
Async XLA Ops:
  7.2 83.6 %all-gather.4.cloned.1.call-start = ((), (), s32[]{:S(2)}) async-start(), calls=%async_computation.16 | async-start | bytes 10616832 | tf_op jit(solution)/shard_map/all_gather | solution.py:627
  14.3 151.0 %all-gather.6.cloned.1.call-start = ((), (), s32[]{:S(2)}) async-start(), calls=%async_computation.17 | async-start | bytes 10616832 | tf_op jit(solution)/shard_map/all_gather | solution.py:627
  15.1 197.2 %all-gather.8.cloned.1.call-start = ((), (), s32[]{:S(2)}) async-start(), calls=%async_computation.18 | async-start | bytes 5308416 | tf_op jit(solution)/shard_map/all_gather | solution.py:644
  27.9 39.8 %collective-permute-start.2 = (bf16[768,768]{1,0:T(8,128)(2,1)S(1)}, bf16[768,768]{1,0:T(8,128)(2,1)S(1)}, u32[]{:S(2)}, u32[]{:S(2)}) collective-permute-start(bf16[768,768]{1,0:T(8,128)(2,1)S(1)} %constant_dynamic-slice_fusion.32), channel_id=1, source_target_pairs={{0,1},{1,0},{2,3},{3,2},{4,5},{5,4},{6,7},{7,6},{8,9},{9,8},{10,11... | collective-permute-start | bytes 3538952 | tf_op jit(solution)/shard_map/ppermute | solution.py:557
  94.9 28.3 %all-to-all-start = ((bf16[4,192,576]{2,1,0:T(8,128)(2,1)}), bf16[4,192,576]{2,1,0:T(8,128)(2,1)}, u32[]{:S(2)}, u32[]{:S(2)}) async-start(bf16[4,192,576]{2,1,0:T(8,128)(2,1)} %get-tuple-element.82), calls=%async_computation | async-start | bytes 1966080 | tf_op jit(solution)/shard_map/all_to_all | solution.py:566
  530.3 51.2 %collective-permute-start.19 = (bf16[1536,768]{1,0:T(8,128)(2,1)}, bf16[1536,768]{1,0:T(8,128)(2,1)S(1)}, u32[]{:S(2)}, u32[]{:S(2)}) collective-permute-start(bf16[1536,768]{1,0:T(8,128)(2,1)} %convolution_convert_fusion.11.refs_5_), channel_id=1, source_target_pairs={{0,8},{8,0},{1,9},{9,1},{2,10},{10,2},{3,11},{11,3},{4,12},{12,4},... | collective-permute-start | bytes 7077896 | tf_op jit(solution)/shard_map/ppermute | solution.py:557
  571.0 49.0 %collective-permute-start.21 = (bf16[384,3072]{1,0:T(8,128)(2,1)}, bf16[384,3072]{1,0:T(8,128)(2,1)}, u32[]{:S(2)}, u32[]{:S(2)}) collective-permute-start(bf16[384,3072]{1,0:T(8,128)(2,1)} %convolution_convert_fusion.7.refs_7_), channel_id=1, source_target_pairs={{0,8},{8,0},{1,9},{9,1},{2,10},{10,2},{3,11},{11,3},{4,12},{12,4},... | collective-permute-start | bytes 7077896 | tf_op jit(solution)/shard_map/ppermute | solution.py:557
  587.8 44.2 %collective-permute-start.20 = (bf16[768,768]{1,0:T(8,128)(2,1)}, bf16[768,768]{1,0:T(8,128)(2,1)}, u32[]{:S(2)}, u32[]{:S(2)}) collective-permute-start(bf16[768,768]{1,0:T(8,128)(2,1)} %get-tuple-element.118.refs_5_), channel_id=1, source_target_pairs={{0,1},{1,0},{2,3},{3,2},{4,5},{5,4},{6,7},{7,6},{8,9},{9,8},{10,11... | collective-permute-start | bytes 3538952 | tf_op jit(solution)/shard_map/ppermute | solution.py:557
  612.1 56.7 %collective-permute-start.25 = (bf16[544,2304]{1,0:T(8,128)(2,1)}, bf16[544,2304]{1,0:T(8,128)(2,1)S(1)}, u32[]{:S(2)}, u32[]{:S(2)}) collective-permute-start(bf16[544,2304]{1,0:T(8,128)(2,1)} %bitcast.44.refs_8_), channel_id=1, source_target_pairs={{0,8},{8,0},{1,9},{9,1},{2,10},{10,2},{3,11},{11,3},{4,12},{12,4},... | collective-permute-start | bytes 7520264 | tf_op jit(solution)/shard_map/ppermute | solution.py:557
  614.5 80.0 %collective-permute-start.26 = (bf16[1536,768]{1,0:T(8,128)(2,1)}, bf16[1536,768]{1,0:T(8,128)(2,1)}, u32[]{:S(2)}, u32[]{:S(2)}) collective-permute-start(bf16[1536,768]{1,0:T(8,128)(2,1)} %convolution_convert_fusion.9.refs_10_), channel_id=1, source_target_pairs={{0,8},{8,0},{1,9},{9,1},{2,10},{10,2},{3,11},{11,3},{4,12},{12,4},... | collective-permute-start | bytes 7077896 | tf_op jit(solution)/shard_map/ppermute | solution.py:557
  617.2 81.8 %collective-permute-start.27 = (bf16[384,3072]{1,0:T(8,128)(2,1)}, bf16[384,3072]{1,0:T(8,128)(2,1)}, u32[]{:S(2)}, u32[]{:S(2)}) collective-permute-start(bf16[384,3072]{1,0:T(8,128)(2,1)} %convolution_convert_fusion.3.refs_12_), channel_id=1, source_target_pairs={{0,8},{8,0},{1,9},{9,1},{2,10},{10,2},{3,11},{11,3},{4,12},{12,4},... | collective-permute-start | bytes 7077896 | tf_op jit(solution)/shard_map/ppermute | solution.py:557
  625.7 31.4 %collective-permute-start.24 = (bf16[192,3072]{1,0:T(8,128)(2,1)}, bf16[192,3072]{1,0:T(8,128)(2,1)S(1)}, u32[]{:S(2)}, u32[]{:S(2)}) collective-permute-start(bf16[192,3072]{1,0:T(8,128)(2,1)} %get-tuple-element.124.refs_6_), channel_id=1, source_target_pairs={{0,1},{1,0},{2,3},{3,2},{4,5},{5,4},{6,7},{7,6},{8,9},{9,8},{10,11... | collective-permute-start | bytes 3538952 | tf_op jit(solution)/shard_map/ppermute | solution.py:557
  635.5 28.6 %collective-permute-start.23 = (bf16[768,768]{1,0:T(8,128)(2,1)}, bf16[768,768]{1,0:T(8,128)(2,1)S(1)}, u32[]{:S(2)}, u32[]{:S(2)}) collective-permute-start(bf16[768,768]{1,0:T(8,128)(2,1)} %shard_map.204.refs_5_.one_ref), channel_id=1, source_target_pairs={{0,2},{6,4},{1,3},{7,5},{8,10},{14,12},{9,11},{15,13},{16,18},{22,... | collective-permute-start | bytes 3538952 | tf_op jit(solution)/shard_map/ppermute | solution.py:725
  678.1 26.0 %all-to-all-start.15 = ((bf16[4,192,576]{2,1,0:T(8,128)(2,1)}), bf16[4,192,576]{2,1,0:T(8,128)(2,1)}, u32[]{:S(2)}, u32[]{:S(2)}) async-start(bf16[4,192,576]{2,1,0:T(8,128)(2,1)} %bitcast.210), calls=%async_computation.15 | async-start | bytes 1966080 | tf_op jit(solution)/shard_map/all_to_all | solution.py:566
  687.4 52.2 %collective-permute-start.36 = (bf16[192,3072]{1,0:T(8,128)(2,1)S(1)}, bf16[192,3072]{1,0:T(8,128)(2,1)}, u32[]{:S(2)}, u32[]{:S(2)}) collective-permute-start(bf16[192,3072]{1,0:T(8,128)(2,1)S(1)} %copy-done.8), channel_id=1, source_target_pairs={{0,2},{6,4},{1,3},{7,5},{8,10},{14,12},{9,11},{15,13},{16,18},{22,... | collective-permute-start | bytes 3538952 | tf_op jit(solution)/shard_map/ppermute | solution.py:725
  692.7 49.8 %collective-permute-start.35 = (bf16[768,768]{1,0:T(8,128)(2,1)S(1)}, bf16[768,768]{1,0:T(8,128)(2,1)}, u32[]{:S(2)}, u32[]{:S(2)}) collective-permute-start(bf16[768,768]{1,0:T(8,128)(2,1)S(1)} %copy-done.9), channel_id=1, source_target_pairs={{2,4},{4,2},{3,5},{5,3},{10,12},{12,10},{11,13},{13,11},{18,20},{2... | collective-permute-start | bytes 3538952 | tf_op jit(solution)/shard_map/ppermute | solution.py:725
  703.0 28.1 %collective-permute-start.32 = (bf16[272,2304]{1,0:T(8,128)(2,1)}, bf16[272,2304]{1,0:T(8,128)(2,1)}, u32[]{:S(2)}, u32[]{:S(2)}) collective-permute-start(bf16[272,2304]{1,0:T(8,128)(2,1)} %get-tuple-element.137.rest_2_), channel_id=1, source_target_pairs={{0,1},{1,0},{2,3},{3,2},{4,5},{5,4},{6,7},{7,6},{8,9},{9,8},{10,11... | collective-permute-start | bytes 3760136 | tf_op jit(solution)/shard_map/ppermute | solution.py:557
  713.7 65.3 %collective-permute-start.30 = (bf16[544,2304]{1,0:T(8,128)(2,1)}, bf16[544,2304]{1,0:T(8,128)(2,1)}, u32[]{:S(2)}, u32[]{:S(2)}) collective-permute-start(bf16[544,2304]{1,0:T(8,128)(2,1)} %bitcast.60.rest_1_), channel_id=1, source_target_pairs={{0,8},{8,0},{1,9},{9,1},{2,10},{10,2},{3,11},{11,3},{4,12},{12,4},... | collective-permute-start | bytes 7520264 | tf_op jit(solution)/shard_map/ppermute | solution.py:557
  746.1 30.3 %collective-permute-start.41 = (bf16[768,768]{1,0:T(8,128)(2,1)}, bf16[768,768]{1,0:T(8,128)(2,1)}, u32[]{:S(2)}, u32[]{:S(2)}) collective-permute-start(bf16[768,768]{1,0:T(8,128)(2,1)} %shard_map.217.rest_0_), channel_id=1, source_target_pairs={{2,0},{4,6},{3,1},{5,7},{10,8},{12,14},{11,9},{13,15},{18,16},{20,... | collective-permute-start | bytes 3538952 | tf_op jit(solution)/shard_map/ppermute | solution.py:725
  747.6 39.4 %collective-permute-start.33 = (bf16[272,2304]{1,0:T(8,128)(2,1)S(1)}, bf16[272,2304]{1,0:T(8,128)(2,1)}, u32[]{:S(2)}, u32[]{:S(2)}) collective-permute-start(bf16[272,2304]{1,0:T(8,128)(2,1)S(1)} %copy-done.3), channel_id=1, source_target_pairs={{0,2},{6,4},{1,3},{7,5},{8,10},{14,12},{9,11},{15,13},{16,18},{22,... | collective-permute-start | bytes 3760136 | tf_op jit(solution)/shard_map/ppermute | solution.py:725
  754.2 29.2 %collective-permute-start.34 = (bf16[768,768]{1,0:T(8,128)(2,1)}, bf16[768,768]{1,0:T(8,128)(2,1)}, u32[]{:S(2)}, u32[]{:S(2)}) collective-permute-start(bf16[768,768]{1,0:T(8,128)(2,1)} %get-tuple-element.140.refs_5_), channel_id=1, source_target_pairs={{0,1},{1,0},{2,3},{3,2},{4,5},{5,4},{6,7},{7,6},{8,9},{9,8},{10,11... | collective-permute-start | bytes 3538952 | tf_op jit(solution)/shard_map/ppermute | solution.py:557
  754.3 35.6 %collective-permute-start.40 = (bf16[192,3072]{1,0:T(8,128)(2,1)}, bf16[192,3072]{1,0:T(8,128)(2,1)}, u32[]{:S(2)}, u32[]{:S(2)}) collective-permute-start(bf16[192,3072]{1,0:T(8,128)(2,1)} %shard_map.216.rest_0_.one_ref), channel_id=1, source_target_pairs={{2,4},{4,2},{3,5},{5,3},{10,12},{12,10},{11,13},{13,11},{18,20},{2... | collective-permute-start | bytes 3538952 | tf_op jit(solution)/shard_map/ppermute | solution.py:725
  776.4 32.3 %collective-permute-start.39 = (bf16[192,3072]{1,0:T(8,128)(2,1)}, bf16[192,3072]{1,0:T(8,128)(2,1)}, u32[]{:S(2)}, u32[]{:S(2)}) collective-permute-start(bf16[192,3072]{1,0:T(8,128)(2,1)} %get-tuple-element.142.refs_7_), channel_id=1, source_target_pairs={{0,1},{1,0},{2,3},{3,2},{4,5},{5,4},{6,7},{7,6},{8,9},{9,8},{10,11... | collective-permute-start | bytes 3538952 | tf_op jit(solution)/shard_map/ppermute | solution.py:557
  793.0 29.0 %collective-permute-start.42 = (bf16[192,3072]{1,0:T(8,128)(2,1)}, bf16[192,3072]{1,0:T(8,128)(2,1)}, u32[]{:S(2)}, u32[]{:S(2)}) collective-permute-start(bf16[192,3072]{1,0:T(8,128)(2,1)} %shard_map.220.rest_0_), channel_id=1, source_target_pairs={{2,0},{4,6},{3,1},{5,7},{10,8},{12,14},{11,9},{13,15},{18,16},{20,... | collective-permute-start | bytes 3538952 | tf_op jit(solution)/shard_map/ppermute | solution.py:725
  794.4 35.8 %collective-permute-start.37 = (bf16[272,2304]{1,0:T(8,128)(2,1)S(1)}, bf16[272,2304]{1,0:T(8,128)(2,1)S(1)}, u32[]{:S(2)}, u32[]{:S(2)}) collective-permute-start(bf16[272,2304]{1,0:T(8,128)(2,1)S(1)} %copy-done.5), channel_id=1, source_target_pairs={{2,4},{4,2},{3,5},{5,3},{10,12},{12,10},{11,13},{13,11},{18,20},{2... | collective-permute-start | bytes 3760136 | tf_op jit(solution)/shard_map/ppermute | solution.py:725
  795.2 31.5 %collective-permute-start.38 = (bf16[768,768]{1,0:T(8,128)(2,1)S(1)}, bf16[768,768]{1,0:T(8,128)(2,1)}, u32[]{:S(2)}, u32[]{:S(2)}) collective-permute-start(bf16[768,768]{1,0:T(8,128)(2,1)S(1)} %copy-done.13), channel_id=1, source_target_pairs={{0,2},{6,4},{1,3},{7,5},{8,10},{14,12},{9,11},{15,13},{16,18},{22,... | collective-permute-start | bytes 3538952 | tf_op jit(solution)/shard_map/ppermute | solution.py:725
  804.0 38.1 %collective-permute-start.31 = (bf16[272,2304]{1,0:T(8,128)(2,1)S(1)}, bf16[272,2304]{1,0:T(8,128)(2,1)S(1)}, u32[]{:S(2)}, u32[]{:S(2)}) collective-permute-start(bf16[272,2304]{1,0:T(8,128)(2,1)S(1)} %copy-done.4), channel_id=1, source_target_pairs={{0,1},{1,0},{2,3},{3,2},{4,5},{5,4},{6,7},{7,6},{8,9},{9,8},{10,11... | collective-permute-start | bytes 3760136 | tf_op jit(solution)/shard_map/ppermute | solution.py:557
  834.4 35.2 %collective-permute-start.46 = (bf16[272,2304]{1,0:T(8,128)(2,1)}, bf16[272,2304]{1,0:T(8,128)(2,1)S(1)}, u32[]{:S(2)}, u32[]{:S(2)}) collective-permute-start(bf16[272,2304]{1,0:T(8,128)(2,1)} %shard_map.223.rest_0_), channel_id=1, source_target_pairs={{2,0},{4,6},{3,1},{5,7},{10,8},{12,14},{11,9},{13,15},{18,16},{20,... | collective-permute-start | bytes 3760136 | tf_op jit(solution)/shard_map/ppermute | solution.py:725
  835.7 31.0 %collective-permute-start.45 = (bf16[192,3072]{1,0:T(8,128)(2,1)S(1)}, bf16[192,3072]{1,0:T(8,128)(2,1)}, u32[]{:S(2)}, u32[]{:S(2)}) collective-permute-start(bf16[192,3072]{1,0:T(8,128)(2,1)S(1)} %copy-done.14), channel_id=1, source_target_pairs={{0,2},{6,4},{1,3},{7,5},{8,10},{14,12},{9,11},{15,13},{16,18},{22,... | collective-permute-start | bytes 3538952 | tf_op jit(solution)/shard_map/ppermute | solution.py:725
  841.3 29.5 %collective-permute-start.44 = (bf16[768,768]{1,0:T(8,128)(2,1)S(1)}, bf16[768,768]{1,0:T(8,128)(2,1)S(1)}, u32[]{:S(2)}, u32[]{:S(2)}) collective-permute-start(bf16[768,768]{1,0:T(8,128)(2,1)S(1)} %copy-done.15), channel_id=1, source_target_pairs={{2,4},{4,2},{3,5},{5,3},{10,12},{12,10},{11,13},{13,11},{18,20},{2... | collective-permute-start | bytes 3538952 | tf_op jit(solution)/shard_map/ppermute | solution.py:725
  846.1 43.9 %collective-permute-start.43 = (bf16[272,2304]{1,0:T(8,128)(2,1)}, bf16[272,2304]{1,0:T(8,128)(2,1)S(1)}, u32[]{:S(2)}, u32[]{:S(2)}) collective-permute-start(bf16[272,2304]{1,0:T(8,128)(2,1)} %shard_map.224.rest_0_.one_ref), channel_id=1, source_target_pairs={{0,2},{6,4},{1,3},{7,5},{8,10},{14,12},{9,11},{15,13},{16,18},{22,... | collective-permute-start | bytes 3760136 | tf_op jit(solution)/shard_map/ppermute | solution.py:725
  906.2 27.5 %collective-permute-start.54 = (bf16[768,768]{1,0:T(8,128)(2,1)S(1)}, bf16[768,768]{1,0:T(8,128)(2,1)}, u32[]{:S(2)}, u32[]{:S(2)}) collective-permute-start(bf16[768,768]{1,0:T(8,128)(2,1)S(1)} %get-tuple-element.154), channel_id=1, source_target_pairs={{0,8},{8,0},{1,9},{9,1},{2,10},{10,2},{3,11},{11,3},{4,12},{12,4},... | collective-permute-start | bytes 3538952 | tf_op jit(solution)/shard_map/ppermute | solution.py:557
  (155 other events, 1114.6 us)
Sparse Core Ops, SparseCore 0:
  14.4 76.2 all-gather.3
  92.3 72.9 all-gather.5
  167.5 41.7 all-gather.7
